TPU v7x, 32 devices: a whole 2x2x4 slice. The times are simulated.
32 devices in a mesh: groups: 2 (over y), patch: 4 (over z), tensor: 4 (over x, core).
Axes of the slice: x: 2, y: 2, z: 4, core: 2. Of those that a mesh axis runs over, the one named last changes fastest.
Arguments:
- hidden_in: bfloat16 [2048, 5120], P(('groups', 'patch'), 'tensor'), parts along dimension 0, may hold values from -10.5 to 10.5
- w_query: bfloat16 [5120, 3072], P('patch', 'tensor'), may hold values from -0.08385255 to 0.08385255
- w_key: bfloat16 [5120, 3072], P('patch', 'tensor'), may hold values from -0.08385255 to 0.08385255
- w_value: bfloat16 [5120, 3072], P('patch', 'tensor'), may hold values from -0.078125 to 0.078125
- w_out: bfloat16 [3072, 5120], P('tensor'), may hold values from -6 to 6
- stale_kv: bfloat16 [2, 2048, 3072], P(None, 'groups', 'tensor'), parts along dimension 1, may hold values from -6 to 6
Outputs:
- attended: bfloat16 [2048, 5120], P(('groups', 'patch'), 'tensor'), parts along dimension 0
- refreshed: bfloat16 [2, 2048, 3072], P(None, 'groups', 'tensor'), parts along dimension 1
There are 2 independent parts, one for each index of `groups`. A program takes and returns all parts, laid end to end along the dimension named above; an argument that names none is the same for every part. Nothing has to cross between parts.
All inputs are finite; a program needn't handle non-finite values.
Results may differ from a plain program's by a relative error of at most 0.0073.
Values may be sent and summed in bfloat16 or wider, within the bound.
No kernel may reach another device: no remote copies, remote signals or barrier semaphores. Data moves between devices by JAX's collectives and lax.ppermute only.
A program may use at most 128 MiB of HBM per device.

v0:
```python
import jax
import jax.numpy as jnp
from jax import lax
from jax.sharding import PartitionSpec as P

HEAD_DIM = 128


def shards(hidden_in, w_query, w_key, w_value, w_out, stale_kv):
    features = lax.all_gather(hidden_in, "tensor", axis=1, tiled=True)
    rows = features.shape[0]
    width = w_query.shape[1]

    def add_rows(piece):
        return jnp.dot(features, piece, preferred_element_type=jnp.float32)

    slab_start = lax.axis_index("patch") * rows
    own_stale = lax.dynamic_slice_in_dim(stale_kv, slab_start, rows, 1).astype(jnp.float32)
    pieces = (
        lax.all_gather(w_query, "patch", axis=0, tiled=True),
        lax.all_gather(w_key, "patch", axis=0, tiled=True),
        lax.all_gather(w_value, "patch", axis=0, tiled=True),
    )
    query_sum, key_sum, value_sum = tuple((add_rows(piece) for piece in pieces))
    fresh = jnp.stack([key_sum.astype(jnp.bfloat16), value_sum.astype(jnp.bfloat16)]).astype(
        jnp.float32
    )
    moved = lax.all_gather((fresh - own_stale).astype(jnp.bfloat16), "patch", axis=1, tiled=True)
    query = query_sum.astype(jnp.bfloat16)
    refreshed = (stale_kv.astype(jnp.float32) + moved.astype(jnp.float32)).astype(jnp.bfloat16)
    own_new = lax.dynamic_slice_in_dim(refreshed, slab_start, rows, 1)
    used = lax.dynamic_update_slice_in_dim(stale_kv, own_new, slab_start, 1)
    heads = width // HEAD_DIM
    query_h = query.reshape(rows, heads, HEAD_DIM)
    keys_h = used[0].reshape(-1, heads, HEAD_DIM)
    values_h = used[1].reshape(-1, heads, HEAD_DIM)
    scale = 1.0 / HEAD_DIM**0.5
    scores = jnp.einsum("thd,shd->hts", query_h, keys_h, preferred_element_type=jnp.float32) * scale
    top = jnp.max(scores, axis=-1, keepdims=True)
    expo = jnp.exp(scores - top)
    total = jnp.sum(expo, axis=-1)
    weights = expo.astype(jnp.bfloat16)
    mixed = jnp.einsum("hts,shd->thd", weights, values_h, preferred_element_type=jnp.float32)
    mixed = mixed / jnp.transpose(total)[:, :, None]
    heads_out = mixed.astype(jnp.bfloat16).reshape(rows, width)
    partial_value = jnp.dot(heads_out, w_out, preferred_element_type=jnp.float32)
    summed = lax.psum_scatter(partial_value, "tensor", scatter_dimension=1, tiled=True)
    return (summed.astype(jnp.bfloat16), refreshed)


def solution(mesh):
    in_specs = (
        P(("groups", "patch"), "tensor"),
        P("patch", "tensor"),
        P("patch", "tensor"),
        P("patch", "tensor"),
        P("tensor", None),
        P(None, "groups", "tensor"),
    )
    out_specs = (P(("groups", "patch"), "tensor"), P(None, "groups", "tensor"))
    return jax.shard_map(shards, mesh=mesh, in_specs=in_specs, out_specs=out_specs, check_vma=False)
```

profile of v0, /device:TPU:0, one launch (start us, length us, event | category | flops | bytes accessed | tf_op | source)
XLA Modules:
  0.0 604.1 jit_solution(14057038659399216054)
XLA Ops:
  7.2 0.0 all-gather.6.cloned.1.call-start
  7.2 0.7 all-gather.6.cloned.1.call-update
  7.9 0.0 all-gather.8.cloned.1.call-start
  7.9 0.7 all-gather.8.cloned.1.call-update
  8.6 0.0 all-gather.10.cloned.1.call-start
  8.7 0.7 all-gather.10.cloned.1.call-update
  9.4 0.0 all-gather.14.cloned.1.call-start
  9.4 0.5 all-gather.14.cloned.1.call-update
  10.0 0.0 all-gather.12.cloned.1.call-start
  10.0 27.8 %all-gather.6.cloned.1.call-done = bf16[256,5120]{1,0:T(8,128)(2,1)} async-done(((bf16[256,1280]{1,0:T(8,128)(2,1)}), bf16[256,5120]{1,0:T(8,128)(2,1)}) %all-gather.6.cloned.1.call-update) | async-done | bytes 2621456 | tf_op jit(solution)/shard_map/all_gather | solution.py:10
  37.8 142.7 %all-gather.8.cloned.1.call-done = bf16[5120,768]{1,0:T(8,128)(2,1)} async-done(((bf16[1280,768]{1,0:T(8,128)(2,1)}), bf16[5120,768]{1,0:T(8,128)(2,1)}) %all-gather.8.cloned.1.call-update) | async-done | bytes 7864336 | tf_op jit(solution)/shard_map/all_gather | solution.py:21
  180.5 6.2 %fusion.9 = bf16[1,256,768]{2,1,0:T(8,128)(2,1)S(1)} fusion(bf16[256,5120]{1,0:T(8,128)(2,1)} %all-gather.6.cloned.1.call-done, bf16[5120,768]{1,0:T(8,128)(2,1)} %all-gather.8.cloned.1.call-done), kind=kOutput, calls=%fused_computation.13 | convolution fusion | flops 2013462528 | bytes 10878976 | tf_op jit(solution)/shard_map/dot_general | solution.py:15
  186.7 0.0 copy-start
  186.8 134.7 %all-gather.10.cloned.1.call-done = bf16[5120,768]{1,0:T(8,128)(2,1)} async-done(((bf16[1280,768]{1,0:T(8,128)(2,1)}), bf16[5120,768]{1,0:T(8,128)(2,1)}) %all-gather.10.cloned.1.call-update) | async-done | bytes 7864336 | tf_op jit(solution)/shard_map/all_gather | solution.py:22
  321.4 6.2 %fusion.10 = bf16[1,256,768]{2,1,0:T(8,128)(2,1)S(1)} fusion(bf16[256,5120]{1,0:T(8,128)(2,1)} %all-gather.6.cloned.1.call-done, bf16[5120,768]{1,0:T(8,128)(2,1)} %all-gather.10.cloned.1.call-done), kind=kOutput, calls=%fused_computation.14 | convolution fusion | flops 2013462528 | bytes 10878976 | tf_op jit(solution)/shard_map/dot_general | solution.py:15
  327.7 0.0 copy-done
  327.7 1.1 subtract_convert_fusion
  328.8 0.0 all-gather.12.cloned.1.call-update
  328.8 0.2 reduce-scatter.2.cloned.1.call-start
  329.0 3.0 copy.10
  332.0 130.2 %all-gather.14.cloned.1.call-done = bf16[5120,768]{1,0:T(8,128)(2,1)} async-done(((bf16[1280,768]{1,0:T(8,128)(2,1)}), bf16[5120,768]{1,0:T(8,128)(2,1)}) %all-gather.14.cloned.1.call-update) | async-done | bytes 7864336 | tf_op jit(solution)/shard_map/all_gather | solution.py:20
  462.2 7.0 %convolution_convert_fusion = bf16[256,768]{1,0:T(8,128)(2,1)} fusion(bf16[256,5120]{1,0:T(8,128)(2,1)} %all-gather.6.cloned.1.call-done, bf16[5120,768]{1,0:T(8,128)(2,1)} %all-gather.14.cloned.1.call-done), kind=kOutput, calls=%fused_computation.10 | convolution fusion | flops 2013462528 | bytes 10878976 | tf_op jit(solution)/shard_map/dot_general | solution.py:15
  469.2 1.2 copy.12
  470.4 55.5 %all-gather.12.cloned.1.call-done = bf16[2,1024,768]{2,1,0:T(8,128)(2,1)} async-done(((bf16[2,256,768]{2,1,0:T(8,128)(2,1)}), bf16[2,1024,768]{2,1,0:T(8,128)(2,1)}) %all-gather.12.cloned.1.call-update) | async-done | bytes 3145744 | tf_op jit(solution)/shard_map/all_gather | solution.py:28
  525.9 2.6 add_convert_fusion
  528.5 0.0 copy-start.2
  528.6 1.7 copy-done.2
  530.2 0.0 copy-start.1
  530.2 1.0 constant_dynamic-slice_fusion
  531.2 2.6 copy.11
  533.7 0.0 copy-done.1
  533.7 1.2 constant_dynamic-update-slice_fusion
  535.0 0.3 fusion.18
  535.3 1.1 multiply_reduce_fusion
  536.4 0.0 slice-start
  536.4 1.3 fusion
  537.8 0.0 slice-start.1
  537.8 1.5 fusion.14
  539.2 0.0 slice-done
  539.2 0.8 slice-done.1
  540.0 4.7 fusion.19
  544.7 0.0 reduce-scatter.2.cloned.1.call-update
  544.8 50.2 %reduce-scatter.2.cloned.1.call-done = f32[256,1280]{1,0:T(8,128)} async-done(((f32[256,5120]{1,0:T(8,128)}), f32[256,1280]{1,0:T(8,128)}) %reduce-scatter.2.cloned.1.call-update) | async-done | bytes 1310736 | tf_op jit(solution)/shard_map/reduce_scatter | solution.py:47
  595.0 2.2 convert_element_type.47
  (1 shorter events, 0.0 us)
Async XLA Ops:
  7.2 30.7 %all-gather.6.cloned.1.call-start = ((), (), s32[]{:S(2)}) async-start(), calls=%async_computation.1 | async-start | bytes 3276800 | tf_op jit(solution)/shard_map/all_gather | solution.py:10
  7.9 172.6 %all-gather.8.cloned.1.call-start = ((), (), s32[]{:S(2)}) async-start(), calls=%async_computation.2 | async-start | bytes 9830400 | tf_op jit(solution)/shard_map/all_gather | solution.py:21
  8.6 312.8 %all-gather.10.cloned.1.call-start = ((), (), s32[]{:S(2)}) async-start(), calls=%async_computation.3 | async-start | bytes 9830400 | tf_op jit(solution)/shard_map/all_gather | solution.py:22
  9.4 452.8 %all-gather.14.cloned.1.call-start = ((), (), s32[]{:S(2)}) async-start(), calls=%async_computation.5 | async-start | bytes 9830400 | tf_op jit(solution)/shard_map/all_gather | solution.py:20
  10.0 515.9 %all-gather.12.cloned.1.call-start = ((), (), s32[]{:S(2)}) async-start(), calls=%async_computation.4 | async-start | bytes 3932160 | tf_op jit(solution)/shard_map/all_gather | solution.py:28
  186.7 140.9 %copy-start = (bf16[2,1024,768]{2,1,0:T(8,128)(2,1)S(1)}, bf16[2,1024,768]{2,1,0:T(8,128)(2,1)}, u32[]{:S(2)}) copy-start(bf16[2,1024,768]{2,1,0:T(8,128)(2,1)} %param.11) | copy-start | bytes 9437188
  328.8 266.2 %reduce-scatter.2.cloned.1.call-start = ((), (), s32[]{:S(2)}) async-start(), calls=%async_computation.6 | async-start | bytes 6553600 | tf_op jit(solution)/shard_map/reduce_scatter | solution.py:47
  528.5 1.7 copy-start.2
  530.2 3.5 copy-start.1
  536.4 2.8 slice-start
  537.8 2.3 slice-start.1
Sparse Core Ops, SparseCore 0:
  9.6 28.2 all-gather.5
  39.4 141.0 all-gather.7
  182.1 139.2 all-gather.9
  322.9 139.2 all-gather.13
  464.2 61.6 all-gather.11
  544.9 50.0 reduce-scatter.1
where the time goes:
time: 604 us
  waiting for transfers between devices  544 us (90%)
  matrix products  26.7 us (4%)
  between operations  14.2 us (2%)
  local copies, waits for them, and re-layouts  11.7 us (2%)
  other arithmetic  7.28 us (1%)
    all_gather x1, waiting for transfers between devices, shards(): lax.all_gather(w_key, 'patch', axis=0, tiled=True)  143 us
    all_gather x1, waiting for transfers between devices, shards(): lax.all_gather(w_value, 'patch', axis=0, tiled=True)  135 us
    all_gather x1, waiting for transfers between devices, shards(): lax.all_gather(w_query, 'patch', axis=0, tiled=True)  130 us
    all_gather x1, waiting for transfers between devices, shards(): lax.all_gather((fresh - own_stale).astype(jnp.bfloat16), 'patch', axis=1,...  55.5 us
    reduce_scatter x1, waiting for transfers between devices, shards(): lax.psum_scatter(partial_value, 'tensor', scatter_dimension=1, tiled=True)  50.2 us
    all_gather x1, waiting for transfers between devices, shards(): features = lax.all_gather(hidden_in, 'tensor', axis=1, tiled=True)  27.8 us
    dot_general x3, matrix products, add_rows(): return jnp.dot(features, piece, preferred_element_type=jnp.float32)  19.4 us
  transfers between devices with their start and end apart: 6, of which 6 were waited for; matrix products, arithmetic and copies ran while one was open for 4% of the time, Pallas kernels for 0%

commit v1 on v0

v1 whole, which is shorter than its diff:
```python
import jax
import jax.numpy as jnp
from jax import lax
from jax.sharding import PartitionSpec as P

HEAD_DIM = 128
F32 = jnp.float32
BF16 = jnp.bfloat16


def spread_features(hidden, patches, ranks):
    if patches == ranks and ranks % 2 == 0:
        half = ranks // 2
        place = [(s % half) * 2 + s // half for s in range(patches)]
        pairs = [(s * ranks + t, t * ranks + place[s]) for s in range(patches) for t in range(ranks)]
        block = lax.ppermute(hidden, ("patch", "tensor"), pairs)
        return lax.all_gather(block, "tensor", axis=0, tiled=True), lambda s: (s % half) * 2 + s // half
    features = lax.all_gather(hidden, "tensor", axis=1, tiled=True)
    return lax.all_to_all(features, "patch", split_axis=1, concat_axis=0, tiled=True), lambda s: s


def sum_own_slab(parts, rows, place, patches):
    me = lax.axis_index("patch")

    def mine(slab):
        slab = jnp.clip(slab, 0, patches - 1)
        return lax.dynamic_slice_in_dim(parts, place(slab) * rows, rows, 0)

    up = down = None
    for step in range(1, patches):
        send_up = mine(patches - step + me)
        send_down = mine(step - patches + me)
        if step > 1:
            send_up = send_up + up.astype(F32)
            send_down = send_down + down.astype(F32)
        up = lax.ppermute(send_up.astype(BF16), "patch", [(i, i + 1) for i in range(step)])
        down = lax.ppermute(
            send_down.astype(BF16), "patch", [(patches - 1 - i, patches - 2 - i) for i in range(step)]
        )
    total = mine(me)
    if patches > 1:
        total = total + (up.astype(F32) + down.astype(F32))
    return total


def sum_columns(heads_out, w_out, ranks):
    rank = lax.axis_index("tensor")
    core, chip, chips = rank % 2, rank // 2, ranks // 2
    depth = w_out.shape[0]
    width = w_out.shape[1] // ranks
    by_core = w_out.reshape(depth, chips, 2, width)

    def columns(which):
        picked = lax.dynamic_index_in_dim(by_core, which, 2, keepdims=False)
        return jnp.dot(heads_out, picked.reshape(depth, chips * width), preferred_element_type=F32)

    swap = [(r, r ^ 1) for r in range(ranks)]
    other = lax.ppermute(columns(1 - core).astype(BF16), "tensor", swap)
    both = columns(core) + other.astype(F32)
    if chips == 1:
        return both.astype(BF16)
    both = both.reshape(-1, chips, width)
    total = None
    for hop in range(1, chips):
        target = (chip + hop) % chips
        block = lax.dynamic_index_in_dim(both, target, 1, keepdims=False)
        pairs = [(r, (r + 2 * hop) % ranks) for r in range(ranks)]
        got = lax.ppermute(block.astype(BF16), "tensor", pairs).astype(F32)
        total = got if total is None else total + got
    total = total + lax.dynamic_index_in_dim(both, chip, 1, keepdims=False)
    return total.astype(BF16)


def make_shards(patches, ranks):
    def shards(hidden_in, w_query, w_key, w_value, w_out, stale_kv):
        rows = hidden_in.shape[0]
        width = w_query.shape[1]
        heads = width // HEAD_DIM
        me = lax.axis_index("patch")
        features, place = spread_features(hidden_in, patches, ranks)

        def project(weight):
            parts = jnp.dot(features, weight, preferred_element_type=F32)
            return sum_own_slab(parts, rows, place, patches).astype(BF16)

        own_stale = lax.dynamic_slice_in_dim(stale_kv, me * rows, rows, 1).astype(F32)

        def refresh(fresh, stale):
            delta = (fresh.astype(F32) - stale).astype(BF16)
            return (stale + delta.astype(F32)).astype(BF16)

        key_new = refresh(project(w_key), own_stale[0])
        query = project(w_query)
        value_new = refresh(project(w_value), own_stale[1])
        keys_all = lax.all_gather(key_new, "patch", axis=0, tiled=True)
        values_all = lax.all_gather(value_new, "patch", axis=0, tiled=True)
        refreshed = jnp.stack([keys_all, values_all])

        def split(matrix):
            return matrix.reshape(-1, heads, HEAD_DIM)

        scale = 1.0 / HEAD_DIM**0.5
        query_h = split(query)

        def score(keys):
            return jnp.einsum("thd,shd->hts", query_h, split(keys), preferred_element_type=F32) * scale

        slab_of = jnp.arange(stale_kv.shape[1], dtype=jnp.int32) // rows
        old = jnp.where(slab_of[None, None, :] == me, -jnp.inf, score(stale_kv[0]))
        new = score(key_new)
        top = jnp.maximum(jnp.max(old, -1, keepdims=True), jnp.max(new, -1, keepdims=True))
        old, new = jnp.exp(old - top), jnp.exp(new - top)
        total = jnp.sum(old, -1) + jnp.sum(new, -1)

        def mix(weights, values):
            return jnp.einsum(
                "hts,shd->thd", weights.astype(BF16), split(values), preferred_element_type=F32
            )

        mixed = mix(old, stale_kv[1]) + mix(new, value_new)
        mixed = mixed / jnp.transpose(total)[:, :, None]
        heads_out = mixed.astype(BF16).reshape(rows, width)
        return (sum_columns(heads_out, w_out, ranks), refreshed)

    return shards


def solution(mesh):
    in_specs = (
        P(("groups", "patch"), "tensor"),
        P("patch", "tensor"),
        P("patch", "tensor"),
        P("patch", "tensor"),
        P("tensor", None),
        P(None, "groups", "tensor"),
    )
    out_specs = (P(("groups", "patch"), "tensor"), P(None, "groups", "tensor"))
    return jax.shard_map(
        make_shards(mesh.shape["patch"], mesh.shape["tensor"]),
        mesh=mesh,
        in_specs=in_specs,
        out_specs=out_specs,
        check_vma=False,
    )
```

time: 604 us -> 256 us (0.42)
  waiting for transfers between devices: 544 us -> 114 us
  starting transfers between devices: 0.41 us -> 43.9 us
  local copies, waits for them, and re-layouts: 11.7 us -> 43.7 us
  other arithmetic: 7.28 us -> 20.1 us
  matrix products: 26.7 us -> 19.3 us
    all_gather x5 -> x3, waiting for transfers between devices: 491 us -> 67.8 us  [the longest x1 39.3 us: spread_features(): lax.all_gather(block, 'tensor', axis=0, tiled=True)]
    reduce_scatter x1 -> x0, waiting for transfers between devices: 50.2 us -> none  [shards(): lax.psum_scatter(partial_value, 'tensor', scatter_dimension=1, tiled=True)]
    ppermute x0 -> x21, waiting for transfers between devices: none -> 46 us  [the longest x9 22.8 us: sum_own_slab(): lax.ppermute(send_up.astype(BF16), 'patch', [(i, i + 1) for i in range(st...]
    ppermute x0 -> x21, starting transfers between devices: none -> 43.8 us  [the longest x9 32.3 us: sum_own_slab(): lax.ppermute(send_up.astype(BF16), 'patch', [(i, i + 1) for i in range(st...]
    unnamed x11 -> x33, local copies, waits for them, and re-layouts: 5.4 us -> 20 us
    dynamic_slice x2 -> x4, local copies, waits for them, and re-layouts: 3.52 us -> 13.9 us  [the longest x1 6.92 us: columns(): picked = lax.dynamic_index_in_dim(by_core, which, 2, keepdims=False)]
    convert_element_type x3 -> x13, other arithmetic: 5.95 us -> 14.3 us  [the longest x3 3.88 us: sum_own_slab(): send_down.astype(BF16)]
    dot_general x6 -> x9, matrix products: 26.7 us -> 19.3 us  [the longest x3 8.62 us: project(): parts = jnp.dot(features, weight, preferred_element_type=F32)]
  transfers between devices with their start and end apart: 6 -> 24, of which waited for: 6 -> 12; matrix products, arithmetic and copies ran while one was open for 4% -> 27% of each run, Pallas kernels for 0% -> 0%
where the time goes in v1:
time: 256 us; the launch traced here: 255 us
  waiting for transfers between devices  114 us (45%)
  starting transfers between devices  43.9 us (17%)
  local copies, waits for them, and re-layouts  43.7 us (17%)
  other arithmetic  20.1 us (8%)
  matrix products  19.3 us (8%)
  between operations  14.3 us (6%)
    all_gather x1, waiting for transfers between devices, spread_features(): lax.all_gather(block, 'tensor', axis=0, tiled=True)  39.3 us
    ppermute x9, starting transfers between devices, sum_own_slab(): lax.ppermute(send_up.astype(BF16), 'patch', [(i, i + 1) for i in range(st...  32.3 us
    all_gather x1, waiting for transfers between devices, shards(): keys_all = lax.all_gather(key_new, 'patch', axis=0, tiled=True)  28.5 us
    ppermute x9, waiting for transfers between devices, sum_own_slab(): lax.ppermute(send_up.astype(BF16), 'patch', [(i, i + 1) for i in range(st...  22.8 us
    unnamed x33, local copies, waits for them, and re-layouts  20 us
    ppermute x1, waiting for transfers between devices, sum_columns(): got = lax.ppermute(block.astype(BF16), 'tensor', pairs).astype(F32)  13.3 us
    ppermute x9, starting transfers between devices, sum_own_slab(): lax.ppermute(send_down.astype(BF16), 'patch', [(patches - 1 - i, patches...  8.96 us
    dot_general x3, matrix products, project(): parts = jnp.dot(features, weight, preferred_element_type=F32)  8.62 us
  transfers between devices with their start and end apart: 24, of which 12 were waited for; matrix products, arithmetic and copies ran while one was open for 27% of the time, Pallas kernels for 0%

profile of v1, /device:TPU:0, one launch (start us, length us, event | category | flops | bytes accessed | tf_op | source)
XLA Modules:
  0.0 255.3 jit_solution(35078410932774989)
XLA Ops:
  7.2 1.9 collective-permute-start
  9.1 0.8 copy-done.10
  10.1 10.7 %copy.34 = bf16[768,5120]{0,1:T(8,128)(2,1)} copy(bf16[768,5120]{1,0:T(8,128)(2,1)} %param.10) | data formatting | bytes 15728640 | tf_op args[4]
  20.8 3.3 %fusion.27 = (bf16[1,1024,768]{2,1,0:T(8,128)(2,1)}, bf16[1,1024,768]{2,1,0:T(8,128)(2,1)S(1)}) fusion(bf16[2,1024,768]{2,1,0:T(8,128)(2,1)} %param.11), kind=kLoop, calls=%fused_computation.70 | loop fusion | bytes 6291456 | tf_op jit(solution)/shard_map/slice | solution.py:109
  24.1 6.9 %constant_dynamic-slice_fusion.2 = (bf16[768,2,1,1280]{0,3,2,1:T(8,128)(2,1)}, bf16[768,2,1,1280]{0,3,2,1:T(8,128)(2,1)}) fusion(bf16[768,2,2,1280]{0,3,2,1:T(8,128)(2,1)} %bitcast.54, s32[]{:T(128)S(6)} %select_n.197, s32[]{:T(128)S(6)} %select_n.196), kind=kLoop, calls=%fused_computation.60 | loop fusion | bytes 15728648 | tf_op jit(solution)/shard_map/jit(dynamic_index_in_dim)/dynamic_slice | solution.py:54
  31.0 39.3 %all-gather.4.cloned.1.call-done = bf16[1024,1280]{1,0:T(8,128)(2,1)} async-done(((bf16[256,1280]{1,0:T(8,128)(2,1)}), bf16[1024,1280]{1,0:T(8,128)(2,1)}) %all-gather.4.cloned.1.call-update) | async-done | bytes 2621456 | tf_op jit(solution)/shard_map/all_gather | solution.py:17
  70.3 4.1 %fusion.31 = f32[1024,768]{0,1:T(8,128)S(1)} fusion(bf16[1024,1280]{1,0:T(8,128)(2,1)} %all-gather.4.cloned.1.call-done, bf16[1280,768]{1,0:T(8,128)(2,1)S(1)} %copy-done), kind=kOutput, calls=%fused_computation.74 | convolution fusion | flops 2013265920 | bytes 7733248 | tf_op jit(solution)/shard_map/dot_general | solution.py:83
  74.5 3.4 %collective-permute-start.13 = (bf16[256,768]{0,1:T(8,128)(2,1)S(1)}, bf16[256,768]{0,1:T(8,128)(2,1)S(1)}, u32[]{:S(2)}, u32[]{:S(2)}) collective-permute-start(bf16[256,768]{0,1:T(8,128)(2,1)S(1)} %get-tuple-element.12), channel_id=1, source_target_pairs={{0,4},{1,5},{2,6},{3,7},{16,20},{17,21},{18,22},{19,23}} | collective-permute-start | bytes 1179656 | tf_op jit(solution)/shard_map/ppermute | solution.py:36
  78.0 0.8 collective-permute-start.16
  78.8 2.2 fusion.30
  81.2 1.3 collective-permute-start.7
  82.5 2.2 fusion.29
  84.9 1.3 collective-permute-start.1
  86.3 0.7 collective-permute-start.4
  86.9 0.4 collective-permute-done.13
  87.4 0.7 collective-permute-start.10
  88.2 7.6 %collective-permute-done.7 = bf16[256,768]{0,1:T(8,128)(2,1)S(1)} collective-permute-done((bf16[256,768]{0,1:T(8,128)(2,1)S(1)}, bf16[256,768]{0,1:T(8,128)(2,1)S(1)}, u32[]{:S(2)}, u32[]{:S(2)}) %collective-permute-start.7) | collective-permute-done | bytes 393248 | tf_op jit(solution)/shard_map/ppermute | solution.py:36
  95.8 4.4 %collective-permute-start.14 = (bf16[256,768]{0,1:T(8,128)(2,1)S(1)}, bf16[256,768]{0,1:T(8,128)(2,1)S(1)}, u32[]{:S(2)}, u32[]{:S(2)}) collective-permute-start(bf16[256,768]{0,1:T(8,128)(2,1)S(1)} %add_convert_fusion.5), channel_id=1, source_target_pairs={{0,4},{4,8},{1,5},{5,9},{2,6},{6,10},{3,7},{7,11},{16,20},{20,24},... | collective-permute-start | bytes 1179656 | tf_op jit(solution)/shard_map/ppermute | solution.py:36
  100.4 3.9 %collective-permute-done.1 = bf16[256,768]{0,1:T(8,128)(2,1)S(1)} collective-permute-done((bf16[256,768]{0,1:T(8,128)(2,1)S(1)}, bf16[256,768]{0,1:T(8,128)(2,1)S(1)}, u32[]{:S(2)}, u32[]{:S(2)}) %collective-permute-start.1) | collective-permute-done | bytes 393248 | tf_op jit(solution)/shard_map/ppermute | solution.py:36
  104.2 4.4 %collective-permute-start.8 = (bf16[256,768]{0,1:T(8,128)(2,1)S(1)}, bf16[256,768]{0,1:T(8,128)(2,1)S(1)}, u32[]{:S(2)}, u32[]{:S(2)}) collective-permute-start(bf16[256,768]{0,1:T(8,128)(2,1)S(1)} %add_convert_fusion.11), channel_id=1, source_target_pairs={{0,4},{4,8},{1,5},{5,9},{2,6},{6,10},{3,7},{7,11},{16,20},{20,24},... | collective-permute-start | bytes 1179656 | tf_op jit(solution)/shard_map/ppermute | solution.py:36
  108.8 1.9 collective-permute-start.2
  110.8 1.9 collective-permute-done.14
  112.7 1.0 add_convert_fusion.4
  113.7 4.4 %collective-permute-start.15 = (bf16[256,768]{0,1:T(8,128)(2,1)}, bf16[256,768]{0,1:T(8,128)(2,1)S(1)}, u32[]{:S(2)}, u32[]{:S(2)}) collective-permute-start(bf16[256,768]{0,1:T(8,128)(2,1)} %get-tuple-element.10), channel_id=1, source_target_pairs={{0,4},{4,8},{8,12},{1,5},{5,9},{9,13},{2,6},{6,10},{10,14},{3,7},{... | collective-permute-start | bytes 1179656 | tf_op jit(solution)/shard_map/ppermute | solution.py:36
  118.1 0.7 collective-permute-start.17
  118.8 2.3 collective-permute-done.8
  121.1 1.0 add_convert_fusion.10
  122.2 0.7 collective-permute-start.11
  122.8 6.7 %collective-permute-done.2 = bf16[256,768]{0,1:T(8,128)(2,1)S(1)} collective-permute-done((bf16[256,768]{0,1:T(8,128)(2,1)S(1)}, bf16[256,768]{0,1:T(8,128)(2,1)S(1)}, u32[]{:S(2)}, u32[]{:S(2)}) %collective-permute-start.2) | collective-permute-done | bytes 393248 | tf_op jit(solution)/shard_map/ppermute | solution.py:36
  129.5 1.2 add_convert_fusion.15
  130.7 1.4 collective-permute-start.5
  132.1 5.1 %collective-permute-start.9 = (bf16[256,768]{0,1:T(8,128)(2,1)}, bf16[256,768]{0,1:T(8,128)(2,1)}, u32[]{:S(2)}, u32[]{:S(2)}) collective-permute-start(bf16[256,768]{0,1:T(8,128)(2,1)} %get-tuple-element.14), channel_id=1, source_target_pairs={{0,4},{4,8},{8,12},{1,5},{5,9},{9,13},{2,6},{6,10},{10,14},{3,7},{... | collective-permute-start | bytes 1179656 | tf_op jit(solution)/shard_map/ppermute | solution.py:36
  137.2 0.9 add_convert_fusion.2
  138.1 1.3 collective-permute-start.18
  139.4 0.9 add_convert_fusion.8
  140.3 1.5 collective-permute-start.12
  141.8 1.2 constant_dynamic-slice_fusion.4
  143.3 1.3 convert_element_type.184
  144.5 1.7 copy.43
  146.2 1.7 copy.32
  147.9 6.1 %collective-permute-start.3 = (bf16[256,768]{0,1:T(8,128)(2,1)}, bf16[256,768]{0,1:T(8,128)(2,1)}, u32[]{:S(2)}, u32[]{:S(2)}) collective-permute-start(bf16[256,768]{0,1:T(8,128)(2,1)} %get-tuple-element.20), channel_id=1, source_target_pairs={{0,4},{4,8},{8,12},{1,5},{5,9},{9,13},{2,6},{6,10},{10,14},{3,7},{... | collective-permute-start | bytes 1179656 | tf_op jit(solution)/shard_map/ppermute | solution.py:36
  154.0 2.1 add_convert_fusion.13
  156.1 1.3 collective-permute-start.6
  157.4 0.7 collective-permute-done.12
  158.2 3.0 %add_convert_fusion = (bf16[256,768]{0,1:T(8,128)(2,1)}, bf16[256,768]{0,1:T(8,128)(2,1)}) fusion(f32[2,256,768]{1,2,0:T(8,128)S(1)} %copy-done.5, bf16[256,768]{0,1:T(8,128)(2,1)} %collective-permute-done.18, bf16[256,768]{0,1:T(8,128)(2,1)S(1)} %collective-permute-done.15, f32[1024,768]{0,1:T(8,128)} %copy-done.3, s32[]{:T(128)S(6)} %select_n.174, ...), kind=kLoop, calls=%fused_computation.28 | loop fusion | flops 4325376 | bytes 5505028 | tf_op jit(solution)/shard_map/convert_element_type | solution.py:90
  161.2 6.0 %collective-permute-done.6 = bf16[256,768]{0,1:T(8,128)(2,1)} collective-permute-done((bf16[256,768]{0,1:T(8,128)(2,1)}, bf16[256,768]{0,1:T(8,128)(2,1)}, u32[]{:S(2)}, u32[]{:S(2)}) %collective-permute-start.6) | collective-permute-done | bytes 393248 | tf_op jit(solution)/shard_map/ppermute | solution.py:37
  167.2 1.5 add_convert_fusion.12
  168.7 0.4 fusion.28
  169.2 1.1 fusion
  170.3 1.6 fusion.1
  172.2 1.5 fusion.14
  174.2 1.7 copy-done.6
  175.9 2.3 convolution_convert_fusion
  178.3 3.2 %collective-permute-done.19 = bf16[256,2560]{1,0:T(8,128)(2,1)S(1)} collective-permute-done((bf16[256,2560]{1,0:T(8,128)(2,1)}, bf16[256,2560]{1,0:T(8,128)(2,1)S(1)}, u32[]{:S(2)}, u32[]{:S(2)}) %collective-permute-start.19) | collective-permute-done | bytes 1310752 | tf_op jit(solution)/shard_map/ppermute | solution.py:58
  181.4 4.9 %convert_add_fusion = f32[256,2560]{1,0:T(8,128)} fusion(bf16[256,2560]{1,0:T(8,128)(2,1)S(1)} %collective-permute-done.19, bf16[256,768]{0,1:T(8,128)(2,1)S(1)} %bitcast.67, bf16[768,2560]{0,1:T(8,128)(2,1)} %bitcast.55), kind=kOutput, calls=%fused_computation.12 | convolution fusion | flops 1007943680 | bytes 8257536 | tf_op jit(solution)/shard_map/dot_general | solution.py:55
  186.3 4.5 %reshape.60 = f32[256,2,1280]{2,1,0:T(2,128)} reshape(f32[256,2560]{1,0:T(8,128)} %convert_add_fusion) | data formatting | bytes 5242880 | tf_op jit(solution)/shard_map/reshape | solution.py:62
  190.8 2.9 %constant_dynamic-slice_fusion.1 = bf16[256,1,1280]{2,1,0:T(2,128)(2,1)S(1)} fusion(f32[256,2,1280]{2,1,0:T(2,128)} %reshape.60, s32[]{:T(128)S(6)} %select_n.200), kind=kLoop, calls=%fused_computation.59 | loop fusion | bytes 1310724 | tf_op jit(solution)/shard_map/jit(dynamic_index_in_dim)/dynamic_slice | solution.py:66
  193.8 0.7 collective-permute-start.20
  194.5 2.9 %constant_dynamic-slice_fusion = f32[256,1,1280]{2,1,0:T(1,128)S(1)} fusion(f32[256,2,1280]{2,1,0:T(2,128)} %reshape.60, s32[]{:T(128)S(6)} %select_n.201), kind=kLoop, calls=%fused_computation.58 | loop fusion | bytes 2621444 | tf_op jit(solution)/shard_map/jit(dynamic_index_in_dim)/dynamic_slice | solution.py:70
  197.3 13.3 %collective-permute-done.20 = bf16[256,1280]{1,0:T(8,128)(2,1)S(1)} collective-permute-done((bf16[256,1280]{1,0:T(8,128)(2,1)S(1)}, bf16[256,1280]{1,0:T(8,128)(2,1)S(1)}, u32[]{:S(2)}, u32[]{:S(2)}) %collective-permute-start.20) | collective-permute-done | bytes 655392 | tf_op jit(solution)/shard_map/ppermute | solution.py:68
  210.7 1.0 fusion.11
  211.6 28.5 %all-gather.6.cloned.1.call-done = bf16[1024,768]{0,1:T(8,128)(2,1)} async-done(((bf16[256,768]{0,1:T(8,128)(2,1)}), bf16[1024,768]{0,1:T(8,128)(2,1)}) %all-gather.6.cloned.1.call-update) | async-done | bytes 1572880 | tf_op jit(solution)/shard_map/all_gather | solution.py:95
  240.2 4.0 %pad_maximum_fusion = bf16[2,1024,768]{1,2,0:T(8,128)(2,1)} fusion(bf16[1,1024,768]{1,2,0:T(8,128)(2,1)} %bitcast.63, bf16[1,1024,768]{1,2,0:T(8,128)(2,1)} %bitcast.64), kind=kLoop, calls=%fused_computation.7 | loop fusion | flops 1572864 | bytes 6291456 | tf_op jit(solution)/shard_map/stack | solution.py:97
  244.1 4.6 %copy.36 = bf16[2,1024,768]{2,1,0:T(8,128)(2,1)} copy(bf16[2,1024,768]{1,2,0:T(8,128)(2,1)} %pad_maximum_fusion) | data formatting | bytes 6291456
  (58 shorter events, 2.1 us)
Async XLA Ops:
  7.2 63.1 %copy-start = (bf16[1280,768]{1,0:T(8,128)(2,1)S(1)}, bf16[1280,768]{1,0:T(8,128)(2,1)}, u32[]{:S(2)}) copy-start(bf16[1280,768]{1,0:T(8,128)(2,1)} %param.9) | copy-start | bytes 5898244
  7.2 63.1 %all-gather.4.cloned.1.call-start = ((), (), s32[]{:S(2)}) async-start(), calls=%async_computation | async-start | bytes 3276800 | tf_op jit(solution)/shard_map/all_gather | solution.py:17
  7.2 1.9 collective-permute-start
  9.1 0.8 copy-start.10
  10.0 201.7 %all-gather.8.cloned.1.call-start = ((), (), s32[]{:S(2)}) async-start(), calls=%async_computation.2 | async-start | bytes 1966080 | tf_op jit(solution)/shard_map/all_gather | solution.py:96
  70.3 8.5 %copy-start.11 = (bf16[1024,1280]{1,0:T(8,128)(2,1)S(1)}, bf16[1024,1280]{1,0:T(8,128)(2,1)}, u32[]{:S(2)}) copy-start(bf16[1024,1280]{1,0:T(8,128)(2,1)} %all-gather.4.cloned.1.call-done) | copy-start | bytes 7864324
  70.3 8.5 %copy-start.12 = (bf16[1280,768]{1,0:T(8,128)(2,1)S(1)}, bf16[1280,768]{1,0:T(8,128)(2,1)}, u32[]{:S(2)}) copy-start(bf16[1280,768]{1,0:T(8,128)(2,1)} %param.8) | copy-start | bytes 5898244
  74.4 62.8 %copy-start.3 = (f32[1024,768]{0,1:T(8,128)}, f32[1024,768]{0,1:T(8,128)S(1)}, u32[]{:S(2)}) copy-start(f32[1024,768]{0,1:T(8,128)S(1)} %fusion.31) | copy-start | bytes 9437188
  74.5 12.8 %collective-permute-start.13 = (bf16[256,768]{0,1:T(8,128)(2,1)S(1)}, bf16[256,768]{0,1:T(8,128)(2,1)S(1)}, u32[]{:S(2)}, u32[]{:S(2)}) collective-permute-start(bf16[256,768]{0,1:T(8,128)(2,1)S(1)} %get-tuple-element.12), channel_id=1, source_target_pairs={{0,4},{1,5},{2,6},{3,7},{16,20},{17,21},{18,22},{19,23}} | collective-permute-start | bytes 1179656 | tf_op jit(solution)/shard_map/ppermute | solution.py:36
  78.0 4.6 %copy-start.13 = (bf16[1280,768]{1,0:T(8,128)(2,1)S(1)}, bf16[1280,768]{1,0:T(8,128)(2,1)}, u32[]{:S(2)}) copy-start(bf16[1280,768]{1,0:T(8,128)(2,1)} %param.7) | copy-start | bytes 5898244
  78.0 30.8 %collective-permute-start.16 = (bf16[256,768]{0,1:T(8,128)(2,1)S(1)}, bf16[256,768]{0,1:T(8,128)(2,1)S(1)}, u32[]{:S(2)}, u32[]{:S(2)}) collective-permute-start(bf16[256,768]{0,1:T(8,128)(2,1)S(1)} %get-tuple-element.13), channel_id=1, source_target_pairs={{12,8},{13,9},{14,10},{15,11},{28,24},{29,25},{30,26},{31,27}} | collective-permute-start | bytes 1179656 | tf_op jit(solution)/shard_map/ppermute | solution.py:37
  81.1 58.3 %copy-start.4 = (f32[1024,768]{0,1:T(8,128)}, f32[1024,768]{0,1:T(8,128)S(1)}, u32[]{:S(2)}) copy-start(f32[1024,768]{0,1:T(8,128)S(1)} %fusion.30) | copy-start | bytes 9437188
  81.2 14.6 %collective-permute-start.7 = (bf16[256,768]{0,1:T(8,128)(2,1)S(1)}, bf16[256,768]{0,1:T(8,128)(2,1)S(1)}, u32[]{:S(2)}, u32[]{:S(2)}) collective-permute-start(bf16[256,768]{0,1:T(8,128)(2,1)S(1)} %get-tuple-element.16), channel_id=1, source_target_pairs={{0,4},{1,5},{2,6},{3,7},{16,20},{17,21},{18,22},{19,23}} | collective-permute-start | bytes 1179656 | tf_op jit(solution)/shard_map/ppermute | solution.py:36
  84.8 44.7 %copy-start.2 = (f32[1024,768]{0,1:T(8,128)}, f32[1024,768]{0,1:T(8,128)S(1)}, u32[]{:S(2)}) copy-start(f32[1024,768]{0,1:T(8,128)S(1)} %fusion.29) | copy-start | bytes 9437188
  84.9 19.3 %collective-permute-start.1 = (bf16[256,768]{0,1:T(8,128)(2,1)S(1)}, bf16[256,768]{0,1:T(8,128)(2,1)S(1)}, u32[]{:S(2)}, u32[]{:S(2)}) collective-permute-start(bf16[256,768]{0,1:T(8,128)(2,1)S(1)} %get-tuple-element.22), channel_id=1, source_target_pairs={{0,4},{1,5},{2,6},{3,7},{16,20},{17,21},{18,22},{19,23}} | collective-permute-start | bytes 1179656 | tf_op jit(solution)/shard_map/ppermute | solution.py:36
  86.3 36.6 %collective-permute-start.4 = (bf16[256,768]{0,1:T(8,128)(2,1)S(1)}, bf16[256,768]{0,1:T(8,128)(2,1)S(1)}, u32[]{:S(2)}, u32[]{:S(2)}) collective-permute-start(bf16[256,768]{0,1:T(8,128)(2,1)S(1)} %get-tuple-element.23), channel_id=1, source_target_pairs={{12,8},{13,9},{14,10},{15,11},{28,24},{29,25},{30,26},{31,27}} | collective-permute-start | bytes 1179656 | tf_op jit(solution)/shard_map/ppermute | solution.py:37
  87.4 30.7 %collective-permute-start.10 = (bf16[256,768]{0,1:T(8,128)(2,1)S(1)}, bf16[256,768]{0,1:T(8,128)(2,1)S(1)}, u32[]{:S(2)}, u32[]{:S(2)}) collective-permute-start(bf16[256,768]{0,1:T(8,128)(2,1)S(1)} %get-tuple-element.17), channel_id=1, source_target_pairs={{12,8},{13,9},{14,10},{15,11},{28,24},{29,25},{30,26},{31,27}} | collective-permute-start | bytes 1179656 | tf_op jit(solution)/shard_map/ppermute | solution.py:37
  95.8 16.9 %collective-permute-start.14 = (bf16[256,768]{0,1:T(8,128)(2,1)S(1)}, bf16[256,768]{0,1:T(8,128)(2,1)S(1)}, u32[]{:S(2)}, u32[]{:S(2)}) collective-permute-start(bf16[256,768]{0,1:T(8,128)(2,1)S(1)} %add_convert_fusion.5), channel_id=1, source_target_pairs={{0,4},{4,8},{1,5},{5,9},{2,6},{6,10},{3,7},{7,11},{16,20},{20,24},... | collective-permute-start | bytes 1179656 | tf_op jit(solution)/shard_map/ppermute | solution.py:36
  104.2 16.9 %collective-permute-start.8 = (bf16[256,768]{0,1:T(8,128)(2,1)S(1)}, bf16[256,768]{0,1:T(8,128)(2,1)S(1)}, u32[]{:S(2)}, u32[]{:S(2)}) collective-permute-start(bf16[256,768]{0,1:T(8,128)(2,1)S(1)} %add_convert_fusion.11), channel_id=1, source_target_pairs={{0,4},{4,8},{1,5},{5,9},{2,6},{6,10},{3,7},{7,11},{16,20},{20,24},... | collective-permute-start | bytes 1179656 | tf_op jit(solution)/shard_map/ppermute | solution.py:36
  108.8 20.7 %collective-permute-start.2 = (bf16[256,768]{0,1:T(8,128)(2,1)S(1)}, bf16[256,768]{0,1:T(8,128)(2,1)S(1)}, u32[]{:S(2)}, u32[]{:S(2)}) collective-permute-start(bf16[256,768]{0,1:T(8,128)(2,1)S(1)} %add_convert_fusion.16), channel_id=1, source_target_pairs={{0,4},{4,8},{1,5},{5,9},{2,6},{6,10},{3,7},{7,11},{16,20},{20,24},... | collective-permute-start | bytes 1179656 | tf_op jit(solution)/shard_map/ppermute | solution.py:36
  113.7 42.4 %collective-permute-start.15 = (bf16[256,768]{0,1:T(8,128)(2,1)}, bf16[256,768]{0,1:T(8,128)(2,1)S(1)}, u32[]{:S(2)}, u32[]{:S(2)}) collective-permute-start(bf16[256,768]{0,1:T(8,128)(2,1)} %get-tuple-element.10), channel_id=1, source_target_pairs={{0,4},{4,8},{8,12},{1,5},{5,9},{9,13},{2,6},{6,10},{10,14},{3,7},{... | collective-permute-start | bytes 1179656 | tf_op jit(solution)/shard_map/ppermute | solution.py:36
  118.1 19.1 %collective-permute-start.17 = (bf16[256,768]{0,1:T(8,128)(2,1)S(1)}, bf16[256,768]{0,1:T(8,128)(2,1)S(1)}, u32[]{:S(2)}, u32[]{:S(2)}) collective-permute-start(bf16[256,768]{0,1:T(8,128)(2,1)S(1)} %get-tuple-element.11), channel_id=1, source_target_pairs={{12,8},{8,4},{13,9},{9,5},{14,10},{10,6},{15,11},{11,7},{28,24},{2... | collective-permute-start | bytes 1179656 | tf_op jit(solution)/shard_map/ppermute | solution.py:37
  122.2 17.2 %collective-permute-start.11 = (bf16[256,768]{0,1:T(8,128)(2,1)S(1)}, bf16[256,768]{0,1:T(8,128)(2,1)S(1)}, u32[]{:S(2)}, u32[]{:S(2)}) collective-permute-start(bf16[256,768]{0,1:T(8,128)(2,1)S(1)} %get-tuple-element.15), channel_id=1, source_target_pairs={{12,8},{8,4},{13,9},{9,5},{14,10},{10,6},{15,11},{11,7},{28,24},{2... | collective-permute-start | bytes 1179656 | tf_op jit(solution)/shard_map/ppermute | solution.py:37
  130.7 17.2 %collective-permute-start.5 = (bf16[256,768]{0,1:T(8,128)(2,1)}, bf16[256,768]{0,1:T(8,128)(2,1)}, u32[]{:S(2)}, u32[]{:S(2)}) collective-permute-start(bf16[256,768]{0,1:T(8,128)(2,1)} %get-tuple-element.21), channel_id=1, source_target_pairs={{12,8},{8,4},{13,9},{9,5},{14,10},{10,6},{15,11},{11,7},{28,24},{2... | collective-permute-start | bytes 1179656 | tf_op jit(solution)/shard_map/ppermute | solution.py:37
  132.1 25.3 %collective-permute-start.9 = (bf16[256,768]{0,1:T(8,128)(2,1)}, bf16[256,768]{0,1:T(8,128)(2,1)}, u32[]{:S(2)}, u32[]{:S(2)}) collective-permute-start(bf16[256,768]{0,1:T(8,128)(2,1)} %get-tuple-element.14), channel_id=1, source_target_pairs={{0,4},{4,8},{8,12},{1,5},{5,9},{9,13},{2,6},{6,10},{10,14},{3,7},{... | collective-permute-start | bytes 1179656 | tf_op jit(solution)/shard_map/ppermute | solution.py:36
  138.1 19.3 %collective-permute-start.18 = (bf16[256,768]{0,1:T(8,128)(2,1)}, bf16[256,768]{0,1:T(8,128)(2,1)}, u32[]{:S(2)}, u32[]{:S(2)}) collective-permute-start(bf16[256,768]{0,1:T(8,128)(2,1)} %add_convert_fusion.2), channel_id=1, source_target_pairs={{12,8},{8,4},{4,0},{13,9},{9,5},{5,1},{14,10},{10,6},{6,2},{15,11}... | collective-permute-start | bytes 1179656 | tf_op jit(solution)/shard_map/ppermute | solution.py:37
  140.3 17.9 %collective-permute-start.12 = (bf16[256,768]{0,1:T(8,128)(2,1)}, bf16[256,768]{0,1:T(8,128)(2,1)}, u32[]{:S(2)}, u32[]{:S(2)}) collective-permute-start(bf16[256,768]{0,1:T(8,128)(2,1)} %add_convert_fusion.8), channel_id=1, source_target_pairs={{12,8},{8,4},{4,0},{13,9},{9,5},{5,1},{14,10},{10,6},{6,2},{15,11}... | collective-permute-start | bytes 1179656 | tf_op jit(solution)/shard_map/ppermute | solution.py:37
  147.9 10.3 %copy-start.5 = (f32[2,256,768]{1,2,0:T(8,128)S(1)}, f32[2,256,768]{1,2,0:T(8,128)}, u32[]{:S(2)}) copy-start(f32[2,256,768]{1,2,0:T(8,128)} %convert_element_type.184) | copy-start | bytes 4718596
  147.9 13.3 %collective-permute-start.3 = (bf16[256,768]{0,1:T(8,128)(2,1)}, bf16[256,768]{0,1:T(8,128)(2,1)}, u32[]{:S(2)}, u32[]{:S(2)}) collective-permute-start(bf16[256,768]{0,1:T(8,128)(2,1)} %get-tuple-element.20), channel_id=1, source_target_pairs={{0,4},{4,8},{8,12},{1,5},{5,9},{9,13},{2,6},{6,10},{10,14},{3,7},{... | collective-permute-start | bytes 1179656 | tf_op jit(solution)/shard_map/ppermute | solution.py:36
  156.1 11.1 %collective-permute-start.6 = (bf16[256,768]{0,1:T(8,128)(2,1)}, bf16[256,768]{0,1:T(8,128)(2,1)}, u32[]{:S(2)}, u32[]{:S(2)}) collective-permute-start(bf16[256,768]{0,1:T(8,128)(2,1)} %add_convert_fusion.13), channel_id=1, source_target_pairs={{12,8},{8,4},{4,0},{13,9},{9,5},{5,1},{14,10},{10,6},{6,2},{15,11}... | collective-permute-start | bytes 1179656 | tf_op jit(solution)/shard_map/ppermute | solution.py:37
  161.1 7.6 %copy-start.7 = (bf16[256,768]{0,1:T(8,128)(2,1)S(1)}, bf16[256,768]{0,1:T(8,128)(2,1)}, u32[]{:S(2)}) copy-start(bf16[256,768]{0,1:T(8,128)(2,1)} %get-tuple-element.25) | copy-start | bytes 1179652
  161.2 79.0 %all-gather.6.cloned.1.call-start = ((), (), s32[]{:S(2)}) async-start(), calls=%async_computation.1 | async-start | bytes 1966080 | tf_op jit(solution)/shard_map/all_gather | solution.py:95
  170.3 1.8 copy-start.8
  172.2 1.6 copy-start.9
  173.7 2.2 copy-start.6
  178.2 3.2 %collective-permute-start.19 = (bf16[256,2560]{1,0:T(8,128)(2,1)}, bf16[256,2560]{1,0:T(8,128)(2,1)S(1)}, u32[]{:S(2)}, u32[]{:S(2)}) collective-permute-start(bf16[256,2560]{1,0:T(8,128)(2,1)} %convolution_convert_fusion), channel_id=1, source_target_pairs={{0,1},{1,0},{2,3},{3,2},{4,5},{5,4},{6,7},{7,6},{8,9},{9,8},{10,11... | collective-permute-start | bytes 3932168 | tf_op jit(solution)/shard_map/ppermute | solution.py:58
  193.8 16.8 %collective-permute-start.20 = (bf16[256,1280]{1,0:T(8,128)(2,1)S(1)}, bf16[256,1280]{1,0:T(8,128)(2,1)S(1)}, u32[]{:S(2)}, u32[]{:S(2)}) collective-permute-start(bf16[256,1280]{1,0:T(8,128)(2,1)S(1)} %bitcast.65), channel_id=1, source_target_pairs={{0,2},{1,3},{2,0},{3,1},{4,6},{5,7},{6,4},{7,5},{8,10},{9,11},{10,... | collective-permute-start | bytes 1966088 | tf_op jit(solution)/shard_map/ppermute | solution.py:68
  240.2 8.6 %copy-start.1 = (bf16[1280,768]{1,0:T(8,128)(2,1)S(1)}, bf16[1280,768]{1,0:T(8,128)(2,1)}, u32[]{:S(2)}) copy-start(bf16[1280,768]{1,0:T(8,128)(2,1)} %param.9) | copy-start | bytes 5898244
Sparse Core Ops, SparseCore 0:
  10.1 60.0 all-gather.3
  161.3 41.2 all-gather.7
  204.2 35.9 all-gather.5

commit v2 on v1

v2 whole, which is shorter than its diff:
```python
import functools

import jax
import jax.numpy as jnp
from jax import lax
from jax.experimental import pallas as pl
from jax.experimental.pallas import tpu as pltpu
from jax.sharding import PartitionSpec as P

HEAD_DIM = 128
F32 = jnp.float32
BF16 = jnp.bfloat16
F16 = jnp.float16
LIFT = 8.0


def spread_features(hidden, patches, ranks):
    if not (patches == ranks == 4):
        features = lax.all_gather(hidden, "tensor", axis=1, tiled=True)
        features = lax.all_to_all(features, "patch", split_axis=1, concat_axis=0, tiled=True)
        return features, lambda s: s
    both = ("patch", "tensor")
    rank = lax.axis_index("tensor")
    core, chip = rank % 2, rank // 2
    half = hidden.shape[0] // 2
    straight, crossing = hidden[:half], hidden[half:]
    across = [(r, r ^ 2) for r in range(ranks)]
    crossing = lax.ppermute(crossing, "tensor", across)

    def along(block, flip, pair):
        pairs = []
        for s in (2 * pair, 2 * pair + 1):
            for r in range(ranks):
                pairs.append((s * ranks + r, (r ^ flip) * ranks + (r // 2) * 2 + s % 2))
        return lax.ppermute(block, both, pairs)

    first = [along(straight, 0, pair) for pair in range(2)]
    second = [along(crossing, 2, pair) for pair in range(2)]
    is_straight = lax.axis_index("patch") // 2 == chip
    held = jnp.stack([jnp.where(is_straight, first[i], second[i]) for i in range(2)])
    other = lax.ppermute(held, "tensor", across)
    low = jnp.where(is_straight, held, other)
    high = jnp.where(is_straight, other, held)
    mine = jnp.concatenate([low, high], axis=1)
    theirs = lax.ppermute(mine, "tensor", [(r, r ^ 1) for r in range(ranks)])
    features = jnp.concatenate([mine, theirs]).reshape(4 * hidden.shape[0], -1)
    return features, lambda s: ((s % 2) ^ core) * 2 + s // 2


def sum_own_slab(parts, rows, place, patches, after=None):
    me = lax.axis_index("patch")

    def mine(slab):
        slab = jnp.clip(slab, 0, patches - 1)
        return lax.dynamic_slice_in_dim(parts, place(slab) * rows, rows, 0) * LIFT

    up = down = None
    steps = []
    for step in range(1, patches):
        send_up = mine(patches - step + me)
        send_down = mine(step - patches + me)
        if step > 1:
            send_up = send_up + up.astype(F32)
            send_down = send_down + down.astype(F32)
        send_up, send_down = send_up.astype(F16), send_down.astype(F16)
        if step == 1 and after is not None:
            send_up, send_down, _ = lax.optimization_barrier((send_up, send_down, after))
        up = lax.ppermute(send_up, "patch", [(i, i + 1) for i in range(step)])
        down = lax.ppermute(send_down, "patch", [(patches - 1 - i, patches - 2 - i) for i in range(step)])
        steps.append((up, down))
    total = mine(me)
    if patches > 1:
        total = total + (up.astype(F32) + down.astype(F32))
    return (total * (1.0 / LIFT)).astype(BF16), steps


def attend_head(patches, rows, scale, me_ref, query_ref, stale_ref, fresh_ref, out_ref):
    me = me_ref[0]
    query = query_ref[...]
    starts = [pl.multiple_of(lax.rem(me + j, patches) * rows, rows) for j in range(1, patches)]
    dims = (((1,), (1,)), ((), ()))
    keys = [fresh_ref[0]] + [stale_ref[0, pl.ds(start, rows), :] for start in starts]
    scores = [lax.dot_general(query, key, dims, preferred_element_type=F32) * scale for key in keys]
    top = functools.reduce(jnp.maximum, [jnp.max(s, axis=-1, keepdims=True) for s in scores])
    total = mixed = None
    values = [fresh_ref[1]] + [stale_ref[1, pl.ds(start, rows), :] for start in starts]
    for s, value in zip(scores, values):
        expo = jnp.exp(s - top)
        count = jnp.sum(expo, axis=-1, keepdims=True)
        part = jnp.dot(expo.astype(BF16), value, preferred_element_type=F32)
        total = count if total is None else total + count
        mixed = part if mixed is None else mixed + part
    out_ref[...] = (mixed / total).astype(BF16)


def attend(query, stale_kv, fresh_kv, patches):
    rows, width = query.shape
    tokens = stale_kv.shape[1]
    me = lax.axis_index("patch").astype(jnp.int32)[None]
    return pl.pallas_call(
        functools.partial(attend_head, patches, rows, 1.0 / HEAD_DIM**0.5),
        out_shape=jax.ShapeDtypeStruct((rows, width), BF16),
        grid_spec=pltpu.PrefetchScalarGridSpec(
            num_scalar_prefetch=1,
            grid=(width // HEAD_DIM,),
            in_specs=[
                pl.BlockSpec((rows, HEAD_DIM), lambda h, me: (0, h)),
                pl.BlockSpec((2, tokens, HEAD_DIM), lambda h, me: (0, 0, h)),
                pl.BlockSpec((2, rows, HEAD_DIM), lambda h, me: (0, 0, h)),
            ],
            out_specs=pl.BlockSpec((rows, HEAD_DIM), lambda h, me: (0, h)),
        ),
        compiler_params=pltpu.CompilerParams(vmem_limit_bytes=32 * 2**20),
        cost_estimate=pl.CostEstimate(
            flops=4 * rows * tokens * width,
            bytes_accessed=4 * (tokens + 2 * rows) * width,
            transcendentals=rows * tokens * (width // HEAD_DIM),
        ),
    )(me, query, stale_kv, fresh_kv)


def product(blocks_ref, heads_ref, w_ref, out_ref):
    out_ref[...] = jnp.dot(heads_ref[...], w_ref[...], preferred_element_type=F32).astype(out_ref.dtype)


def product_plus(blocks_ref, heads_ref, w_ref, got_ref, out_ref):
    total = jnp.dot(heads_ref[...], w_ref[...], preferred_element_type=F32) + got_ref[...].astype(F32)
    out_ref[...] = total.astype(out_ref.dtype)


def project_columns(heads_out, w_out, blocks, count, width, dtype, got=None, got_at=0):
    rows, depth = heads_out.shape
    in_specs = [
        pl.BlockSpec((rows, depth), lambda j, b: (0, 0)),
        pl.BlockSpec((depth, width), lambda j, b: (0, b[j])),
    ]
    operands = [heads_out, w_out]
    if got is not None:
        in_specs.append(pl.BlockSpec((rows, width), lambda j, b: (0, j + got_at)))
        operands.append(got)
    return pl.pallas_call(
        product if got is None else product_plus,
        out_shape=jax.ShapeDtypeStruct((rows, count * width), dtype),
        grid_spec=pltpu.PrefetchScalarGridSpec(
            num_scalar_prefetch=1,
            grid=(count,),
            in_specs=in_specs,
            out_specs=pl.BlockSpec((rows, width), lambda j, b: (0, j)),
        ),
        compiler_params=pltpu.CompilerParams(vmem_limit_bytes=32 * 2**20),
        cost_estimate=pl.CostEstimate(
            flops=2 * rows * depth * count * width,
            bytes_accessed=2 * (depth + rows) * count * width,
            transcendentals=0,
        ),
    )(blocks, *operands)


def sum_columns(heads_out, w_out, ranks):
    rank = lax.axis_index("tensor").astype(jnp.int32)
    core, chip, chips = rank % 2, rank // 2, ranks // 2
    width = w_out.shape[1] // ranks
    order = [(chip + hop) % chips for hop in range(1, chips)] + [chip]
    theirs = jnp.stack([2 * c + 1 - core for c in order])
    ours = jnp.stack([2 * c + core for c in order])
    send = project_columns(heads_out, w_out, theirs, chips, width, BF16)
    got = lax.ppermute(send, "tensor", [(r, r ^ 1) for r in range(ranks)])
    arrived = []
    for hop in range(1, chips):
        block = project_columns(heads_out, w_out, ours[hop - 1 : hop], 1, width, BF16, got, hop - 1)
        pairs = [(r, (r + 2 * hop) % ranks) for r in range(ranks)]
        arrived.append(lax.ppermute(block, "tensor", pairs))
    total = project_columns(heads_out, w_out, ours[chips - 1 :], 1, width, F32, got, chips - 1)
    for block in arrived:
        total = total + block.astype(F32)
    return total.astype(BF16)


def make_shards(patches, ranks):
    def shards(hidden_in, w_query, w_key, w_value, w_out, stale_kv):
        rows = hidden_in.shape[0]
        me = lax.axis_index("patch")
        features, place = spread_features(hidden_in, patches, ranks)

        def project(weight, after=None):
            parts = jnp.dot(features, weight, preferred_element_type=F32)
            return sum_own_slab(parts, rows, place, patches, after)

        key_fresh, key_steps = project(w_key)
        value_fresh, _ = project(w_value)
        query, _ = project(w_query, key_steps[-2] if patches > 2 else None)

        own_stale = lax.dynamic_slice_in_dim(stale_kv, me * rows, rows, 1).astype(F32)
        fresh = jnp.stack([key_fresh, value_fresh]).astype(F32)
        delta = (fresh - own_stale).astype(BF16)
        own_new = (own_stale + delta.astype(F32)).astype(BF16)
        refreshed = lax.all_gather(own_new, "patch", axis=1, tiled=True)
        heads_out = attend(query, stale_kv, own_new, patches)
        return (sum_columns(heads_out, w_out, ranks), refreshed)

    return shards


def solution(mesh):
    in_specs = (
        P(("groups", "patch"), "tensor"),
        P("patch", "tensor"),
        P("patch", "tensor"),
        P("patch", "tensor"),
        P("tensor", None),
        P(None, "groups", "tensor"),
    )
    out_specs = (P(("groups", "patch"), "tensor"), P(None, "groups", "tensor"))
    return jax.shard_map(
        make_shards(mesh.shape["patch"], mesh.shape["tensor"]),
        mesh=mesh,
        in_specs=in_specs,
        out_specs=out_specs,
        check_vma=False,
    )
```

time: 256 us -> 271 us (1.059)
  the two profiles are of different devices: /device:TPU:0 before, /device:TPU:8 now
where the time goes in v2:
time: 271 us; the launch traced here: 270 us
  waiting for transfers between devices  138 us (51%)
  starting transfers between devices  50.8 us (19%)
  other arithmetic  27.4 us (10%)
  local copies, waits for them, and re-layouts  18.2 us (7%)
  between operations  14.7 us (5%)
  Pallas kernels  11.6 us (4%)
  matrix products  8.93 us (3%)
    ppermute x9, waiting for transfers between devices, sum_own_slab(): lax.ppermute(send_down, 'patch', [(patches - 1 - i, patches - 2 - i) for...  45.6 us
    ppermute x9, waiting for transfers between devices, sum_own_slab(): up = lax.ppermute(send_up, 'patch', [(i, i + 1) for i in range(step)])  41.6 us
    ppermute x9, starting transfers between devices, sum_own_slab(): up = lax.ppermute(send_up, 'patch', [(i, i + 1) for i in range(step)])  24.8 us
    convert_element_type x13, other arithmetic, sum_own_slab(): send_up, send_down = (send_up.astype(F16), send_down.astype(F16))  17.3 us
    unnamed x25, local copies, waits for them, and re-layouts  16.9 us
    ppermute x4, waiting for transfers between devices, along(): return lax.ppermute(block, both, pairs)  15.1 us
    ppermute x9, starting transfers between devices, sum_own_slab(): lax.ppermute(send_down, 'patch', [(patches - 1 - i, patches - 2 - i) for...  14.6 us
    ppermute x1, waiting for transfers between devices, sum_columns(): arrived.append(lax.ppermute(block, 'tensor', pairs))  11.7 us
  transfers between devices with their start and end apart: 28, of which 16 were waited for; matrix products, arithmetic and copies ran while one was open for 12% of the time, Pallas kernels for 4%

profile of v2, /device:TPU:8, one launch (start us, length us, event | category | flops | bytes accessed | tf_op | source)
XLA Modules:
  0.0 269.8 jit_solution(770280349261661619)
XLA Ops:
  7.2 1.2 fusion.4
  8.5 1.6 collective-permute-start.1
  10.0 1.9 collective-permute-start
  11.9 6.1 %collective-permute-done.1 = bf16[128,1280]{1,0:T(8,128)(2,1)} collective-permute-done((bf16[128,1280]{1,0:T(8,128)(2,1)S(1)}, bf16[128,1280]{1,0:T(8,128)(2,1)}, u32[]{:S(2)}, u32[]{:S(2)}) %collective-permute-start.1) | collective-permute-done | bytes 327712 | tf_op jit(solution)/shard_map/ppermute | solution.py:28
  18.1 2.1 collective-permute-start.2
  20.2 1.3 collective-permute-start.3
  22.2 13.0 %collective-permute-done.2 = bf16[128,1280]{1,0:T(8,128)(2,1)S(1)} collective-permute-done((bf16[128,1280]{1,0:T(8,128)(2,1)}, bf16[128,1280]{1,0:T(8,128)(2,1)S(1)}, u32[]{:S(2)}, u32[]{:S(2)}) %collective-permute-start.2) | collective-permute-done | bytes 327712 | tf_op jit(solution)/shard_map/ppermute | solution.py:35
  35.2 2.0 collective-permute-done.3
  37.4 3.8 %collective-permute-start.5 = (bf16[2,128,1280]{2,1,0:T(8,128)(2,1)S(1)}, bf16[2,128,1280]{2,1,0:T(8,128)(2,1)S(1)}, u32[]{:S(2)}, u32[]{:S(2)}) collective-permute-start(bf16[2,128,1280]{2,1,0:T(8,128)(2,1)S(1)} %pad_maximum_fusion.2), channel_id=1, source_target_pairs={{0,2},{1,3},{2,0},{3,1},{4,6},{5,7},{6,4},{7,5},{8,10},{9,11},{10,... | collective-permute-start | bytes 1966088 | tf_op jit(solution)/shard_map/ppermute | solution.py:41
  41.2 11.4 %collective-permute-done.5 = bf16[2,128,1280]{2,1,0:T(8,128)(2,1)S(1)} collective-permute-done((bf16[2,128,1280]{2,1,0:T(8,128)(2,1)S(1)}, bf16[2,128,1280]{2,1,0:T(8,128)(2,1)S(1)}, u32[]{:S(2)}, u32[]{:S(2)}) %collective-permute-start.5) | collective-permute-done | bytes 655392 | tf_op jit(solution)/shard_map/ppermute | solution.py:41
  53.8 3.4 %collective-permute-done.6 = bf16[2,256,1280]{2,1,0:T(8,128)(2,1)} collective-permute-done((bf16[2,256,1280]{2,1,0:T(8,128)(2,1)}, bf16[2,256,1280]{2,1,0:T(8,128)(2,1)}, u32[]{:S(2)}, u32[]{:S(2)}) %collective-permute-start.6) | collective-permute-done | bytes 1310752 | tf_op jit(solution)/shard_map/ppermute | solution.py:45
  57.2 1.5 pad_maximum_fusion
  58.7 2.2 fusion.7
  61.0 1.3 collective-permute-start.19
  62.3 2.2 fusion.6
  64.6 1.5 copy-done.8
  66.9 7.2 %collective-permute-done.19 = f16[256,768]{1,0:T(8,128)(2,1)S(1)} collective-permute-done((f16[256,768]{1,0:T(8,128)(2,1)S(1)}, f16[256,768]{1,0:T(8,128)(2,1)S(1)}, u32[]{:S(2)}, u32[]{:S(2)}) %collective-permute-start.19) | collective-permute-done | bytes 393248 | tf_op jit(solution)/shard_map/ppermute | solution.py:68
  74.1 2.0 add_convert_fusion.4
  76.1 1.9 collective-permute-start.20
  78.0 1.6 add_convert_fusion.11
  79.6 1.3 collective-permute-start.7
  80.9 9.3 %collective-permute-done.20 = f16[256,768]{1,0:T(8,128)(2,1)S(1)} collective-permute-done((f16[256,768]{1,0:T(8,128)(2,1)}, f16[256,768]{1,0:T(8,128)(2,1)S(1)}, u32[]{:S(2)}, u32[]{:S(2)}) %collective-permute-start.20) | collective-permute-done | bytes 393248 | tf_op jit(solution)/shard_map/ppermute | solution.py:68
  90.2 1.6 add_convert_fusion.3
  92.4 1.3 collective-permute-start.10
  93.7 3.3 %collective-permute-done.7 = f16[256,768]{1,0:T(8,128)(2,1)} collective-permute-done((f16[256,768]{1,0:T(8,128)(2,1)S(1)}, f16[256,768]{1,0:T(8,128)(2,1)}, u32[]{:S(2)}, u32[]{:S(2)}) %collective-permute-start.7) | collective-permute-done | bytes 393248 | tf_op jit(solution)/shard_map/ppermute | solution.py:68
  97.0 2.1 add_convert_fusion.12
  99.1 1.9 collective-permute-start.8
  101.0 1.3 add_convert_fusion.2
  102.3 1.3 collective-permute-start.23
  103.7 6.0 %collective-permute-start.21 = (f16[256,768]{1,0:T(8,128)(2,1)S(1)}, f16[256,768]{1,0:T(8,128)(2,1)S(1)}, u32[]{:S(2)}, u32[]{:S(2)}) collective-permute-start(f16[256,768]{1,0:T(8,128)(2,1)S(1)} %get-tuple-element.8), channel_id=1, source_target_pairs={{0,4},{4,8},{8,12},{1,5},{5,9},{9,13},{2,6},{6,10},{10,14},{3,7},{... | collective-permute-start | bytes 1179656 | tf_op jit(solution)/shard_map/ppermute | solution.py:68
  109.7 3.7 %collective-permute-done.8 = f16[256,768]{1,0:T(8,128)(2,1)} collective-permute-done((f16[256,768]{1,0:T(8,128)(2,1)}, f16[256,768]{1,0:T(8,128)(2,1)}, u32[]{:S(2)}, u32[]{:S(2)}) %collective-permute-start.8) | collective-permute-done | bytes 393248 | tf_op jit(solution)/shard_map/ppermute | solution.py:68
  113.4 1.8 add_convert_fusion.6
  115.2 1.9 collective-permute-start.17
  117.1 3.9 %collective-permute-start.18 = (f16[256,768]{1,0:T(8,128)(2,1)S(1)}, f16[256,768]{1,0:T(8,128)(2,1)S(1)}, u32[]{:S(2)}, u32[]{:S(2)}) collective-permute-start(f16[256,768]{1,0:T(8,128)(2,1)S(1)} %get-tuple-element.7), channel_id=1, source_target_pairs={{12,8},{8,4},{4,0},{13,9},{9,5},{5,1},{14,10},{10,6},{6,2},{15,11}... | collective-permute-start | bytes 1179656 | tf_op jit(solution)/shard_map/ppermute | solution.py:69
  121.2 1.9 collective-permute-start.24
  123.2 4.5 %fusion.5 = f32[1024,768]{1,0:T(8,128)S(1)} fusion(bf16[1024,1280]{1,0:T(8,128)(2,1)} %bitcast.22, bf16[1280,768]{1,0:T(8,128)(2,1)} %param.7), kind=kOutput, calls=%fused_computation.37 | convolution fusion | flops 2013265920 | bytes 7733248 | tf_op jit(solution)/shard_map/dot_general | solution.py:186
  128.8 1.3 collective-permute-start.11
  130.1 1.4 collective-permute-start.14
  131.5 1.3 fusion.2
  133.7 2.3 fusion.1.fresh_ref
  136.0 3.2 %collective-permute-done.11 = f16[256,768]{1,0:T(8,128)(2,1)S(1)} collective-permute-done((f16[256,768]{1,0:T(8,128)(2,1)}, f16[256,768]{1,0:T(8,128)(2,1)S(1)}, u32[]{:S(2)}, u32[]{:S(2)}) %collective-permute-start.11) | collective-permute-done | bytes 393248 | tf_op jit(solution)/shard_map/ppermute | solution.py:68
  139.3 1.3 add_convert_fusion.10
  140.5 4.2 %collective-permute-start.12 = (f16[256,768]{1,0:T(8,128)(2,1)S(1)}, f16[256,768]{1,0:T(8,128)(2,1)S(1)}, u32[]{:S(2)}, u32[]{:S(2)}) collective-permute-start(f16[256,768]{1,0:T(8,128)(2,1)S(1)} %add_convert_fusion.10), channel_id=1, source_target_pairs={{0,4},{4,8},{1,5},{5,9},{2,6},{6,10},{3,7},{7,11},{16,20},{20,24},... | collective-permute-start | bytes 1179656 | tf_op jit(solution)/shard_map/ppermute | solution.py:68
  144.8 14.9 %collective-permute-done.12 = f16[256,768]{1,0:T(8,128)(2,1)S(1)} collective-permute-done((f16[256,768]{1,0:T(8,128)(2,1)S(1)}, f16[256,768]{1,0:T(8,128)(2,1)S(1)}, u32[]{:S(2)}, u32[]{:S(2)}) %collective-permute-start.12) | collective-permute-done | bytes 393248 | tf_op jit(solution)/shard_map/ppermute | solution.py:68
  159.7 2.4 add_convert_fusion.9
  162.1 1.3 collective-permute-start.15
  163.4 5.0 %collective-permute-start.13 = (f16[256,768]{1,0:T(8,128)(2,1)}, f16[256,768]{1,0:T(8,128)(2,1)S(1)}, u32[]{:S(2)}, u32[]{:S(2)}) collective-permute-start(f16[256,768]{1,0:T(8,128)(2,1)} %get-tuple-element.10), channel_id=1, source_target_pairs={{0,4},{4,8},{8,12},{1,5},{5,9},{9,13},{2,6},{6,10},{10,14},{3,7},{... | collective-permute-start | bytes 1179656 | tf_op jit(solution)/shard_map/ppermute | solution.py:68
  168.4 23.0 %collective-permute-done.15 = f16[256,768]{1,0:T(8,128)(2,1)S(1)} collective-permute-done((f16[256,768]{1,0:T(8,128)(2,1)S(1)}, f16[256,768]{1,0:T(8,128)(2,1)S(1)}, u32[]{:S(2)}, u32[]{:S(2)}) %collective-permute-start.15) | collective-permute-done | bytes 393248 | tf_op jit(solution)/shard_map/ppermute | solution.py:69
  191.5 2.0 add_convert_fusion.7
  193.5 2.1 collective-permute-start.16
  195.7 21.8 %collective-permute-done.16 = f16[256,768]{1,0:T(8,128)(2,1)S(1)} collective-permute-done((f16[256,768]{1,0:T(8,128)(2,1)}, f16[256,768]{1,0:T(8,128)(2,1)S(1)}, u32[]{:S(2)}, u32[]{:S(2)}) %collective-permute-start.16) | collective-permute-done | bytes 393248 | tf_op jit(solution)/shard_map/ppermute | solution.py:69
  217.4 1.3 multiply_convert_fusion.4.query_ref
  218.8 1.9 copy-done.5
  220.6 4.8 %shard_map.77.heads_ref = bf16[256,768]{1,0:T(8,128)(2,1)S(1)} custom-call(s32[1]{0:T(128)} %bitcast.1.me_ref, bf16[256,768]{1,0:T(8,128)(2,1)S(1)} %multiply_convert_fusion.4.query_ref, bf16[2,1024,768]{2,1,0:T(8,128)(2,1)S(1)} %copy-done.5, bf16[2,256,768]{2,1,0:T(8,128)(2,1)S(1)} %copy-done.4), custom_call_target="tpu_custom_call" | custom-call | flops 805306368 | bytes 4718592 | tf_op jit(solution)/shard_map/pallas_call | solution.py:100
  225.4 3.2 %copy-done.1 = bf16[768,5120]{1,0:T(8,128)(2,1)S(1)} copy-done((bf16[768,5120]{1,0:T(8,128)(2,1)S(1)}, bf16[768,5120]{1,0:T(8,128)(2,1)}, u32[]{:S(2)}) %copy-start.1) | copy-done | bytes 7864344
  228.7 3.1 %shard_map.78 = bf16[256,2560]{1,0:T(8,128)(2,1)} custom-call(s32[2]{0:T(128)S(1)} %pad_add_fusion.blocks_ref, bf16[256,768]{1,0:T(8,128)(2,1)S(1)} %shard_map.77.heads_ref, bf16[768,5120]{1,0:T(8,128)(2,1)S(1)} %copy-done.1), custom_call_target="tpu_custom_call" | custom-call | flops 1006632960 | bytes 5242880 | tf_op jit(solution)/shard_map/pallas_call | solution.py:141
  231.7 3.4 %collective-permute-done.25.got_ref = bf16[256,2560]{1,0:T(8,128)(2,1)} collective-permute-done((bf16[256,2560]{1,0:T(8,128)(2,1)}, bf16[256,2560]{1,0:T(8,128)(2,1)}, u32[]{:S(2)}, u32[]{:S(2)}) %collective-permute-start.25) | collective-permute-done | bytes 1310752 | tf_op jit(solution)/shard_map/ppermute | solution.py:167
  235.1 3.2 %copy-done.2 = bf16[768,5120]{1,0:T(8,128)(2,1)S(1)} copy-done((bf16[768,5120]{1,0:T(8,128)(2,1)S(1)}, bf16[768,5120]{1,0:T(8,128)(2,1)}, u32[]{:S(2)}) %copy-start.2) | copy-done | bytes 7864344
  238.3 1.9 shard_map.80
  240.3 3.2 %copy-done.3 = bf16[768,5120]{1,0:T(8,128)(2,1)S(1)} copy-done((bf16[768,5120]{1,0:T(8,128)(2,1)S(1)}, bf16[768,5120]{1,0:T(8,128)(2,1)}, u32[]{:S(2)}) %copy-start.3) | copy-done | bytes 7864344
  243.6 1.9 shard_map.79
  245.5 11.7 %collective-permute-done.26 = bf16[256,1280]{1,0:T(8,128)(2,1)} collective-permute-done((bf16[256,1280]{1,0:T(8,128)(2,1)S(1)}, bf16[256,1280]{1,0:T(8,128)(2,1)}, u32[]{:S(2)}, u32[]{:S(2)}) %collective-permute-start.26) | collective-permute-done | bytes 655392 | tf_op jit(solution)/shard_map/ppermute | solution.py:172
  257.2 2.0 add_convert_fusion
  259.2 3.8 %copy.9 = bf16[2,1024,768]{2,1,0:T(8,128)(2,1)} copy(bf16[2,1024,768]{2,1,0:T(8,128)(2,1)} %all-gather.2.cloned.1.call-done) | data formatting | bytes 6291456
  (51 shorter events, 6.0 us)
Async XLA Ops:
  7.2 51.5 %copy-start = (bf16[1280,768]{1,0:T(8,128)(2,1)S(1)}, bf16[1280,768]{1,0:T(8,128)(2,1)}, u32[]{:S(2)}) copy-start(bf16[1280,768]{1,0:T(8,128)(2,1)} %param.9) | copy-start | bytes 5898244
  7.2 252.0 %all-gather.2.cloned.1.call-start = ((), (), s32[]{:S(2)}) async-start(), calls=%async_computation | async-start | bytes 3932160 | tf_op jit(solution)/shard_map/all_gather | solution.py:197
  8.5 9.6 %collective-permute-start.1 = (bf16[128,1280]{1,0:T(8,128)(2,1)S(1)}, bf16[128,1280]{1,0:T(8,128)(2,1)}, u32[]{:S(2)}, u32[]{:S(2)}) collective-permute-start(bf16[128,1280]{1,0:T(8,128)(2,1)S(1)} %get-tuple-element.18), channel_id=1, source_target_pairs={{0,2},{1,3},{2,0},{3,1},{4,6},{5,7},{6,4},{7,5},{8,10},{9,11},{10,... | collective-permute-start | bytes 983048 | tf_op jit(solution)/shard_map/ppermute | solution.py:28
  10.0 12.1 %collective-permute-start = (bf16[128,1280]{1,0:T(8,128)(2,1)S(1)}, bf16[128,1280]{1,0:T(8,128)(2,1)S(1)}, u32[]{:S(2)}, u32[]{:S(2)}) collective-permute-start(bf16[128,1280]{1,0:T(8,128)(2,1)S(1)} %get-tuple-element.19), channel_id=1, source_target_pairs={{0,0},{1,4},{2,10},{3,14},{4,1},{5,5},{6,11},{7,15},{16,16},{17,20... | collective-permute-start | bytes 983048 | tf_op jit(solution)/shard_map/ppermute | solution.py:35
  18.1 17.1 %collective-permute-start.2 = (bf16[128,1280]{1,0:T(8,128)(2,1)}, bf16[128,1280]{1,0:T(8,128)(2,1)S(1)}, u32[]{:S(2)}, u32[]{:S(2)}) collective-permute-start(bf16[128,1280]{1,0:T(8,128)(2,1)} %collective-permute-done.1), channel_id=1, source_target_pairs={{0,8},{1,12},{2,2},{3,6},{4,9},{5,13},{6,3},{7,7},{16,24},{17,28},... | collective-permute-start | bytes 983048 | tf_op jit(solution)/shard_map/ppermute | solution.py:35
  20.2 17.1 %collective-permute-start.3 = (bf16[128,1280]{1,0:T(8,128)(2,1)S(1)}, bf16[128,1280]{1,0:T(8,128)(2,1)S(1)}, u32[]{:S(2)}, u32[]{:S(2)}) collective-permute-start(bf16[128,1280]{1,0:T(8,128)(2,1)S(1)} %get-tuple-element.19), channel_id=1, source_target_pairs={{8,0},{9,4},{10,10},{11,14},{12,1},{13,5},{14,11},{15,15},{24,16},... | collective-permute-start | bytes 983048 | tf_op jit(solution)/shard_map/ppermute | solution.py:35
  21.5 15.8 %collective-permute-start.4 = (bf16[128,1280]{1,0:T(8,128)(2,1)}, bf16[128,1280]{1,0:T(8,128)(2,1)S(1)}, u32[]{:S(2)}, u32[]{:S(2)}) collective-permute-start(bf16[128,1280]{1,0:T(8,128)(2,1)} %collective-permute-done.1), channel_id=1, source_target_pairs={{8,8},{9,12},{10,2},{11,6},{12,9},{13,13},{14,3},{15,7},{24,24},{2... | collective-permute-start | bytes 983048 | tf_op jit(solution)/shard_map/ppermute | solution.py:35
  37.4 15.2 %collective-permute-start.5 = (bf16[2,128,1280]{2,1,0:T(8,128)(2,1)S(1)}, bf16[2,128,1280]{2,1,0:T(8,128)(2,1)S(1)}, u32[]{:S(2)}, u32[]{:S(2)}) collective-permute-start(bf16[2,128,1280]{2,1,0:T(8,128)(2,1)S(1)} %pad_maximum_fusion.2), channel_id=1, source_target_pairs={{0,2},{1,3},{2,0},{3,1},{4,6},{5,7},{6,4},{7,5},{8,10},{9,11},{10,... | collective-permute-start | bytes 1966088 | tf_op jit(solution)/shard_map/ppermute | solution.py:41
  53.8 3.4 %collective-permute-start.6 = (bf16[2,256,1280]{2,1,0:T(8,128)(2,1)}, bf16[2,256,1280]{2,1,0:T(8,128)(2,1)}, u32[]{:S(2)}, u32[]{:S(2)}) collective-permute-start(bf16[2,256,1280]{2,1,0:T(8,128)(2,1)} %pad_maximum_fusion.1), channel_id=1, source_target_pairs={{0,1},{1,0},{2,3},{3,2},{4,5},{5,4},{6,7},{7,6},{8,9},{9,8},{10,11... | collective-permute-start | bytes 3932168 | tf_op jit(solution)/shard_map/ppermute | solution.py:45
  58.7 3.6 %copy-start.10 = (bf16[4,256,1280]{2,1,0:T(8,128)(2,1)}, bf16[4,256,1280]{2,1,0:T(8,128)(2,1)S(1)}, u32[]{:S(2)}) copy-start(bf16[4,256,1280]{2,1,0:T(8,128)(2,1)S(1)} %pad_maximum_fusion) | copy-start | bytes 7864324
  58.7 3.6 %copy-start.11 = (bf16[1280,768]{1,0:T(8,128)(2,1)S(1)}, bf16[1280,768]{1,0:T(8,128)(2,1)}, u32[]{:S(2)}) copy-start(bf16[1280,768]{1,0:T(8,128)(2,1)} %param.8) | copy-start | bytes 5898244
  60.9 3.6 %copy-start.6 = (f32[1024,768]{1,0:T(8,128)}, f32[1024,768]{1,0:T(8,128)S(1)}, u32[]{:S(2)}) copy-start(f32[1024,768]{1,0:T(8,128)S(1)} %fusion.7) | copy-start | bytes 9437188
  61.0 13.0 %collective-permute-start.19 = (f16[256,768]{1,0:T(8,128)(2,1)S(1)}, f16[256,768]{1,0:T(8,128)(2,1)S(1)}, u32[]{:S(2)}, u32[]{:S(2)}) collective-permute-start(f16[256,768]{1,0:T(8,128)(2,1)S(1)} %multiply_convert_fusion.2), channel_id=1, source_target_pairs={{0,4},{1,5},{2,6},{3,7},{16,20},{17,21},{18,22},{19,23}} | collective-permute-start | bytes 1179656 | tf_op jit(solution)/shard_map/ppermute | solution.py:68
  64.5 1.6 copy-start.8
  66.2 11.8 %collective-permute-start.9 = (f16[256,768]{1,0:T(8,128)(2,1)S(1)}, f16[256,768]{1,0:T(8,128)(2,1)S(1)}, u32[]{:S(2)}, u32[]{:S(2)}) collective-permute-start(f16[256,768]{1,0:T(8,128)(2,1)S(1)} %multiply_convert_fusion.5), channel_id=1, source_target_pairs={{12,8},{13,9},{14,10},{15,11},{28,24},{29,25},{30,26},{31,27}} | collective-permute-start | bytes 1179656 | tf_op jit(solution)/shard_map/ppermute | solution.py:69
  76.1 14.1 %collective-permute-start.20 = (f16[256,768]{1,0:T(8,128)(2,1)}, f16[256,768]{1,0:T(8,128)(2,1)S(1)}, u32[]{:S(2)}, u32[]{:S(2)}) collective-permute-start(f16[256,768]{1,0:T(8,128)(2,1)} %add_convert_fusion.4), channel_id=1, source_target_pairs={{0,4},{4,8},{1,5},{5,9},{2,6},{6,10},{3,7},{7,11},{16,20},{20,24},... | collective-permute-start | bytes 1179656 | tf_op jit(solution)/shard_map/ppermute | solution.py:68
  79.6 17.4 %collective-permute-start.7 = (f16[256,768]{1,0:T(8,128)(2,1)S(1)}, f16[256,768]{1,0:T(8,128)(2,1)}, u32[]{:S(2)}, u32[]{:S(2)}) collective-permute-start(f16[256,768]{1,0:T(8,128)(2,1)S(1)} %get-tuple-element.13), channel_id=1, source_target_pairs={{0,4},{1,5},{2,6},{3,7},{16,20},{17,21},{18,22},{19,23}} | collective-permute-start | bytes 1179656 | tf_op jit(solution)/shard_map/ppermute | solution.py:68
  91.8 9.3 %collective-permute-start.22 = (f16[256,768]{1,0:T(8,128)(2,1)S(1)}, f16[256,768]{1,0:T(8,128)(2,1)S(1)}, u32[]{:S(2)}, u32[]{:S(2)}) collective-permute-start(f16[256,768]{1,0:T(8,128)(2,1)S(1)} %get-tuple-element.9), channel_id=1, source_target_pairs={{12,8},{13,9},{14,10},{15,11},{28,24},{29,25},{30,26},{31,27}} | collective-permute-start | bytes 1179656 | tf_op jit(solution)/shard_map/ppermute | solution.py:69
  92.4 17.2 %collective-permute-start.10 = (f16[256,768]{1,0:T(8,128)(2,1)S(1)}, f16[256,768]{1,0:T(8,128)(2,1)}, u32[]{:S(2)}, u32[]{:S(2)}) collective-permute-start(f16[256,768]{1,0:T(8,128)(2,1)S(1)} %get-tuple-element.12), channel_id=1, source_target_pairs={{12,8},{8,4},{13,9},{9,5},{14,10},{10,6},{15,11},{11,7},{28,24},{2... | collective-permute-start | bytes 1179656 | tf_op jit(solution)/shard_map/ppermute | solution.py:69
  99.1 14.3 %collective-permute-start.8 = (f16[256,768]{1,0:T(8,128)(2,1)}, f16[256,768]{1,0:T(8,128)(2,1)}, u32[]{:S(2)}, u32[]{:S(2)}) collective-permute-start(f16[256,768]{1,0:T(8,128)(2,1)} %add_convert_fusion.12), channel_id=1, source_target_pairs={{0,4},{4,8},{1,5},{5,9},{2,6},{6,10},{3,7},{7,11},{16,20},{20,24},... | collective-permute-start | bytes 1179656 | tf_op jit(solution)/shard_map/ppermute | solution.py:68
  102.3 18.8 %collective-permute-start.23 = (f16[256,768]{1,0:T(8,128)(2,1)S(1)}, f16[256,768]{1,0:T(8,128)(2,1)S(1)}, u32[]{:S(2)}, u32[]{:S(2)}) collective-permute-start(f16[256,768]{1,0:T(8,128)(2,1)S(1)} %add_convert_fusion.2), channel_id=1, source_target_pairs={{12,8},{8,4},{13,9},{9,5},{14,10},{10,6},{15,11},{11,7},{28,24},{2... | collective-permute-start | bytes 1179656 | tf_op jit(solution)/shard_map/ppermute | solution.py:69
  103.6 17.4 %copy-start.7 = (f32[1024,768]{1,0:T(8,128)S(1)}, f32[1024,768]{1,0:T(8,128)}, u32[]{:S(2)}) copy-start(f32[1024,768]{1,0:T(8,128)} %copy-done.6) | copy-start | bytes 9437188
  103.7 29.1 %collective-permute-start.21 = (f16[256,768]{1,0:T(8,128)(2,1)S(1)}, f16[256,768]{1,0:T(8,128)(2,1)S(1)}, u32[]{:S(2)}, u32[]{:S(2)}) collective-permute-start(f16[256,768]{1,0:T(8,128)(2,1)S(1)} %get-tuple-element.8), channel_id=1, source_target_pairs={{0,4},{4,8},{8,12},{1,5},{5,9},{9,13},{2,6},{6,10},{10,14},{3,7},{... | collective-permute-start | bytes 1179656 | tf_op jit(solution)/shard_map/ppermute | solution.py:68
  115.2 14.9 %collective-permute-start.17 = (f16[256,768]{1,0:T(8,128)(2,1)S(1)}, f16[256,768]{1,0:T(8,128)(2,1)S(1)}, u32[]{:S(2)}, u32[]{:S(2)}) collective-permute-start(f16[256,768]{1,0:T(8,128)(2,1)S(1)} %get-tuple-element.6), channel_id=1, source_target_pairs={{0,4},{4,8},{8,12},{1,5},{5,9},{9,13},{2,6},{6,10},{10,14},{3,7},{... | collective-permute-start | bytes 1179656 | tf_op jit(solution)/shard_map/ppermute | solution.py:68
  117.1 14.3 %collective-permute-start.18 = (f16[256,768]{1,0:T(8,128)(2,1)S(1)}, f16[256,768]{1,0:T(8,128)(2,1)S(1)}, u32[]{:S(2)}, u32[]{:S(2)}) collective-permute-start(f16[256,768]{1,0:T(8,128)(2,1)S(1)} %get-tuple-element.7), channel_id=1, source_target_pairs={{12,8},{8,4},{4,0},{13,9},{9,5},{5,1},{14,10},{10,6},{6,2},{15,11}... | collective-permute-start | bytes 1179656 | tf_op jit(solution)/shard_map/ppermute | solution.py:69
  121.2 12.3 %collective-permute-start.24 = (f16[256,768]{1,0:T(8,128)(2,1)S(1)}, f16[256,768]{1,0:T(8,128)(2,1)S(1)}, u32[]{:S(2)}, u32[]{:S(2)}) collective-permute-start(f16[256,768]{1,0:T(8,128)(2,1)S(1)} %add_convert_fusion.1), channel_id=1, source_target_pairs={{12,8},{8,4},{4,0},{13,9},{9,5},{5,1},{14,10},{10,6},{6,2},{15,11}... | collective-permute-start | bytes 1179656 | tf_op jit(solution)/shard_map/ppermute | solution.py:69
  127.7 6.0 %copy-start.9 = (f32[1024,768]{1,0:T(8,128)}, f32[1024,768]{1,0:T(8,128)S(1)}, u32[]{:S(2)}) copy-start(f32[1024,768]{1,0:T(8,128)S(1)} %fusion.5) | copy-start | bytes 9437188
  128.8 10.5 %collective-permute-start.11 = (f16[256,768]{1,0:T(8,128)(2,1)}, f16[256,768]{1,0:T(8,128)(2,1)S(1)}, u32[]{:S(2)}, u32[]{:S(2)}) collective-permute-start(f16[256,768]{1,0:T(8,128)(2,1)} %get-tuple-element.4), channel_id=1, source_target_pairs={{0,4},{1,5},{2,6},{3,7},{16,20},{17,21},{18,22},{19,23}} | collective-permute-start | bytes 1179656 | tf_op jit(solution)/shard_map/ppermute | solution.py:68
  130.1 14.7 %collective-permute-start.14 = (f16[256,768]{1,0:T(8,128)(2,1)S(1)}, f16[256,768]{1,0:T(8,128)(2,1)}, u32[]{:S(2)}, u32[]{:S(2)}) collective-permute-start(f16[256,768]{1,0:T(8,128)(2,1)S(1)} %get-tuple-element.5), channel_id=1, source_target_pairs={{12,8},{13,9},{14,10},{15,11},{28,24},{29,25},{30,26},{31,27}} | collective-permute-start | bytes 1179656 | tf_op jit(solution)/shard_map/ppermute | solution.py:69
  140.5 78.2 %copy-start.4 = (bf16[2,256,768]{2,1,0:T(8,128)(2,1)S(1)}, bf16[2,256,768]{2,1,0:T(8,128)(2,1)}, u32[]{:S(2)}) copy-start(bf16[2,256,768]{2,1,0:T(8,128)(2,1)} %fusion.1.fresh_ref) | copy-start | bytes 2359300
  140.5 19.1 %collective-permute-start.12 = (f16[256,768]{1,0:T(8,128)(2,1)S(1)}, f16[256,768]{1,0:T(8,128)(2,1)S(1)}, u32[]{:S(2)}, u32[]{:S(2)}) collective-permute-start(f16[256,768]{1,0:T(8,128)(2,1)S(1)} %add_convert_fusion.10), channel_id=1, source_target_pairs={{0,4},{4,8},{1,5},{5,9},{2,6},{6,10},{3,7},{7,11},{16,20},{20,24},... | collective-permute-start | bytes 1179656 | tf_op jit(solution)/shard_map/ppermute | solution.py:68
  162.1 29.3 %collective-permute-start.15 = (f16[256,768]{1,0:T(8,128)(2,1)S(1)}, f16[256,768]{1,0:T(8,128)(2,1)S(1)}, u32[]{:S(2)}, u32[]{:S(2)}) collective-permute-start(f16[256,768]{1,0:T(8,128)(2,1)S(1)} %get-tuple-element.11), channel_id=1, source_target_pairs={{12,8},{8,4},{13,9},{9,5},{14,10},{10,6},{15,11},{11,7},{28,24},{2... | collective-permute-start | bytes 1179656 | tf_op jit(solution)/shard_map/ppermute | solution.py:69
  163.4 32.2 %collective-permute-start.13 = (f16[256,768]{1,0:T(8,128)(2,1)}, f16[256,768]{1,0:T(8,128)(2,1)S(1)}, u32[]{:S(2)}, u32[]{:S(2)}) collective-permute-start(f16[256,768]{1,0:T(8,128)(2,1)} %get-tuple-element.10), channel_id=1, source_target_pairs={{0,4},{4,8},{8,12},{1,5},{5,9},{9,13},{2,6},{6,10},{10,14},{3,7},{... | collective-permute-start | bytes 1179656 | tf_op jit(solution)/shard_map/ppermute | solution.py:68
  193.5 24.0 %collective-permute-start.16 = (f16[256,768]{1,0:T(8,128)(2,1)}, f16[256,768]{1,0:T(8,128)(2,1)S(1)}, u32[]{:S(2)}, u32[]{:S(2)}) collective-permute-start(f16[256,768]{1,0:T(8,128)(2,1)} %add_convert_fusion.7), channel_id=1, source_target_pairs={{12,8},{8,4},{4,0},{13,9},{9,5},{5,1},{14,10},{10,6},{6,2},{15,11}... | collective-permute-start | bytes 1179656 | tf_op jit(solution)/shard_map/ppermute | solution.py:69
  218.8 1.9 copy-start.5
  225.4 3.2 %copy-start.1 = (bf16[768,5120]{1,0:T(8,128)(2,1)S(1)}, bf16[768,5120]{1,0:T(8,128)(2,1)}, u32[]{:S(2)}) copy-start(bf16[768,5120]{1,0:T(8,128)(2,1)} %w_ref.5) | copy-start | bytes 23592964
  231.7 3.4 %collective-permute-start.25 = (bf16[256,2560]{1,0:T(8,128)(2,1)}, bf16[256,2560]{1,0:T(8,128)(2,1)}, u32[]{:S(2)}, u32[]{:S(2)}) collective-permute-start(bf16[256,2560]{1,0:T(8,128)(2,1)} %shard_map.78), channel_id=1, source_target_pairs={{0,1},{1,0},{2,3},{3,2},{4,5},{5,4},{6,7},{7,6},{8,9},{9,8},{10,11... | collective-permute-start | bytes 3932168 | tf_op jit(solution)/shard_map/ppermute | solution.py:167
  235.1 3.2 %copy-start.2 = (bf16[768,5120]{1,0:T(8,128)(2,1)S(1)}, bf16[768,5120]{1,0:T(8,128)(2,1)}, u32[]{:S(2)}) copy-start(bf16[768,5120]{1,0:T(8,128)(2,1)} %w_ref.5) | copy-start | bytes 23592964
  240.2 16.9 %collective-permute-start.26 = (bf16[256,1280]{1,0:T(8,128)(2,1)S(1)}, bf16[256,1280]{1,0:T(8,128)(2,1)}, u32[]{:S(2)}, u32[]{:S(2)}) collective-permute-start(bf16[256,1280]{1,0:T(8,128)(2,1)S(1)} %shard_map.80), channel_id=1, source_target_pairs={{0,2},{1,3},{2,0},{3,1},{4,6},{5,7},{6,4},{7,5},{8,10},{9,11},{10,... | collective-permute-start | bytes 1966088 | tf_op jit(solution)/shard_map/ppermute | solution.py:172
  240.3 3.2 %copy-start.3 = (bf16[768,5120]{1,0:T(8,128)(2,1)S(1)}, bf16[768,5120]{1,0:T(8,128)(2,1)}, u32[]{:S(2)}) copy-start(bf16[768,5120]{1,0:T(8,128)(2,1)} %w_ref.5) | copy-start | bytes 23592964
Sparse Core Ops, SparseCore 0:
  136.2 80.7 all-gather.1

commit v3 on v1

v3 whole, which is shorter than its diff:
```python
import functools

import jax
import jax.numpy as jnp
from jax import lax
from jax.experimental import pallas as pl
from jax.experimental.pallas import tpu as pltpu
from jax.sharding import PartitionSpec as P

HEAD_DIM = 128
F32 = jnp.float32
BF16 = jnp.bfloat16
F16 = jnp.float16
LIFT = 8.0


def spread_features(hidden):
    features = lax.all_gather(hidden, "tensor", axis=1, tiled=True)
    return lax.all_to_all(features, "patch", split_axis=1, concat_axis=0, tiled=True)


def spread_in_pairs(hidden):
    rank, patch = lax.axis_index("tensor"), lax.axis_index("patch")
    half = hidden.shape[0] // 2
    across = [(r, r ^ 2) for r in range(4)]
    straight = hidden[:half]
    crossing = lax.ppermute(hidden[half:], "tensor", across)
    is_straight = patch // 2 == rank // 2

    def along(block, flip, far):
        pairs = [
            (4 * s + r, 4 * (r ^ flip) + 2 * (r // 2) + s % 2)
            for s in range(4)
            for r in range(4)
            if ((r ^ flip) // 2 != s // 2) == far
        ]
        return lax.ppermute(block, ("patch", "tensor"), pairs)

    def both_slabs(far):
        held = jnp.where(is_straight, along(straight, 0, far), along(crossing, 2, far))
        other = lax.ppermute(held, "tensor", across)
        low = jnp.where(is_straight, held, other)
        high = jnp.where(is_straight, other, held)
        mine = jnp.concatenate([low, high])
        theirs = lax.ppermute(mine, "tensor", [(r, r ^ 1) for r in range(4)])
        return jnp.concatenate([mine, theirs])

    return both_slabs(True), both_slabs(False)


def sum_in_pairs(far, near, weight):
    rank, patch = lax.axis_index("tensor"), lax.axis_index("patch")
    core = rank % 2
    rows, width = far.shape[0] // 2, weight.shape[1]

    def parts(features):
        return (jnp.dot(features, weight, preferred_element_type=F32) * LIFT).reshape(2, rows, width)

    def slab(pair, odd):
        return lax.dynamic_index_in_dim(pair, odd ^ core, 0, keepdims=False)

    far_parts, near_parts = parts(far), parts(near)
    outer = lax.ppermute(far_parts.astype(F16), "patch", [(0, 1), (3, 2)])
    direct = slab(near_parts, 1 - patch % 2).astype(F16)
    direct, outer = lax.optimization_barrier((direct, outer))
    direct = lax.ppermute(direct, "patch", [(0, 1), (1, 0), (2, 3), (3, 2)])
    summed = (far_parts + outer.astype(F32)).astype(F16)
    over = patch // 2
    inner_got = lax.ppermute(slab(summed, over), "patch", [(1, 2), (2, 1)])
    outer_got = lax.ppermute(slab(summed, 1 - over), "patch", [(1, 3), (2, 0)])
    total = slab(near_parts, patch % 2) + direct.astype(F32)
    total = total + jnp.where((patch == 1) | (patch == 2), inner_got, outer_got).astype(F32)
    return (total * (1.0 / LIFT)).astype(BF16)


def sum_own_slab(features, weight, patches):
    me = lax.axis_index("patch")
    rows = features.shape[0] // patches
    parts = jnp.dot(features, weight, preferred_element_type=F32) * LIFT

    def mine(slab):
        slab = jnp.clip(slab, 0, patches - 1)
        return lax.dynamic_slice_in_dim(parts, slab * rows, rows, 0)

    up = down = None
    for step in range(1, patches):
        send_up = mine(patches - step + me)
        send_down = mine(step - patches + me)
        if step > 1:
            send_up = send_up + up.astype(F32)
            send_down = send_down + down.astype(F32)
        up = lax.ppermute(send_up.astype(F16), "patch", [(i, i + 1) for i in range(step)])
        down = lax.ppermute(
            send_down.astype(F16), "patch", [(patches - 1 - i, patches - 2 - i) for i in range(step)]
        )
    total = mine(me)
    if patches > 1:
        total = total + (up.astype(F32) + down.astype(F32))
    return (total * (1.0 / LIFT)).astype(BF16)


def attend_and_project(patches, heads, chips, place_ref, query_ref, stale_ref, key_ref, value_ref, w_ref, send_ref, keep_ref, sums):
    me = place_ref[0]
    rows = query_ref.shape[0]
    width = w_ref.shape[1] // (2 * chips)
    scale = 1.0 / HEAD_DIM**0.5
    starts = [pl.multiple_of(lax.rem(me + j, patches) * rows, rows) for j in range(1, patches)]
    dims = (((1,), (1,)), ((), ()))
    mixed_heads = []
    for h in range(heads):
        columns = slice(h * HEAD_DIM, (h + 1) * HEAD_DIM)
        query = query_ref[:, columns]
        keys = [key_ref[:, columns]] + [stale_ref[0, pl.ds(start, rows), columns] for start in starts]
        values = [value_ref[:, columns]] + [stale_ref[1, pl.ds(start, rows), columns] for start in starts]
        scores = [lax.dot_general(query, key, dims, preferred_element_type=F32) * scale for key in keys]
        top = functools.reduce(jnp.maximum, [jnp.max(s, axis=-1, keepdims=True) for s in scores])
        total = mixed = None
        for s, value in zip(scores, values):
            expo = jnp.exp(s - top)
            count = jnp.sum(expo, axis=-1, keepdims=True)
            part = jnp.dot(expo.astype(BF16), value, preferred_element_type=F32)
            total = count if total is None else total + count
            mixed = part if mixed is None else mixed + part
        mixed_heads.append((mixed / total).astype(BF16))
    heads_out = jnp.concatenate(mixed_heads, axis=1) if heads > 1 else mixed_heads[0]
    product = jnp.dot(heads_out, w_ref[...], preferred_element_type=F32)

    @pl.when(pl.program_id(0) == 0)
    def _():
        sums[...] = product

    @pl.when(pl.program_id(0) > 0)
    def _():
        sums[...] += product

    @pl.when(pl.program_id(0) == pl.num_programs(0) - 1)
    def _():
        for j in range(chips):
            theirs = pl.multiple_of(place_ref[1 + j] * width, width)
            ours = pl.multiple_of(place_ref[1 + chips + j] * width, width)
            send_ref[:, j * width : (j + 1) * width] = sums[:, pl.ds(theirs, width)].astype(BF16)
            keep_ref[:, j * width : (j + 1) * width] = sums[:, pl.ds(ours, width)]


def attend(query, stale_kv, key_new, value_new, w_out, patches, ranks):
    rows, depth = query.shape
    tokens, model = stale_kv.shape[1], w_out.shape[1]
    rank = lax.axis_index("tensor").astype(jnp.int32)
    core, chip, chips = rank % 2, rank // 2, ranks // 2
    width = model // ranks
    order = [(chip + hop) % chips for hop in range(1, chips)] + [chip]
    me = lax.axis_index("patch").astype(jnp.int32)
    place = jnp.stack([me] + [2 * c + 1 - core for c in order] + [2 * c + core for c in order])
    heads = 2 if depth % (2 * HEAD_DIM) == 0 else 1
    block = heads * HEAD_DIM
    send, keep = pl.pallas_call(
        functools.partial(attend_and_project, patches, heads, chips),
        out_shape=(
            jax.ShapeDtypeStruct((rows, chips * width), BF16),
            jax.ShapeDtypeStruct((rows, chips * width), F32),
        ),
        grid_spec=pltpu.PrefetchScalarGridSpec(
            num_scalar_prefetch=1,
            grid=(depth // block,),
            in_specs=[
                pl.BlockSpec((rows, block), lambda h, p: (0, h)),
                pl.BlockSpec((2, tokens, block), lambda h, p: (0, 0, h)),
                pl.BlockSpec((rows, block), lambda h, p: (0, h)),
                pl.BlockSpec((rows, block), lambda h, p: (0, h)),
                pl.BlockSpec((block, model), lambda h, p: (h, 0)),
            ],
            out_specs=(
                pl.BlockSpec((rows, chips * width), lambda h, p: (0, 0)),
                pl.BlockSpec((rows, chips * width), lambda h, p: (0, 0)),
            ),
            scratch_shapes=[pltpu.VMEM((rows, model), F32)],
        ),
        compiler_params=pltpu.CompilerParams(vmem_limit_bytes=48 * 2**20),
        cost_estimate=pl.CostEstimate(
            flops=4 * rows * tokens * depth + 2 * rows * depth * model,
            bytes_accessed=4 * tokens * depth + 2 * depth * model + 6 * rows * chips * width,
            transcendentals=rows * tokens * (depth // HEAD_DIM),
        ),
    )(place, query, stale_kv, key_new, value_new, w_out)
    got = lax.ppermute(send, "tensor", [(r, r ^ 1) for r in range(ranks)])

    def summed(j):
        return keep[:, j * width : (j + 1) * width] + got[:, j * width : (j + 1) * width].astype(F32)

    arrived = []
    for hop in range(1, chips):
        pairs = [(r, (r + 2 * hop) % ranks) for r in range(ranks)]
        arrived.append(lax.ppermute(summed(hop - 1).astype(BF16), "tensor", pairs))
    total = summed(chips - 1)
    for block in arrived:
        total = total + block.astype(F32)
    return total.astype(BF16)


def make_shards(patches, ranks):
    def shards(hidden_in, w_query, w_key, w_value, w_out, stale_kv):
        rows = hidden_in.shape[0]
        me = lax.axis_index("patch")
        if patches == ranks == 4:
            far, near = spread_in_pairs(hidden_in)
            project = functools.partial(sum_in_pairs, far, near)
        else:
            features = spread_features(hidden_in)
            project = lambda weight: sum_own_slab(features, weight, patches)
        own_stale = lax.dynamic_slice_in_dim(stale_kv, me * rows, rows, 1).astype(F32)

        def refresh(fresh, stale):
            fresh = lax.reduce_precision(fresh.astype(F32), 8, 7)
            delta = lax.reduce_precision(fresh - stale, 8, 7)
            return (stale + delta).astype(BF16)

        key_new = refresh(project(w_key), own_stale[0])
        keys_all = lax.all_gather(key_new, "patch", axis=0, tiled=True)
        query = project(w_query)
        value_new = refresh(project(w_value), own_stale[1])
        values_all = lax.all_gather(value_new, "patch", axis=0, tiled=True)
        refreshed = jnp.broadcast_to(keys_all[None], stale_kv.shape).at[1].set(values_all)
        attended = attend(query, stale_kv, key_new, value_new, w_out, patches, ranks)
        return (attended, refreshed)

    return shards


def solution(mesh):
    in_specs = (
        P(("groups", "patch"), "tensor"),
        P("patch", "tensor"),
        P("patch", "tensor"),
        P("patch", "tensor"),
        P("tensor", None),
        P(None, "groups", "tensor"),
    )
    out_specs = (P(("groups", "patch"), "tensor"), P(None, "groups", "tensor"))
    return jax.shard_map(
        make_shards(mesh.shape["patch"], mesh.shape["tensor"]),
        mesh=mesh,
        in_specs=in_specs,
        out_specs=out_specs,
        check_vma=False,
    )
```

time: 256 us -> 241 us (0.941)
  local copies, waits for them, and re-layouts: 43.7 us -> 10.3 us
  waiting for transfers between devices: 114 us -> 130 us
  Pallas kernels: 0 us -> 11.2 us
  matrix products: 19.3 us -> 10.9 us
  other arithmetic: 20.1 us -> 13.4 us
  starting transfers between devices: 43.9 us -> 49.9 us
    ppermute x21 -> x23, waiting for transfers between devices: 46 us -> 117 us  [the longest x3 29.2 us: sum_in_pairs(): outer_got = lax.ppermute(slab(summed, 1 - over), 'patch', [(1, 3), (2, 0)])]
    all_gather x1 -> x0, waiting for transfers between devices: 39.3 us -> none  [spread_features(): lax.all_gather(block, 'tensor', axis=0, tiled=True)]
    all_gather x1, waiting for transfers between devices: 28.5 us -> 0.01 us  [shards(): keys_all = lax.all_gather(key_new, 'patch', axis=0, tiled=True)]
    unnamed x33 -> x40, local copies, waits for them, and re-layouts: 20 us -> 4.12 us
    dynamic_slice x4 -> x0, local copies, waits for them, and re-layouts: 13.9 us -> none  [the longest x1 6.92 us: columns(): picked = lax.dynamic_index_in_dim(by_core, which, 2, keepdims=False)]
    all_gather x1, waiting for transfers between devices: 0.01 us -> 13.8 us  [shards(): values_all = lax.all_gather(value_new, 'patch', axis=0, tiled=True)]
    pallas_call x0 -> x1, Pallas kernels: none -> 11.2 us  [attend(): pl.pallas_call(functools.partial(attend_and_project, patches, heads, chip...]
    dot_general x9 -> x6, matrix products: 19.3 us -> 10.9 us  [parts(): jnp.dot(features, weight, preferred_element_type=F32) * LIFT]
  transfers between devices with their start and end apart: 24 -> 25, of which waited for: 12 -> 16; matrix products, arithmetic and copies ran while one was open for 27% -> 11% of each run, Pallas kernels for 0% -> 5%
where the time goes in v3:
time: 241 us
  waiting for transfers between devices  130 us (54%)
  starting transfers between devices  49.9 us (21%)
  between operations  14.6 us (6%)
  other arithmetic  13.4 us (6%)
  Pallas kernels  11.2 us (5%)
  matrix products  10.9 us (5%)
  local copies, waits for them, and re-layouts  10.3 us (4%)
    ppermute x3, waiting for transfers between devices, sum_in_pairs(): outer_got = lax.ppermute(slab(summed, 1 - over), 'patch', [(1, 3), (2, 0)])  29.2 us
    ppermute x3, waiting for transfers between devices, sum_in_pairs(): direct = lax.ppermute(direct, 'patch', [(0, 1), (1, 0), (2, 3), (3, 2)])  24.3 us
    ppermute x3, waiting for transfers between devices, sum_in_pairs(): outer = lax.ppermute(far_parts.astype(F16), 'patch', [(0, 1), (3, 2)])  24 us
    ppermute x1, waiting for transfers between devices, attend(): arrived.append(lax.ppermute(summed(hop - 1).astype(BF16), 'tensor', pairs))  15.3 us
    all_gather x1, waiting for transfers between devices, shards(): values_all = lax.all_gather(value_new, 'patch', axis=0, tiled=True)  13.8 us
    ppermute x3, starting transfers between devices, sum_in_pairs(): outer = lax.ppermute(far_parts.astype(F16), 'patch', [(0, 1), (3, 2)])  11.4 us
    pallas_call x1, Pallas kernels, attend(): pl.pallas_call(functools.partial(attend_and_project, patches, heads, chip...  11.2 us
    dot_general x6, matrix products, parts(): jnp.dot(features, weight, preferred_element_type=F32) * LIFT  10.9 us
  transfers between devices with their start and end apart: 25, of which 16 were waited for; matrix products, arithmetic and copies ran while one was open for 11% of the time, Pallas kernels for 5%

profile of v3, /device:TPU:0, one launch (start us, length us, event | category | flops | bytes accessed | tf_op | source)
XLA Modules:
  0.0 240.6 jit_solution(13655522354719028945)
XLA Ops:
  7.2 1.2 fusion.12
  8.5 3.0 %collective-permute-start.1 = (bf16[128,1280]{1,0:T(8,128)(2,1)S(1)}, bf16[128,1280]{1,0:T(8,128)(2,1)}, u32[]{:S(2)}, u32[]{:S(2)}) collective-permute-start(bf16[128,1280]{1,0:T(8,128)(2,1)S(1)} %get-tuple-element.42), channel_id=1, source_target_pairs={{0,2},{1,3},{2,0},{3,1},{4,6},{5,7},{6,4},{7,5},{8,10},{9,11},{10,... | collective-permute-start | bytes 983048 | tf_op jit(solution)/shard_map/ppermute | solution.py:27
  11.5 1.3 collective-permute-start.5
  12.8 6.5 %collective-permute-done.1 = bf16[128,1280]{1,0:T(8,128)(2,1)} collective-permute-done((bf16[128,1280]{1,0:T(8,128)(2,1)S(1)}, bf16[128,1280]{1,0:T(8,128)(2,1)}, u32[]{:S(2)}, u32[]{:S(2)}) %collective-permute-start.1) | collective-permute-done | bytes 327712 | tf_op jit(solution)/shard_map/ppermute | solution.py:27
  19.3 5.5 %collective-permute-start.6 = (bf16[128,1280]{1,0:T(8,128)(2,1)}, bf16[128,1280]{1,0:T(8,128)(2,1)}, u32[]{:S(2)}, u32[]{:S(2)}) collective-permute-start(bf16[128,1280]{1,0:T(8,128)(2,1)} %collective-permute-done.1), channel_id=1, source_target_pairs={{0,8},{1,12},{4,9},{5,13},{10,2},{11,6},{14,3},{15,7},{16,24},{17,... | collective-permute-start | bytes 983048 | tf_op jit(solution)/shard_map/ppermute | solution.py:37
  24.8 0.7 collective-permute-start
  25.5 0.7 collective-permute-start.2
  26.2 5.3 %collective-permute-done.5 = bf16[128,1280]{1,0:T(8,128)(2,1)S(1)} collective-permute-done((bf16[128,1280]{1,0:T(8,128)(2,1)S(1)}, bf16[128,1280]{1,0:T(8,128)(2,1)S(1)}, u32[]{:S(2)}, u32[]{:S(2)}) %collective-permute-start.5) | collective-permute-done | bytes 327712 | tf_op jit(solution)/shard_map/ppermute | solution.py:37
  31.5 0.6 collective-permute-done.6
  32.2 9.7 %collective-permute-start.7 = (bf16[128,1280]{1,0:T(8,128)(2,1)S(1)}, bf16[128,1280]{1,0:T(8,128)(2,1)S(1)}, u32[]{:S(2)}, u32[]{:S(2)}) collective-permute-start(bf16[128,1280]{1,0:T(8,128)(2,1)S(1)} %broadcast_select_fusion.2), channel_id=1, source_target_pairs={{0,2},{1,3},{2,0},{3,1},{4,6},{5,7},{6,4},{7,5},{8,10},{9,11},{10,... | collective-permute-start | bytes 983048 | tf_op jit(solution)/shard_map/ppermute | solution.py:41
  41.9 0.1 collective-permute-start.3
  42.0 4.9 %collective-permute-done.7 = bf16[128,1280]{1,0:T(8,128)(2,1)S(1)} collective-permute-done((bf16[128,1280]{1,0:T(8,128)(2,1)S(1)}, bf16[128,1280]{1,0:T(8,128)(2,1)S(1)}, u32[]{:S(2)}, u32[]{:S(2)}) %collective-permute-start.7) | collective-permute-done | bytes 327712 | tf_op jit(solution)/shard_map/ppermute | solution.py:41
  47.1 3.3 %collective-permute-done.3 = bf16[128,1280]{1,0:T(8,128)(2,1)S(1)} collective-permute-done((bf16[128,1280]{1,0:T(8,128)(2,1)S(1)}, bf16[128,1280]{1,0:T(8,128)(2,1)S(1)}, u32[]{:S(2)}, u32[]{:S(2)}) %collective-permute-start.3) | collective-permute-done | bytes 327712 | tf_op jit(solution)/shard_map/ppermute | solution.py:41
  50.6 1.2 convolution_multiply_fusion
  51.9 0.1 convert_element_type.123
  52.0 7.1 %collective-permute-start.17 = (f16[2,256,768]{2,1,0:T(8,128)(2,1)S(1)}, f16[2,256,768]{2,1,0:T(8,128)(2,1)S(1)}, u32[]{:S(2)}, u32[]{:S(2)}) collective-permute-start(f16[2,256,768]{2,1,0:T(8,128)(2,1)S(1)} %convert_element_type.123), channel_id=1, source_target_pairs={{0,4},{12,8},{1,5},{13,9},{2,6},{14,10},{3,7},{15,11},{16,20},{28,... | collective-permute-start | bytes 2359304 | tf_op jit(solution)/shard_map/ppermute | solution.py:63
  59.1 1.2 convolution_multiply_fusion.2
  60.4 1.3 collective-permute-start.13
  61.7 1.2 convolution_multiply_fusion.1
  63.0 1.2 convolution_multiply_fusion.3
  64.2 0.9 fusion.10
  65.1 11.7 %collective-permute-done.17 = f16[2,256,768]{2,1,0:T(8,128)(2,1)S(1)} collective-permute-done((f16[2,256,768]{2,1,0:T(8,128)(2,1)S(1)}, f16[2,256,768]{2,1,0:T(8,128)(2,1)S(1)}, u32[]{:S(2)}, u32[]{:S(2)}) %collective-permute-start.17) | collective-permute-done | bytes 786464 | tf_op jit(solution)/shard_map/ppermute | solution.py:63
  76.9 2.5 %collective-permute-start.18 = (f16[256,768]{1,0:T(8,128)(2,1)S(1)}, f16[256,768]{1,0:T(8,128)(2,1)S(1)}, u32[]{:S(2)}, u32[]{:S(2)}) collective-permute-start(f16[256,768]{1,0:T(8,128)(2,1)S(1)} %fusion.11), channel_id=1, source_target_pairs={{0,4},{4,0},{8,12},{12,8},{1,5},{5,1},{9,13},{13,9},{2,6},{6,2},{1... | collective-permute-start | bytes 1179656 | tf_op jit(solution)/shard_map/ppermute | solution.py:66
  79.3 0.2 add_convert_fusion
  79.5 1.1 dynamic-slice_bitcast_fusion
  80.6 1.4 collective-permute-start.19
  82.0 1.3 collective-permute-start.20
  83.3 10.4 %collective-permute-done.13 = f16[2,256,768]{2,1,0:T(8,128)(2,1)S(1)} collective-permute-done((f16[2,256,768]{2,1,0:T(8,128)(2,1)S(1)}, f16[2,256,768]{2,1,0:T(8,128)(2,1)S(1)}, u32[]{:S(2)}, u32[]{:S(2)}) %collective-permute-start.13) | collective-permute-done | bytes 786464 | tf_op jit(solution)/shard_map/ppermute | solution.py:63
  93.7 0.2 add_convert_fusion.1
  93.9 1.1 dynamic-slice_bitcast_fusion.2
  95.0 1.4 collective-permute-start.15
  96.4 1.3 collective-permute-start.16
  97.7 4.0 %collective-permute-done.18 = f16[256,768]{1,0:T(8,128)(2,1)S(1)} collective-permute-done((f16[256,768]{1,0:T(8,128)(2,1)S(1)}, f16[256,768]{1,0:T(8,128)(2,1)S(1)}, u32[]{:S(2)}, u32[]{:S(2)}) %collective-permute-start.18) | collective-permute-done | bytes 393248 | tf_op jit(solution)/shard_map/ppermute | solution.py:66
  101.7 0.7 copy-done.15
  102.5 2.5 %collective-permute-start.14 = (f16[256,768]{1,0:T(8,128)(2,1)}, f16[256,768]{1,0:T(8,128)(2,1)}, u32[]{:S(2)}, u32[]{:S(2)}) collective-permute-start(f16[256,768]{1,0:T(8,128)(2,1)} %fusion.10), channel_id=1, source_target_pairs={{0,4},{4,0},{8,12},{12,8},{1,5},{5,1},{9,13},{13,9},{2,6},{6,2},{1... | collective-permute-start | bytes 1179656 | tf_op jit(solution)/shard_map/ppermute | solution.py:66
  104.9 2.4 dynamic-slice_convert_fusion.2
  107.3 3.1 %convolution_multiply_fusion.4 = f32[512,768]{1,0:T(8,128)S(1)} fusion(bf16[1280,768]{1,0:T(8,128)(2,1)} %param.9, bf16[256,1280]{1,0:T(8,128)(2,1)} %copy-done.19, bf16[128,1280]{1,0:T(8,128)(2,1)S(1)} %get-tuple-element.39, bf16[128,1280]{1,0:T(8,128)(2,1)S(1)} %get-tuple-element.38), kind=kOutput, calls=%fused_computation.8 | convolution fusion | flops 1010958336 | bytes 4849664 | tf_op jit(solution)/shard_map/dot_general | solution.py:57
  110.4 1.0 convert_element_type.104
  111.4 2.9 %collective-permute-start.9 = (f16[2,256,768]{2,1,0:T(8,128)(2,1)}, f16[2,256,768]{2,1,0:T(8,128)(2,1)}, u32[]{:S(2)}, u32[]{:S(2)}) collective-permute-start(f16[2,256,768]{2,1,0:T(8,128)(2,1)} %convert_element_type.104), channel_id=1, source_target_pairs={{0,4},{12,8},{1,5},{13,9},{2,6},{14,10},{3,7},{15,11},{16,20},{28,... | collective-permute-start | bytes 2359304 | tf_op jit(solution)/shard_map/ppermute | solution.py:63
  114.4 3.5 %collective-permute-done.16 = f16[256,768]{1,0:T(8,128)(2,1)} collective-permute-done((f16[256,768]{1,0:T(8,128)(2,1)}, f16[256,768]{1,0:T(8,128)(2,1)}, u32[]{:S(2)}, u32[]{:S(2)}) %collective-permute-start.16) | collective-permute-done | bytes 393248 | tf_op jit(solution)/shard_map/ppermute | solution.py:70
  117.9 4.8 %collective-permute-done.14 = f16[256,768]{1,0:T(8,128)(2,1)} collective-permute-done((f16[256,768]{1,0:T(8,128)(2,1)}, f16[256,768]{1,0:T(8,128)(2,1)}, u32[]{:S(2)}, u32[]{:S(2)}) %collective-permute-start.14) | collective-permute-done | bytes 393248 | tf_op jit(solution)/shard_map/ppermute | solution.py:66
  122.8 2.7 %add_convert_fusion.5 = (bf16[256,768]{1,0:T(8,128)(2,1)S(1)}, bf16[256,768]{1,0:T(8,128)(2,1)}) fusion(f32[2,256,768]{2,1,0:T(8,128)S(1)} %copy-done.7, f16[256,768]{1,0:T(8,128)(2,1)S(1)} %copy-done.16, f32[2,256,768]{2,1,0:T(8,128)S(1)} %bitcast.82, s32[]{:T(128)S(6)} %select_n.120, f16[256,768]{1,0:T(8,128)(2,1)} %collective-permute-done.19, ...), kind=kLoop, calls=%fused_computation.28 | loop fusion | flops 5111808 | bytes 6291461 | tf_op jit(solution)/shard_map/convert_element_type | solution.py:215
  125.6 3.0 %convolution_multiply_fusion.5 = f32[512,768]{1,0:T(8,128)S(1)} fusion(bf16[1280,768]{1,0:T(8,128)(2,1)} %param.9, bf16[256,1280]{1,0:T(8,128)(2,1)} %copy-done.18, bf16[128,1280]{1,0:T(8,128)(2,1)S(1)} %get-tuple-element.41, bf16[128,1280]{1,0:T(8,128)(2,1)S(1)} %get-tuple-element.40), kind=kOutput, calls=%fused_computation.9 | convolution fusion | flops 1010958336 | bytes 4849664 | tf_op jit(solution)/shard_map/dot_general | solution.py:57
  128.7 1.8 collective-permute-done.9
  130.5 2.5 %collective-permute-start.10 = (f16[256,768]{1,0:T(8,128)(2,1)S(1)}, f16[256,768]{1,0:T(8,128)(2,1)}, u32[]{:S(2)}, u32[]{:S(2)}) collective-permute-start(f16[256,768]{1,0:T(8,128)(2,1)S(1)} %fusion.9), channel_id=1, source_target_pairs={{0,4},{4,0},{8,12},{12,8},{1,5},{5,1},{9,13},{13,9},{2,6},{6,2},{1... | collective-permute-start | bytes 1179656 | tf_op jit(solution)/shard_map/ppermute | solution.py:66
  133.0 1.4 add_convert_fusion.2
  134.4 0.9 dynamic-slice_bitcast_fusion.4
  135.3 1.6 collective-permute-start.11
  136.9 1.5 collective-permute-start.12
  138.4 15.4 %collective-permute-done.10 = f16[256,768]{1,0:T(8,128)(2,1)} collective-permute-done((f16[256,768]{1,0:T(8,128)(2,1)S(1)}, f16[256,768]{1,0:T(8,128)(2,1)}, u32[]{:S(2)}, u32[]{:S(2)}) %collective-permute-start.10) | collective-permute-done | bytes 393248 | tf_op jit(solution)/shard_map/ppermute | solution.py:66
  153.9 25.6 %collective-permute-done.12 = f16[256,768]{1,0:T(8,128)(2,1)} collective-permute-done((f16[256,768]{1,0:T(8,128)(2,1)S(1)}, f16[256,768]{1,0:T(8,128)(2,1)}, u32[]{:S(2)}, u32[]{:S(2)}) %collective-permute-start.12) | collective-permute-done | bytes 393248 | tf_op jit(solution)/shard_map/ppermute | solution.py:70
  179.5 1.5 fusion.8.query_ref
  181.1 11.2 %shard_map.77 = (bf16[256,2560]{1,0:T(8,128)(2,1)}, f32[256,2560]{1,0:T(8,128)S(1)}) custom-call(s32[5]{0:T(128)S(1)} %stack.23.place_ref, bf16[256,768]{1,0:T(8,128)(2,1)S(1)} %fusion.8.query_ref, bf16[2,1024,768]{2,1,0:T(8,128)(2,1)} %stale_ref.1, bf16[256,768]{1,0:T(8,128)(2,1)S(1)} %copy-done.2, bf16[256,768]{1,0:T(8,128)(2,1)S(1)} %get-tuple-element.30.value_ref, ...), custom_call_target="tpu_custom_call" | custom-call | flops 2818572288 | bytes 14942208 | tf_op jit(solution)/shard_map/pallas_call | solution.py:156
  192.2 1.5 copy-done.3
  193.8 3.2 %collective-permute-done.21 = bf16[256,2560]{1,0:T(8,128)(2,1)S(1)} collective-permute-done((bf16[256,2560]{1,0:T(8,128)(2,1)}, bf16[256,2560]{1,0:T(8,128)(2,1)S(1)}, u32[]{:S(2)}, u32[]{:S(2)}) %collective-permute-start.21) | collective-permute-done | bytes 1310752 | tf_op jit(solution)/shard_map/ppermute | solution.py:185
  197.0 1.4 add_convert_fusion.4
  198.4 1.5 collective-permute-start.22
  199.9 15.3 %collective-permute-done.22 = bf16[256,1280]{1,0:T(8,128)(2,1)S(1)} collective-permute-done((bf16[256,1280]{1,0:T(8,128)(2,1)S(1)}, bf16[256,1280]{1,0:T(8,128)(2,1)S(1)}, u32[]{:S(2)}, u32[]{:S(2)}) %collective-permute-start.22) | collective-permute-done | bytes 655392 | tf_op jit(solution)/shard_map/ppermute | solution.py:193
  215.2 1.1 add_convert_fusion.3
  216.3 13.8 %all-gather.5.cloned.1.call-done = bf16[1024,768]{1,0:T(8,128)(2,1)} async-done(((bf16[256,768]{1,0:T(8,128)(2,1)}), bf16[1024,768]{1,0:T(8,128)(2,1)}) %all-gather.5.cloned.1.call-update) | async-done | bytes 1572880 | tf_op jit(solution)/shard_map/all_gather | solution.py:221
  230.1 1.7 broadcast_in_dim.2
  231.8 0.1 copy-done.9
  232.0 0.1 bitcast_dynamic-update-slice_fusion
  232.1 1.7 copy-done.8
  (62 shorter events, 0.9 us)
Async XLA Ops:
  7.2 43.5 %copy-start = (bf16[1280,768]{1,0:T(8,128)(2,1)S(1)}, bf16[1280,768]{1,0:T(8,128)(2,1)}, u32[]{:S(2)}) copy-start(bf16[1280,768]{1,0:T(8,128)(2,1)} %param.11) | copy-start | bytes 5898244
  7.2 209.2 %all-gather.3.cloned.1.call-start = ((), (), s32[]{:S(2)}) async-start(), calls=%async_computation | async-start | bytes 1966080 | tf_op jit(solution)/shard_map/all_gather | solution.py:218
  8.5 10.8 %collective-permute-start.1 = (bf16[128,1280]{1,0:T(8,128)(2,1)S(1)}, bf16[128,1280]{1,0:T(8,128)(2,1)}, u32[]{:S(2)}, u32[]{:S(2)}) collective-permute-start(bf16[128,1280]{1,0:T(8,128)(2,1)S(1)} %get-tuple-element.42), channel_id=1, source_target_pairs={{0,2},{1,3},{2,0},{3,1},{4,6},{5,7},{6,4},{7,5},{8,10},{9,11},{10,... | collective-permute-start | bytes 983048 | tf_op jit(solution)/shard_map/ppermute | solution.py:27
  11.5 20.0 %collective-permute-start.5 = (bf16[128,1280]{1,0:T(8,128)(2,1)S(1)}, bf16[128,1280]{1,0:T(8,128)(2,1)S(1)}, u32[]{:S(2)}, u32[]{:S(2)}) collective-permute-start(bf16[128,1280]{1,0:T(8,128)(2,1)S(1)} %get-tuple-element.43), channel_id=1, source_target_pairs={{2,10},{3,14},{6,11},{7,15},{8,0},{9,4},{12,1},{13,5},{18,26},{19,... | collective-permute-start | bytes 983048 | tf_op jit(solution)/shard_map/ppermute | solution.py:37
  19.3 12.8 %collective-permute-start.6 = (bf16[128,1280]{1,0:T(8,128)(2,1)}, bf16[128,1280]{1,0:T(8,128)(2,1)}, u32[]{:S(2)}, u32[]{:S(2)}) collective-permute-start(bf16[128,1280]{1,0:T(8,128)(2,1)} %collective-permute-done.1), channel_id=1, source_target_pairs={{0,8},{1,12},{4,9},{5,13},{10,2},{11,6},{14,3},{15,7},{16,24},{17,... | collective-permute-start | bytes 983048 | tf_op jit(solution)/shard_map/ppermute | solution.py:37
  24.8 17.1 %collective-permute-start = (bf16[128,1280]{1,0:T(8,128)(2,1)S(1)}, bf16[128,1280]{1,0:T(8,128)(2,1)S(1)}, u32[]{:S(2)}, u32[]{:S(2)}) collective-permute-start(bf16[128,1280]{1,0:T(8,128)(2,1)S(1)} %get-tuple-element.43), channel_id=1, source_target_pairs={{0,0},{1,4},{4,1},{5,5},{10,10},{11,14},{14,11},{15,15},{16,16},{1... | collective-permute-start | bytes 983048 | tf_op jit(solution)/shard_map/ppermute | solution.py:37
  25.5 16.4 %collective-permute-start.2 = (bf16[128,1280]{1,0:T(8,128)(2,1)}, bf16[128,1280]{1,0:T(8,128)(2,1)S(1)}, u32[]{:S(2)}, u32[]{:S(2)}) collective-permute-start(bf16[128,1280]{1,0:T(8,128)(2,1)} %collective-permute-done.1), channel_id=1, source_target_pairs={{2,2},{3,6},{6,3},{7,7},{8,8},{9,12},{12,9},{13,13},{18,18},{19,22... | collective-permute-start | bytes 983048 | tf_op jit(solution)/shard_map/ppermute | solution.py:37
  32.2 14.8 %collective-permute-start.7 = (bf16[128,1280]{1,0:T(8,128)(2,1)S(1)}, bf16[128,1280]{1,0:T(8,128)(2,1)S(1)}, u32[]{:S(2)}, u32[]{:S(2)}) collective-permute-start(bf16[128,1280]{1,0:T(8,128)(2,1)S(1)} %broadcast_select_fusion.2), channel_id=1, source_target_pairs={{0,2},{1,3},{2,0},{3,1},{4,6},{5,7},{6,4},{7,5},{8,10},{9,11},{10,... | collective-permute-start | bytes 983048 | tf_op jit(solution)/shard_map/ppermute | solution.py:41
  41.9 8.5 %collective-permute-start.3 = (bf16[128,1280]{1,0:T(8,128)(2,1)S(1)}, bf16[128,1280]{1,0:T(8,128)(2,1)S(1)}, u32[]{:S(2)}, u32[]{:S(2)}) collective-permute-start(bf16[128,1280]{1,0:T(8,128)(2,1)S(1)} %broadcast_select_fusion.5), channel_id=1, source_target_pairs={{0,2},{1,3},{2,0},{3,1},{4,6},{5,7},{6,4},{7,5},{8,10},{9,11},{10,... | collective-permute-start | bytes 983048 | tf_op jit(solution)/shard_map/ppermute | solution.py:41
  47.0 3.6 %collective-permute-start.8 = (bf16[256,1280]{1,0:T(8,128)(2,1)S(1)}, bf16[256,1280]{1,0:T(8,128)(2,1)S(1)}, u32[]{:S(2)}, u32[]{:S(2)}) collective-permute-start(bf16[256,1280]{1,0:T(8,128)(2,1)S(1)} %pad_maximum_fusion.3), channel_id=1, source_target_pairs={{0,1},{1,0},{2,3},{3,2},{4,5},{5,4},{6,7},{7,6},{8,9},{9,8},{10,11... | collective-permute-start | bytes 1966088 | tf_op jit(solution)/shard_map/ppermute | solution.py:45
  50.5 11.2 %collective-permute-start.4 = (bf16[256,1280]{1,0:T(8,128)(2,1)S(1)}, bf16[256,1280]{1,0:T(8,128)(2,1)S(1)}, u32[]{:S(2)}, u32[]{:S(2)}) collective-permute-start(bf16[256,1280]{1,0:T(8,128)(2,1)S(1)} %pad_maximum_fusion.2), channel_id=1, source_target_pairs={{0,1},{1,0},{2,3},{3,2},{4,5},{5,4},{6,7},{7,6},{8,9},{9,8},{10,11... | collective-permute-start | bytes 1966088 | tf_op jit(solution)/shard_map/ppermute | solution.py:45
  50.6 8.4 %copy-start.19 = (bf16[256,1280]{1,0:T(8,128)(2,1)}, bf16[256,1280]{1,0:T(8,128)(2,1)S(1)}, u32[]{:S(2)}) copy-start(bf16[256,1280]{1,0:T(8,128)(2,1)S(1)} %collective-permute-done.8) | copy-start | bytes 1966084
  51.8 7.2 %copy-start.17 = (bf16[1280,768]{1,0:T(8,128)(2,1)S(1)}, bf16[1280,768]{1,0:T(8,128)(2,1)}, u32[]{:S(2)}) copy-start(bf16[1280,768]{1,0:T(8,128)(2,1)} %param.10) | copy-start | bytes 5898244
  52.0 24.9 %collective-permute-start.17 = (f16[2,256,768]{2,1,0:T(8,128)(2,1)S(1)}, f16[2,256,768]{2,1,0:T(8,128)(2,1)S(1)}, u32[]{:S(2)}, u32[]{:S(2)}) collective-permute-start(f16[2,256,768]{2,1,0:T(8,128)(2,1)S(1)} %convert_element_type.123), channel_id=1, source_target_pairs={{0,4},{12,8},{1,5},{13,9},{2,6},{14,10},{3,7},{15,11},{16,20},{28,... | collective-permute-start | bytes 2359304 | tf_op jit(solution)/shard_map/ppermute | solution.py:63
  60.4 33.3 %collective-permute-start.13 = (f16[2,256,768]{2,1,0:T(8,128)(2,1)S(1)}, f16[2,256,768]{2,1,0:T(8,128)(2,1)S(1)}, u32[]{:S(2)}, u32[]{:S(2)}) collective-permute-start(f16[2,256,768]{2,1,0:T(8,128)(2,1)S(1)} %convert_element_type.113), channel_id=1, source_target_pairs={{0,4},{12,8},{1,5},{13,9},{2,6},{14,10},{3,7},{15,11},{16,20},{28,... | collective-permute-start | bytes 2359304 | tf_op jit(solution)/shard_map/ppermute | solution.py:63
  61.7 2.4 %copy-start.18 = (bf16[256,1280]{1,0:T(8,128)(2,1)}, bf16[256,1280]{1,0:T(8,128)(2,1)S(1)}, u32[]{:S(2)}) copy-start(bf16[256,1280]{1,0:T(8,128)(2,1)S(1)} %collective-permute-done.4) | copy-start | bytes 1966084
  62.9 1.2 copy-start.11
  64.2 15.4 %copy-start.13 = (f32[512,768]{1,0:T(8,128)}, f32[512,768]{1,0:T(8,128)S(1)}, u32[]{:S(2)}) copy-start(f32[512,768]{1,0:T(8,128)S(1)} %convolution_multiply_fusion.3) | copy-start | bytes 4718596
  76.9 24.9 %collective-permute-start.18 = (f16[256,768]{1,0:T(8,128)(2,1)S(1)}, f16[256,768]{1,0:T(8,128)(2,1)S(1)}, u32[]{:S(2)}, u32[]{:S(2)}) collective-permute-start(f16[256,768]{1,0:T(8,128)(2,1)S(1)} %fusion.11), channel_id=1, source_target_pairs={{0,4},{4,0},{8,12},{12,8},{1,5},{5,1},{9,13},{13,9},{2,6},{6,2},{1... | collective-permute-start | bytes 1179656 | tf_op jit(solution)/shard_map/ppermute | solution.py:66
  80.6 30.8 %collective-permute-start.19 = (f16[256,768]{1,0:T(8,128)(2,1)}, f16[256,768]{1,0:T(8,128)(2,1)}, u32[]{:S(2)}, u32[]{:S(2)}) collective-permute-start(f16[256,768]{1,0:T(8,128)(2,1)} %get-tuple-element.33), channel_id=1, source_target_pairs={{4,8},{8,4},{5,9},{9,5},{6,10},{10,6},{7,11},{11,7},{20,24},{24,20... | collective-permute-start | bytes 1179656 | tf_op jit(solution)/shard_map/ppermute | solution.py:69
  82.0 32.4 %collective-permute-start.20 = (f16[256,768]{1,0:T(8,128)(2,1)}, f16[256,768]{1,0:T(8,128)(2,1)}, u32[]{:S(2)}, u32[]{:S(2)}) collective-permute-start(f16[256,768]{1,0:T(8,128)(2,1)} %get-tuple-element.32), channel_id=1, source_target_pairs={{4,12},{8,0},{5,13},{9,1},{6,14},{10,2},{7,15},{11,3},{20,28},{24,... | collective-permute-start | bytes 1179656 | tf_op jit(solution)/shard_map/ppermute | solution.py:70
  95.0 19.4 %collective-permute-start.15 = (f16[256,768]{1,0:T(8,128)(2,1)}, f16[256,768]{1,0:T(8,128)(2,1)}, u32[]{:S(2)}, u32[]{:S(2)}) collective-permute-start(f16[256,768]{1,0:T(8,128)(2,1)} %get-tuple-element.35), channel_id=1, source_target_pairs={{4,8},{8,4},{5,9},{9,5},{6,10},{10,6},{7,11},{11,7},{20,24},{24,20... | collective-permute-start | bytes 1179656 | tf_op jit(solution)/shard_map/ppermute | solution.py:69
  96.4 21.5 %collective-permute-start.16 = (f16[256,768]{1,0:T(8,128)(2,1)}, f16[256,768]{1,0:T(8,128)(2,1)}, u32[]{:S(2)}, u32[]{:S(2)}) collective-permute-start(f16[256,768]{1,0:T(8,128)(2,1)} %get-tuple-element.34), channel_id=1, source_target_pairs={{4,12},{8,0},{5,13},{9,1},{6,14},{10,2},{7,15},{11,3},{20,28},{24,... | collective-permute-start | bytes 1179656 | tf_op jit(solution)/shard_map/ppermute | solution.py:70
  101.7 0.7 copy-start.15
  102.5 20.3 %collective-permute-start.14 = (f16[256,768]{1,0:T(8,128)(2,1)}, f16[256,768]{1,0:T(8,128)(2,1)}, u32[]{:S(2)}, u32[]{:S(2)}) collective-permute-start(f16[256,768]{1,0:T(8,128)(2,1)} %fusion.10), channel_id=1, source_target_pairs={{0,4},{4,0},{8,12},{12,8},{1,5},{5,1},{9,13},{13,9},{2,6},{6,2},{1... | collective-permute-start | bytes 1179656 | tf_op jit(solution)/shard_map/ppermute | solution.py:66
  107.3 15.4 %copy-start.12 = (f32[512,768]{1,0:T(8,128)S(1)}, f32[512,768]{1,0:T(8,128)}, u32[]{:S(2)}) copy-start(f32[512,768]{1,0:T(8,128)} %copy-done.11) | copy-start | bytes 4718596
  107.3 15.4 %copy-start.14 = (f32[512,768]{1,0:T(8,128)S(1)}, f32[512,768]{1,0:T(8,128)}, u32[]{:S(2)}) copy-start(f32[512,768]{1,0:T(8,128)} %copy-done.13) | copy-start | bytes 4718596
  110.4 7.5 %copy-start.5 = (f32[512,768]{1,0:T(8,128)}, f32[512,768]{1,0:T(8,128)S(1)}, u32[]{:S(2)}) copy-start(f32[512,768]{1,0:T(8,128)S(1)} %convolution_multiply_fusion.4) | copy-start | bytes 4718596
  110.4 12.3 %copy-start.7 = (f32[2,256,768]{2,1,0:T(8,128)S(1)}, f32[2,256,768]{2,1,0:T(8,128)}, u32[]{:S(2)}) copy-start(f32[2,256,768]{2,1,0:T(8,128)} %dynamic-slice_convert_fusion.2) | copy-start | bytes 4718596
  110.4 12.3 %copy-start.16 = (f16[256,768]{1,0:T(8,128)(2,1)S(1)}, f16[256,768]{1,0:T(8,128)(2,1)}, u32[]{:S(2)}) copy-start(f16[256,768]{1,0:T(8,128)(2,1)} %copy-done.15) | copy-start | bytes 1179652
  111.4 19.1 %collective-permute-start.9 = (f16[2,256,768]{2,1,0:T(8,128)(2,1)}, f16[2,256,768]{2,1,0:T(8,128)(2,1)}, u32[]{:S(2)}, u32[]{:S(2)}) collective-permute-start(f16[2,256,768]{2,1,0:T(8,128)(2,1)} %convert_element_type.104), channel_id=1, source_target_pairs={{0,4},{12,8},{1,5},{13,9},{2,6},{14,10},{3,7},{15,11},{16,20},{28,... | collective-permute-start | bytes 2359304 | tf_op jit(solution)/shard_map/ppermute | solution.py:63
  125.5 55.5 %copy-start.1 = (bf16[256,768]{1,0:T(8,128)(2,1)}, bf16[256,768]{1,0:T(8,128)(2,1)S(1)}, u32[]{:S(2)}) copy-start(bf16[256,768]{1,0:T(8,128)(2,1)S(1)} %get-tuple-element.30.value_ref) | copy-start | bytes 1179652
  125.5 104.6 %all-gather.5.cloned.1.call-start = ((), (), s32[]{:S(2)}) async-start(), calls=%async_computation.1 | async-start | bytes 1966080 | tf_op jit(solution)/shard_map/all_gather | solution.py:221
  125.6 7.4 %copy-start.6 = (f32[512,768]{1,0:T(8,128)S(1)}, f32[512,768]{1,0:T(8,128)}, u32[]{:S(2)}) copy-start(f32[512,768]{1,0:T(8,128)} %copy-done.5) | copy-start | bytes 4718596
  128.6 1.9 copy-start.10
  130.5 23.3 %collective-permute-start.10 = (f16[256,768]{1,0:T(8,128)(2,1)S(1)}, f16[256,768]{1,0:T(8,128)(2,1)}, u32[]{:S(2)}, u32[]{:S(2)}) collective-permute-start(f16[256,768]{1,0:T(8,128)(2,1)S(1)} %fusion.9), channel_id=1, source_target_pairs={{0,4},{4,0},{8,12},{12,8},{1,5},{5,1},{9,13},{13,9},{2,6},{6,2},{1... | collective-permute-start | bytes 1179656 | tf_op jit(solution)/shard_map/ppermute | solution.py:66
  135.3 45.7 %copy-start.2 = (bf16[256,768]{1,0:T(8,128)(2,1)S(1)}, bf16[256,768]{1,0:T(8,128)(2,1)}, u32[]{:S(2)}) copy-start(bf16[256,768]{1,0:T(8,128)(2,1)} %get-tuple-element.31.key_ref) | copy-start | bytes 1179652
  135.3 18.5 %collective-permute-start.11 = (f16[256,768]{1,0:T(8,128)(2,1)}, f16[256,768]{1,0:T(8,128)(2,1)}, u32[]{:S(2)}, u32[]{:S(2)}) collective-permute-start(f16[256,768]{1,0:T(8,128)(2,1)} %get-tuple-element.37), channel_id=1, source_target_pairs={{4,8},{8,4},{5,9},{9,5},{6,10},{10,6},{7,11},{11,7},{20,24},{24,20... | collective-permute-start | bytes 1179656 | tf_op jit(solution)/shard_map/ppermute | solution.py:69
  136.9 42.6 %collective-permute-start.12 = (f16[256,768]{1,0:T(8,128)(2,1)S(1)}, f16[256,768]{1,0:T(8,128)(2,1)}, u32[]{:S(2)}, u32[]{:S(2)}) collective-permute-start(f16[256,768]{1,0:T(8,128)(2,1)S(1)} %get-tuple-element.36), channel_id=1, source_target_pairs={{4,12},{8,0},{5,13},{9,1},{6,14},{10,2},{7,15},{11,3},{20,28},{24,... | collective-permute-start | bytes 1179656 | tf_op jit(solution)/shard_map/ppermute | solution.py:70
  192.2 1.5 copy-start.3
  193.7 3.2 %collective-permute-start.21 = (bf16[256,2560]{1,0:T(8,128)(2,1)}, bf16[256,2560]{1,0:T(8,128)(2,1)S(1)}, u32[]{:S(2)}, u32[]{:S(2)}) collective-permute-start(bf16[256,2560]{1,0:T(8,128)(2,1)} %get-tuple-element.29), channel_id=1, source_target_pairs={{0,1},{1,0},{2,3},{3,2},{4,5},{5,4},{6,7},{7,6},{8,9},{9,8},{10,11... | collective-permute-start | bytes 3932168 | tf_op jit(solution)/shard_map/ppermute | solution.py:185
  193.7 21.5 %copy-start.4 = (f32[256,2560]{1,0:T(8,128)S(1)}, f32[256,2560]{1,0:T(8,128)}, u32[]{:S(2)}) copy-start(f32[256,2560]{1,0:T(8,128)} %copy-done.3) | copy-start | bytes 7864324
  198.4 16.8 %collective-permute-start.22 = (bf16[256,1280]{1,0:T(8,128)(2,1)S(1)}, bf16[256,1280]{1,0:T(8,128)(2,1)S(1)}, u32[]{:S(2)}, u32[]{:S(2)}) collective-permute-start(bf16[256,1280]{1,0:T(8,128)(2,1)S(1)} %add_convert_fusion.4), channel_id=1, source_target_pairs={{0,2},{1,3},{2,0},{3,1},{4,6},{5,7},{6,4},{7,5},{8,10},{9,11},{10,... | collective-permute-start | bytes 1966088 | tf_op jit(solution)/shard_map/ppermute | solution.py:193
  230.1 1.9 copy-start.9
  232.1 1.7 copy-start.8
Sparse Core Ops, SparseCore 0:
  125.6 48.7 all-gather.2
  193.9 36.1 all-gather.4

commit v4 on v3

--- a/solution.py
+++ b/solution.py
@@ -48,29 +48,64 @@
     return both_slabs(True), both_slabs(False)
 
 
-def sum_in_pairs(far, near, weight):
-    rank, patch = lax.axis_index("tensor"), lax.axis_index("patch")
-    core = rank % 2
-    rows, width = far.shape[0] // 2, weight.shape[1]
-
-    def parts(features):
-        return (jnp.dot(features, weight, preferred_element_type=F32) * LIFT).reshape(2, rows, width)
-
-    def slab(pair, odd):
-        return lax.dynamic_index_in_dim(pair, odd ^ core, 0, keepdims=False)
-
-    far_parts, near_parts = parts(far), parts(near)
-    outer = lax.ppermute(far_parts.astype(F16), "patch", [(0, 1), (3, 2)])
-    direct = slab(near_parts, 1 - patch % 2).astype(F16)
-    direct, outer = lax.optimization_barrier((direct, outer))
-    direct = lax.ppermute(direct, "patch", [(0, 1), (1, 0), (2, 3), (3, 2)])
-    summed = (far_parts + outer.astype(F32)).astype(F16)
-    over = patch // 2
-    inner_got = lax.ppermute(slab(summed, over), "patch", [(1, 2), (2, 1)])
-    outer_got = lax.ppermute(slab(summed, 1 - over), "patch", [(1, 3), (2, 0)])
-    total = slab(near_parts, patch % 2) + direct.astype(F32)
-    total = total + jnp.where((patch == 1) | (patch == 2), inner_got, outer_got).astype(F32)
-    return (total * (1.0 / LIFT)).astype(BF16)
+def after(value, *earlier):
+    return lax.optimization_barrier((value, *earlier))[0]
+
+
+class PairSum:
+    def __init__(self, far, near, weight):
+        self.patch = lax.axis_index("patch")
+        self.core = lax.axis_index("tensor") % 2
+        self.far, self.near = self.parts(far, weight), self.parts(near, weight)
+
+    def parts(self, features, weight):
+        product = jnp.dot(features, weight, preferred_element_type=F32) * LIFT
+        return product.reshape(2, features.shape[0] // 2, weight.shape[1])
+
+    def slab(self, pair, odd):
+        return lax.dynamic_index_in_dim(pair, odd ^ self.core, 0, keepdims=False)
+
+    def to_inner(self, *earlier):
+        send = after(self.far.astype(F16), *earlier)
+        self.outer = lax.ppermute(send, "patch", [(0, 1), (3, 2)])
+
+    def send_on(self):
+        direct = after(self.slab(self.near, 1 - self.patch % 2).astype(F16), self.outer)
+        summed = (self.far + self.outer.astype(F32)).astype(F16)
+        over = self.patch // 2
+        self.inner_got = lax.ppermute(self.slab(summed, over), "patch", [(1, 2), (2, 1)])
+        self.outer_got = lax.ppermute(self.slab(summed, 1 - over), "patch", [(1, 3), (2, 0)])
+        self.direct = lax.ppermute(direct, "patch", [(0, 1), (1, 0), (2, 3), (3, 2)])
+
+    def total(self, *earlier):
+        direct = after(self.direct, *earlier)
+        is_inner = (self.patch == 1) | (self.patch == 2)
+        total = self.slab(self.near, self.patch % 2) + direct.astype(F32)
+        total = total + jnp.where(is_inner, self.inner_got, self.outer_got).astype(F32)
+        return (total * (1.0 / LIFT)).astype(BF16)
+
+
+class PairGather:
+    def __init__(self, own):
+        self.own = own
+        self.mate = lax.ppermute(own, "patch", [(0, 1), (1, 0), (2, 3), (3, 2)])
+        self.across = lax.ppermute(own, "patch", [(1, 2), (2, 1)])
+
+    def into(self, whole, index, earlier):
+        patch = lax.axis_index("patch")
+        rows = self.own.shape[0]
+        is_inner = (patch == 1) | (patch == 2)
+        outward = [(1, 0), (2, 3)]
+        across_mate = lax.ppermute(self.mate, "patch", [(1, 2), (2, 1)])
+        far_inner = jnp.where(is_inner, self.across, lax.ppermute(self.across, "patch", outward))
+        last = lax.ppermute(after(across_mate, earlier), "patch", outward)
+        far_outer = jnp.where(is_inner, across_mate, last)
+        own = after(self.own, self.mate)
+        low = patch < 2
+        slabs = (patch, patch ^ 1, jnp.where(low, 2, 1), jnp.where(low, 3, 0))
+        for slab, block in zip(slabs, (own, self.mate, far_inner, far_outer)):
+            whole = lax.dynamic_update_slice(whole, block[None], (index, slab * rows, 0))
+        return whole
 
 
 def sum_own_slab(features, weight, patches):
@@ -194,19 +229,13 @@
     total = summed(chips - 1)
     for block in arrived:
         total = total + block.astype(F32)
-    return total.astype(BF16)
+    return total.astype(BF16), got
 
 
 def make_shards(patches, ranks):
     def shards(hidden_in, w_query, w_key, w_value, w_out, stale_kv):
         rows = hidden_in.shape[0]
         me = lax.axis_index("patch")
-        if patches == ranks == 4:
-            far, near = spread_in_pairs(hidden_in)
-            project = functools.partial(sum_in_pairs, far, near)
-        else:
-            features = spread_features(hidden_in)
-            project = lambda weight: sum_own_slab(features, weight, patches)
         own_stale = lax.dynamic_slice_in_dim(stale_kv, me * rows, rows, 1).astype(F32)
 
         def refresh(fresh, stale):
@@ -214,13 +243,35 @@
             delta = lax.reduce_precision(fresh - stale, 8, 7)
             return (stale + delta).astype(BF16)
 
-        key_new = refresh(project(w_key), own_stale[0])
-        keys_all = lax.all_gather(key_new, "patch", axis=0, tiled=True)
-        query = project(w_query)
-        value_new = refresh(project(w_value), own_stale[1])
-        values_all = lax.all_gather(value_new, "patch", axis=0, tiled=True)
-        refreshed = jnp.broadcast_to(keys_all[None], stale_kv.shape).at[1].set(values_all)
-        attended = attend(query, stale_kv, key_new, value_new, w_out, patches, ranks)
+        def gather(own):
+            return lax.all_gather(own, "patch", axis=0, tiled=True)
+
+        if patches == ranks == 4:
+            far, near = spread_in_pairs(hidden_in)
+            sums = [PairSum(far, near, weight) for weight in (w_key, w_value, w_query)]
+            keys, values, queries = sums
+            keys.to_inner()
+            values.to_inner()
+            queries.to_inner(keys.outer)
+            for each in sums:
+                each.send_on()
+            key_new = refresh(keys.total(), own_stale[0])
+            keys_all = gather(key_new)
+            value_new = refresh(values.total(key_new, queries.outer), own_stale[1])
+            gathered = PairGather(value_new)
+            query = after(queries.total(keys_all), gathered.mate, gathered.across)
+        else:
+            features = spread_features(hidden_in)
+            key_new, value_new = (
+                refresh(sum_own_slab(features, weight, patches), own_stale[i])
+                for i, weight in enumerate((w_key, w_value))
+            )
+            query = sum_own_slab(features, w_query, patches)
+        attended, got = attend(query, stale_kv, key_new, value_new, w_out, patches, ranks)
+        if patches == ranks == 4:
+            refreshed = gathered.into(jnp.broadcast_to(keys_all[None], stale_kv.shape), 1, got)
+        else:
+            refreshed = jnp.stack([gather(key_new), gather(value_new)])
         return (attended, refreshed)
 
     return shards

time: 241 us -> 243 us (level)
  the two profiles are of different devices: /device:TPU:0 before, /device:TPU:14 now
where the time goes in v4:
time: 243 us; the launch traced here: 242 us
  waiting for transfers between devices  135 us (56%)
  starting transfers between devices  42 us (17%)
  other arithmetic  18 us (7%)
  between operations  14.7 us (6%)
  matrix products  13.6 us (6%)
  Pallas kernels  11.2 us (5%)
  local copies, waits for them, and re-layouts  7.77 us (3%)
    ppermute x3, waiting for transfers between devices, send_on(): lax.ppermute(direct, 'patch', [(0, 1), (1, 0), (2, 3), (3, 2)])  56.3 us
    ppermute x3, waiting for transfers between devices, to_inner(): self.outer = lax.ppermute(send, 'patch', [(0, 1), (3, 2)])  17 us
    ppermute x4, waiting for transfers between devices, along(): return lax.ppermute(block, ('patch', 'tensor'), pairs)  14.7 us
    dot_general x6, matrix products, parts(): product = jnp.dot(features, weight, preferred_element_type=F32) * LIFT  13.6 us
    ppermute x2, waiting for transfers between devices, both_slabs(): other = lax.ppermute(held, 'tensor', across)  12.1 us
    pallas_call x1, Pallas kernels, attend(): pl.pallas_call(functools.partial(attend_and_project, patches, heads, chip...  11.2 us
    ppermute x1, waiting for transfers between devices, attend(): arrived.append(lax.ppermute(summed(hop - 1).astype(BF16), 'tensor', pairs))  9.05 us
    ppermute x3, starting transfers between devices, send_on(): lax.ppermute(self.slab(summed, over), 'patch', [(1, 2), (2, 1)])  7.96 us
  transfers between devices with their start and end apart: 29, of which 15 were waited for; matrix products, arithmetic and copies ran while one was open for 13% of the time, Pallas kernels for 0%

profile of v4, /device:TPU:14, one launch (start us, length us, event | category | flops | bytes accessed | tf_op | source)
XLA Modules:
  0.0 242.5 jit_solution(15496448077898079418)
XLA Ops:
  7.2 1.2 fusion.12
  8.5 0.6 collective-permute-start.1
  9.1 2.6 %collective-permute-start.5 = (bf16[128,1280]{1,0:T(8,128)(2,1)S(1)}, bf16[128,1280]{1,0:T(8,128)(2,1)S(1)}, u32[]{:S(2)}, u32[]{:S(2)}) collective-permute-start(bf16[128,1280]{1,0:T(8,128)(2,1)S(1)} %get-tuple-element.35), channel_id=1, source_target_pairs={{2,10},{3,14},{6,11},{7,15},{8,0},{9,4},{12,1},{13,5},{18,26},{19,... | collective-permute-start | bytes 983048 | tf_op jit(solution)/shard_map/ppermute | solution.py:37
  11.7 6.4 %collective-permute-done.1 = bf16[128,1280]{1,0:T(8,128)(2,1)} collective-permute-done((bf16[128,1280]{1,0:T(8,128)(2,1)S(1)}, bf16[128,1280]{1,0:T(8,128)(2,1)}, u32[]{:S(2)}, u32[]{:S(2)}) %collective-permute-start.1) | collective-permute-done | bytes 327712 | tf_op jit(solution)/shard_map/ppermute | solution.py:27
  18.1 1.3 collective-permute-start.6
  19.4 0.7 collective-permute-start
  20.1 1.9 collective-permute-start.2
  22.0 4.4 %collective-permute-done.5 = bf16[128,1280]{1,0:T(8,128)(2,1)S(1)} collective-permute-done((bf16[128,1280]{1,0:T(8,128)(2,1)S(1)}, bf16[128,1280]{1,0:T(8,128)(2,1)S(1)}, u32[]{:S(2)}, u32[]{:S(2)}) %collective-permute-start.5) | collective-permute-done | bytes 327712 | tf_op jit(solution)/shard_map/ppermute | solution.py:37
  26.5 10.2 %collective-permute-done.6 = bf16[128,1280]{1,0:T(8,128)(2,1)S(1)} collective-permute-done((bf16[128,1280]{1,0:T(8,128)(2,1)}, bf16[128,1280]{1,0:T(8,128)(2,1)S(1)}, u32[]{:S(2)}, u32[]{:S(2)}) %collective-permute-start.6) | collective-permute-done | bytes 327712 | tf_op jit(solution)/shard_map/ppermute | solution.py:37
  36.9 2.1 collective-permute-start.3
  38.9 8.5 %collective-permute-done.7 = bf16[128,1280]{1,0:T(8,128)(2,1)S(1)} collective-permute-done((bf16[128,1280]{1,0:T(8,128)(2,1)S(1)}, bf16[128,1280]{1,0:T(8,128)(2,1)S(1)}, u32[]{:S(2)}, u32[]{:S(2)}) %collective-permute-start.7) | collective-permute-done | bytes 327712 | tf_op jit(solution)/shard_map/ppermute | solution.py:41
  47.6 3.6 %collective-permute-done.3 = bf16[128,1280]{1,0:T(8,128)(2,1)S(1)} collective-permute-done((bf16[128,1280]{1,0:T(8,128)(2,1)S(1)}, bf16[128,1280]{1,0:T(8,128)(2,1)S(1)}, u32[]{:S(2)}, u32[]{:S(2)}) %collective-permute-start.3) | collective-permute-done | bytes 327712 | tf_op jit(solution)/shard_map/ppermute | solution.py:41
  51.3 1.0 pad_maximum_fusion.2
  52.4 1.2 convolution_multiply_fusion.3
  53.6 1.0 convert_element_type.105
  54.6 1.3 collective-permute-start.9
  55.9 2.5 %convolution_multiply_fusion.2 = f32[512,768]{1,0:T(8,128)S(1)} fusion(bf16[1280,768]{1,0:T(8,128)(2,1)S(1)} %copy-done, bf16[256,1280]{1,0:T(8,128)(2,1)} %collective-permute-done.4, bf16[128,1280]{1,0:T(8,128)(2,1)} %copy-done.16, bf16[128,1280]{1,0:T(8,128)(2,1)} %copy-done.14), kind=kOutput, calls=%fused_computation.5 | convolution fusion | flops 1010958336 | bytes 4849664 | tf_op jit(solution)/shard_map/dot_general | solution.py:62
  58.4 0.9 fusion.10
  59.3 0.4 copy-done.8
  59.7 17.0 %collective-permute-done.9 = f16[2,256,768]{2,1,0:T(8,128)(2,1)} collective-permute-done((f16[2,256,768]{2,1,0:T(8,128)(2,1)}, f16[2,256,768]{2,1,0:T(8,128)(2,1)}, u32[]{:S(2)}, u32[]{:S(2)}) %collective-permute-start.9) | collective-permute-done | bytes 786464 | tf_op jit(solution)/shard_map/ppermute | solution.py:70
  76.7 1.3 add_convert_fusion.2
  78.0 1.0 dynamic-slice_bitcast_fusion.4
  79.0 3.9 %collective-permute-start.13 = (f16[256,768]{1,0:T(8,128)(2,1)}, f16[256,768]{1,0:T(8,128)(2,1)}, u32[]{:S(2)}, u32[]{:S(2)}) collective-permute-start(f16[256,768]{1,0:T(8,128)(2,1)} %get-tuple-element.29), channel_id=1, source_target_pairs={{4,8},{8,4},{5,9},{9,5},{6,10},{10,6},{7,11},{11,7},{20,24},{24,20... | collective-permute-start | bytes 1179656 | tf_op jit(solution)/shard_map/ppermute | solution.py:76
  82.9 2.0 collective-permute-start.14
  85.0 2.4 dynamic-slice_convert_fusion.2
  87.3 3.2 %convolution_multiply_fusion = f32[512,768]{1,0:T(8,128)S(1)} fusion(bf16[1280,768]{1,0:T(8,128)(2,1)} %param.9, bf16[256,1280]{1,0:T(8,128)(2,1)} %copy-done.19, bf16[128,1280]{1,0:T(8,128)(2,1)} %copy-done.12, bf16[128,1280]{1,0:T(8,128)(2,1)} %copy-done.10), kind=kOutput, calls=%fused_computation.3 | convolution fusion | flops 1010958336 | bytes 4849664 | tf_op jit(solution)/shard_map/dot_general | solution.py:62
  90.6 1.0 convert_element_type.123
  91.6 1.3 collective-permute-start.17
  92.9 9.0 %collective-permute-done.12 = f16[256,768]{1,0:T(8,128)(2,1)} collective-permute-done((f16[256,768]{1,0:T(8,128)(2,1)}, f16[256,768]{1,0:T(8,128)(2,1)}, u32[]{:S(2)}, u32[]{:S(2)}) %collective-permute-start.12) | collective-permute-done | bytes 393248 | tf_op jit(solution)/shard_map/ppermute | solution.py:78
  101.9 2.2 add_convert_fusion.6.key_ref
  104.2 3.3 %convolution_multiply_fusion.1 = f32[512,768]{1,0:T(8,128)S(1)} fusion(bf16[1280,768]{1,0:T(8,128)(2,1)} %param.9, bf16[256,1280]{1,0:T(8,128)(2,1)} %collective-permute-done.4, bf16[128,1280]{1,0:T(8,128)(2,1)} %copy-done.16, bf16[128,1280]{1,0:T(8,128)(2,1)} %copy-done.14), kind=kOutput, calls=%fused_computation.4 | convolution fusion | flops 1010958336 | bytes 4849664 | tf_op jit(solution)/shard_map/dot_general | solution.py:62
  107.6 1.2 convolution_multiply_fusion.4
  108.9 1.4 collective-permute-start.10
  110.3 2.3 convolution_multiply_fusion.5
  112.7 0.9 fusion.9
  113.6 0.3 copy-done.7
  113.9 2.7 %collective-permute-start.18 = (f16[256,768]{1,0:T(8,128)(2,1)S(1)}, f16[256,768]{1,0:T(8,128)(2,1)S(1)}, u32[]{:S(2)}, u32[]{:S(2)}) collective-permute-start(f16[256,768]{1,0:T(8,128)(2,1)S(1)} %fusion.11), channel_id=1, source_target_pairs={{0,4},{4,0},{8,12},{12,8},{1,5},{5,1},{9,13},{13,9},{2,6},{6,2},{1... | collective-permute-start | bytes 1179656 | tf_op jit(solution)/shard_map/ppermute | solution.py:78
  116.6 1.3 add_convert_fusion
  118.1 2.2 collective-permute-start.19
  120.2 1.3 collective-permute-start.20
  121.6 41.5 %collective-permute-done.18 = f16[256,768]{1,0:T(8,128)(2,1)S(1)} collective-permute-done((f16[256,768]{1,0:T(8,128)(2,1)S(1)}, f16[256,768]{1,0:T(8,128)(2,1)S(1)}, u32[]{:S(2)}, u32[]{:S(2)}) %collective-permute-start.18) | collective-permute-done | bytes 393248 | tf_op jit(solution)/shard_map/ppermute | solution.py:78
  163.1 0.2 add_convert_fusion.1
  163.3 1.0 dynamic-slice_bitcast_fusion.2
  164.3 1.9 collective-permute-start.15
  166.2 2.1 collective-permute-start.16
  168.3 0.3 add_convert_fusion.5.value_ref
  168.6 2.1 collective-permute-start.21
  170.7 4.1 %collective-permute-start.22 = (bf16[256,768]{1,0:T(8,128)(2,1)S(1)}, bf16[256,768]{1,0:T(8,128)(2,1)S(1)}, u32[]{:S(2)}, u32[]{:S(2)}) collective-permute-start(bf16[256,768]{1,0:T(8,128)(2,1)S(1)} %add_convert_fusion.5.value_ref), channel_id=1, source_target_pairs={{4,8},{8,4},{5,9},{9,5},{6,10},{10,6},{7,11},{11,7},{20,24},{24,20... | collective-permute-start | bytes 1179656 | tf_op jit(solution)/shard_map/ppermute | solution.py:92
  174.9 5.8 %collective-permute-done.11 = f16[256,768]{1,0:T(8,128)(2,1)} collective-permute-done((f16[256,768]{1,0:T(8,128)(2,1)}, f16[256,768]{1,0:T(8,128)(2,1)}, u32[]{:S(2)}, u32[]{:S(2)}) %collective-permute-start.11) | collective-permute-done | bytes 393248 | tf_op jit(solution)/shard_map/ppermute | solution.py:78
  180.7 1.4 collective-permute-done.16
  182.1 1.5 fusion.8.query_ref
  183.6 4.6 %collective-permute-done.21 = bf16[256,768]{1,0:T(8,128)(2,1)S(1)} collective-permute-done((bf16[256,768]{1,0:T(8,128)(2,1)S(1)}, bf16[256,768]{1,0:T(8,128)(2,1)S(1)}, u32[]{:S(2)}, u32[]{:S(2)}) %collective-permute-start.21) | collective-permute-done | bytes 393248 | tf_op jit(solution)/shard_map/ppermute | solution.py:91
  188.2 0.2 collective-permute-done.22
  188.4 11.2 %shard_map.77 = (bf16[256,2560]{1,0:T(8,128)(2,1)}, f32[256,2560]{1,0:T(8,128)S(1)}) custom-call(s32[5]{0:T(128)S(1)} %stack.23.place_ref, bf16[256,768]{1,0:T(8,128)(2,1)S(1)} %fusion.8.query_ref, bf16[2,1024,768]{2,1,0:T(8,128)(2,1)} %stale_ref.1, bf16[256,768]{1,0:T(8,128)(2,1)S(1)} %copy-done.1, bf16[256,768]{1,0:T(8,128)(2,1)S(1)} %add_convert_fusion.5.value_ref, ...), custom_call_target="tpu_custom_call" | custom-call | flops 2818572288 | bytes 14942208 | tf_op jit(solution)/shard_map/pallas_call | solution.py:191
  199.6 1.5 copy-done.2
  201.1 3.4 %collective-permute-start.26 = (bf16[256,768]{1,0:T(8,128)(2,1)S(1)}, bf16[256,768]{1,0:T(8,128)(2,1)S(1)}, u32[]{:S(2)}, u32[]{:S(2)}) collective-permute-start(bf16[256,768]{1,0:T(8,128)(2,1)S(1)} %collective-permute-done.21), channel_id=1, source_target_pairs={{4,8},{8,4},{5,9},{9,5},{6,10},{10,6},{7,11},{11,7},{20,24},{24,20... | collective-permute-start | bytes 1179656 | tf_op jit(solution)/shard_map/ppermute | solution.py:99
  204.5 1.5 collective-permute-start.25
  206.0 1.8 broadcast_in_dim.18
  207.8 6.7 %collective-permute-done.26 = bf16[256,768]{1,0:T(8,128)(2,1)S(1)} collective-permute-done((bf16[256,768]{1,0:T(8,128)(2,1)S(1)}, bf16[256,768]{1,0:T(8,128)(2,1)S(1)}, u32[]{:S(2)}, u32[]{:S(2)}) %collective-permute-start.26) | collective-permute-done | bytes 393248 | tf_op jit(solution)/shard_map/ppermute | solution.py:99
  214.5 1.3 collective-permute-start.27
  215.8 1.2 add_convert_fusion.4
  217.4 6.9 %collective-permute-done.27 = bf16[256,768]{1,0:T(8,128)(2,1)S(1)} collective-permute-done((bf16[256,768]{1,0:T(8,128)(2,1)S(1)}, bf16[256,768]{1,0:T(8,128)(2,1)S(1)}, u32[]{:S(2)}, u32[]{:S(2)}) %collective-permute-start.27) | collective-permute-done | bytes 393248 | tf_op jit(solution)/shard_map/ppermute | solution.py:101
  224.4 9.1 %collective-permute-done.24 = bf16[256,1280]{1,0:T(8,128)(2,1)S(1)} collective-permute-done((bf16[256,1280]{1,0:T(8,128)(2,1)S(1)}, bf16[256,1280]{1,0:T(8,128)(2,1)S(1)}, u32[]{:S(2)}, u32[]{:S(2)}) %collective-permute-start.24) | collective-permute-done | bytes 655392 | tf_op jit(solution)/shard_map/ppermute | solution.py:228
  233.5 2.2 add_convert_fusion.3
  (75 shorter events, 1.5 us)
Async XLA Ops:
  7.2 45.2 %copy-start = (bf16[1280,768]{1,0:T(8,128)(2,1)S(1)}, bf16[1280,768]{1,0:T(8,128)(2,1)}, u32[]{:S(2)}) copy-start(bf16[1280,768]{1,0:T(8,128)(2,1)} %param.8) | copy-start | bytes 5898244
  7.2 173.5 %all-gather.2.cloned.1.call-start = ((), (), s32[]{:S(2)}) async-start(), calls=%async_computation | async-start | bytes 1966080 | tf_op jit(solution)/shard_map/all_gather | solution.py:247
  8.5 9.6 %collective-permute-start.1 = (bf16[128,1280]{1,0:T(8,128)(2,1)S(1)}, bf16[128,1280]{1,0:T(8,128)(2,1)}, u32[]{:S(2)}, u32[]{:S(2)}) collective-permute-start(bf16[128,1280]{1,0:T(8,128)(2,1)S(1)} %get-tuple-element.34), channel_id=1, source_target_pairs={{0,2},{1,3},{2,0},{3,1},{4,6},{5,7},{6,4},{7,5},{8,10},{9,11},{10,... | collective-permute-start | bytes 983048 | tf_op jit(solution)/shard_map/ppermute | solution.py:27
  9.1 17.4 %collective-permute-start.5 = (bf16[128,1280]{1,0:T(8,128)(2,1)S(1)}, bf16[128,1280]{1,0:T(8,128)(2,1)S(1)}, u32[]{:S(2)}, u32[]{:S(2)}) collective-permute-start(bf16[128,1280]{1,0:T(8,128)(2,1)S(1)} %get-tuple-element.35), channel_id=1, source_target_pairs={{2,10},{3,14},{6,11},{7,15},{8,0},{9,4},{12,1},{13,5},{18,26},{19,... | collective-permute-start | bytes 983048 | tf_op jit(solution)/shard_map/ppermute | solution.py:37
  18.1 18.6 %collective-permute-start.6 = (bf16[128,1280]{1,0:T(8,128)(2,1)}, bf16[128,1280]{1,0:T(8,128)(2,1)S(1)}, u32[]{:S(2)}, u32[]{:S(2)}) collective-permute-start(bf16[128,1280]{1,0:T(8,128)(2,1)} %collective-permute-done.1), channel_id=1, source_target_pairs={{0,8},{1,12},{4,9},{5,13},{10,2},{11,6},{14,3},{15,7},{16,24},{17,... | collective-permute-start | bytes 983048 | tf_op jit(solution)/shard_map/ppermute | solution.py:37
  19.4 17.4 %collective-permute-start = (bf16[128,1280]{1,0:T(8,128)(2,1)S(1)}, bf16[128,1280]{1,0:T(8,128)(2,1)S(1)}, u32[]{:S(2)}, u32[]{:S(2)}) collective-permute-start(bf16[128,1280]{1,0:T(8,128)(2,1)S(1)} %get-tuple-element.35), channel_id=1, source_target_pairs={{0,0},{1,4},{4,1},{5,5},{10,10},{11,14},{14,11},{15,15},{16,16},{1... | collective-permute-start | bytes 983048 | tf_op jit(solution)/shard_map/ppermute | solution.py:37
  20.1 16.7 %collective-permute-start.2 = (bf16[128,1280]{1,0:T(8,128)(2,1)}, bf16[128,1280]{1,0:T(8,128)(2,1)S(1)}, u32[]{:S(2)}, u32[]{:S(2)}) collective-permute-start(bf16[128,1280]{1,0:T(8,128)(2,1)} %collective-permute-done.1), channel_id=1, source_target_pairs={{2,2},{3,6},{6,3},{7,7},{8,8},{9,12},{12,9},{13,13},{18,18},{19,22... | collective-permute-start | bytes 983048 | tf_op jit(solution)/shard_map/ppermute | solution.py:37
  36.7 10.7 %collective-permute-start.7 = (bf16[128,1280]{1,0:T(8,128)(2,1)S(1)}, bf16[128,1280]{1,0:T(8,128)(2,1)S(1)}, u32[]{:S(2)}, u32[]{:S(2)}) collective-permute-start(bf16[128,1280]{1,0:T(8,128)(2,1)S(1)} %broadcast_select_fusion.2), channel_id=1, source_target_pairs={{0,2},{1,3},{2,0},{3,1},{4,6},{5,7},{6,4},{7,5},{8,10},{9,11},{10,... | collective-permute-start | bytes 983048 | tf_op jit(solution)/shard_map/ppermute | solution.py:41
  36.9 14.3 %collective-permute-start.3 = (bf16[128,1280]{1,0:T(8,128)(2,1)S(1)}, bf16[128,1280]{1,0:T(8,128)(2,1)S(1)}, u32[]{:S(2)}, u32[]{:S(2)}) collective-permute-start(bf16[128,1280]{1,0:T(8,128)(2,1)S(1)} %broadcast_select_fusion.5), channel_id=1, source_target_pairs={{0,2},{1,3},{2,0},{3,1},{4,6},{5,7},{6,4},{7,5},{8,10},{9,11},{10,... | collective-permute-start | bytes 983048 | tf_op jit(solution)/shard_map/ppermute | solution.py:41
  47.5 4.8 %copy-start.10 = (bf16[128,1280]{1,0:T(8,128)(2,1)}, bf16[128,1280]{1,0:T(8,128)(2,1)S(1)}, u32[]{:S(2)}) copy-start(bf16[128,1280]{1,0:T(8,128)(2,1)S(1)} %get-tuple-element.30) | copy-start | bytes 983044
  47.5 4.8 %copy-start.12 = (bf16[128,1280]{1,0:T(8,128)(2,1)}, bf16[128,1280]{1,0:T(8,128)(2,1)S(1)}, u32[]{:S(2)}) copy-start(bf16[128,1280]{1,0:T(8,128)(2,1)S(1)} %get-tuple-element.31) | copy-start | bytes 983044
  47.6 4.8 %collective-permute-start.8 = (bf16[256,1280]{1,0:T(8,128)(2,1)S(1)}, bf16[256,1280]{1,0:T(8,128)(2,1)S(1)}, u32[]{:S(2)}, u32[]{:S(2)}) collective-permute-start(bf16[256,1280]{1,0:T(8,128)(2,1)S(1)} %pad_maximum_fusion.3), channel_id=1, source_target_pairs={{0,1},{1,0},{2,3},{3,2},{4,5},{5,4},{6,7},{7,6},{8,9},{9,8},{10,11... | collective-permute-start | bytes 1966088 | tf_op jit(solution)/shard_map/ppermute | solution.py:45
  51.3 1.0 copy-start.14
  51.3 1.1 copy-start.16
  52.2 3.7 %collective-permute-start.4 = (bf16[256,1280]{1,0:T(8,128)(2,1)}, bf16[256,1280]{1,0:T(8,128)(2,1)}, u32[]{:S(2)}, u32[]{:S(2)}) collective-permute-start(bf16[256,1280]{1,0:T(8,128)(2,1)} %pad_maximum_fusion.2), channel_id=1, source_target_pairs={{0,1},{1,0},{2,3},{3,2},{4,5},{5,4},{6,7},{7,6},{8,9},{9,8},{10,11... | collective-permute-start | bytes 1966088 | tf_op jit(solution)/shard_map/ppermute | solution.py:45
  52.4 1.2 copy-start.19
  54.6 22.1 %collective-permute-start.9 = (f16[2,256,768]{2,1,0:T(8,128)(2,1)}, f16[2,256,768]{2,1,0:T(8,128)(2,1)}, u32[]{:S(2)}, u32[]{:S(2)}) collective-permute-start(f16[2,256,768]{2,1,0:T(8,128)(2,1)} %convert_element_type.105), channel_id=1, source_target_pairs={{0,4},{12,8},{1,5},{13,9},{2,6},{14,10},{3,7},{15,11},{16,20},{28,... | collective-permute-start | bytes 2359304 | tf_op jit(solution)/shard_map/ppermute | solution.py:70
  58.4 1.3 copy-start.8
  79.0 22.9 %collective-permute-start.13 = (f16[256,768]{1,0:T(8,128)(2,1)}, f16[256,768]{1,0:T(8,128)(2,1)}, u32[]{:S(2)}, u32[]{:S(2)}) collective-permute-start(f16[256,768]{1,0:T(8,128)(2,1)} %get-tuple-element.29), channel_id=1, source_target_pairs={{4,8},{8,4},{5,9},{9,5},{6,10},{10,6},{7,11},{11,7},{20,24},{24,20... | collective-permute-start | bytes 1179656 | tf_op jit(solution)/shard_map/ppermute | solution.py:76
  82.9 19.0 %collective-permute-start.14 = (f16[256,768]{1,0:T(8,128)(2,1)}, f16[256,768]{1,0:T(8,128)(2,1)}, u32[]{:S(2)}, u32[]{:S(2)}) collective-permute-start(f16[256,768]{1,0:T(8,128)(2,1)} %get-tuple-element.28), channel_id=1, source_target_pairs={{4,12},{8,0},{5,13},{9,1},{6,14},{10,2},{7,15},{11,3},{20,28},{24,... | collective-permute-start | bytes 1179656 | tf_op jit(solution)/shard_map/ppermute | solution.py:77
  85.0 16.9 %collective-permute-start.12 = (f16[256,768]{1,0:T(8,128)(2,1)}, f16[256,768]{1,0:T(8,128)(2,1)}, u32[]{:S(2)}, u32[]{:S(2)}) collective-permute-start(f16[256,768]{1,0:T(8,128)(2,1)} %fusion.10), channel_id=1, source_target_pairs={{0,4},{4,0},{8,12},{12,8},{1,5},{5,1},{9,13},{13,9},{2,6},{6,2},{1... | collective-permute-start | bytes 1179656 | tf_op jit(solution)/shard_map/ppermute | solution.py:78
  87.3 14.6 %copy-start.9 = (f32[512,768]{1,0:T(8,128)S(1)}, f32[512,768]{1,0:T(8,128)}, u32[]{:S(2)}) copy-start(f32[512,768]{1,0:T(8,128)} %copy-done.8) | copy-start | bytes 4718596
  90.6 11.3 %copy-start.4 = (f32[2,256,768]{2,1,0:T(8,128)S(1)}, f32[2,256,768]{2,1,0:T(8,128)}, u32[]{:S(2)}) copy-start(f32[2,256,768]{2,1,0:T(8,128)} %dynamic-slice_convert_fusion.2) | copy-start | bytes 4718596
  91.6 22.0 %collective-permute-start.17 = (f16[2,256,768]{2,1,0:T(8,128)(2,1)}, f16[2,256,768]{2,1,0:T(8,128)(2,1)}, u32[]{:S(2)}, u32[]{:S(2)}) collective-permute-start(f16[2,256,768]{2,1,0:T(8,128)(2,1)} %convert_element_type.123), channel_id=1, source_target_pairs={{0,4},{12,8},{1,5},{13,9},{2,6},{14,10},{3,7},{15,11},{16,20},{28,... | collective-permute-start | bytes 2359304 | tf_op jit(solution)/shard_map/ppermute | solution.py:70
  104.2 3.3 %copy-start.11 = (bf16[128,1280]{1,0:T(8,128)(2,1)S(1)}, bf16[128,1280]{1,0:T(8,128)(2,1)}, u32[]{:S(2)}) copy-start(bf16[128,1280]{1,0:T(8,128)(2,1)} %copy-done.10) | copy-start | bytes 983044
  104.2 3.3 %copy-start.13 = (bf16[128,1280]{1,0:T(8,128)(2,1)S(1)}, bf16[128,1280]{1,0:T(8,128)(2,1)}, u32[]{:S(2)}) copy-start(bf16[128,1280]{1,0:T(8,128)(2,1)} %copy-done.12) | copy-start | bytes 983044
  104.2 3.3 %copy-start.18 = (bf16[1280,768]{1,0:T(8,128)(2,1)S(1)}, bf16[1280,768]{1,0:T(8,128)(2,1)}, u32[]{:S(2)}) copy-start(bf16[1280,768]{1,0:T(8,128)(2,1)} %param.7) | copy-start | bytes 5898244
  104.2 3.3 %copy-start.20 = (bf16[256,1280]{1,0:T(8,128)(2,1)S(1)}, bf16[256,1280]{1,0:T(8,128)(2,1)}, u32[]{:S(2)}) copy-start(bf16[256,1280]{1,0:T(8,128)(2,1)} %copy-done.19) | copy-start | bytes 1966084
  108.8 1.6 copy-start.15
  108.8 1.6 copy-start.17
  108.9 54.2 %collective-permute-start.10 = (f16[2,256,768]{2,1,0:T(8,128)(2,1)S(1)}, f16[2,256,768]{2,1,0:T(8,128)(2,1)S(1)}, u32[]{:S(2)}, u32[]{:S(2)}) collective-permute-start(f16[2,256,768]{2,1,0:T(8,128)(2,1)S(1)} %convert_element_type.104), channel_id=1, source_target_pairs={{0,4},{12,8},{1,5},{13,9},{2,6},{14,10},{3,7},{15,11},{16,20},{28,... | collective-permute-start | bytes 2359304 | tf_op jit(solution)/shard_map/ppermute | solution.py:70
  112.6 1.3 copy-start.7
  113.9 49.2 %collective-permute-start.18 = (f16[256,768]{1,0:T(8,128)(2,1)S(1)}, f16[256,768]{1,0:T(8,128)(2,1)S(1)}, u32[]{:S(2)}, u32[]{:S(2)}) collective-permute-start(f16[256,768]{1,0:T(8,128)(2,1)S(1)} %fusion.11), channel_id=1, source_target_pairs={{0,4},{4,0},{8,12},{12,8},{1,5},{5,1},{9,13},{13,9},{2,6},{6,2},{1... | collective-permute-start | bytes 1179656 | tf_op jit(solution)/shard_map/ppermute | solution.py:78
  118.1 50.2 %collective-permute-start.19 = (f16[256,768]{1,0:T(8,128)(2,1)S(1)}, f16[256,768]{1,0:T(8,128)(2,1)S(1)}, u32[]{:S(2)}, u32[]{:S(2)}) collective-permute-start(f16[256,768]{1,0:T(8,128)(2,1)S(1)} %get-tuple-element.25), channel_id=1, source_target_pairs={{4,8},{8,4},{5,9},{9,5},{6,10},{10,6},{7,11},{11,7},{20,24},{24,20... | collective-permute-start | bytes 1179656 | tf_op jit(solution)/shard_map/ppermute | solution.py:76
  120.2 48.0 %collective-permute-start.20 = (f16[256,768]{1,0:T(8,128)(2,1)S(1)}, f16[256,768]{1,0:T(8,128)(2,1)S(1)}, u32[]{:S(2)}, u32[]{:S(2)}) collective-permute-start(f16[256,768]{1,0:T(8,128)(2,1)S(1)} %get-tuple-element.24), channel_id=1, source_target_pairs={{4,12},{8,0},{5,13},{9,1},{6,14},{10,2},{7,15},{11,3},{20,28},{24,... | collective-permute-start | bytes 1179656 | tf_op jit(solution)/shard_map/ppermute | solution.py:77
  163.3 5.0 %copy-start.5 = (f32[2,256,768]{2,1,0:T(8,128)S(1)}, f32[2,256,768]{2,1,0:T(8,128)}, u32[]{:S(2)}) copy-start(f32[2,256,768]{2,1,0:T(8,128)} %dynamic-slice_convert_fusion.2) | copy-start | bytes 4718596
  164.3 16.4 %collective-permute-start.15 = (f16[256,768]{1,0:T(8,128)(2,1)}, f16[256,768]{1,0:T(8,128)(2,1)}, u32[]{:S(2)}, u32[]{:S(2)}) collective-permute-start(f16[256,768]{1,0:T(8,128)(2,1)} %get-tuple-element.27), channel_id=1, source_target_pairs={{4,8},{8,4},{5,9},{9,5},{6,10},{10,6},{7,11},{11,7},{20,24},{24,20... | collective-permute-start | bytes 1179656 | tf_op jit(solution)/shard_map/ppermute | solution.py:76
  166.2 15.9 %collective-permute-start.16 = (f16[256,768]{1,0:T(8,128)(2,1)}, f16[256,768]{1,0:T(8,128)(2,1)}, u32[]{:S(2)}, u32[]{:S(2)}) collective-permute-start(f16[256,768]{1,0:T(8,128)(2,1)} %get-tuple-element.26), channel_id=1, source_target_pairs={{4,12},{8,0},{5,13},{9,1},{6,14},{10,2},{7,15},{11,3},{20,28},{24,... | collective-permute-start | bytes 1179656 | tf_op jit(solution)/shard_map/ppermute | solution.py:77
  168.3 12.4 %collective-permute-start.11 = (f16[256,768]{1,0:T(8,128)(2,1)}, f16[256,768]{1,0:T(8,128)(2,1)}, u32[]{:S(2)}, u32[]{:S(2)}) collective-permute-start(f16[256,768]{1,0:T(8,128)(2,1)} %fusion.9), channel_id=1, source_target_pairs={{0,4},{4,0},{8,12},{12,8},{1,5},{5,1},{9,13},{13,9},{2,6},{6,2},{1... | collective-permute-start | bytes 1179656 | tf_op jit(solution)/shard_map/ppermute | solution.py:78
  168.6 19.8 %copy-start.1 = (bf16[256,768]{1,0:T(8,128)(2,1)S(1)}, bf16[256,768]{1,0:T(8,128)(2,1)}, u32[]{:S(2)}) copy-start(bf16[256,768]{1,0:T(8,128)(2,1)} %add_convert_fusion.6.key_ref) | copy-start | bytes 1179652
  168.6 19.6 %collective-permute-start.21 = (bf16[256,768]{1,0:T(8,128)(2,1)S(1)}, bf16[256,768]{1,0:T(8,128)(2,1)S(1)}, u32[]{:S(2)}, u32[]{:S(2)}) collective-permute-start(bf16[256,768]{1,0:T(8,128)(2,1)S(1)} %add_convert_fusion.5.value_ref), channel_id=1, source_target_pairs={{0,4},{4,0},{8,12},{12,8},{1,5},{5,1},{9,13},{13,9},{2,6},{6,2},{1... | collective-permute-start | bytes 1179656 | tf_op jit(solution)/shard_map/ppermute | solution.py:91
  170.7 17.7 %collective-permute-start.22 = (bf16[256,768]{1,0:T(8,128)(2,1)S(1)}, bf16[256,768]{1,0:T(8,128)(2,1)S(1)}, u32[]{:S(2)}, u32[]{:S(2)}) collective-permute-start(bf16[256,768]{1,0:T(8,128)(2,1)S(1)} %add_convert_fusion.5.value_ref), channel_id=1, source_target_pairs={{4,8},{8,4},{5,9},{9,5},{6,10},{10,6},{7,11},{11,7},{20,24},{24,20... | collective-permute-start | bytes 1179656 | tf_op jit(solution)/shard_map/ppermute | solution.py:92
  199.6 1.5 copy-start.2
  201.1 13.4 %collective-permute-start.23 = (bf16[256,2560]{1,0:T(8,128)(2,1)}, bf16[256,2560]{1,0:T(8,128)(2,1)}, u32[]{:S(2)}, u32[]{:S(2)}) collective-permute-start(bf16[256,2560]{1,0:T(8,128)(2,1)} %get-tuple-element.21), channel_id=1, source_target_pairs={{0,1},{1,0},{2,3},{3,2},{4,5},{5,4},{6,7},{7,6},{8,9},{9,8},{10,11... | collective-permute-start | bytes 3932168 | tf_op jit(solution)/shard_map/ppermute | solution.py:220
  201.1 13.4 %collective-permute-start.26 = (bf16[256,768]{1,0:T(8,128)(2,1)S(1)}, bf16[256,768]{1,0:T(8,128)(2,1)S(1)}, u32[]{:S(2)}, u32[]{:S(2)}) collective-permute-start(bf16[256,768]{1,0:T(8,128)(2,1)S(1)} %collective-permute-done.21), channel_id=1, source_target_pairs={{4,8},{8,4},{5,9},{9,5},{6,10},{10,6},{7,11},{11,7},{20,24},{24,20... | collective-permute-start | bytes 1179656 | tf_op jit(solution)/shard_map/ppermute | solution.py:99
  204.5 12.7 %collective-permute-start.25 = (bf16[256,768]{1,0:T(8,128)(2,1)S(1)}, bf16[256,768]{1,0:T(8,128)(2,1)S(1)}, u32[]{:S(2)}, u32[]{:S(2)}) collective-permute-start(bf16[256,768]{1,0:T(8,128)(2,1)S(1)} %collective-permute-done.22), channel_id=1, source_target_pairs={{4,0},{8,12},{5,1},{9,13},{6,2},{10,14},{7,3},{11,15},{20,16},{24,... | collective-permute-start | bytes 1179656 | tf_op jit(solution)/shard_map/ppermute | solution.py:100
  206.0 9.8 %copy-start.3 = (f32[256,2560]{1,0:T(8,128)S(1)}, f32[256,2560]{1,0:T(8,128)}, u32[]{:S(2)}) copy-start(f32[256,2560]{1,0:T(8,128)} %copy-done.2) | copy-start | bytes 7864324
  214.5 9.8 %collective-permute-start.27 = (bf16[256,768]{1,0:T(8,128)(2,1)S(1)}, bf16[256,768]{1,0:T(8,128)(2,1)S(1)}, u32[]{:S(2)}, u32[]{:S(2)}) collective-permute-start(bf16[256,768]{1,0:T(8,128)(2,1)S(1)} %collective-permute-done.26), channel_id=1, source_target_pairs={{4,0},{8,12},{5,1},{9,13},{6,2},{10,14},{7,3},{11,15},{20,16},{24,... | collective-permute-start | bytes 1179656 | tf_op jit(solution)/shard_map/ppermute | solution.py:101
  217.1 16.4 %collective-permute-start.24 = (bf16[256,1280]{1,0:T(8,128)(2,1)S(1)}, bf16[256,1280]{1,0:T(8,128)(2,1)S(1)}, u32[]{:S(2)}, u32[]{:S(2)}) collective-permute-start(bf16[256,1280]{1,0:T(8,128)(2,1)S(1)} %add_convert_fusion.4), channel_id=1, source_target_pairs={{0,2},{1,3},{2,0},{3,1},{4,6},{5,7},{6,4},{7,5},{8,10},{9,11},{10,... | collective-permute-start | bytes 1966088 | tf_op jit(solution)/shard_map/ppermute | solution.py:228
  224.4 11.2 %copy-start.6 = (bf16[2,1024,768]{2,1,0:T(8,128)(2,1)}, bf16[2,1024,768]{2,1,0:T(8,128)(2,1)S(1)}, u32[]{:S(2)}) copy-start(bf16[2,1024,768]{2,1,0:T(8,128)(2,1)S(1)} %bitcast_dynamic-update-slice_fusion) | copy-start | bytes 9437188
Sparse Core Ops, SparseCore 0:
  104.3 59.0 all-gather.1

commit v5 on v4

--- a/solution.py
+++ b/solution.py
@@ -49,6 +49,8 @@
 
 
 def after(value, *earlier):
+    if not earlier:
+        return value
     return lax.optimization_barrier((value, *earlier))[0]
 
 
@@ -59,19 +61,19 @@
         self.far, self.near = self.parts(far, weight), self.parts(near, weight)
 
     def parts(self, features, weight):
-        product = jnp.dot(features, weight, preferred_element_type=F32) * LIFT
+        product = (jnp.dot(features, weight, preferred_element_type=F32) * LIFT).astype(F16)
         return product.reshape(2, features.shape[0] // 2, weight.shape[1])
 
     def slab(self, pair, odd):
         return lax.dynamic_index_in_dim(pair, odd ^ self.core, 0, keepdims=False)
 
     def to_inner(self, *earlier):
-        send = after(self.far.astype(F16), *earlier)
-        self.outer = lax.ppermute(send, "patch", [(0, 1), (3, 2)])
-
-    def send_on(self):
-        direct = after(self.slab(self.near, 1 - self.patch % 2).astype(F16), self.outer)
-        summed = (self.far + self.outer.astype(F32)).astype(F16)
+        self.outer = lax.ppermute(after(self.far, *earlier), "patch", [(0, 1), (3, 2)])
+
+    def send_on(self, *earlier):
+        outer, *earlier = lax.optimization_barrier((self.outer, *earlier))
+        direct = after(self.slab(self.near, 1 - self.patch % 2), outer)
+        summed = (self.far.astype(F32) + outer.astype(F32)).astype(F16)
         over = self.patch // 2
         self.inner_got = lax.ppermute(self.slab(summed, over), "patch", [(1, 2), (2, 1)])
         self.outer_got = lax.ppermute(self.slab(summed, 1 - over), "patch", [(1, 3), (2, 0)])
@@ -80,7 +82,7 @@
     def total(self, *earlier):
         direct = after(self.direct, *earlier)
         is_inner = (self.patch == 1) | (self.patch == 2)
-        total = self.slab(self.near, self.patch % 2) + direct.astype(F32)
+        total = self.slab(self.near, self.patch % 2).astype(F32) + direct.astype(F32)
         total = total + jnp.where(is_inner, self.inner_got, self.outer_got).astype(F32)
         return (total * (1.0 / LIFT)).astype(BF16)
 
@@ -253,11 +255,12 @@
             keys.to_inner()
             values.to_inner()
             queries.to_inner(keys.outer)
-            for each in sums:
-                each.send_on()
+            keys.send_on(values.outer)
+            values.send_on(queries.outer)
+            queries.send_on()
             key_new = refresh(keys.total(), own_stale[0])
             keys_all = gather(key_new)
-            value_new = refresh(values.total(key_new, queries.outer), own_stale[1])
+            value_new = refresh(values.total(key_new), own_stale[1])
             gathered = PairGather(value_new)
             query = after(queries.total(keys_all), gathered.mate, gathered.across)
         else:

time: 243 us -> 262 us (1.078)
  the two profiles are of different devices: /device:TPU:14 before, /device:TPU:8 now
where the time goes in v5:
time: 262 us
  waiting for transfers between devices  159 us (61%)
  starting transfers between devices  47.4 us (18%)
  between operations  14.7 us (6%)
  Pallas kernels  11.2 us (4%)
  other arithmetic  10.7 us (4%)
  local copies, waits for them, and re-layouts  9.99 us (4%)
  matrix products  9.02 us (3%)
    ppermute x3, waiting for transfers between devices, to_inner(): lax.ppermute(after(self.far, *earlier), 'patch', [(0, 1), (3, 2)])  66 us
    ppermute x3, waiting for transfers between devices, send_on(): lax.ppermute(direct, 'patch', [(0, 1), (1, 0), (2, 3), (3, 2)])  19.1 us
    ppermute x3, waiting for transfers between devices, send_on(): lax.ppermute(self.slab(summed, over), 'patch', [(1, 2), (2, 1)])  18.8 us
    ppermute x2, waiting for transfers between devices, both_slabs(): other = lax.ppermute(held, 'tensor', across)  13.8 us
    ppermute x3, starting transfers between devices, send_on(): lax.ppermute(self.slab(summed, over), 'patch', [(1, 2), (2, 1)])  11.3 us
    pallas_call x1, Pallas kernels, attend(): pl.pallas_call(functools.partial(attend_and_project, patches, heads, chip...  11.2 us
    ppermute x3, starting transfers between devices, send_on(): lax.ppermute(self.slab(summed, 1 - over), 'patch', [(1, 3), (2, 0)])  10.3 us
    ppermute x4, starting transfers between devices, along(): return lax.ppermute(block, ('patch', 'tensor'), pairs)  9.55 us
  transfers between devices with their start and end apart: 29, of which 18 were waited for; matrix products, arithmetic and copies ran while one was open for 9% of the time, Pallas kernels for 0%

profile of v5, /device:TPU:8, one launch (start us, length us, event | category | flops | bytes accessed | tf_op | source)
XLA Modules:
  0.0 261.6 jit_solution(2312382307222523437)
XLA Ops:
  7.2 1.2 fusion.9
  8.5 1.6 collective-permute-start.1
  10.0 1.3 collective-permute-start.5
  11.3 6.8 %collective-permute-done.1 = bf16[128,1280]{1,0:T(8,128)(2,1)} collective-permute-done((bf16[128,1280]{1,0:T(8,128)(2,1)S(1)}, bf16[128,1280]{1,0:T(8,128)(2,1)}, u32[]{:S(2)}, u32[]{:S(2)}) %collective-permute-start.1) | collective-permute-done | bytes 327712 | tf_op jit(solution)/shard_map/ppermute | solution.py:27
  18.1 2.1 collective-permute-start.6
  20.2 5.5 %collective-permute-start = (bf16[128,1280]{1,0:T(8,128)(2,1)S(1)}, bf16[128,1280]{1,0:T(8,128)(2,1)S(1)}, u32[]{:S(2)}, u32[]{:S(2)}) collective-permute-start(bf16[128,1280]{1,0:T(8,128)(2,1)S(1)} %get-tuple-element.39), channel_id=1, source_target_pairs={{0,0},{1,4},{4,1},{5,5},{10,10},{11,14},{14,11},{15,15},{16,16},{1... | collective-permute-start | bytes 983048 | tf_op jit(solution)/shard_map/ppermute | solution.py:37
  25.8 0.7 collective-permute-start.2
  26.5 2.3 collective-permute-done.5
  28.8 6.4 %collective-permute-done.6 = bf16[128,1280]{1,0:T(8,128)(2,1)S(1)} collective-permute-done((bf16[128,1280]{1,0:T(8,128)(2,1)}, bf16[128,1280]{1,0:T(8,128)(2,1)S(1)}, u32[]{:S(2)}, u32[]{:S(2)}) %collective-permute-start.6) | collective-permute-done | bytes 327712 | tf_op jit(solution)/shard_map/ppermute | solution.py:37
  35.2 3.0 %collective-permute-start.7 = (bf16[128,1280]{1,0:T(8,128)(2,1)S(1)}, bf16[128,1280]{1,0:T(8,128)(2,1)S(1)}, u32[]{:S(2)}, u32[]{:S(2)}) collective-permute-start(bf16[128,1280]{1,0:T(8,128)(2,1)S(1)} %broadcast_select_fusion.2), channel_id=1, source_target_pairs={{0,2},{1,3},{2,0},{3,1},{4,6},{5,7},{6,4},{7,5},{8,10},{9,11},{10,... | collective-permute-start | bytes 983048 | tf_op jit(solution)/shard_map/ppermute | solution.py:41
  38.4 8.5 %collective-permute-done.7 = bf16[128,1280]{1,0:T(8,128)(2,1)S(1)} collective-permute-done((bf16[128,1280]{1,0:T(8,128)(2,1)S(1)}, bf16[128,1280]{1,0:T(8,128)(2,1)S(1)}, u32[]{:S(2)}, u32[]{:S(2)}) %collective-permute-start.7) | collective-permute-done | bytes 327712 | tf_op jit(solution)/shard_map/ppermute | solution.py:41
  47.1 5.3 %collective-permute-done.3 = bf16[128,1280]{1,0:T(8,128)(2,1)S(1)} collective-permute-done((bf16[128,1280]{1,0:T(8,128)(2,1)S(1)}, bf16[128,1280]{1,0:T(8,128)(2,1)S(1)}, u32[]{:S(2)}, u32[]{:S(2)}) %collective-permute-start.3) | collective-permute-done | bytes 327712 | tf_op jit(solution)/shard_map/ppermute | solution.py:41
  52.6 1.2 multiply_convert_fusion.1
  53.8 1.3 collective-permute-start.12
  55.2 1.2 multiply_convert_fusion.3
  56.4 1.3 collective-permute-start.9
  57.7 1.2 multiply_convert_fusion.2
  58.9 1.2 multiply_convert_fusion
  60.1 1.1 dynamic-slice_bitcast_fusion.2
  61.3 14.8 %collective-permute-done.12 = f16[2,256,768]{2,1,0:T(8,128)(2,1)S(1)} collective-permute-done((f16[2,256,768]{2,1,0:T(8,128)(2,1)S(1)}, f16[2,256,768]{2,1,0:T(8,128)(2,1)S(1)}, u32[]{:S(2)}, u32[]{:S(2)}) %collective-permute-start.12) | collective-permute-done | bytes 786464 | tf_op jit(solution)/shard_map/ppermute | solution.py:71
  76.1 16.4 %collective-permute-done.9 = f16[2,256,768]{2,1,0:T(8,128)(2,1)S(1)} collective-permute-done((f16[2,256,768]{2,1,0:T(8,128)(2,1)S(1)}, f16[2,256,768]{2,1,0:T(8,128)(2,1)S(1)}, u32[]{:S(2)}, u32[]{:S(2)}) %collective-permute-start.9) | collective-permute-done | bytes 786464 | tf_op jit(solution)/shard_map/ppermute | solution.py:71
  92.5 0.2 add_convert_fusion.2
  92.8 1.0 dynamic-slice_bitcast_fusion.5
  93.9 4.7 %collective-permute-start.15 = (f16[256,768]{1,0:T(8,128)(2,1)}, f16[256,768]{1,0:T(8,128)(2,1)}, u32[]{:S(2)}, u32[]{:S(2)}) collective-permute-start(f16[256,768]{1,0:T(8,128)(2,1)} %get-tuple-element.32), channel_id=1, source_target_pairs={{4,12},{8,0},{5,13},{9,1},{6,14},{10,2},{7,15},{11,3},{20,28},{24,... | collective-permute-start | bytes 1179656 | tf_op jit(solution)/shard_map/ppermute | solution.py:79
  98.6 3.3 %collective-permute-start.14 = (f16[256,768]{1,0:T(8,128)(2,1)}, f16[256,768]{1,0:T(8,128)(2,1)}, u32[]{:S(2)}, u32[]{:S(2)}) collective-permute-start(f16[256,768]{1,0:T(8,128)(2,1)} %get-tuple-element.33), channel_id=1, source_target_pairs={{4,8},{8,4},{5,9},{9,5},{6,10},{10,6},{7,11},{11,7},{20,24},{24,20... | collective-permute-start | bytes 1179656 | tf_op jit(solution)/shard_map/ppermute | solution.py:78
  101.9 1.3 dynamic-slice_convert_fusion
  103.2 6.8 %collective-permute-done.13 = f16[256,768]{1,0:T(8,128)(2,1)} collective-permute-done((f16[256,768]{1,0:T(8,128)(2,1)}, f16[256,768]{1,0:T(8,128)(2,1)}, u32[]{:S(2)}, u32[]{:S(2)}) %collective-permute-start.13) | collective-permute-done | bytes 393248 | tf_op jit(solution)/shard_map/ppermute | solution.py:80
  110.1 6.3 %collective-permute-done.14 = f16[256,768]{1,0:T(8,128)(2,1)} collective-permute-done((f16[256,768]{1,0:T(8,128)(2,1)}, f16[256,768]{1,0:T(8,128)(2,1)}, u32[]{:S(2)}, u32[]{:S(2)}) %collective-permute-start.14) | collective-permute-done | bytes 393248 | tf_op jit(solution)/shard_map/ppermute | solution.py:78
  116.4 2.2 add_convert_fusion.6.key_ref
  118.6 3.1 %multiply_convert_fusion.4 = f16[512,768]{1,0:T(8,128)(2,1)S(1)} fusion(bf16[1280,768]{1,0:T(8,128)(2,1)} %param.7, bf16[256,1280]{1,0:T(8,128)(2,1)} %copy-done.20, bf16[128,1280]{1,0:T(8,128)(2,1)S(1)} %get-tuple-element.35, bf16[128,1280]{1,0:T(8,128)(2,1)S(1)} %get-tuple-element.34), kind=kOutput, calls=%fused_computation.7 | convolution fusion | flops 1011351552 | bytes 4063232 | tf_op jit(solution)/shard_map/dot_general | solution.py:64
  121.7 1.4 collective-permute-start.10
  123.2 1.2 multiply_convert_fusion.5
  124.4 0.9 dynamic-slice_bitcast_fusion.8
  125.3 34.8 %collective-permute-done.10 = f16[2,256,768]{2,1,0:T(8,128)(2,1)S(1)} collective-permute-done((f16[2,256,768]{2,1,0:T(8,128)(2,1)S(1)}, f16[2,256,768]{2,1,0:T(8,128)(2,1)S(1)}, u32[]{:S(2)}, u32[]{:S(2)}) %collective-permute-start.10) | collective-permute-done | bytes 786464 | tf_op jit(solution)/shard_map/ppermute | solution.py:71
  160.1 0.2 add_convert_fusion
  160.3 0.1 dynamic-slice_bitcast_fusion
  160.5 1.4 collective-permute-start.20
  161.9 6.1 %collective-permute-start.19 = (f16[256,768]{1,0:T(8,128)(2,1)S(1)}, f16[256,768]{1,0:T(8,128)(2,1)S(1)}, u32[]{:S(2)}, u32[]{:S(2)}) collective-permute-start(f16[256,768]{1,0:T(8,128)(2,1)S(1)} %get-tuple-element.29), channel_id=1, source_target_pairs={{4,8},{8,4},{5,9},{9,5},{6,10},{10,6},{7,11},{11,7},{20,24},{24,20... | collective-permute-start | bytes 1179656 | tf_op jit(solution)/shard_map/ppermute | solution.py:78
  168.1 0.2 add_convert_fusion.1
  168.3 1.0 dynamic-slice_bitcast_fusion.3
  169.3 4.3 %collective-permute-start.17 = (f16[256,768]{1,0:T(8,128)(2,1)}, f16[256,768]{1,0:T(8,128)(2,1)}, u32[]{:S(2)}, u32[]{:S(2)}) collective-permute-start(f16[256,768]{1,0:T(8,128)(2,1)} %get-tuple-element.30), channel_id=1, source_target_pairs={{4,12},{8,0},{5,13},{9,1},{6,14},{10,2},{7,15},{11,3},{20,28},{24,... | collective-permute-start | bytes 1179656 | tf_op jit(solution)/shard_map/ppermute | solution.py:79
  173.6 6.2 %collective-permute-done.18 = f16[256,768]{1,0:T(8,128)(2,1)S(1)} collective-permute-done((f16[256,768]{1,0:T(8,128)(2,1)S(1)}, f16[256,768]{1,0:T(8,128)(2,1)S(1)}, u32[]{:S(2)}, u32[]{:S(2)}) %collective-permute-start.18) | collective-permute-done | bytes 393248 | tf_op jit(solution)/shard_map/ppermute | solution.py:80
  179.8 1.9 collective-permute-start.16
  181.7 4.7 %collective-permute-done.19 = f16[256,768]{1,0:T(8,128)(2,1)S(1)} collective-permute-done((f16[256,768]{1,0:T(8,128)(2,1)S(1)}, f16[256,768]{1,0:T(8,128)(2,1)S(1)}, u32[]{:S(2)}, u32[]{:S(2)}) %collective-permute-start.19) | collective-permute-done | bytes 393248 | tf_op jit(solution)/shard_map/ppermute | solution.py:78
  186.4 0.3 add_convert_fusion.5.value_ref
  186.8 2.2 collective-permute-start.22
  189.2 6.1 %collective-permute-done.11 = f16[256,768]{1,0:T(8,128)(2,1)} collective-permute-done((f16[256,768]{1,0:T(8,128)(2,1)}, f16[256,768]{1,0:T(8,128)(2,1)}, u32[]{:S(2)}, u32[]{:S(2)}) %collective-permute-start.11) | collective-permute-done | bytes 393248 | tf_op jit(solution)/shard_map/ppermute | solution.py:80
  195.3 7.8 %collective-permute-done.16 = f16[256,768]{1,0:T(8,128)(2,1)} collective-permute-done((f16[256,768]{1,0:T(8,128)(2,1)}, f16[256,768]{1,0:T(8,128)(2,1)}, u32[]{:S(2)}, u32[]{:S(2)}) %collective-permute-start.16) | collective-permute-done | bytes 393248 | tf_op jit(solution)/shard_map/ppermute | solution.py:78
  203.1 1.3 fusion.8.query_ref
  204.4 2.9 %collective-permute-done.22 = bf16[256,768]{1,0:T(8,128)(2,1)} collective-permute-done((bf16[256,768]{1,0:T(8,128)(2,1)S(1)}, bf16[256,768]{1,0:T(8,128)(2,1)}, u32[]{:S(2)}, u32[]{:S(2)}) %collective-permute-start.22) | collective-permute-done | bytes 393248 | tf_op jit(solution)/shard_map/ppermute | solution.py:94
  207.3 11.2 %shard_map.77 = (bf16[256,2560]{1,0:T(8,128)(2,1)}, f32[256,2560]{1,0:T(8,128)S(1)}) custom-call(s32[5]{0:T(128)S(1)} %stack.23.place_ref, bf16[256,768]{1,0:T(8,128)(2,1)S(1)} %fusion.8.query_ref, bf16[2,1024,768]{2,1,0:T(8,128)(2,1)} %stale_ref.1, bf16[256,768]{1,0:T(8,128)(2,1)S(1)} %copy-done.1, bf16[256,768]{1,0:T(8,128)(2,1)S(1)} %add_convert_fusion.5.value_ref, ...), custom_call_target="tpu_custom_call" | custom-call | flops 2818572288 | bytes 14942208 | tf_op jit(solution)/shard_map/pallas_call | solution.py:193
  218.5 1.5 copy-done.2
  220.0 1.9 collective-permute-start.26
  221.9 1.3 collective-permute-start.25
  223.2 1.8 broadcast_in_dim.18
  225.1 8.5 %collective-permute-done.26 = bf16[256,768]{1,0:T(8,128)(2,1)S(1)} collective-permute-done((bf16[256,768]{1,0:T(8,128)(2,1)}, bf16[256,768]{1,0:T(8,128)(2,1)S(1)}, u32[]{:S(2)}, u32[]{:S(2)}) %collective-permute-start.26) | collective-permute-done | bytes 393248 | tf_op jit(solution)/shard_map/ppermute | solution.py:101
  233.6 1.3 collective-permute-start.27
  234.9 1.2 add_convert_fusion.4
  236.2 0.3 collective-permute-start.24
  236.5 1.0 bitcast_dynamic-update-slice_fusion.2
  237.5 1.1 bitcast_dynamic-update-slice_fusion.1
  238.6 4.8 %collective-permute-done.27 = bf16[256,768]{1,0:T(8,128)(2,1)S(1)} collective-permute-done((bf16[256,768]{1,0:T(8,128)(2,1)S(1)}, bf16[256,768]{1,0:T(8,128)(2,1)S(1)}, u32[]{:S(2)}, u32[]{:S(2)}) %collective-permute-start.27) | collective-permute-done | bytes 393248 | tf_op jit(solution)/shard_map/ppermute | solution.py:103
  243.5 9.1 %collective-permute-done.24 = bf16[256,1280]{1,0:T(8,128)(2,1)S(1)} collective-permute-done((bf16[256,1280]{1,0:T(8,128)(2,1)S(1)}, bf16[256,1280]{1,0:T(8,128)(2,1)S(1)}, u32[]{:S(2)}, u32[]{:S(2)}) %collective-permute-start.24) | collective-permute-done | bytes 655392 | tf_op jit(solution)/shard_map/ppermute | solution.py:230
  252.6 2.2 add_convert_fusion.3
  (75 shorter events, 1.1 us)
Async XLA Ops:
  7.2 48.0 %copy-start = (bf16[1280,768]{1,0:T(8,128)(2,1)S(1)}, bf16[1280,768]{1,0:T(8,128)(2,1)}, u32[]{:S(2)}) copy-start(bf16[1280,768]{1,0:T(8,128)(2,1)} %param.8) | copy-start | bytes 5898244
  7.2 188.1 %all-gather.2.cloned.1.call-start = ((), (), s32[]{:S(2)}) async-start(), calls=%async_computation | async-start | bytes 1966080 | tf_op jit(solution)/shard_map/all_gather | solution.py:249
  8.5 9.6 %collective-permute-start.1 = (bf16[128,1280]{1,0:T(8,128)(2,1)S(1)}, bf16[128,1280]{1,0:T(8,128)(2,1)}, u32[]{:S(2)}, u32[]{:S(2)}) collective-permute-start(bf16[128,1280]{1,0:T(8,128)(2,1)S(1)} %get-tuple-element.38), channel_id=1, source_target_pairs={{0,2},{1,3},{2,0},{3,1},{4,6},{5,7},{6,4},{7,5},{8,10},{9,11},{10,... | collective-permute-start | bytes 983048 | tf_op jit(solution)/shard_map/ppermute | solution.py:27
  10.0 18.8 %collective-permute-start.5 = (bf16[128,1280]{1,0:T(8,128)(2,1)S(1)}, bf16[128,1280]{1,0:T(8,128)(2,1)S(1)}, u32[]{:S(2)}, u32[]{:S(2)}) collective-permute-start(bf16[128,1280]{1,0:T(8,128)(2,1)S(1)} %get-tuple-element.39), channel_id=1, source_target_pairs={{2,10},{3,14},{6,11},{7,15},{8,0},{9,4},{12,1},{13,5},{18,26},{19,... | collective-permute-start | bytes 983048 | tf_op jit(solution)/shard_map/ppermute | solution.py:37
  18.1 17.1 %collective-permute-start.6 = (bf16[128,1280]{1,0:T(8,128)(2,1)}, bf16[128,1280]{1,0:T(8,128)(2,1)S(1)}, u32[]{:S(2)}, u32[]{:S(2)}) collective-permute-start(bf16[128,1280]{1,0:T(8,128)(2,1)} %collective-permute-done.1), channel_id=1, source_target_pairs={{0,8},{1,12},{4,9},{5,13},{10,2},{11,6},{14,3},{15,7},{16,24},{17,... | collective-permute-start | bytes 983048 | tf_op jit(solution)/shard_map/ppermute | solution.py:37
  20.2 18.1 %collective-permute-start = (bf16[128,1280]{1,0:T(8,128)(2,1)S(1)}, bf16[128,1280]{1,0:T(8,128)(2,1)S(1)}, u32[]{:S(2)}, u32[]{:S(2)}) collective-permute-start(bf16[128,1280]{1,0:T(8,128)(2,1)S(1)} %get-tuple-element.39), channel_id=1, source_target_pairs={{0,0},{1,4},{4,1},{5,5},{10,10},{11,14},{14,11},{15,15},{16,16},{1... | collective-permute-start | bytes 983048 | tf_op jit(solution)/shard_map/ppermute | solution.py:37
  25.8 12.5 %collective-permute-start.2 = (bf16[128,1280]{1,0:T(8,128)(2,1)}, bf16[128,1280]{1,0:T(8,128)(2,1)S(1)}, u32[]{:S(2)}, u32[]{:S(2)}) collective-permute-start(bf16[128,1280]{1,0:T(8,128)(2,1)} %collective-permute-done.1), channel_id=1, source_target_pairs={{2,2},{3,6},{6,3},{7,7},{8,8},{9,12},{12,9},{13,13},{18,18},{19,22... | collective-permute-start | bytes 983048 | tf_op jit(solution)/shard_map/ppermute | solution.py:37
  35.2 11.7 %collective-permute-start.7 = (bf16[128,1280]{1,0:T(8,128)(2,1)S(1)}, bf16[128,1280]{1,0:T(8,128)(2,1)S(1)}, u32[]{:S(2)}, u32[]{:S(2)}) collective-permute-start(bf16[128,1280]{1,0:T(8,128)(2,1)S(1)} %broadcast_select_fusion.2), channel_id=1, source_target_pairs={{0,2},{1,3},{2,0},{3,1},{4,6},{5,7},{6,4},{7,5},{8,10},{9,11},{10,... | collective-permute-start | bytes 983048 | tf_op jit(solution)/shard_map/ppermute | solution.py:41
  38.3 14.1 %collective-permute-start.3 = (bf16[128,1280]{1,0:T(8,128)(2,1)S(1)}, bf16[128,1280]{1,0:T(8,128)(2,1)S(1)}, u32[]{:S(2)}, u32[]{:S(2)}) collective-permute-start(bf16[128,1280]{1,0:T(8,128)(2,1)S(1)} %broadcast_select_fusion.5), channel_id=1, source_target_pairs={{0,2},{1,3},{2,0},{3,1},{4,6},{5,7},{6,4},{7,5},{8,10},{9,11},{10,... | collective-permute-start | bytes 983048 | tf_op jit(solution)/shard_map/ppermute | solution.py:41
  47.0 5.6 %copy-start.18 = (bf16[1280,768]{1,0:T(8,128)(2,1)S(1)}, bf16[1280,768]{1,0:T(8,128)(2,1)}, u32[]{:S(2)}) copy-start(bf16[1280,768]{1,0:T(8,128)(2,1)} %param.9) | copy-start | bytes 5898244
  47.0 5.6 %collective-permute-start.8 = (bf16[256,1280]{1,0:T(8,128)(2,1)S(1)}, bf16[256,1280]{1,0:T(8,128)(2,1)S(1)}, u32[]{:S(2)}, u32[]{:S(2)}) collective-permute-start(bf16[256,1280]{1,0:T(8,128)(2,1)S(1)} %pad_maximum_fusion.3), channel_id=1, source_target_pairs={{0,1},{1,0},{2,3},{3,2},{4,5},{5,4},{6,7},{7,6},{8,9},{9,8},{10,11... | collective-permute-start | bytes 1966088 | tf_op jit(solution)/shard_map/ppermute | solution.py:45
  52.5 5.1 %collective-permute-start.4 = (bf16[256,1280]{1,0:T(8,128)(2,1)S(1)}, bf16[256,1280]{1,0:T(8,128)(2,1)S(1)}, u32[]{:S(2)}, u32[]{:S(2)}) collective-permute-start(bf16[256,1280]{1,0:T(8,128)(2,1)S(1)} %pad_maximum_fusion.2), channel_id=1, source_target_pairs={{0,1},{1,0},{2,3},{3,2},{4,5},{5,4},{6,7},{7,6},{8,9},{9,8},{10,11... | collective-permute-start | bytes 1966088 | tf_op jit(solution)/shard_map/ppermute | solution.py:45
  52.6 2.5 copy-start.20
  53.8 2.5 copy-start.13
  53.8 22.2 %collective-permute-start.12 = (f16[2,256,768]{2,1,0:T(8,128)(2,1)S(1)}, f16[2,256,768]{2,1,0:T(8,128)(2,1)S(1)}, u32[]{:S(2)}, u32[]{:S(2)}) collective-permute-start(f16[2,256,768]{2,1,0:T(8,128)(2,1)S(1)} %bitcast.66), channel_id=1, source_target_pairs={{0,4},{12,8},{1,5},{13,9},{2,6},{14,10},{3,7},{15,11},{16,20},{28,... | collective-permute-start | bytes 2359304 | tf_op jit(solution)/shard_map/ppermute | solution.py:71
  56.4 36.1 %collective-permute-start.9 = (f16[2,256,768]{2,1,0:T(8,128)(2,1)S(1)}, f16[2,256,768]{2,1,0:T(8,128)(2,1)S(1)}, u32[]{:S(2)}, u32[]{:S(2)}) collective-permute-start(f16[2,256,768]{2,1,0:T(8,128)(2,1)S(1)} %bitcast.70), channel_id=1, source_target_pairs={{0,4},{12,8},{1,5},{13,9},{2,6},{14,10},{3,7},{15,11},{16,20},{28,... | collective-permute-start | bytes 2359304 | tf_op jit(solution)/shard_map/ppermute | solution.py:71
  57.7 1.2 copy-start.21
  58.9 1.2 copy-start.11
  60.1 32.6 %copy-start.7 = (f16[512,768]{1,0:T(8,128)(2,1)}, f16[512,768]{1,0:T(8,128)(2,1)S(1)}, u32[]{:S(2)}) copy-start(f16[512,768]{1,0:T(8,128)(2,1)S(1)} %multiply_convert_fusion) | copy-start | bytes 2359300
  76.1 17.8 %copy-start.15 = (f16[2,256,768]{2,1,0:T(8,128)(2,1)}, f16[2,256,768]{2,1,0:T(8,128)(2,1)S(1)}, u32[]{:S(2)}) copy-start(f16[2,256,768]{2,1,0:T(8,128)(2,1)S(1)} %collective-permute-done.12) | copy-start | bytes 2359300
  92.8 17.3 %collective-permute-start.13 = (f16[256,768]{1,0:T(8,128)(2,1)}, f16[256,768]{1,0:T(8,128)(2,1)}, u32[]{:S(2)}, u32[]{:S(2)}) collective-permute-start(f16[256,768]{1,0:T(8,128)(2,1)} %get-tuple-element.18), channel_id=1, source_target_pairs={{0,4},{4,0},{8,12},{12,8},{1,5},{5,1},{9,13},{13,9},{2,6},{6,2},{1... | collective-permute-start | bytes 1179656 | tf_op jit(solution)/shard_map/ppermute | solution.py:80
  93.9 16.2 %collective-permute-start.15 = (f16[256,768]{1,0:T(8,128)(2,1)}, f16[256,768]{1,0:T(8,128)(2,1)}, u32[]{:S(2)}, u32[]{:S(2)}) collective-permute-start(f16[256,768]{1,0:T(8,128)(2,1)} %get-tuple-element.32), channel_id=1, source_target_pairs={{4,12},{8,0},{5,13},{9,1},{6,14},{10,2},{7,15},{11,3},{20,28},{24,... | collective-permute-start | bytes 1179656 | tf_op jit(solution)/shard_map/ppermute | solution.py:79
  98.6 17.8 %collective-permute-start.14 = (f16[256,768]{1,0:T(8,128)(2,1)}, f16[256,768]{1,0:T(8,128)(2,1)}, u32[]{:S(2)}, u32[]{:S(2)}) collective-permute-start(f16[256,768]{1,0:T(8,128)(2,1)} %get-tuple-element.33), channel_id=1, source_target_pairs={{4,8},{8,4},{5,9},{9,5},{6,10},{10,6},{7,11},{11,7},{20,24},{24,20... | collective-permute-start | bytes 1179656 | tf_op jit(solution)/shard_map/ppermute | solution.py:78
  101.9 14.5 %copy-start.12 = (f16[512,768]{1,0:T(8,128)(2,1)S(1)}, f16[512,768]{1,0:T(8,128)(2,1)}, u32[]{:S(2)}) copy-start(f16[512,768]{1,0:T(8,128)(2,1)} %copy-done.11) | copy-start | bytes 2359300
  103.2 13.2 %copy-start.4 = (f32[2,256,768]{2,1,0:T(8,128)}, f32[2,256,768]{2,1,0:T(8,128)S(1)}, u32[]{:S(2)}) copy-start(f32[2,256,768]{2,1,0:T(8,128)S(1)} %dynamic-slice_convert_fusion) | copy-start | bytes 4718596
  118.6 4.6 %copy-start.19 = (bf16[1280,768]{1,0:T(8,128)(2,1)S(1)}, bf16[1280,768]{1,0:T(8,128)(2,1)}, u32[]{:S(2)}) copy-start(bf16[1280,768]{1,0:T(8,128)(2,1)} %param.7) | copy-start | bytes 5898244
  118.6 4.6 %copy-start.22 = (bf16[256,1280]{1,0:T(8,128)(2,1)S(1)}, bf16[256,1280]{1,0:T(8,128)(2,1)}, u32[]{:S(2)}) copy-start(bf16[256,1280]{1,0:T(8,128)(2,1)} %copy-done.21) | copy-start | bytes 1966084
  121.7 38.4 %copy-start.17 = (f16[256,768]{1,0:T(8,128)(2,1)S(1)}, f16[256,768]{1,0:T(8,128)(2,1)}, u32[]{:S(2)}) copy-start(f16[256,768]{1,0:T(8,128)(2,1)} %get-tuple-element.21) | copy-start | bytes 1179652
  121.7 38.4 %copy-start.14 = (f16[512,768]{1,0:T(8,128)(2,1)S(1)}, f16[512,768]{1,0:T(8,128)(2,1)}, u32[]{:S(2)}) copy-start(f16[512,768]{1,0:T(8,128)(2,1)} %copy-done.13) | copy-start | bytes 2359300
  121.7 38.3 %copy-start.16 = (f16[2,256,768]{2,1,0:T(8,128)(2,1)S(1)}, f16[2,256,768]{2,1,0:T(8,128)(2,1)}, u32[]{:S(2)}) copy-start(f16[2,256,768]{2,1,0:T(8,128)(2,1)} %copy-done.15) | copy-start | bytes 2359300
  121.7 38.3 %collective-permute-start.10 = (f16[2,256,768]{2,1,0:T(8,128)(2,1)S(1)}, f16[2,256,768]{2,1,0:T(8,128)(2,1)S(1)}, u32[]{:S(2)}, u32[]{:S(2)}) collective-permute-start(f16[2,256,768]{2,1,0:T(8,128)(2,1)S(1)} %bitcast.68), channel_id=1, source_target_pairs={{0,4},{12,8},{1,5},{13,9},{2,6},{14,10},{3,7},{15,11},{16,20},{28,... | collective-permute-start | bytes 2359304 | tf_op jit(solution)/shard_map/ppermute | solution.py:71
  124.4 35.9 %copy-start.9 = (f16[512,768]{1,0:T(8,128)(2,1)}, f16[512,768]{1,0:T(8,128)(2,1)S(1)}, u32[]{:S(2)}) copy-start(f16[512,768]{1,0:T(8,128)(2,1)S(1)} %multiply_convert_fusion.5) | copy-start | bytes 2359300
  160.1 19.7 %collective-permute-start.18 = (f16[256,768]{1,0:T(8,128)(2,1)S(1)}, f16[256,768]{1,0:T(8,128)(2,1)S(1)}, u32[]{:S(2)}, u32[]{:S(2)}) collective-permute-start(f16[256,768]{1,0:T(8,128)(2,1)S(1)} %copy-done.17), channel_id=1, source_target_pairs={{0,4},{4,0},{8,12},{12,8},{1,5},{5,1},{9,13},{13,9},{2,6},{6,2},{1... | collective-permute-start | bytes 1179656 | tf_op jit(solution)/shard_map/ppermute | solution.py:80
  160.5 21.2 %collective-permute-start.20 = (f16[256,768]{1,0:T(8,128)(2,1)S(1)}, f16[256,768]{1,0:T(8,128)(2,1)S(1)}, u32[]{:S(2)}, u32[]{:S(2)}) collective-permute-start(f16[256,768]{1,0:T(8,128)(2,1)S(1)} %get-tuple-element.28), channel_id=1, source_target_pairs={{4,12},{8,0},{5,13},{9,1},{6,14},{10,2},{7,15},{11,3},{20,28},{24,... | collective-permute-start | bytes 1179656 | tf_op jit(solution)/shard_map/ppermute | solution.py:79
  161.9 24.6 %copy-start.5 = (f32[2,256,768]{2,1,0:T(8,128)S(1)}, f32[2,256,768]{2,1,0:T(8,128)}, u32[]{:S(2)}) copy-start(f32[2,256,768]{2,1,0:T(8,128)} %copy-done.4) | copy-start | bytes 4718596
  161.9 24.5 %copy-start.8 = (f16[512,768]{1,0:T(8,128)(2,1)S(1)}, f16[512,768]{1,0:T(8,128)(2,1)}, u32[]{:S(2)}) copy-start(f16[512,768]{1,0:T(8,128)(2,1)} %copy-done.7) | copy-start | bytes 2359300
  161.9 24.5 %collective-permute-start.19 = (f16[256,768]{1,0:T(8,128)(2,1)S(1)}, f16[256,768]{1,0:T(8,128)(2,1)S(1)}, u32[]{:S(2)}, u32[]{:S(2)}) collective-permute-start(f16[256,768]{1,0:T(8,128)(2,1)S(1)} %get-tuple-element.29), channel_id=1, source_target_pairs={{4,8},{8,4},{5,9},{9,5},{6,10},{10,6},{7,11},{11,7},{20,24},{24,20... | collective-permute-start | bytes 1179656 | tf_op jit(solution)/shard_map/ppermute | solution.py:78
  168.0 27.3 %collective-permute-start.11 = (f16[256,768]{1,0:T(8,128)(2,1)}, f16[256,768]{1,0:T(8,128)(2,1)}, u32[]{:S(2)}, u32[]{:S(2)}) collective-permute-start(f16[256,768]{1,0:T(8,128)(2,1)} %dynamic-slice_bitcast_fusion.8), channel_id=1, source_target_pairs={{0,4},{4,0},{8,12},{12,8},{1,5},{5,1},{9,13},{13,9},{2,6},{6,2},{1... | collective-permute-start | bytes 1179656 | tf_op jit(solution)/shard_map/ppermute | solution.py:80
  169.3 33.8 %copy-start.10 = (f16[512,768]{1,0:T(8,128)(2,1)S(1)}, f16[512,768]{1,0:T(8,128)(2,1)}, u32[]{:S(2)}) copy-start(f16[512,768]{1,0:T(8,128)(2,1)} %copy-done.9) | copy-start | bytes 2359300
  169.3 26.0 %collective-permute-start.17 = (f16[256,768]{1,0:T(8,128)(2,1)}, f16[256,768]{1,0:T(8,128)(2,1)}, u32[]{:S(2)}, u32[]{:S(2)}) collective-permute-start(f16[256,768]{1,0:T(8,128)(2,1)} %get-tuple-element.30), channel_id=1, source_target_pairs={{4,12},{8,0},{5,13},{9,1},{6,14},{10,2},{7,15},{11,3},{20,28},{24,... | collective-permute-start | bytes 1179656 | tf_op jit(solution)/shard_map/ppermute | solution.py:79
  179.8 23.3 %collective-permute-start.16 = (f16[256,768]{1,0:T(8,128)(2,1)}, f16[256,768]{1,0:T(8,128)(2,1)}, u32[]{:S(2)}, u32[]{:S(2)}) collective-permute-start(f16[256,768]{1,0:T(8,128)(2,1)} %get-tuple-element.31), channel_id=1, source_target_pairs={{4,8},{8,4},{5,9},{9,5},{6,10},{10,6},{7,11},{11,7},{20,24},{24,20... | collective-permute-start | bytes 1179656 | tf_op jit(solution)/shard_map/ppermute | solution.py:78
  186.8 20.5 %copy-start.1 = (bf16[256,768]{1,0:T(8,128)(2,1)S(1)}, bf16[256,768]{1,0:T(8,128)(2,1)}, u32[]{:S(2)}) copy-start(bf16[256,768]{1,0:T(8,128)(2,1)} %add_convert_fusion.6.key_ref) | copy-start | bytes 1179652
  186.8 20.5 %collective-permute-start.22 = (bf16[256,768]{1,0:T(8,128)(2,1)S(1)}, bf16[256,768]{1,0:T(8,128)(2,1)}, u32[]{:S(2)}, u32[]{:S(2)}) collective-permute-start(bf16[256,768]{1,0:T(8,128)(2,1)S(1)} %add_convert_fusion.5.value_ref), channel_id=1, source_target_pairs={{4,8},{8,4},{5,9},{9,5},{6,10},{10,6},{7,11},{11,7},{20,24},{24,20... | collective-permute-start | bytes 1179656 | tf_op jit(solution)/shard_map/ppermute | solution.py:94
  189.0 18.3 %collective-permute-start.21 = (bf16[256,768]{1,0:T(8,128)(2,1)S(1)}, bf16[256,768]{1,0:T(8,128)(2,1)}, u32[]{:S(2)}, u32[]{:S(2)}) collective-permute-start(bf16[256,768]{1,0:T(8,128)(2,1)S(1)} %add_convert_fusion.5.value_ref), channel_id=1, source_target_pairs={{0,4},{4,0},{8,12},{12,8},{1,5},{5,1},{9,13},{13,9},{2,6},{6,2},{1... | collective-permute-start | bytes 1179656 | tf_op jit(solution)/shard_map/ppermute | solution.py:93
  218.5 1.5 copy-start.2
  220.0 13.6 %collective-permute-start.23 = (bf16[256,2560]{1,0:T(8,128)(2,1)}, bf16[256,2560]{1,0:T(8,128)(2,1)}, u32[]{:S(2)}, u32[]{:S(2)}) collective-permute-start(bf16[256,2560]{1,0:T(8,128)(2,1)} %get-tuple-element.25), channel_id=1, source_target_pairs={{0,1},{1,0},{2,3},{3,2},{4,5},{5,4},{6,7},{7,6},{8,9},{9,8},{10,11... | collective-permute-start | bytes 3932168 | tf_op jit(solution)/shard_map/ppermute | solution.py:222
  220.0 13.6 %collective-permute-start.26 = (bf16[256,768]{1,0:T(8,128)(2,1)}, bf16[256,768]{1,0:T(8,128)(2,1)S(1)}, u32[]{:S(2)}, u32[]{:S(2)}) collective-permute-start(bf16[256,768]{1,0:T(8,128)(2,1)} %collective-permute-done.21), channel_id=1, source_target_pairs={{4,8},{8,4},{5,9},{9,5},{6,10},{10,6},{7,11},{11,7},{20,24},{24,20... | collective-permute-start | bytes 1179656 | tf_op jit(solution)/shard_map/ppermute | solution.py:101
  221.9 15.6 %collective-permute-start.25 = (bf16[256,768]{1,0:T(8,128)(2,1)}, bf16[256,768]{1,0:T(8,128)(2,1)S(1)}, u32[]{:S(2)}, u32[]{:S(2)}) collective-permute-start(bf16[256,768]{1,0:T(8,128)(2,1)} %collective-permute-done.22), channel_id=1, source_target_pairs={{4,0},{8,12},{5,1},{9,13},{6,2},{10,14},{7,3},{11,15},{20,16},{24,... | collective-permute-start | bytes 1179656 | tf_op jit(solution)/shard_map/ppermute | solution.py:102
  223.2 11.7 %copy-start.3 = (f32[256,2560]{1,0:T(8,128)S(1)}, f32[256,2560]{1,0:T(8,128)}, u32[]{:S(2)}) copy-start(f32[256,2560]{1,0:T(8,128)} %copy-done.2) | copy-start | bytes 7864324
  233.6 9.8 %collective-permute-start.27 = (bf16[256,768]{1,0:T(8,128)(2,1)S(1)}, bf16[256,768]{1,0:T(8,128)(2,1)S(1)}, u32[]{:S(2)}, u32[]{:S(2)}) collective-permute-start(bf16[256,768]{1,0:T(8,128)(2,1)S(1)} %collective-permute-done.26), channel_id=1, source_target_pairs={{4,0},{8,12},{5,1},{9,13},{6,2},{10,14},{7,3},{11,15},{20,16},{24,... | collective-permute-start | bytes 1179656 | tf_op jit(solution)/shard_map/ppermute | solution.py:103
  236.2 16.4 %collective-permute-start.24 = (bf16[256,1280]{1,0:T(8,128)(2,1)S(1)}, bf16[256,1280]{1,0:T(8,128)(2,1)S(1)}, u32[]{:S(2)}, u32[]{:S(2)}) collective-permute-start(bf16[256,1280]{1,0:T(8,128)(2,1)S(1)} %add_convert_fusion.4), channel_id=1, source_target_pairs={{0,2},{1,3},{2,0},{3,1},{4,6},{5,7},{6,4},{7,5},{8,10},{9,11},{10,... | collective-permute-start | bytes 1966088 | tf_op jit(solution)/shard_map/ppermute | solution.py:230
  243.5 11.2 %copy-start.6 = (bf16[2,1024,768]{2,1,0:T(8,128)(2,1)}, bf16[2,1024,768]{2,1,0:T(8,128)(2,1)S(1)}, u32[]{:S(2)}) copy-start(bf16[2,1024,768]{2,1,0:T(8,128)(2,1)S(1)} %bitcast_dynamic-update-slice_fusion) | copy-start | bytes 9437188
Sparse Core Ops, SparseCore 0:
  118.7 57.4 all-gather.1

commit v6 on v3

v6 whole, which is shorter than its diff:
```python
import functools

import jax
import jax.numpy as jnp
from jax import lax
from jax.experimental import pallas as pl
from jax.experimental.pallas import tpu as pltpu
from jax.sharding import PartitionSpec as P

HEAD_DIM = 128
F32 = jnp.float32
BF16 = jnp.bfloat16
F16 = jnp.float16
LIFT = 8.0


def spread_features(hidden):
    features = lax.all_gather(hidden, "tensor", axis=1, tiled=True)
    return lax.all_to_all(features, "patch", split_axis=1, concat_axis=0, tiled=True)


def spread_in_pairs(hidden):
    rank, patch = lax.axis_index("tensor"), lax.axis_index("patch")
    half = hidden.shape[0] // 2
    across = [(r, r ^ 2) for r in range(4)]
    straight = hidden[:half]
    crossing = lax.ppermute(hidden[half:], "tensor", across)
    is_straight = patch // 2 == rank // 2

    def along(block, flip, far):
        pairs = [
            (4 * s + r, 4 * (r ^ flip) + 2 * (r // 2) + s % 2)
            for s in range(4)
            for r in range(4)
            if ((r ^ flip) // 2 != s // 2) == far
        ]
        return lax.ppermute(block, ("patch", "tensor"), pairs)

    def both_slabs(far):
        held = jnp.where(is_straight, along(straight, 0, far), along(crossing, 2, far))
        other = lax.ppermute(held, "tensor", across)
        low = jnp.where(is_straight, held, other)
        high = jnp.where(is_straight, other, held)
        mine = jnp.concatenate([low, high])
        theirs = lax.ppermute(mine, "tensor", [(r, r ^ 1) for r in range(4)])
        return jnp.concatenate([mine, theirs])

    return both_slabs(True), both_slabs(False)


def sum_in_pairs(far, near, weight):
    patch, core = lax.axis_index("patch"), lax.axis_index("tensor") % 2

    def project(features):
        product = (jnp.dot(features, weight, preferred_element_type=F32) * LIFT).astype(F16)
        return product.reshape(2, features.shape[0] // 2, weight.shape[1])

    far, near = project(far), project(near)

    def mine(slab, step):
        slab = jnp.clip(slab, 0, 3)
        place = (slab % 2) ^ core
        part = lax.dynamic_index_in_dim(far, place, 0, keepdims=False)
        if step == 3:
            other = lax.dynamic_index_in_dim(near, place, 0, keepdims=False)
            part = jnp.where(slab // 2 == patch // 2, other, part)
        return part

    up = down = None
    for step in range(1, 4):
        send_up, send_down = mine(4 - step + patch, step), mine(step - 4 + patch, step)
        if step > 1:
            send_up = (send_up.astype(F32) + up.astype(F32)).astype(F16)
            send_down = (send_down.astype(F32) + down.astype(F32)).astype(F16)
        up = lax.ppermute(send_up, "patch", [(i, i + 1) for i in range(step)])
        down = lax.ppermute(send_down, "patch", [(3 - i, 2 - i) for i in range(step)])
    own = lax.dynamic_index_in_dim(near, (patch % 2) ^ core, 0, keepdims=False)
    total = own.astype(F32) + (up.astype(F32) + down.astype(F32))
    return (total * (1.0 / LIFT)).astype(BF16)


def sum_own_slab(features, weight, patches):
    me = lax.axis_index("patch")
    rows = features.shape[0] // patches
    parts = jnp.dot(features, weight, preferred_element_type=F32) * LIFT

    def mine(slab):
        slab = jnp.clip(slab, 0, patches - 1)
        return lax.dynamic_slice_in_dim(parts, slab * rows, rows, 0)

    up = down = None
    for step in range(1, patches):
        send_up = mine(patches - step + me)
        send_down = mine(step - patches + me)
        if step > 1:
            send_up = send_up + up.astype(F32)
            send_down = send_down + down.astype(F32)
        up = lax.ppermute(send_up.astype(F16), "patch", [(i, i + 1) for i in range(step)])
        down = lax.ppermute(
            send_down.astype(F16), "patch", [(patches - 1 - i, patches - 2 - i) for i in range(step)]
        )
    total = mine(me)
    if patches > 1:
        total = total + (up.astype(F32) + down.astype(F32))
    return (total * (1.0 / LIFT)).astype(BF16)


def attend_and_project(patches, heads, chips, chunks, place_ref, query_ref, stale_ref, fresh_ref, w_ref, *out_refs):
    *out_refs, sums = out_refs
    send_refs, keep_refs = out_refs[:chunks], out_refs[chunks:]
    me = place_ref[0]
    rows = query_ref.shape[0]
    width = w_ref.shape[1] // (2 * chips)
    scale = 1.0 / HEAD_DIM**0.5
    starts = [pl.multiple_of(lax.rem(me + j, patches) * rows, rows) for j in range(1, patches)]
    dims = (((1,), (1,)), ((), ()))
    mixed_heads = []
    for h in range(heads):
        columns = slice(h * HEAD_DIM, (h + 1) * HEAD_DIM)
        query = query_ref[:, columns]
        keys = [fresh_ref[0, :, columns]] + [stale_ref[0, pl.ds(start, rows), columns] for start in starts]
        values = [fresh_ref[1, :, columns]] + [stale_ref[1, pl.ds(start, rows), columns] for start in starts]
        scores = [lax.dot_general(query, key, dims, preferred_element_type=F32) * scale for key in keys]
        top = functools.reduce(jnp.maximum, [jnp.max(s, axis=-1, keepdims=True) for s in scores])
        total = mixed = None
        for s, value in zip(scores, values):
            expo = jnp.exp(s - top)
            count = jnp.sum(expo, axis=-1, keepdims=True)
            part = jnp.dot(expo.astype(BF16), value, preferred_element_type=F32)
            total = count if total is None else total + count
            mixed = part if mixed is None else mixed + part
        mixed_heads.append((mixed / total).astype(BF16))
    heads_out = jnp.concatenate(mixed_heads, axis=1) if heads > 1 else mixed_heads[0]
    product = jnp.dot(heads_out, w_ref[...], preferred_element_type=F32)

    @pl.when(pl.program_id(0) == 0)
    def _():
        sums[...] = product

    @pl.when(pl.program_id(0) > 0)
    def _():
        sums[...] += product

    @pl.when(pl.program_id(0) == pl.num_programs(0) - 1)
    def _():
        part = width // chunks
        for c in range(chunks):
            for j in range(chips):
                theirs = pl.multiple_of(place_ref[1 + j] * width + c * part, part)
                ours = pl.multiple_of(place_ref[1 + chips + j] * width + c * part, part)
                there = slice(j * part, (j + 1) * part)
                send_refs[c][:, there] = sums[:, pl.ds(theirs, part)].astype(BF16)
                keep_refs[c][:, there] = sums[:, pl.ds(ours, part)]


def attend(query, stale_kv, fresh_kv, w_out, patches, ranks):
    rows, depth = query.shape
    tokens, model = stale_kv.shape[1], w_out.shape[1]
    rank = lax.axis_index("tensor").astype(jnp.int32)
    core, chip, chips = rank % 2, rank // 2, ranks // 2
    width = model // ranks
    order = [(chip + hop) % chips for hop in range(1, chips)] + [chip]
    me = lax.axis_index("patch").astype(jnp.int32)
    place = jnp.stack([me] + [2 * c + 1 - core for c in order] + [2 * c + core for c in order])
    heads = 2 if depth % (2 * HEAD_DIM) == 0 else 1
    block = heads * HEAD_DIM
    chunks = 2 if width % (2 * 128) == 0 else 1
    part = width // chunks
    results = pl.pallas_call(
        functools.partial(attend_and_project, patches, heads, chips, chunks),
        out_shape=[jax.ShapeDtypeStruct((rows, chips * part), BF16)] * chunks
        + [jax.ShapeDtypeStruct((rows, chips * part), F32)] * chunks,
        grid_spec=pltpu.PrefetchScalarGridSpec(
            num_scalar_prefetch=1,
            grid=(depth // block,),
            in_specs=[
                pl.BlockSpec((rows, block), lambda h, p: (0, h)),
                pl.BlockSpec((2, tokens, block), lambda h, p: (0, 0, h)),
                pl.BlockSpec((2, rows, block), lambda h, p: (0, 0, h)),
                pl.BlockSpec((block, model), lambda h, p: (h, 0)),
            ],
            out_specs=[pl.BlockSpec((rows, chips * part), lambda h, p: (0, 0))] * (2 * chunks),
            scratch_shapes=[pltpu.VMEM((rows, model), F32)],
        ),
        compiler_params=pltpu.CompilerParams(vmem_limit_bytes=48 * 2**20),
        cost_estimate=pl.CostEstimate(
            flops=4 * rows * tokens * depth + 2 * rows * depth * model,
            bytes_accessed=4 * tokens * depth + 2 * depth * model + 6 * rows * chips * width,
            transcendentals=rows * tokens * (depth // HEAD_DIM),
        ),
    )(place, query, stale_kv, fresh_kv, w_out)
    across = [(r, r ^ 1) for r in range(ranks)]
    got = [lax.ppermute(send, "tensor", across) for send in results[:chunks]]
    pieces = []
    for mine, theirs in zip(results[chunks:], got):

        def summed(j):
            return mine[:, j * part : (j + 1) * part] + theirs[:, j * part : (j + 1) * part].astype(F32)

        arrived = []
        for hop in range(1, chips):
            pairs = [(r, (r + 2 * hop) % ranks) for r in range(ranks)]
            arrived.append(lax.ppermute(summed(hop - 1).astype(BF16), "tensor", pairs))
        total = summed(chips - 1)
        for piece in arrived:
            total = total + piece.astype(F32)
        pieces.append(total.astype(BF16))
    return jnp.concatenate(pieces, axis=1)


def make_shards(patches, ranks):
    def shards(hidden_in, w_query, w_key, w_value, w_out, stale_kv):
        rows = hidden_in.shape[0]
        me = lax.axis_index("patch")
        own_stale = lax.dynamic_slice_in_dim(stale_kv, me * rows, rows, 1).astype(F32)
        w_both = jnp.concatenate([w_key, w_value], axis=1)
        if patches == ranks == 4:
            far, near = spread_in_pairs(hidden_in)
            both = sum_in_pairs(far, near, w_both)
            query = sum_in_pairs(far, near, w_query)
        else:
            features = spread_features(hidden_in)
            both = sum_own_slab(features, w_both, patches)
            query = sum_own_slab(features, w_query, patches)
        width = w_key.shape[1]
        fresh = lax.reduce_precision(both.astype(F32), 8, 7)
        fresh = jnp.stack([fresh[:, :width], fresh[:, width:]])
        delta = lax.reduce_precision(fresh - own_stale, 8, 7)
        own_new = (own_stale + delta).astype(BF16)
        refreshed = lax.all_gather(own_new, "patch", axis=1, tiled=True)
        attended = attend(query, stale_kv, own_new, w_out, patches, ranks)
        return (attended, refreshed)

    return shards


def solution(mesh):
    in_specs = (
        P(("groups", "patch"), "tensor"),
        P("patch", "tensor"),
        P("patch", "tensor"),
        P("patch", "tensor"),
        P("tensor", None),
        P(None, "groups", "tensor"),
    )
    out_specs = (P(("groups", "patch"), "tensor"), P(None, "groups", "tensor"))
    return jax.shard_map(
        make_shards(mesh.shape["patch"], mesh.shape["tensor"]),
        mesh=mesh,
        in_specs=in_specs,
        out_specs=out_specs,
        check_vma=False,
    )
```

time: 241 us -> 253 us (1.050)
  the two profiles are of different devices: /device:TPU:0 before, /device:TPU:8 now
where the time goes in v6:
time: 253 us; the launch traced here: 252 us
  waiting for transfers between devices  147 us (58%)
  starting transfers between devices  43.4 us (17%)
  other arithmetic  17.3 us (7%)
  between operations  14.7 us (6%)
  matrix products  10.4 us (4%)
  Pallas kernels  10.1 us (4%)
  local copies, waits for them, and re-layouts  9.45 us (4%)
    ppermute x6, waiting for transfers between devices, sum_in_pairs(): up = lax.ppermute(send_up, 'patch', [(i, i + 1) for i in range(step)])  88.8 us
    ppermute x6, waiting for transfers between devices, sum_in_pairs(): lax.ppermute(send_down, 'patch', [(3 - i, 2 - i) for i in range(step)])  16.8 us
    ppermute x4, waiting for transfers between devices, along(): return lax.ppermute(block, ('patch', 'tensor'), pairs)  15.6 us
    ppermute x2, waiting for transfers between devices, attend(): arrived.append(lax.ppermute(summed(hop - 1).astype(BF16), 'tensor', pairs))  14.3 us
    ppermute x6, starting transfers between devices, sum_in_pairs(): lax.ppermute(send_down, 'patch', [(3 - i, 2 - i) for i in range(step)])  13.8 us
    ppermute x6, starting transfers between devices, sum_in_pairs(): up = lax.ppermute(send_up, 'patch', [(i, i + 1) for i in range(step)])  13.5 us
    dot_general x4, matrix products, project(): jnp.dot(features, weight, preferred_element_type=F32) * LIFT  10.4 us
    pallas_call x1, Pallas kernels, attend(): pl.pallas_call(functools.partial(attend_and_project, patches, heads, chip...  10.1 us
  transfers between devices with their start and end apart: 26, of which 19 were waited for; matrix products, arithmetic and copies ran while one was open for 10% of the time, Pallas kernels for 4%

profile of v6, /device:TPU:8, one launch (start us, length us, event | category | flops | bytes accessed | tf_op | source)
XLA Modules:
  0.0 252.1 jit_solution(13141260556587968631)
XLA Ops:
  7.2 1.2 fusion.20
  8.5 1.6 collective-permute-start.1
  10.0 1.3 collective-permute-start.5
  11.3 6.7 %collective-permute-done.1 = bf16[128,1280]{1,0:T(8,128)(2,1)S(1)} collective-permute-done((bf16[128,1280]{1,0:T(8,128)(2,1)S(1)}, bf16[128,1280]{1,0:T(8,128)(2,1)S(1)}, u32[]{:S(2)}, u32[]{:S(2)}) %collective-permute-start.1) | collective-permute-done | bytes 327712 | tf_op jit(solution)/shard_map/ppermute | solution.py:27
  18.0 2.1 collective-permute-start.6
  20.1 8.7 %collective-permute-done.5 = bf16[128,1280]{1,0:T(8,128)(2,1)S(1)} collective-permute-done((bf16[128,1280]{1,0:T(8,128)(2,1)S(1)}, bf16[128,1280]{1,0:T(8,128)(2,1)S(1)}, u32[]{:S(2)}, u32[]{:S(2)}) %collective-permute-start.5) | collective-permute-done | bytes 327712 | tf_op jit(solution)/shard_map/ppermute | solution.py:37
  28.8 6.0 %collective-permute-done.6 = bf16[128,1280]{1,0:T(8,128)(2,1)S(1)} collective-permute-done((bf16[128,1280]{1,0:T(8,128)(2,1)S(1)}, bf16[128,1280]{1,0:T(8,128)(2,1)S(1)}, u32[]{:S(2)}, u32[]{:S(2)}) %collective-permute-start.6) | collective-permute-done | bytes 327712 | tf_op jit(solution)/shard_map/ppermute | solution.py:37
  34.8 3.1 %collective-permute-start.7 = (bf16[128,1280]{1,0:T(8,128)(2,1)S(1)}, bf16[128,1280]{1,0:T(8,128)(2,1)S(1)}, u32[]{:S(2)}, u32[]{:S(2)}) collective-permute-start(bf16[128,1280]{1,0:T(8,128)(2,1)S(1)} %broadcast_select_fusion.2), channel_id=1, source_target_pairs={{0,2},{1,3},{2,0},{3,1},{4,6},{5,7},{6,4},{7,5},{8,10},{9,11},{10,... | collective-permute-start | bytes 983048 | tf_op jit(solution)/shard_map/ppermute | solution.py:41
  37.9 1.9 collective-permute-start
  39.9 1.7 constant_dynamic-update-slice_fusion.1
  41.7 0.8 collective-permute-start.2
  42.5 2.5 collective-permute-done.7
  45.2 0.1 constant_dynamic-update-slice_fusion
  45.4 0.9 collective-permute-done
  46.3 1.1 broadcast_select_fusion.5
  47.4 2.4 collective-permute-start.3
  49.8 2.2 fusion.1
  52.0 1.4 dynamic-slice_bitcast_fusion.1
  53.4 1.3 collective-permute-start.15
  54.7 1.6 collective-permute-start.18
  56.3 0.4 collective-permute-done.3
  56.7 1.1 broadcast_select_fusion.4
  57.8 0.7 copy-done.8
  58.5 0.9 pad_maximum_fusion.2
  59.5 13.4 %collective-permute-done.15 = f16[256,1536]{1,0:T(8,128)(2,1)} collective-permute-done((f16[256,1536]{1,0:T(8,128)(2,1)}, f16[256,1536]{1,0:T(8,128)(2,1)}, u32[]{:S(2)}, u32[]{:S(2)}) %collective-permute-start.15) | collective-permute-done | bytes 786464 | tf_op jit(solution)/shard_map/ppermute | solution.py:75
  72.8 3.0 %fusion.6 = (f16[256,1536]{1,0:T(8,128)(2,1)}, f16[256,1536]{1,0:T(8,128)(2,1)}) fusion(f16[256,1536]{1,0:T(8,128)(2,1)} %collective-permute-done.15, f16[2,256,1536]{2,1,0:T(8,128)(2,1)S(1)} %bitcast.56, s32[]{:T(128)S(6)} %select_n.193, f16[256,1536]{1,0:T(8,128)(2,1)} %collective-permute-done.18, s32[]{:T(128)S(6)} %select_n.202), kind=kLoop, calls=%fused_computation.13 | loop fusion | flops 3145728 | bytes 4718600 | tf_op jit(solution)/shard_map/convert_element_type | solution.py:73
  75.8 5.1 %collective-permute-start.16 = (f16[256,1536]{1,0:T(8,128)(2,1)}, f16[256,1536]{1,0:T(8,128)(2,1)}, u32[]{:S(2)}, u32[]{:S(2)}) collective-permute-start(f16[256,1536]{1,0:T(8,128)(2,1)} %get-tuple-element.14), channel_id=1, source_target_pairs={{0,4},{4,8},{1,5},{5,9},{2,6},{6,10},{3,7},{7,11},{16,20},{20,24},... | collective-permute-start | bytes 2359304 | tf_op jit(solution)/shard_map/ppermute | solution.py:75
  80.9 1.3 collective-permute-start.19
  82.2 4.7 %fusion = f16[512,1536]{1,0:T(8,128)(2,1)S(1)} fusion(bf16[1280,1536]{1,0:T(8,128)(2,1)} %copy-done.12, bf16[256,1280]{1,0:T(8,128)(2,1)} %collective-permute-done.4, bf16[128,1280]{1,0:T(8,128)(2,1)} %copy-done.10, bf16[128,1280]{1,0:T(8,128)(2,1)} %copy-done.8), kind=kOutput, calls=%fused_computation.2 | convolution fusion | flops 2018770944 | bytes 6815744 | tf_op jit(solution)/shard_map/dot_general | solution.py:55
  87.0 10.9 %collective-permute-done.16 = f16[256,1536]{1,0:T(8,128)(2,1)} collective-permute-done((f16[256,1536]{1,0:T(8,128)(2,1)}, f16[256,1536]{1,0:T(8,128)(2,1)}, u32[]{:S(2)}, u32[]{:S(2)}) %collective-permute-start.16) | collective-permute-done | bytes 786464 | tf_op jit(solution)/shard_map/ppermute | solution.py:75
  97.9 4.1 %collective-permute-done.19 = f16[256,1536]{1,0:T(8,128)(2,1)} collective-permute-done((f16[256,1536]{1,0:T(8,128)(2,1)}, f16[256,1536]{1,0:T(8,128)(2,1)}, u32[]{:S(2)}, u32[]{:S(2)}) %collective-permute-start.19) | collective-permute-done | bytes 786464 | tf_op jit(solution)/shard_map/ppermute | solution.py:76
  102.0 3.2 %fusion.7 = (f16[256,1536]{1,0:T(8,128)(2,1)}, f16[256,1536]{1,0:T(8,128)(2,1)}) fusion(f16[256,1536]{1,0:T(8,128)(2,1)} %collective-permute-done.16, f16[2,256,1536]{2,1,0:T(8,128)(2,1)S(1)} %bitcast.57, s32[]{:T(128)S(6)} %select_n.187, f16[2,256,1536]{2,1,0:T(8,128)(2,1)S(1)} %bitcast.61, pred[]{:T(512)S(6)} %eq.31, ...), kind=kLoop, calls=%fused_computation.15 | loop fusion | flops 3932160 | bytes 6291466 | tf_op jit(solution)/shard_map/convert_element_type | solution.py:73
  105.2 1.9 collective-permute-start.17
  107.2 4.0 %collective-permute-start.20 = (f16[256,1536]{1,0:T(8,128)(2,1)}, f16[256,1536]{1,0:T(8,128)(2,1)S(1)}, u32[]{:S(2)}, u32[]{:S(2)}) collective-permute-start(f16[256,1536]{1,0:T(8,128)(2,1)} %get-tuple-element.11), channel_id=1, source_target_pairs={{12,8},{8,4},{4,0},{13,9},{9,5},{5,1},{14,10},{10,6},{6,2},{15,11}... | collective-permute-start | bytes 2359304 | tf_op jit(solution)/shard_map/ppermute | solution.py:76
  111.2 14.2 %collective-permute-done.17 = f16[256,1536]{1,0:T(8,128)(2,1)S(1)} collective-permute-done((f16[256,1536]{1,0:T(8,128)(2,1)}, f16[256,1536]{1,0:T(8,128)(2,1)S(1)}, u32[]{:S(2)}, u32[]{:S(2)}) %collective-permute-start.17) | collective-permute-done | bytes 786464 | tf_op jit(solution)/shard_map/ppermute | solution.py:75
  125.4 1.9 collective-permute-done.20
  127.3 1.5 convert_reduce-precision_fusion
  128.9 2.4 fusion.3.fresh_ref
  131.4 1.2 multiply_convert_fusion
  132.6 0.1 dynamic-slice_bitcast_fusion.3
  132.7 0.8 collective-permute-start.12
  133.6 1.3 collective-permute-start.9
  134.9 17.6 %collective-permute-done.9 = f16[256,768]{1,0:T(8,128)(2,1)S(1)} collective-permute-done((f16[256,768]{1,0:T(8,128)(2,1)S(1)}, f16[256,768]{1,0:T(8,128)(2,1)S(1)}, u32[]{:S(2)}, u32[]{:S(2)}) %collective-permute-start.9) | collective-permute-done | bytes 393248 | tf_op jit(solution)/shard_map/ppermute | solution.py:75
  152.5 0.2 fusion.12
  152.7 1.9 collective-permute-start.10
  154.6 1.3 collective-permute-start.13
  155.9 2.3 multiply_convert_fusion.1
  158.2 19.5 %collective-permute-done.10 = f16[256,768]{1,0:T(8,128)(2,1)S(1)} collective-permute-done((f16[256,768]{1,0:T(8,128)(2,1)S(1)}, f16[256,768]{1,0:T(8,128)(2,1)S(1)}, u32[]{:S(2)}, u32[]{:S(2)}) %collective-permute-start.10) | collective-permute-done | bytes 393248 | tf_op jit(solution)/shard_map/ppermute | solution.py:75
  177.8 6.2 %collective-permute-done.13 = f16[256,768]{1,0:T(8,128)(2,1)S(1)} collective-permute-done((f16[256,768]{1,0:T(8,128)(2,1)S(1)}, f16[256,768]{1,0:T(8,128)(2,1)S(1)}, u32[]{:S(2)}, u32[]{:S(2)}) %collective-permute-start.13) | collective-permute-done | bytes 393248 | tf_op jit(solution)/shard_map/ppermute | solution.py:76
  184.0 1.3 fusion.13
  185.3 2.0 collective-permute-start.11
  187.3 4.9 %collective-permute-start.14 = (f16[256,768]{1,0:T(8,128)(2,1)}, f16[256,768]{1,0:T(8,128)(2,1)}, u32[]{:S(2)}, u32[]{:S(2)}) collective-permute-start(f16[256,768]{1,0:T(8,128)(2,1)} %get-tuple-element.19), channel_id=1, source_target_pairs={{12,8},{8,4},{4,0},{13,9},{9,5},{5,1},{14,10},{10,6},{6,2},{15,11}... | collective-permute-start | bytes 1179656 | tf_op jit(solution)/shard_map/ppermute | solution.py:76
  192.3 13.1 %collective-permute-done.11 = f16[256,768]{1,0:T(8,128)(2,1)} collective-permute-done((f16[256,768]{1,0:T(8,128)(2,1)}, f16[256,768]{1,0:T(8,128)(2,1)}, u32[]{:S(2)}, u32[]{:S(2)}) %collective-permute-start.11) | collective-permute-done | bytes 393248 | tf_op jit(solution)/shard_map/ppermute | solution.py:75
  205.4 4.5 %collective-permute-done.14 = f16[256,768]{1,0:T(8,128)(2,1)} collective-permute-done((f16[256,768]{1,0:T(8,128)(2,1)}, f16[256,768]{1,0:T(8,128)(2,1)}, u32[]{:S(2)}, u32[]{:S(2)}) %collective-permute-start.14) | collective-permute-done | bytes 393248 | tf_op jit(solution)/shard_map/ppermute | solution.py:76
  210.0 1.3 fusion.15.query_ref
  211.3 10.1 %shard_map.77 = (bf16[256,1280]{1,0:T(8,128)(2,1)S(1)}, bf16[256,1280]{1,0:T(8,128)(2,1)S(1)}, f32[256,1280]{1,0:T(8,128)S(1)}, f32[256,1280]{1,0:T(8,128)S(1)}) custom-call(s32[5]{0:T(128)S(1)} %stack.32.place_ref, bf16[256,768]{1,0:T(8,128)(2,1)S(1)} %fusion.15.query_ref, bf16[2,1024,768]{2,1,0:T(8,128)(2,1)} %stale_ref.1, ...), custom_call_target="tpu_custom_call" | custom-call | flops 2818572288 | bytes 14942208 | tf_op jit(solution)/shard_map/pallas_call | solution.py:169
  221.5 0.5 collective-permute-start.23
  222.0 1.6 collective-permute-done.21
  223.6 1.5 collective-permute-start.22
  225.2 0.9 collective-permute-start.24
  226.1 8.2 %collective-permute-done.22 = bf16[256,640]{1,0:T(8,128)(2,1)S(1)} collective-permute-done((bf16[256,640]{1,0:T(8,128)(2,1)S(1)}, bf16[256,640]{1,0:T(8,128)(2,1)S(1)}, u32[]{:S(2)}, u32[]{:S(2)}) %collective-permute-start.22) | collective-permute-done | bytes 327712 | tf_op jit(solution)/shard_map/ppermute | solution.py:203
  234.3 6.1 %collective-permute-done.24 = bf16[256,640]{1,0:T(8,128)(2,1)S(1)} collective-permute-done((bf16[256,640]{1,0:T(8,128)(2,1)S(1)}, bf16[256,640]{1,0:T(8,128)(2,1)S(1)}, u32[]{:S(2)}, u32[]{:S(2)}) %collective-permute-start.24) | collective-permute-done | bytes 327712 | tf_op jit(solution)/shard_map/ppermute | solution.py:203
  240.6 0.9 pad_maximum_fusion.4
  241.5 3.8 %copy.10 = bf16[2,1024,768]{2,1,0:T(8,128)(2,1)} copy(bf16[2,1024,768]{2,1,0:T(8,128)(2,1)} %all-gather.2.cloned.1.call-done) | data formatting | bytes 6291456
  (54 shorter events, 0.9 us)
Async XLA Ops:
  7.2 124.2 %copy-start = (bf16[1280,768]{1,0:T(8,128)(2,1)S(1)}, bf16[1280,768]{1,0:T(8,128)(2,1)}, u32[]{:S(2)}) copy-start(bf16[1280,768]{1,0:T(8,128)(2,1)} %param.7) | copy-start | bytes 5898244
  7.2 234.3 %all-gather.2.cloned.1.call-start = ((), (), s32[]{:S(2)}) async-start(), calls=%async_computation | async-start | bytes 3932160 | tf_op jit(solution)/shard_map/all_gather | solution.py:230
  8.5 9.5 %collective-permute-start.1 = (bf16[128,1280]{1,0:T(8,128)(2,1)S(1)}, bf16[128,1280]{1,0:T(8,128)(2,1)S(1)}, u32[]{:S(2)}, u32[]{:S(2)}) collective-permute-start(bf16[128,1280]{1,0:T(8,128)(2,1)S(1)} %get-tuple-element.28), channel_id=1, source_target_pairs={{0,2},{1,3},{2,0},{3,1},{4,6},{5,7},{6,4},{7,5},{8,10},{9,11},{10,... | collective-permute-start | bytes 983048 | tf_op jit(solution)/shard_map/ppermute | solution.py:27
  10.0 18.8 %collective-permute-start.5 = (bf16[128,1280]{1,0:T(8,128)(2,1)S(1)}, bf16[128,1280]{1,0:T(8,128)(2,1)S(1)}, u32[]{:S(2)}, u32[]{:S(2)}) collective-permute-start(bf16[128,1280]{1,0:T(8,128)(2,1)S(1)} %get-tuple-element.29), channel_id=1, source_target_pairs={{2,10},{3,14},{6,11},{7,15},{8,0},{9,4},{12,1},{13,5},{18,26},{19,... | collective-permute-start | bytes 983048 | tf_op jit(solution)/shard_map/ppermute | solution.py:37
  18.0 10.8 %copy-start.15 = (bf16[128,1280]{1,0:T(8,128)(2,1)}, bf16[128,1280]{1,0:T(8,128)(2,1)S(1)}, u32[]{:S(2)}) copy-start(bf16[128,1280]{1,0:T(8,128)(2,1)S(1)} %collective-permute-done.1) | copy-start | bytes 983044
  18.0 16.8 %collective-permute-start.6 = (bf16[128,1280]{1,0:T(8,128)(2,1)S(1)}, bf16[128,1280]{1,0:T(8,128)(2,1)S(1)}, u32[]{:S(2)}, u32[]{:S(2)}) collective-permute-start(bf16[128,1280]{1,0:T(8,128)(2,1)S(1)} %collective-permute-done.1), channel_id=1, source_target_pairs={{0,8},{1,12},{4,9},{5,13},{10,2},{11,6},{14,3},{15,7},{16,24},{17,... | collective-permute-start | bytes 983048 | tf_op jit(solution)/shard_map/ppermute | solution.py:37
  34.8 10.2 %collective-permute-start.7 = (bf16[128,1280]{1,0:T(8,128)(2,1)S(1)}, bf16[128,1280]{1,0:T(8,128)(2,1)S(1)}, u32[]{:S(2)}, u32[]{:S(2)}) collective-permute-start(bf16[128,1280]{1,0:T(8,128)(2,1)S(1)} %broadcast_select_fusion.2), channel_id=1, source_target_pairs={{0,2},{1,3},{2,0},{3,1},{4,6},{5,7},{6,4},{7,5},{8,10},{9,11},{10,... | collective-permute-start | bytes 983048 | tf_op jit(solution)/shard_map/ppermute | solution.py:41
  37.9 8.4 %collective-permute-start = (bf16[128,1280]{1,0:T(8,128)(2,1)S(1)}, bf16[128,1280]{1,0:T(8,128)(2,1)S(1)}, u32[]{:S(2)}, u32[]{:S(2)}) collective-permute-start(bf16[128,1280]{1,0:T(8,128)(2,1)S(1)} %get-tuple-element.29), channel_id=1, source_target_pairs={{0,0},{1,4},{4,1},{5,5},{10,10},{11,14},{14,11},{15,15},{16,16},{1... | collective-permute-start | bytes 983048 | tf_op jit(solution)/shard_map/ppermute | solution.py:37
  39.9 1.8 copy-start.16
  41.6 3.5 %copy-start.3 = (bf16[1280,768]{1,0:T(8,128)(2,1)S(1)}, bf16[1280,768]{1,0:T(8,128)(2,1)}, u32[]{:S(2)}) copy-start(bf16[1280,768]{1,0:T(8,128)(2,1)} %param.9) | copy-start | bytes 5898244
  41.7 4.7 %collective-permute-start.2 = (bf16[128,1280]{1,0:T(8,128)(2,1)S(1)}, bf16[128,1280]{1,0:T(8,128)(2,1)S(1)}, u32[]{:S(2)}, u32[]{:S(2)}) collective-permute-start(bf16[128,1280]{1,0:T(8,128)(2,1)S(1)} %copy-done.16), channel_id=1, source_target_pairs={{2,2},{3,6},{6,3},{7,7},{8,8},{9,12},{12,9},{13,13},{18,18},{19,22... | collective-permute-start | bytes 983048 | tf_op jit(solution)/shard_map/ppermute | solution.py:37
  45.0 4.7 %copy-start.4 = (bf16[128,1280]{1,0:T(8,128)(2,1)}, bf16[128,1280]{1,0:T(8,128)(2,1)S(1)}, u32[]{:S(2)}) copy-start(bf16[128,1280]{1,0:T(8,128)(2,1)S(1)} %get-tuple-element.26) | copy-start | bytes 983044
  45.0 4.7 %copy-start.6 = (bf16[128,1280]{1,0:T(8,128)(2,1)}, bf16[128,1280]{1,0:T(8,128)(2,1)S(1)}, u32[]{:S(2)}) copy-start(bf16[128,1280]{1,0:T(8,128)(2,1)S(1)} %get-tuple-element.27) | copy-start | bytes 983044
  45.1 4.6 %collective-permute-start.8 = (bf16[256,1280]{1,0:T(8,128)(2,1)S(1)}, bf16[256,1280]{1,0:T(8,128)(2,1)S(1)}, u32[]{:S(2)}, u32[]{:S(2)}) collective-permute-start(bf16[256,1280]{1,0:T(8,128)(2,1)S(1)} %pad_maximum_fusion.3), channel_id=1, source_target_pairs={{0,1},{1,0},{2,3},{3,2},{4,5},{5,4},{6,7},{7,6},{8,9},{9,8},{10,11... | collective-permute-start | bytes 1966088 | tf_op jit(solution)/shard_map/ppermute | solution.py:45
  45.4 6.6 %copy-start.12 = (bf16[1280,1536]{1,0:T(8,128)(2,1)}, bf16[1280,1536]{1,0:T(8,128)(2,1)S(1)}, u32[]{:S(2)}) copy-start(bf16[1280,1536]{1,0:T(8,128)(2,1)S(1)} %constant_dynamic-update-slice_fusion) | copy-start | bytes 11796484
  47.4 9.3 %collective-permute-start.3 = (bf16[128,1280]{1,0:T(8,128)(2,1)}, bf16[128,1280]{1,0:T(8,128)(2,1)}, u32[]{:S(2)}, u32[]{:S(2)}) collective-permute-start(bf16[128,1280]{1,0:T(8,128)(2,1)} %broadcast_select_fusion.5), channel_id=1, source_target_pairs={{0,2},{1,3},{2,0},{3,1},{4,6},{5,7},{6,4},{7,5},{8,10},{9,11},{10,... | collective-permute-start | bytes 983048 | tf_op jit(solution)/shard_map/ppermute | solution.py:41
  49.8 2.2 copy-start.13
  53.4 19.4 %collective-permute-start.15 = (f16[256,1536]{1,0:T(8,128)(2,1)}, f16[256,1536]{1,0:T(8,128)(2,1)}, u32[]{:S(2)}, u32[]{:S(2)}) collective-permute-start(f16[256,1536]{1,0:T(8,128)(2,1)} %get-tuple-element.16), channel_id=1, source_target_pairs={{0,4},{1,5},{2,6},{3,7},{16,20},{17,21},{18,22},{19,23}} | collective-permute-start | bytes 2359304 | tf_op jit(solution)/shard_map/ppermute | solution.py:75
  54.7 18.1 %collective-permute-start.18 = (f16[256,1536]{1,0:T(8,128)(2,1)}, f16[256,1536]{1,0:T(8,128)(2,1)}, u32[]{:S(2)}, u32[]{:S(2)}) collective-permute-start(f16[256,1536]{1,0:T(8,128)(2,1)} %get-tuple-element.17), channel_id=1, source_target_pairs={{12,8},{13,9},{14,10},{15,11},{28,24},{29,25},{30,26},{31,27}} | collective-permute-start | bytes 2359304 | tf_op jit(solution)/shard_map/ppermute | solution.py:76
  57.8 0.7 copy-start.8
  57.8 1.7 copy-start.10
  59.5 22.8 %collective-permute-start.4 = (bf16[256,1280]{1,0:T(8,128)(2,1)}, bf16[256,1280]{1,0:T(8,128)(2,1)}, u32[]{:S(2)}, u32[]{:S(2)}) collective-permute-start(bf16[256,1280]{1,0:T(8,128)(2,1)} %pad_maximum_fusion.2), channel_id=1, source_target_pairs={{0,1},{1,0},{2,3},{3,2},{4,5},{5,4},{6,7},{7,6},{8,9},{9,8},{10,11... | collective-permute-start | bytes 1966088 | tf_op jit(solution)/shard_map/ppermute | solution.py:45
  75.8 22.1 %collective-permute-start.16 = (f16[256,1536]{1,0:T(8,128)(2,1)}, f16[256,1536]{1,0:T(8,128)(2,1)}, u32[]{:S(2)}, u32[]{:S(2)}) collective-permute-start(f16[256,1536]{1,0:T(8,128)(2,1)} %get-tuple-element.14), channel_id=1, source_target_pairs={{0,4},{4,8},{1,5},{5,9},{2,6},{6,10},{3,7},{7,11},{16,20},{20,24},... | collective-permute-start | bytes 2359304 | tf_op jit(solution)/shard_map/ppermute | solution.py:75
  80.9 21.2 %collective-permute-start.19 = (f16[256,1536]{1,0:T(8,128)(2,1)}, f16[256,1536]{1,0:T(8,128)(2,1)}, u32[]{:S(2)}, u32[]{:S(2)}) collective-permute-start(f16[256,1536]{1,0:T(8,128)(2,1)} %get-tuple-element.15), channel_id=1, source_target_pairs={{12,8},{8,4},{13,9},{9,5},{14,10},{10,6},{15,11},{11,7},{28,24},{2... | collective-permute-start | bytes 2359304 | tf_op jit(solution)/shard_map/ppermute | solution.py:76
  87.0 18.3 %copy-start.2 = (f16[512,1536]{1,0:T(8,128)(2,1)}, f16[512,1536]{1,0:T(8,128)(2,1)S(1)}, u32[]{:S(2)}) copy-start(f16[512,1536]{1,0:T(8,128)(2,1)S(1)} %fusion) | copy-start | bytes 4718596
  105.2 20.1 %collective-permute-start.17 = (f16[256,1536]{1,0:T(8,128)(2,1)}, f16[256,1536]{1,0:T(8,128)(2,1)S(1)}, u32[]{:S(2)}, u32[]{:S(2)}) collective-permute-start(f16[256,1536]{1,0:T(8,128)(2,1)} %get-tuple-element.10), channel_id=1, source_target_pairs={{0,4},{4,8},{8,12},{1,5},{5,9},{9,13},{2,6},{6,10},{10,14},{3,7},{... | collective-permute-start | bytes 2359304 | tf_op jit(solution)/shard_map/ppermute | solution.py:75
  107.2 20.1 %collective-permute-start.20 = (f16[256,1536]{1,0:T(8,128)(2,1)}, f16[256,1536]{1,0:T(8,128)(2,1)S(1)}, u32[]{:S(2)}, u32[]{:S(2)}) collective-permute-start(f16[256,1536]{1,0:T(8,128)(2,1)} %get-tuple-element.11), channel_id=1, source_target_pairs={{12,8},{8,4},{4,0},{13,9},{9,5},{5,1},{14,10},{10,6},{6,2},{15,11}... | collective-permute-start | bytes 2359304 | tf_op jit(solution)/shard_map/ppermute | solution.py:76
  128.9 2.5 copy-start.5
  128.9 2.5 copy-start.7
  128.9 2.5 copy-start.14
  132.7 23.2 %copy-start.9 = (bf16[128,1280]{1,0:T(8,128)(2,1)S(1)}, bf16[128,1280]{1,0:T(8,128)(2,1)}, u32[]{:S(2)}) copy-start(bf16[128,1280]{1,0:T(8,128)(2,1)} %copy-done.8) | copy-start | bytes 983044
  132.7 23.2 %copy-start.11 = (bf16[128,1280]{1,0:T(8,128)(2,1)S(1)}, bf16[128,1280]{1,0:T(8,128)(2,1)}, u32[]{:S(2)}) copy-start(bf16[128,1280]{1,0:T(8,128)(2,1)} %copy-done.10) | copy-start | bytes 983044
  132.7 2.1 collective-permute-start.12
  133.6 18.9 %collective-permute-start.9 = (f16[256,768]{1,0:T(8,128)(2,1)S(1)}, f16[256,768]{1,0:T(8,128)(2,1)S(1)}, u32[]{:S(2)}, u32[]{:S(2)}) collective-permute-start(f16[256,768]{1,0:T(8,128)(2,1)S(1)} %get-tuple-element.22), channel_id=1, source_target_pairs={{0,4},{1,5},{2,6},{3,7},{16,20},{17,21},{18,22},{19,23}} | collective-permute-start | bytes 1179656 | tf_op jit(solution)/shard_map/ppermute | solution.py:75
  152.7 25.1 %collective-permute-start.10 = (f16[256,768]{1,0:T(8,128)(2,1)S(1)}, f16[256,768]{1,0:T(8,128)(2,1)S(1)}, u32[]{:S(2)}, u32[]{:S(2)}) collective-permute-start(f16[256,768]{1,0:T(8,128)(2,1)S(1)} %get-tuple-element.20), channel_id=1, source_target_pairs={{0,4},{4,8},{1,5},{5,9},{2,6},{6,10},{3,7},{7,11},{16,20},{20,24},... | collective-permute-start | bytes 1179656 | tf_op jit(solution)/shard_map/ppermute | solution.py:75
  154.6 29.4 %collective-permute-start.13 = (f16[256,768]{1,0:T(8,128)(2,1)S(1)}, f16[256,768]{1,0:T(8,128)(2,1)S(1)}, u32[]{:S(2)}, u32[]{:S(2)}) collective-permute-start(f16[256,768]{1,0:T(8,128)(2,1)S(1)} %get-tuple-element.21), channel_id=1, source_target_pairs={{12,8},{8,4},{13,9},{9,5},{14,10},{10,6},{15,11},{11,7},{28,24},{2... | collective-permute-start | bytes 1179656 | tf_op jit(solution)/shard_map/ppermute | solution.py:76
  185.3 26.0 %copy-start.1 = (bf16[2,256,768]{2,1,0:T(8,128)(2,1)S(1)}, bf16[2,256,768]{2,1,0:T(8,128)(2,1)}, u32[]{:S(2)}) copy-start(bf16[2,256,768]{2,1,0:T(8,128)(2,1)} %fusion.3.fresh_ref) | copy-start | bytes 2359300
  185.3 20.2 %collective-permute-start.11 = (f16[256,768]{1,0:T(8,128)(2,1)}, f16[256,768]{1,0:T(8,128)(2,1)}, u32[]{:S(2)}, u32[]{:S(2)}) collective-permute-start(f16[256,768]{1,0:T(8,128)(2,1)} %get-tuple-element.18), channel_id=1, source_target_pairs={{0,4},{4,8},{8,12},{1,5},{5,9},{9,13},{2,6},{6,10},{10,14},{3,7},{... | collective-permute-start | bytes 1179656 | tf_op jit(solution)/shard_map/ppermute | solution.py:75
  187.3 22.6 %collective-permute-start.14 = (f16[256,768]{1,0:T(8,128)(2,1)}, f16[256,768]{1,0:T(8,128)(2,1)}, u32[]{:S(2)}, u32[]{:S(2)}) collective-permute-start(f16[256,768]{1,0:T(8,128)(2,1)} %get-tuple-element.19), channel_id=1, source_target_pairs={{12,8},{8,4},{4,0},{13,9},{9,5},{5,1},{14,10},{10,6},{6,2},{15,11}... | collective-permute-start | bytes 1179656 | tf_op jit(solution)/shard_map/ppermute | solution.py:76
  221.4 2.2 collective-permute-start.21
  221.5 3.6 %collective-permute-start.23 = (bf16[256,1280]{1,0:T(8,128)(2,1)S(1)}, bf16[256,1280]{1,0:T(8,128)(2,1)S(1)}, u32[]{:S(2)}, u32[]{:S(2)}) collective-permute-start(bf16[256,1280]{1,0:T(8,128)(2,1)S(1)} %get-tuple-element.9), channel_id=1, source_target_pairs={{0,1},{1,0},{2,3},{3,2},{4,5},{5,4},{6,7},{7,6},{8,9},{9,8},{10,11... | collective-permute-start | bytes 1966088 | tf_op jit(solution)/shard_map/ppermute | solution.py:193
  223.6 10.6 %collective-permute-start.22 = (bf16[256,640]{1,0:T(8,128)(2,1)S(1)}, bf16[256,640]{1,0:T(8,128)(2,1)S(1)}, u32[]{:S(2)}, u32[]{:S(2)}) collective-permute-start(bf16[256,640]{1,0:T(8,128)(2,1)S(1)} %add_convert_fusion.3), channel_id=1, source_target_pairs={{0,2},{1,3},{2,0},{3,1},{4,6},{5,7},{6,4},{7,5},{8,10},{9,11},{10,... | collective-permute-start | bytes 983048 | tf_op jit(solution)/shard_map/ppermute | solution.py:203
  225.2 15.3 %collective-permute-start.24 = (bf16[256,640]{1,0:T(8,128)(2,1)S(1)}, bf16[256,640]{1,0:T(8,128)(2,1)S(1)}, u32[]{:S(2)}, u32[]{:S(2)}) collective-permute-start(bf16[256,640]{1,0:T(8,128)(2,1)S(1)} %add_convert_fusion.1), channel_id=1, source_target_pairs={{0,2},{1,3},{2,0},{3,1},{4,6},{5,7},{6,4},{7,5},{8,10},{9,11},{10,... | collective-permute-start | bytes 983048 | tf_op jit(solution)/shard_map/ppermute | solution.py:203
Sparse Core Ops, SparseCore 0:
  131.5 80.3 all-gather.1

commit v7 on v6

--- a/solution.py
+++ b/solution.py
@@ -227,7 +227,8 @@
         fresh = jnp.stack([fresh[:, :width], fresh[:, width:]])
         delta = lax.reduce_precision(fresh - own_stale, 8, 7)
         own_new = (own_stale + delta).astype(BF16)
-        refreshed = lax.all_gather(own_new, "patch", axis=1, tiled=True)
+        sent, _ = lax.optimization_barrier((own_new, query))
+        refreshed = lax.all_gather(sent, "patch", axis=1, tiled=True)
         attended = attend(query, stale_kv, own_new, w_out, patches, ranks)
         return (attended, refreshed)
 

time: 253 us -> 213 us (0.84)
  the two profiles are of different devices: /device:TPU:8 before, /device:TPU:0 now
where the time goes in v7:
time: 213 us
  waiting for transfers between devices  104 us (49%)
  starting transfers between devices  57.6 us (27%)
  between operations  14.6 us (7%)
  other arithmetic  10.6 us (5%)
  Pallas kernels  10.1 us (5%)
  local copies, waits for them, and re-layouts  8.69 us (4%)
  matrix products  6.77 us (3%)
    ppermute x6, waiting for transfers between devices, sum_in_pairs(): up = lax.ppermute(send_up, 'patch', [(i, i + 1) for i in range(step)])  38.7 us
    all_gather x1, waiting for transfers between devices, shards(): refreshed = lax.all_gather(sent, 'patch', axis=1, tiled=True)  31.8 us
    ppermute x6, starting transfers between devices, sum_in_pairs(): up = lax.ppermute(send_up, 'patch', [(i, i + 1) for i in range(step)])  27.3 us
    ppermute x2, waiting for transfers between devices, attend(): arrived.append(lax.ppermute(summed(hop - 1).astype(BF16), 'tensor', pairs))  14 us
    ppermute x2, starting transfers between devices, both_slabs(): other = lax.ppermute(held, 'tensor', across)  10.6 us
    pallas_call x1, Pallas kernels, attend(): pl.pallas_call(functools.partial(attend_and_project, patches, heads, chip...  10.1 us
    ppermute x4, waiting for transfers between devices, along(): return lax.ppermute(block, ('patch', 'tensor'), pairs)  7.73 us
    ppermute x4, starting transfers between devices, along(): return lax.ppermute(block, ('patch', 'tensor'), pairs)  7.51 us
  transfers between devices with their start and end apart: 26, of which 12 were waited for; matrix products, arithmetic and copies ran while one was open for 7% of the time, Pallas kernels for 5%

profile of v7, /device:TPU:0, one launch (start us, length us, event | category | flops | bytes accessed | tf_op | source)
XLA Modules:
  0.0 212.5 jit_solution(958041852655135151)
XLA Ops:
  7.2 0.0 all-gather.2.cloned.1.call-start
  7.2 1.2 fusion.20
  8.5 3.0 %collective-permute-start.1 = (bf16[128,1280]{1,0:T(8,128)(2,1)S(1)}, bf16[128,1280]{1,0:T(8,128)(2,1)S(1)}, u32[]{:S(2)}, u32[]{:S(2)}) collective-permute-start(bf16[128,1280]{1,0:T(8,128)(2,1)S(1)} %get-tuple-element.30), channel_id=1, source_target_pairs={{0,2},{1,3},{2,0},{3,1},{4,6},{5,7},{6,4},{7,5},{8,10},{9,11},{10,... | collective-permute-start | bytes 983048 | tf_op jit(solution)/shard_map/ppermute | solution.py:27
  11.5 1.3 collective-permute-start.5
  12.8 6.4 %collective-permute-done.1 = bf16[128,1280]{1,0:T(8,128)(2,1)S(1)} collective-permute-done((bf16[128,1280]{1,0:T(8,128)(2,1)S(1)}, bf16[128,1280]{1,0:T(8,128)(2,1)S(1)}, u32[]{:S(2)}, u32[]{:S(2)}) %collective-permute-start.1) | collective-permute-done | bytes 327712 | tf_op jit(solution)/shard_map/ppermute | solution.py:27
  19.2 4.8 %collective-permute-start.6 = (bf16[128,1280]{1,0:T(8,128)(2,1)S(1)}, bf16[128,1280]{1,0:T(8,128)(2,1)S(1)}, u32[]{:S(2)}, u32[]{:S(2)}) collective-permute-start(bf16[128,1280]{1,0:T(8,128)(2,1)S(1)} %collective-permute-done.1), channel_id=1, source_target_pairs={{0,8},{1,12},{4,9},{5,13},{10,2},{11,6},{14,3},{15,7},{16,24},{17,... | collective-permute-start | bytes 983048 | tf_op jit(solution)/shard_map/ppermute | solution.py:37
  24.0 7.4 %collective-permute-done.5 = bf16[128,1280]{1,0:T(8,128)(2,1)S(1)} collective-permute-done((bf16[128,1280]{1,0:T(8,128)(2,1)S(1)}, bf16[128,1280]{1,0:T(8,128)(2,1)S(1)}, u32[]{:S(2)}, u32[]{:S(2)}) %collective-permute-start.5) | collective-permute-done | bytes 327712 | tf_op jit(solution)/shard_map/ppermute | solution.py:37
  31.4 0.3 collective-permute-done.6
  31.7 8.7 %collective-permute-start.7 = (bf16[128,1280]{1,0:T(8,128)(2,1)S(1)}, bf16[128,1280]{1,0:T(8,128)(2,1)S(1)}, u32[]{:S(2)}, u32[]{:S(2)}) collective-permute-start(bf16[128,1280]{1,0:T(8,128)(2,1)S(1)} %broadcast_select_fusion.2), channel_id=1, source_target_pairs={{0,2},{1,3},{2,0},{3,1},{4,6},{5,7},{6,4},{7,5},{8,10},{9,11},{10,... | collective-permute-start | bytes 983048 | tf_op jit(solution)/shard_map/ppermute | solution.py:41
  40.4 0.7 collective-permute-start
  41.2 1.7 constant_dynamic-update-slice_fusion.1
  43.0 0.8 collective-permute-start.2
  43.8 1.7 collective-permute-done.7
  45.6 0.2 collective-permute-start.8
  45.8 0.1 constant_dynamic-update-slice_fusion
  46.1 1.9 collective-permute-start.3
  48.0 2.2 %fusion.1 = f16[512,1536]{1,0:T(8,128)(2,1)S(1)} fusion(bf16[1280,1536]{1,0:T(8,128)(2,1)S(1)} %constant_dynamic-update-slice_fusion, bf16[256,1280]{1,0:T(8,128)(2,1)S(1)} %collective-permute-done.8, bf16[128,1280]{1,0:T(8,128)(2,1)S(1)} %get-tuple-element.29, bf16[128,1280]{1,0:T(8,128)(2,1)S(1)} %get-tuple-element.28), kind=kOutput, calls=%fused_computation.3 | convolution fusion | flops 2018770944 | bytes 6815744 | tf_op jit(solution)/shard_map/dot_general | solution.py:55
  50.2 0.3 dynamic-slice_bitcast_fusion.1
  50.5 6.1 %collective-permute-start.15 = (f16[256,1536]{1,0:T(8,128)(2,1)S(1)}, f16[256,1536]{1,0:T(8,128)(2,1)S(1)}, u32[]{:S(2)}, u32[]{:S(2)}) collective-permute-start(f16[256,1536]{1,0:T(8,128)(2,1)S(1)} %get-tuple-element.18), channel_id=1, source_target_pairs={{0,4},{1,5},{2,6},{3,7},{16,20},{17,21},{18,22},{19,23}} | collective-permute-start | bytes 2359304 | tf_op jit(solution)/shard_map/ppermute | solution.py:75
  56.6 0.7 collective-permute-start.18
  57.5 0.1 collective-permute-start.4
  57.5 1.2 multiply_convert_fusion
  58.7 0.1 dynamic-slice_bitcast_fusion.3
  58.9 0.7 collective-permute-start.12
  59.6 3.2 %collective-permute-start.9 = (f16[256,768]{1,0:T(8,128)(2,1)S(1)}, f16[256,768]{1,0:T(8,128)(2,1)S(1)}, u32[]{:S(2)}, u32[]{:S(2)}) collective-permute-start(f16[256,768]{1,0:T(8,128)(2,1)S(1)} %get-tuple-element.24), channel_id=1, source_target_pairs={{0,4},{1,5},{2,6},{3,7},{16,20},{17,21},{18,22},{19,23}} | collective-permute-start | bytes 1179656 | tf_op jit(solution)/shard_map/ppermute | solution.py:75
  62.8 11.8 %collective-permute-done.15 = f16[256,1536]{1,0:T(8,128)(2,1)S(1)} collective-permute-done((f16[256,1536]{1,0:T(8,128)(2,1)S(1)}, f16[256,1536]{1,0:T(8,128)(2,1)S(1)}, u32[]{:S(2)}, u32[]{:S(2)}) %collective-permute-start.15) | collective-permute-done | bytes 786464 | tf_op jit(solution)/shard_map/ppermute | solution.py:75
  74.6 0.5 fusion.6
  75.0 4.4 %collective-permute-start.16 = (f16[256,1536]{1,0:T(8,128)(2,1)S(1)}, f16[256,1536]{1,0:T(8,128)(2,1)S(1)}, u32[]{:S(2)}, u32[]{:S(2)}) collective-permute-start(f16[256,1536]{1,0:T(8,128)(2,1)S(1)} %get-tuple-element.16), channel_id=1, source_target_pairs={{0,4},{4,8},{1,5},{5,9},{2,6},{6,10},{3,7},{7,11},{16,20},{20,24},... | collective-permute-start | bytes 2359304 | tf_op jit(solution)/shard_map/ppermute | solution.py:75
  79.5 0.7 collective-permute-start.19
  80.2 2.2 %fusion = f16[512,1536]{1,0:T(8,128)(2,1)S(1)} fusion(bf16[1280,1536]{1,0:T(8,128)(2,1)S(1)} %constant_dynamic-update-slice_fusion, bf16[256,1280]{1,0:T(8,128)(2,1)S(1)} %collective-permute-done.4, bf16[128,1280]{1,0:T(8,128)(2,1)S(1)} %get-tuple-element.27, bf16[128,1280]{1,0:T(8,128)(2,1)S(1)} %get-tuple-element.26), kind=kOutput, calls=%fused_computation.2 | convolution fusion | flops 2018770944 | bytes 6815744 | tf_op jit(solution)/shard_map/dot_general | solution.py:55
  82.4 1.2 multiply_convert_fusion.1
  83.6 0.2 fusion.12
  83.9 3.7 %collective-permute-start.10 = (f16[256,768]{1,0:T(8,128)(2,1)S(1)}, f16[256,768]{1,0:T(8,128)(2,1)S(1)}, u32[]{:S(2)}, u32[]{:S(2)}) collective-permute-start(f16[256,768]{1,0:T(8,128)(2,1)S(1)} %get-tuple-element.22), channel_id=1, source_target_pairs={{0,4},{4,8},{1,5},{5,9},{2,6},{6,10},{3,7},{7,11},{16,20},{20,24},... | collective-permute-start | bytes 1179656 | tf_op jit(solution)/shard_map/ppermute | solution.py:75
  87.6 0.7 collective-permute-start.13
  88.3 11.5 %collective-permute-done.16 = f16[256,1536]{1,0:T(8,128)(2,1)S(1)} collective-permute-done((f16[256,1536]{1,0:T(8,128)(2,1)S(1)}, f16[256,1536]{1,0:T(8,128)(2,1)S(1)}, u32[]{:S(2)}, u32[]{:S(2)}) %collective-permute-start.16) | collective-permute-done | bytes 786464 | tf_op jit(solution)/shard_map/ppermute | solution.py:75
  99.8 1.9 fusion.7
  101.7 5.3 %collective-permute-start.17 = (f16[256,1536]{1,0:T(8,128)(2,1)}, f16[256,1536]{1,0:T(8,128)(2,1)}, u32[]{:S(2)}, u32[]{:S(2)}) collective-permute-start(f16[256,1536]{1,0:T(8,128)(2,1)} %get-tuple-element.12), channel_id=1, source_target_pairs={{0,4},{4,8},{8,12},{1,5},{5,9},{9,13},{2,6},{6,10},{10,14},{3,7},{... | collective-permute-start | bytes 2359304 | tf_op jit(solution)/shard_map/ppermute | solution.py:75
  107.0 1.3 collective-permute-start.20
  108.3 1.1 fusion.13
  109.4 4.6 %collective-permute-start.11 = (f16[256,768]{1,0:T(8,128)(2,1)}, f16[256,768]{1,0:T(8,128)(2,1)S(1)}, u32[]{:S(2)}, u32[]{:S(2)}) collective-permute-start(f16[256,768]{1,0:T(8,128)(2,1)} %get-tuple-element.20), channel_id=1, source_target_pairs={{0,4},{4,8},{8,12},{1,5},{5,9},{9,13},{2,6},{6,10},{10,14},{3,7},{... | collective-permute-start | bytes 1179656 | tf_op jit(solution)/shard_map/ppermute | solution.py:75
  114.0 1.5 collective-permute-start.14
  115.5 15.4 %collective-permute-done.11 = f16[256,768]{1,0:T(8,128)(2,1)S(1)} collective-permute-done((f16[256,768]{1,0:T(8,128)(2,1)}, f16[256,768]{1,0:T(8,128)(2,1)S(1)}, u32[]{:S(2)}, u32[]{:S(2)}) %collective-permute-start.11) | collective-permute-done | bytes 393248 | tf_op jit(solution)/shard_map/ppermute | solution.py:75
  130.9 2.2 %collective-permute-done.14 = f16[256,768]{1,0:T(8,128)(2,1)} collective-permute-done((f16[256,768]{1,0:T(8,128)(2,1)S(1)}, f16[256,768]{1,0:T(8,128)(2,1)}, u32[]{:S(2)}, u32[]{:S(2)}) %collective-permute-start.14) | collective-permute-done | bytes 393248 | tf_op jit(solution)/shard_map/ppermute | solution.py:76
  133.0 1.2 fusion.15.query_ref
  134.2 2.0 convert_reduce-precision_fusion
  136.2 0.1 slice_bitcast_fusion.1
  136.3 2.3 %fusion.3.fresh_ref = bf16[2,256,768]{2,1,0:T(8,128)(2,1)} fusion(f32[1,256,768]{2,1,0:T(8,128)S(1)} %get-tuple-element.15, f32[1,256,768]{2,1,0:T(8,128)S(1)} %get-tuple-element.14, bf16[2,1024,768]{2,1,0:T(8,128)(2,1)} %stale_ref.1, s32[]{:T(128)S(6)} %select_n.205), kind=kLoop, calls=%fused_computation.7 | loop fusion | flops 2359296 | bytes 3145732 | tf_op jit(solution)/shard_map/convert_element_type | solution.py:229
  138.7 0.1 stack.32.place_ref
  138.7 1.1 copy-done.1
  139.9 10.1 %shard_map.77 = (bf16[256,1280]{1,0:T(8,128)(2,1)S(1)}, bf16[256,1280]{1,0:T(8,128)(2,1)S(1)}, f32[256,1280]{1,0:T(8,128)S(1)}, f32[256,1280]{1,0:T(8,128)S(1)}) custom-call(s32[5]{0:T(128)S(1)} %stack.32.place_ref, bf16[256,768]{1,0:T(8,128)(2,1)S(1)} %fusion.15.query_ref, bf16[2,1024,768]{2,1,0:T(8,128)(2,1)} %stale_ref.1, ...), custom_call_target="tpu_custom_call" | custom-call | flops 2818572288 | bytes 14942208 | tf_op jit(solution)/shard_map/pallas_call | solution.py:169
  150.0 0.1 collective-permute-start.21
  150.1 0.5 collective-permute-start.23
  150.6 1.6 collective-permute-done.21
  152.2 0.1 add_convert_fusion.3
  152.2 1.9 collective-permute-start.22
  154.1 0.1 add_convert_fusion.1
  154.2 0.9 collective-permute-start.24
  155.0 7.8 %collective-permute-done.22 = bf16[256,640]{1,0:T(8,128)(2,1)S(1)} collective-permute-done((bf16[256,640]{1,0:T(8,128)(2,1)S(1)}, bf16[256,640]{1,0:T(8,128)(2,1)S(1)}, u32[]{:S(2)}, u32[]{:S(2)}) %collective-permute-start.22) | collective-permute-done | bytes 327712 | tf_op jit(solution)/shard_map/ppermute | solution.py:203
  162.8 0.1 add_convert_fusion.2
  162.9 6.2 %collective-permute-done.24 = bf16[256,640]{1,0:T(8,128)(2,1)S(1)} collective-permute-done((bf16[256,640]{1,0:T(8,128)(2,1)S(1)}, bf16[256,640]{1,0:T(8,128)(2,1)S(1)}, u32[]{:S(2)}, u32[]{:S(2)}) %collective-permute-start.24) | collective-permute-done | bytes 327712 | tf_op jit(solution)/shard_map/ppermute | solution.py:203
  169.1 0.1 add_convert_fusion
  169.2 0.9 pad_maximum_fusion.4
  170.1 31.8 %all-gather.2.cloned.1.call-done = bf16[2,1024,768]{2,1,0:T(8,128)(2,1)} async-done(((bf16[2,256,768]{2,1,0:T(8,128)(2,1)}), bf16[2,1024,768]{2,1,0:T(8,128)(2,1)}) %all-gather.2.cloned.1.call-update) | async-done | bytes 3145744 | tf_op jit(solution)/shard_map/all_gather | solution.py:231
  201.9 3.8 %copy.10 = bf16[2,1024,768]{2,1,0:T(8,128)(2,1)} copy(bf16[2,1024,768]{2,1,0:T(8,128)(2,1)} %all-gather.2.cloned.1.call-done) | data formatting | bytes 6291456
  (32 shorter events, 0.4 us)
Async XLA Ops:
  7.2 50.4 %copy-start = (bf16[1280,768]{1,0:T(8,128)(2,1)S(1)}, bf16[1280,768]{1,0:T(8,128)(2,1)}, u32[]{:S(2)}) copy-start(bf16[1280,768]{1,0:T(8,128)(2,1)} %param.7) | copy-start | bytes 5898244
  7.2 194.8 %all-gather.2.cloned.1.call-start = ((), (), s32[]{:S(2)}) async-start(), calls=%async_computation | async-start | bytes 3932160 | tf_op jit(solution)/shard_map/all_gather | solution.py:231
  8.5 10.7 %collective-permute-start.1 = (bf16[128,1280]{1,0:T(8,128)(2,1)S(1)}, bf16[128,1280]{1,0:T(8,128)(2,1)S(1)}, u32[]{:S(2)}, u32[]{:S(2)}) collective-permute-start(bf16[128,1280]{1,0:T(8,128)(2,1)S(1)} %get-tuple-element.30), channel_id=1, source_target_pairs={{0,2},{1,3},{2,0},{3,1},{4,6},{5,7},{6,4},{7,5},{8,10},{9,11},{10,... | collective-permute-start | bytes 983048 | tf_op jit(solution)/shard_map/ppermute | solution.py:27
  11.5 19.9 %collective-permute-start.5 = (bf16[128,1280]{1,0:T(8,128)(2,1)S(1)}, bf16[128,1280]{1,0:T(8,128)(2,1)S(1)}, u32[]{:S(2)}, u32[]{:S(2)}) collective-permute-start(bf16[128,1280]{1,0:T(8,128)(2,1)S(1)} %get-tuple-element.31), channel_id=1, source_target_pairs={{2,10},{3,14},{6,11},{7,15},{8,0},{9,4},{12,1},{13,5},{18,26},{19,... | collective-permute-start | bytes 983048 | tf_op jit(solution)/shard_map/ppermute | solution.py:37
  19.2 12.2 %copy-start.4 = (bf16[128,1280]{1,0:T(8,128)(2,1)}, bf16[128,1280]{1,0:T(8,128)(2,1)S(1)}, u32[]{:S(2)}) copy-start(bf16[128,1280]{1,0:T(8,128)(2,1)S(1)} %collective-permute-done.1) | copy-start | bytes 983044
  19.2 12.5 %collective-permute-start.6 = (bf16[128,1280]{1,0:T(8,128)(2,1)S(1)}, bf16[128,1280]{1,0:T(8,128)(2,1)S(1)}, u32[]{:S(2)}, u32[]{:S(2)}) collective-permute-start(bf16[128,1280]{1,0:T(8,128)(2,1)S(1)} %collective-permute-done.1), channel_id=1, source_target_pairs={{0,8},{1,12},{4,9},{5,13},{10,2},{11,6},{14,3},{15,7},{16,24},{17,... | collective-permute-start | bytes 983048 | tf_op jit(solution)/shard_map/ppermute | solution.py:37
  31.7 13.7 %collective-permute-start.7 = (bf16[128,1280]{1,0:T(8,128)(2,1)S(1)}, bf16[128,1280]{1,0:T(8,128)(2,1)S(1)}, u32[]{:S(2)}, u32[]{:S(2)}) collective-permute-start(bf16[128,1280]{1,0:T(8,128)(2,1)S(1)} %broadcast_select_fusion.2), channel_id=1, source_target_pairs={{0,2},{1,3},{2,0},{3,1},{4,6},{5,7},{6,4},{7,5},{8,10},{9,11},{10,... | collective-permute-start | bytes 983048 | tf_op jit(solution)/shard_map/ppermute | solution.py:41
  40.4 5.6 %collective-permute-start = (bf16[128,1280]{1,0:T(8,128)(2,1)S(1)}, bf16[128,1280]{1,0:T(8,128)(2,1)S(1)}, u32[]{:S(2)}, u32[]{:S(2)}) collective-permute-start(bf16[128,1280]{1,0:T(8,128)(2,1)S(1)} %get-tuple-element.31), channel_id=1, source_target_pairs={{0,0},{1,4},{4,1},{5,5},{10,10},{11,14},{14,11},{15,15},{16,16},{1... | collective-permute-start | bytes 983048 | tf_op jit(solution)/shard_map/ppermute | solution.py:37
  41.2 1.8 copy-start.5
  43.0 2.9 %copy-start.3 = (bf16[1280,768]{1,0:T(8,128)(2,1)S(1)}, bf16[1280,768]{1,0:T(8,128)(2,1)}, u32[]{:S(2)}) copy-start(bf16[1280,768]{1,0:T(8,128)(2,1)} %param.9) | copy-start | bytes 5898244
  43.0 3.0 %collective-permute-start.2 = (bf16[128,1280]{1,0:T(8,128)(2,1)S(1)}, bf16[128,1280]{1,0:T(8,128)(2,1)S(1)}, u32[]{:S(2)}, u32[]{:S(2)}) collective-permute-start(bf16[128,1280]{1,0:T(8,128)(2,1)S(1)} %copy-done.5), channel_id=1, source_target_pairs={{2,2},{3,6},{6,3},{7,7},{8,8},{9,12},{12,9},{13,13},{18,18},{19,22... | collective-permute-start | bytes 983048 | tf_op jit(solution)/shard_map/ppermute | solution.py:37
  45.6 2.4 %collective-permute-start.8 = (bf16[256,1280]{1,0:T(8,128)(2,1)S(1)}, bf16[256,1280]{1,0:T(8,128)(2,1)S(1)}, u32[]{:S(2)}, u32[]{:S(2)}) collective-permute-start(bf16[256,1280]{1,0:T(8,128)(2,1)S(1)} %pad_maximum_fusion.3), channel_id=1, source_target_pairs={{0,1},{1,0},{2,3},{3,2},{4,5},{5,4},{6,7},{7,6},{8,9},{9,8},{10,11... | collective-permute-start | bytes 1966088 | tf_op jit(solution)/shard_map/ppermute | solution.py:45
  46.1 11.3 %collective-permute-start.3 = (bf16[128,1280]{1,0:T(8,128)(2,1)S(1)}, bf16[128,1280]{1,0:T(8,128)(2,1)S(1)}, u32[]{:S(2)}, u32[]{:S(2)}) collective-permute-start(bf16[128,1280]{1,0:T(8,128)(2,1)S(1)} %broadcast_select_fusion.5), channel_id=1, source_target_pairs={{0,2},{1,3},{2,0},{3,1},{4,6},{5,7},{6,4},{7,5},{8,10},{9,11},{10,... | collective-permute-start | bytes 983048 | tf_op jit(solution)/shard_map/ppermute | solution.py:41
  50.5 24.1 %collective-permute-start.15 = (f16[256,1536]{1,0:T(8,128)(2,1)S(1)}, f16[256,1536]{1,0:T(8,128)(2,1)S(1)}, u32[]{:S(2)}, u32[]{:S(2)}) collective-permute-start(f16[256,1536]{1,0:T(8,128)(2,1)S(1)} %get-tuple-element.18), channel_id=1, source_target_pairs={{0,4},{1,5},{2,6},{3,7},{16,20},{17,21},{18,22},{19,23}} | collective-permute-start | bytes 2359304 | tf_op jit(solution)/shard_map/ppermute | solution.py:75
  56.6 17.9 %collective-permute-start.18 = (f16[256,1536]{1,0:T(8,128)(2,1)S(1)}, f16[256,1536]{1,0:T(8,128)(2,1)S(1)}, u32[]{:S(2)}, u32[]{:S(2)}) collective-permute-start(f16[256,1536]{1,0:T(8,128)(2,1)S(1)} %get-tuple-element.19), channel_id=1, source_target_pairs={{12,8},{13,9},{14,10},{15,11},{28,24},{29,25},{30,26},{31,27}} | collective-permute-start | bytes 2359304 | tf_op jit(solution)/shard_map/ppermute | solution.py:76
  57.5 22.7 %collective-permute-start.4 = (bf16[256,1280]{1,0:T(8,128)(2,1)S(1)}, bf16[256,1280]{1,0:T(8,128)(2,1)S(1)}, u32[]{:S(2)}, u32[]{:S(2)}) collective-permute-start(bf16[256,1280]{1,0:T(8,128)(2,1)S(1)} %pad_maximum_fusion.2), channel_id=1, source_target_pairs={{0,1},{1,0},{2,3},{3,2},{4,5},{5,4},{6,7},{7,6},{8,9},{9,8},{10,11... | collective-permute-start | bytes 1966088 | tf_op jit(solution)/shard_map/ppermute | solution.py:45
  58.9 24.7 %collective-permute-start.12 = (f16[256,768]{1,0:T(8,128)(2,1)S(1)}, f16[256,768]{1,0:T(8,128)(2,1)S(1)}, u32[]{:S(2)}, u32[]{:S(2)}) collective-permute-start(f16[256,768]{1,0:T(8,128)(2,1)S(1)} %get-tuple-element.25), channel_id=1, source_target_pairs={{12,8},{13,9},{14,10},{15,11},{28,24},{29,25},{30,26},{31,27}} | collective-permute-start | bytes 1179656 | tf_op jit(solution)/shard_map/ppermute | solution.py:76
  59.6 24.0 %collective-permute-start.9 = (f16[256,768]{1,0:T(8,128)(2,1)S(1)}, f16[256,768]{1,0:T(8,128)(2,1)S(1)}, u32[]{:S(2)}, u32[]{:S(2)}) collective-permute-start(f16[256,768]{1,0:T(8,128)(2,1)S(1)} %get-tuple-element.24), channel_id=1, source_target_pairs={{0,4},{1,5},{2,6},{3,7},{16,20},{17,21},{18,22},{19,23}} | collective-permute-start | bytes 1179656 | tf_op jit(solution)/shard_map/ppermute | solution.py:75
  75.0 24.8 %collective-permute-start.16 = (f16[256,1536]{1,0:T(8,128)(2,1)S(1)}, f16[256,1536]{1,0:T(8,128)(2,1)S(1)}, u32[]{:S(2)}, u32[]{:S(2)}) collective-permute-start(f16[256,1536]{1,0:T(8,128)(2,1)S(1)} %get-tuple-element.16), channel_id=1, source_target_pairs={{0,4},{4,8},{1,5},{5,9},{2,6},{6,10},{3,7},{7,11},{16,20},{20,24},... | collective-permute-start | bytes 2359304 | tf_op jit(solution)/shard_map/ppermute | solution.py:75
  79.5 20.4 %collective-permute-start.19 = (f16[256,1536]{1,0:T(8,128)(2,1)S(1)}, f16[256,1536]{1,0:T(8,128)(2,1)S(1)}, u32[]{:S(2)}, u32[]{:S(2)}) collective-permute-start(f16[256,1536]{1,0:T(8,128)(2,1)S(1)} %get-tuple-element.17), channel_id=1, source_target_pairs={{12,8},{8,4},{13,9},{9,5},{14,10},{10,6},{15,11},{11,7},{28,24},{2... | collective-permute-start | bytes 2359304 | tf_op jit(solution)/shard_map/ppermute | solution.py:76
  82.4 17.4 %copy-start.2 = (f16[512,1536]{1,0:T(8,128)(2,1)}, f16[512,1536]{1,0:T(8,128)(2,1)S(1)}, u32[]{:S(2)}) copy-start(f16[512,1536]{1,0:T(8,128)(2,1)S(1)} %fusion) | copy-start | bytes 4718596
  83.9 24.4 %collective-permute-start.10 = (f16[256,768]{1,0:T(8,128)(2,1)S(1)}, f16[256,768]{1,0:T(8,128)(2,1)S(1)}, u32[]{:S(2)}, u32[]{:S(2)}) collective-permute-start(f16[256,768]{1,0:T(8,128)(2,1)S(1)} %get-tuple-element.22), channel_id=1, source_target_pairs={{0,4},{4,8},{1,5},{5,9},{2,6},{6,10},{3,7},{7,11},{16,20},{20,24},... | collective-permute-start | bytes 1179656 | tf_op jit(solution)/shard_map/ppermute | solution.py:75
  87.6 20.6 %collective-permute-start.13 = (f16[256,768]{1,0:T(8,128)(2,1)S(1)}, f16[256,768]{1,0:T(8,128)(2,1)S(1)}, u32[]{:S(2)}, u32[]{:S(2)}) collective-permute-start(f16[256,768]{1,0:T(8,128)(2,1)S(1)} %get-tuple-element.23), channel_id=1, source_target_pairs={{12,8},{8,4},{13,9},{9,5},{14,10},{10,6},{15,11},{11,7},{28,24},{2... | collective-permute-start | bytes 1179656 | tf_op jit(solution)/shard_map/ppermute | solution.py:76
  101.7 32.5 %collective-permute-start.17 = (f16[256,1536]{1,0:T(8,128)(2,1)}, f16[256,1536]{1,0:T(8,128)(2,1)}, u32[]{:S(2)}, u32[]{:S(2)}) collective-permute-start(f16[256,1536]{1,0:T(8,128)(2,1)} %get-tuple-element.12), channel_id=1, source_target_pairs={{0,4},{4,8},{8,12},{1,5},{5,9},{9,13},{2,6},{6,10},{10,14},{3,7},{... | collective-permute-start | bytes 2359304 | tf_op jit(solution)/shard_map/ppermute | solution.py:75
  107.0 27.2 %collective-permute-start.20 = (f16[256,1536]{1,0:T(8,128)(2,1)}, f16[256,1536]{1,0:T(8,128)(2,1)}, u32[]{:S(2)}, u32[]{:S(2)}) collective-permute-start(f16[256,1536]{1,0:T(8,128)(2,1)} %get-tuple-element.13), channel_id=1, source_target_pairs={{12,8},{8,4},{4,0},{13,9},{9,5},{5,1},{14,10},{10,6},{6,2},{15,11}... | collective-permute-start | bytes 2359304 | tf_op jit(solution)/shard_map/ppermute | solution.py:76
  109.4 21.5 %collective-permute-start.11 = (f16[256,768]{1,0:T(8,128)(2,1)}, f16[256,768]{1,0:T(8,128)(2,1)S(1)}, u32[]{:S(2)}, u32[]{:S(2)}) collective-permute-start(f16[256,768]{1,0:T(8,128)(2,1)} %get-tuple-element.20), channel_id=1, source_target_pairs={{0,4},{4,8},{8,12},{1,5},{5,9},{9,13},{2,6},{6,10},{10,14},{3,7},{... | collective-permute-start | bytes 1179656 | tf_op jit(solution)/shard_map/ppermute | solution.py:75
  114.0 19.1 %collective-permute-start.14 = (f16[256,768]{1,0:T(8,128)(2,1)S(1)}, f16[256,768]{1,0:T(8,128)(2,1)}, u32[]{:S(2)}, u32[]{:S(2)}) collective-permute-start(f16[256,768]{1,0:T(8,128)(2,1)S(1)} %get-tuple-element.21), channel_id=1, source_target_pairs={{12,8},{8,4},{4,0},{13,9},{9,5},{5,1},{14,10},{10,6},{6,2},{15,11}... | collective-permute-start | bytes 1179656 | tf_op jit(solution)/shard_map/ppermute | solution.py:76
  138.7 1.1 copy-start.1
  150.0 2.2 %collective-permute-start.21 = (bf16[256,1280]{1,0:T(8,128)(2,1)S(1)}, bf16[256,1280]{1,0:T(8,128)(2,1)S(1)}, u32[]{:S(2)}, u32[]{:S(2)}) collective-permute-start(bf16[256,1280]{1,0:T(8,128)(2,1)S(1)} %get-tuple-element.8), channel_id=1, source_target_pairs={{0,1},{1,0},{2,3},{3,2},{4,5},{5,4},{6,7},{7,6},{8,9},{9,8},{10,11... | collective-permute-start | bytes 1966088 | tf_op jit(solution)/shard_map/ppermute | solution.py:193
  150.1 4.0 %collective-permute-start.23 = (bf16[256,1280]{1,0:T(8,128)(2,1)S(1)}, bf16[256,1280]{1,0:T(8,128)(2,1)S(1)}, u32[]{:S(2)}, u32[]{:S(2)}) collective-permute-start(bf16[256,1280]{1,0:T(8,128)(2,1)S(1)} %get-tuple-element.10), channel_id=1, source_target_pairs={{0,1},{1,0},{2,3},{3,2},{4,5},{5,4},{6,7},{7,6},{8,9},{9,8},{10,11... | collective-permute-start | bytes 1966088 | tf_op jit(solution)/shard_map/ppermute | solution.py:193
  152.2 10.6 %collective-permute-start.22 = (bf16[256,640]{1,0:T(8,128)(2,1)S(1)}, bf16[256,640]{1,0:T(8,128)(2,1)S(1)}, u32[]{:S(2)}, u32[]{:S(2)}) collective-permute-start(bf16[256,640]{1,0:T(8,128)(2,1)S(1)} %add_convert_fusion.3), channel_id=1, source_target_pairs={{0,2},{1,3},{2,0},{3,1},{4,6},{5,7},{6,4},{7,5},{8,10},{9,11},{10,... | collective-permute-start | bytes 983048 | tf_op jit(solution)/shard_map/ppermute | solution.py:203
  154.2 15.0 %collective-permute-start.24 = (bf16[256,640]{1,0:T(8,128)(2,1)S(1)}, bf16[256,640]{1,0:T(8,128)(2,1)S(1)}, u32[]{:S(2)}, u32[]{:S(2)}) collective-permute-start(bf16[256,640]{1,0:T(8,128)(2,1)S(1)} %add_convert_fusion.1), channel_id=1, source_target_pairs={{0,2},{1,3},{2,0},{3,1},{4,6},{5,7},{6,4},{7,5},{8,10},{9,11},{10,... | collective-permute-start | bytes 983048 | tf_op jit(solution)/shard_map/ppermute | solution.py:203
Sparse Core Ops, SparseCore 0:
  138.8 63.1 all-gather.1

commit v8 on v6

--- a/solution.py
+++ b/solution.py
@@ -19,62 +19,52 @@
     return lax.all_to_all(features, "patch", split_axis=1, concat_axis=0, tiled=True)
 
 
+def after(value, *earlier):
+    return lax.optimization_barrier((value, *earlier))[0] if earlier else value
+
+
 def spread_in_pairs(hidden):
     rank, patch = lax.axis_index("tensor"), lax.axis_index("patch")
-    half = hidden.shape[0] // 2
-    across = [(r, r ^ 2) for r in range(4)]
-    straight = hidden[:half]
-    crossing = lax.ppermute(hidden[half:], "tensor", across)
-    is_straight = patch // 2 == rank // 2
-
-    def along(block, flip, far):
-        pairs = [
-            (4 * s + r, 4 * (r ^ flip) + 2 * (r // 2) + s % 2)
-            for s in range(4)
-            for r in range(4)
-            if ((r ^ flip) // 2 != s // 2) == far
+    core, chip = rank % 2, rank // 2
+
+    def spread(slab_of, to_core, *earlier):
+        along = [(4 * slab_of(z) + z, 4 * z + 2 * (z // 2) + to_core) for z in range(4)]
+        here = lax.ppermute(after(hidden, *earlier), ("patch", "tensor"), along)
+        across = [
+            (4 * z + 2 * (z // 2) + to_core, 4 * z + 2 * (1 - z // 2) + to_core) for z in range(4)
         ]
-        return lax.ppermute(block, ("patch", "tensor"), pairs)
-
-    def both_slabs(far):
-        held = jnp.where(is_straight, along(straight, 0, far), along(crossing, 2, far))
-        other = lax.ppermute(held, "tensor", across)
-        low = jnp.where(is_straight, held, other)
-        high = jnp.where(is_straight, other, held)
-        mine = jnp.concatenate([low, high])
-        theirs = lax.ppermute(mine, "tensor", [(r, r ^ 1) for r in range(4)])
-        return jnp.concatenate([mine, theirs])
-
-    return both_slabs(True), both_slabs(False)
-
-
-def sum_in_pairs(far, near, weight):
-    patch, core = lax.axis_index("patch"), lax.axis_index("tensor") % 2
+        there = lax.ppermute(here, ("patch", "tensor"), across)
+        block = jnp.where(chip == patch // 2, here, there)
+        swap = [(4 * z + 2 * x + to_core, 4 * z + 2 * x + 1 - to_core) for z in range(4) for x in range(2)]
+        other = lax.ppermute(block, ("patch", "tensor"), swap)
+        return jnp.where(core == to_core, block, other), here
+
+    outermost, here = spread(lambda z: 3 if z < 2 else 0, 0)
+    inner, here = spread(lambda z: 2 if z < 2 else 1, 1, here)
+    mate, here = spread(lambda z: z ^ 1, 0, here)
+    own, _ = spread(lambda z: z, 1, here)
+    return outermost, inner, mate, own
+
+
+def sum_in_pairs(blocks, weight):
+    patch = lax.axis_index("patch")
+    is_end = (patch == 0) | (patch == 3)
 
     def project(features):
-        product = (jnp.dot(features, weight, preferred_element_type=F32) * LIFT).astype(F16)
-        return product.reshape(2, features.shape[0] // 2, weight.shape[1])
-
-    far, near = project(far), project(near)
-
-    def mine(slab, step):
-        slab = jnp.clip(slab, 0, 3)
-        place = (slab % 2) ^ core
-        part = lax.dynamic_index_in_dim(far, place, 0, keepdims=False)
-        if step == 3:
-            other = lax.dynamic_index_in_dim(near, place, 0, keepdims=False)
-            part = jnp.where(slab // 2 == patch // 2, other, part)
-        return part
-
-    up = down = None
-    for step in range(1, 4):
-        send_up, send_down = mine(4 - step + patch, step), mine(step - 4 + patch, step)
-        if step > 1:
-            send_up = (send_up.astype(F32) + up.astype(F32)).astype(F16)
-            send_down = (send_down.astype(F32) + down.astype(F32)).astype(F16)
-        up = lax.ppermute(send_up, "patch", [(i, i + 1) for i in range(step)])
-        down = lax.ppermute(send_down, "patch", [(3 - i, 2 - i) for i in range(step)])
-    own = lax.dynamic_index_in_dim(near, (patch % 2) ^ core, 0, keepdims=False)
+        return (jnp.dot(features, weight, preferred_element_type=F32) * LIFT).astype(F16)
+
+    def plus(part, got):
+        return (part.astype(F32) + got.astype(F32)).astype(F16)
+
+    outermost, inner, mate, own = (lax.optimization_barrier(project(block)) for block in blocks)
+    first = lax.ppermute(outermost, "patch", [(0, 1), (3, 2)])
+    second = jnp.where(is_end, inner, plus(outermost, first))
+    up = lax.ppermute(second, "patch", [(0, 1), (1, 2)])
+    down = lax.ppermute(second, "patch", [(3, 2), (2, 1)])
+    third_up = plus(jnp.where(patch == 1, inner, mate), up)
+    third_down = plus(jnp.where(patch == 2, inner, mate), down)
+    up = lax.ppermute(third_up, "patch", [(0, 1), (1, 2), (2, 3)])
+    down = lax.ppermute(third_down, "patch", [(3, 2), (2, 1), (1, 0)])
     total = own.astype(F32) + (up.astype(F32) + down.astype(F32))
     return (total * (1.0 / LIFT)).astype(BF16)
 
@@ -215,9 +205,9 @@
         own_stale = lax.dynamic_slice_in_dim(stale_kv, me * rows, rows, 1).astype(F32)
         w_both = jnp.concatenate([w_key, w_value], axis=1)
         if patches == ranks == 4:
-            far, near = spread_in_pairs(hidden_in)
-            both = sum_in_pairs(far, near, w_both)
-            query = sum_in_pairs(far, near, w_query)
+            blocks = spread_in_pairs(hidden_in)
+            both = sum_in_pairs(blocks, w_both)
+            query = sum_in_pairs(blocks, w_query)
         else:
             features = spread_features(hidden_in)
             both = sum_own_slab(features, w_both, patches)
@@ -227,7 +217,7 @@
         fresh = jnp.stack([fresh[:, :width], fresh[:, width:]])
         delta = lax.reduce_precision(fresh - own_stale, 8, 7)
         own_new = (own_stale + delta).astype(BF16)
-        refreshed = lax.all_gather(own_new, "patch", axis=1, tiled=True)
+        refreshed = lax.all_gather(after(own_new, query), "patch", axis=1, tiled=True)
         attended = attend(query, stale_kv, own_new, w_out, patches, ranks)
         return (attended, refreshed)
 

time: 253 us -> 221 us (0.87)
  the two profiles are of different devices: /device:TPU:8 before, /device:TPU:0 now
where the time goes in v8:
time: 221 us; the launch traced here: 220 us
  waiting for transfers between devices  113 us (51%)
  starting transfers between devices  49.5 us (22%)
  matrix products  17.4 us (8%)
  between operations  14.5 us (7%)
  Pallas kernels  10.1 us (5%)
  local copies, waits for them, and re-layouts  9.6 us (4%)
  other arithmetic  6.69 us (3%)
    all_gather x1, waiting for transfers between devices, shards(): lax.all_gather(after(own_new, query), 'patch', axis=1, tiled=True)  33.8 us
    ppermute x4, waiting for transfers between devices, spread(): here = lax.ppermute(after(hidden, *earlier), ('patch', 'tensor'), along)  29.6 us
    dot_general x8, matrix products, project(): jnp.dot(features, weight, preferred_element_type=F32) * LIFT  17.4 us
    ppermute x2, waiting for transfers between devices, attend(): arrived.append(lax.ppermute(summed(hop - 1).astype(BF16), 'tensor', pairs))  14.5 us
    ppermute x2, waiting for transfers between devices, sum_in_pairs(): up = lax.ppermute(third_up, 'patch', [(0, 1), (1, 2), (2, 3)])  11.7 us
    ppermute x4, starting transfers between devices, spread(): other = lax.ppermute(block, ('patch', 'tensor'), swap)  11.2 us
    ppermute x2, waiting for transfers between devices, sum_in_pairs(): up = lax.ppermute(second, 'patch', [(0, 1), (1, 2)])  10.2 us
    pallas_call x1, Pallas kernels, attend(): pl.pallas_call(functools.partial(attend_and_project, patches, heads, chip...  10.1 us
  transfers between devices with their start and end apart: 27, of which 12 were waited for; matrix products, arithmetic and copies ran while one was open for 12% of the time, Pallas kernels for 5%

profile of v8, /device:TPU:0, one launch (start us, length us, event | category | flops | bytes accessed | tf_op | source)
XLA Modules:
  0.0 220.4 jit_solution(15048575133406931674)
XLA Ops:
  7.2 1.4 collective-permute-start
  8.7 20.6 %collective-permute-done = bf16[256,1280]{1,0:T(8,128)(2,1)S(1)} collective-permute-done((bf16[256,1280]{1,0:T(8,128)(2,1)}, bf16[256,1280]{1,0:T(8,128)(2,1)S(1)}, u32[]{:S(2)}, u32[]{:S(2)}) %collective-permute-start) | collective-permute-done | bytes 655392 | tf_op jit(solution)/shard_map/ppermute | solution.py:32
  29.3 0.7 collective-permute-start.1
  30.0 3.4 %collective-permute-start.10 = (bf16[256,1280]{1,0:T(8,128)(2,1)S(1)}, bf16[256,1280]{1,0:T(8,128)(2,1)}, u32[]{:S(2)}, u32[]{:S(2)}) collective-permute-start(bf16[256,1280]{1,0:T(8,128)(2,1)S(1)} %collective-permute-done), channel_id=1, source_target_pairs={{0,2},{4,6},{10,8},{14,12},{16,18},{20,22},{26,24},{30,28}} | collective-permute-start | bytes 1966088 | tf_op jit(solution)/shard_map/ppermute | solution.py:36
  33.4 3.1 %constant_dynamic-update-slice_fusion.1 = bf16[1280,1536]{1,0:T(8,128)(2,1)} fusion(bf16[1280,768]{1,0:T(8,128)(2,1)} %param.8), kind=kLoop, calls=%fused_computation.47 | loop fusion | bytes 3932160
  36.4 1.6 collective-permute-start.6
  38.1 2.5 %collective-permute-done.10 = bf16[256,1280]{1,0:T(8,128)(2,1)} collective-permute-done((bf16[256,1280]{1,0:T(8,128)(2,1)S(1)}, bf16[256,1280]{1,0:T(8,128)(2,1)}, u32[]{:S(2)}, u32[]{:S(2)}) %collective-permute-start.10) | collective-permute-done | bytes 655392 | tf_op jit(solution)/shard_map/ppermute | solution.py:36
  40.6 0.9 broadcast_select_fusion.2
  41.5 7.3 %collective-permute-start.11 = (bf16[256,1280]{1,0:T(8,128)(2,1)}, bf16[256,1280]{1,0:T(8,128)(2,1)}, u32[]{:S(2)}, u32[]{:S(2)}) collective-permute-start(bf16[256,1280]{1,0:T(8,128)(2,1)} %broadcast_select_fusion.2), channel_id=1, source_target_pairs={{0,1},{2,3},{4,5},{6,7},{8,9},{10,11},{12,13},{14,15},{16,17},{18,... | collective-permute-start | bytes 1966088 | tf_op jit(solution)/shard_map/ppermute | solution.py:39
  48.8 1.3 collective-permute-start.2
  50.1 1.4 constant_dynamic-update-slice_fusion
  51.5 0.1 broadcast_select_fusion.4
  51.6 1.3 collective-permute-start.7
  52.9 9.0 %collective-permute-done.2 = bf16[256,1280]{1,0:T(8,128)(2,1)S(1)} collective-permute-done((bf16[256,1280]{1,0:T(8,128)(2,1)}, bf16[256,1280]{1,0:T(8,128)(2,1)S(1)}, u32[]{:S(2)}, u32[]{:S(2)}) %collective-permute-start.2) | collective-permute-done | bytes 655392 | tf_op jit(solution)/shard_map/ppermute | solution.py:32
  61.9 1.3 collective-permute-start.3
  63.3 1.8 fusion.9
  65.1 2.8 %collective-permute-start.12 = (f16[256,768]{1,0:T(8,128)(2,1)S(1)}, f16[256,768]{1,0:T(8,128)(2,1)S(1)}, u32[]{:S(2)}, u32[]{:S(2)}) collective-permute-start(f16[256,768]{1,0:T(8,128)(2,1)S(1)} %fusion.9), channel_id=1, source_target_pairs={{0,4},{12,8},{1,5},{13,9},{2,6},{14,10},{3,7},{15,11},{16,20},{28,... | collective-permute-start | bytes 1179656 | tf_op jit(solution)/shard_map/ppermute | solution.py:60
  67.8 1.3 collective-permute-start.8
  69.2 3.5 %fusion.3 = f16[256,1536]{1,0:T(8,128)(2,1)S(1)} fusion(bf16[1280,1536]{1,0:T(8,128)(2,1)} %constant_dynamic-update-slice_fusion, bf16[256,1280]{1,0:T(8,128)(2,1)} %broadcast_select_fusion.2, bf16[256,1280]{1,0:T(8,128)(2,1)} %collective-permute-done.11, pred[]{:T(512)S(6)} %eq.37), kind=kOutput, calls=%fused_computation.7 | convolution fusion | flops 1007747072 | bytes 6029313 | tf_op jit(solution)/shard_map/dot_general | solution.py:54
  72.7 1.3 collective-permute-start.17
  74.1 0.7 fusion.7
  74.8 2.3 %collective-permute-done.12 = f16[256,768]{1,0:T(8,128)(2,1)S(1)} collective-permute-done((f16[256,768]{1,0:T(8,128)(2,1)S(1)}, f16[256,768]{1,0:T(8,128)(2,1)S(1)}, u32[]{:S(2)}, u32[]{:S(2)}) %collective-permute-start.12) | collective-permute-done | bytes 393248 | tf_op jit(solution)/shard_map/ppermute | solution.py:60
  77.1 0.2 fusion.11
  77.3 4.4 %collective-permute-start.13 = (f16[256,768]{1,0:T(8,128)(2,1)S(1)}, f16[256,768]{1,0:T(8,128)(2,1)S(1)}, u32[]{:S(2)}, u32[]{:S(2)}) collective-permute-start(f16[256,768]{1,0:T(8,128)(2,1)S(1)} %fusion.11), channel_id=1, source_target_pairs={{0,4},{4,8},{1,5},{5,9},{2,6},{6,10},{3,7},{7,11},{16,20},{20,24},... | collective-permute-start | bytes 1179656 | tf_op jit(solution)/shard_map/ppermute | solution.py:62
  81.7 0.7 collective-permute-start.15
  82.4 0.7 collective-permute-start.4
  83.2 3.3 %fusion.1 = f16[256,1536]{1,0:T(8,128)(2,1)S(1)} fusion(bf16[1280,1536]{1,0:T(8,128)(2,1)} %constant_dynamic-update-slice_fusion, bf16[256,1280]{1,0:T(8,128)(2,1)S(1)} %broadcast_select_fusion.4, bf16[256,1280]{1,0:T(8,128)(2,1)S(1)} %collective-permute-done.7, pred[]{:T(512)S(6)} %eq.34), kind=kOutput, calls=%fused_computation.5 | convolution fusion | flops 1007747072 | bytes 6029313 | tf_op jit(solution)/shard_map/dot_general | solution.py:54
  86.5 1.3 collective-permute-start.9
  87.9 6.1 %collective-permute-done.17 = f16[256,1536]{1,0:T(8,128)(2,1)S(1)} collective-permute-done((f16[256,1536]{1,0:T(8,128)(2,1)S(1)}, f16[256,1536]{1,0:T(8,128)(2,1)S(1)}, u32[]{:S(2)}, u32[]{:S(2)}) %collective-permute-start.17) | collective-permute-done | bytes 786464 | tf_op jit(solution)/shard_map/ppermute | solution.py:60
  94.0 0.3 fusion.10
  94.3 4.4 %collective-permute-start.18 = (f16[256,1536]{1,0:T(8,128)(2,1)S(1)}, f16[256,1536]{1,0:T(8,128)(2,1)S(1)}, u32[]{:S(2)}, u32[]{:S(2)}) collective-permute-start(f16[256,1536]{1,0:T(8,128)(2,1)S(1)} %fusion.10), channel_id=1, source_target_pairs={{0,4},{4,8},{1,5},{5,9},{2,6},{6,10},{3,7},{7,11},{16,20},{20,24},... | collective-permute-start | bytes 2359304 | tf_op jit(solution)/shard_map/ppermute | solution.py:62
  98.8 0.7 collective-permute-start.20
  99.6 1.3 collective-permute-start.5
  100.9 0.7 fusion.8
  101.6 3.3 %fusion.2 = f16[256,1536]{1,0:T(8,128)(2,1)S(1)} fusion(bf16[1280,1536]{1,0:T(8,128)(2,1)} %constant_dynamic-update-slice_fusion, bf16[256,1280]{1,0:T(8,128)(2,1)S(1)} %broadcast_select_fusion.3, bf16[256,1280]{1,0:T(8,128)(2,1)S(1)} %collective-permute-done.9, pred[]{:T(512)S(6)} %eq.37), kind=kOutput, calls=%fused_computation.6 | convolution fusion | flops 1007747072 | bytes 6029313 | tf_op jit(solution)/shard_map/dot_general | solution.py:54
  104.9 0.4 add_convert_fusion.4
  105.3 2.5 %collective-permute-start.14 = (f16[256,768]{1,0:T(8,128)(2,1)S(1)}, f16[256,768]{1,0:T(8,128)(2,1)S(1)}, u32[]{:S(2)}, u32[]{:S(2)}) collective-permute-start(f16[256,768]{1,0:T(8,128)(2,1)S(1)} %get-tuple-element.22), channel_id=1, source_target_pairs={{0,4},{4,8},{8,12},{1,5},{5,9},{9,13},{2,6},{6,10},{10,14},{3,7},{... | collective-permute-start | bytes 1179656 | tf_op jit(solution)/shard_map/ppermute | solution.py:66
  107.8 1.3 collective-permute-start.16
  109.1 10.2 %collective-permute-done.18 = f16[256,1536]{1,0:T(8,128)(2,1)S(1)} collective-permute-done((f16[256,1536]{1,0:T(8,128)(2,1)S(1)}, f16[256,1536]{1,0:T(8,128)(2,1)S(1)}, u32[]{:S(2)}, u32[]{:S(2)}) %collective-permute-start.18) | collective-permute-done | bytes 786464 | tf_op jit(solution)/shard_map/ppermute | solution.py:62
  119.2 0.6 add_convert_fusion.1
  119.8 4.4 %collective-permute-start.19 = (f16[256,1536]{1,0:T(8,128)(2,1)S(1)}, f16[256,1536]{1,0:T(8,128)(2,1)S(1)}, u32[]{:S(2)}, u32[]{:S(2)}) collective-permute-start(f16[256,1536]{1,0:T(8,128)(2,1)S(1)} %get-tuple-element.20), channel_id=1, source_target_pairs={{0,4},{4,8},{8,12},{1,5},{5,9},{9,13},{2,6},{6,10},{10,14},{3,7},{... | collective-permute-start | bytes 2359304 | tf_op jit(solution)/shard_map/ppermute | solution.py:66
  124.3 1.5 collective-permute-start.21
  125.8 3.3 %fusion = f16[256,1536]{1,0:T(8,128)(2,1)S(1)} fusion(bf16[1280,1536]{1,0:T(8,128)(2,1)} %constant_dynamic-update-slice_fusion, bf16[256,1280]{1,0:T(8,128)(2,1)S(1)} %broadcast_select_fusion.5, bf16[256,1280]{1,0:T(8,128)(2,1)S(1)} %collective-permute-done.5, pred[]{:T(512)S(6)} %eq.34), kind=kOutput, calls=%fused_computation.4 | convolution fusion | flops 1007747072 | bytes 6029313 | tf_op jit(solution)/shard_map/dot_general | solution.py:54
  129.1 0.7 fusion.6
  129.8 0.2 multiply_convert_fusion.1.query_ref
  130.0 11.7 %collective-permute-done.19 = f16[256,1536]{1,0:T(8,128)(2,1)S(1)} collective-permute-done((f16[256,1536]{1,0:T(8,128)(2,1)S(1)}, f16[256,1536]{1,0:T(8,128)(2,1)S(1)}, u32[]{:S(2)}, u32[]{:S(2)}) %collective-permute-start.19) | collective-permute-done | bytes 786464 | tf_op jit(solution)/shard_map/ppermute | solution.py:66
  141.7 0.4 convert_reduce-precision_fusion
  142.1 0.1 slice_bitcast_fusion.1
  142.2 2.3 %fusion.5.fresh_ref = bf16[2,256,768]{2,1,0:T(8,128)(2,1)} fusion(f32[1,256,768]{2,1,0:T(8,128)S(1)} %get-tuple-element.19, f32[1,256,768]{2,1,0:T(8,128)S(1)} %get-tuple-element.18, bf16[2,1024,768]{2,1,0:T(8,128)(2,1)} %stale_ref.1, s32[]{:T(128)S(6)} %select_n.128), kind=kLoop, calls=%fused_computation.11 | loop fusion | flops 2359296 | bytes 3145732 | tf_op jit(solution)/shard_map/convert_element_type | solution.py:219
  144.5 0.1 stack.32.place_ref
  144.6 1.1 copy-done.1
  145.8 10.1 %shard_map.77 = (bf16[256,1280]{1,0:T(8,128)(2,1)S(1)}, bf16[256,1280]{1,0:T(8,128)(2,1)S(1)}, f32[256,1280]{1,0:T(8,128)S(1)}, f32[256,1280]{1,0:T(8,128)S(1)}) custom-call(s32[5]{0:T(128)S(1)} %stack.32.place_ref, bf16[256,768]{1,0:T(8,128)(2,1)S(1)} %multiply_convert_fusion.1.query_ref, bf16[2,1024,768]{2,1,0:T(8,128)(2,1)} %stale_ref.1, ...), custom_call_target="tpu_custom_call" | custom-call | flops 2818572288 | bytes 14942208 | tf_op jit(solution)/shard_map/pallas_call | solution.py:159
  156.0 0.5 collective-permute-start.24
  156.5 1.6 collective-permute-done.22
  158.1 0.6 collective-permute-start.23
  158.8 0.2 collective-permute-done.24
  159.1 1.3 collective-permute-start.25
  160.3 8.4 %collective-permute-done.23 = bf16[256,640]{1,0:T(8,128)(2,1)S(1)} collective-permute-done((bf16[256,640]{1,0:T(8,128)(2,1)S(1)}, bf16[256,640]{1,0:T(8,128)(2,1)S(1)}, u32[]{:S(2)}, u32[]{:S(2)}) %collective-permute-start.23) | collective-permute-done | bytes 327712 | tf_op jit(solution)/shard_map/ppermute | solution.py:193
  168.7 0.1 add_convert_fusion.8
  168.8 6.1 %collective-permute-done.25 = bf16[256,640]{1,0:T(8,128)(2,1)S(1)} collective-permute-done((bf16[256,640]{1,0:T(8,128)(2,1)S(1)}, bf16[256,640]{1,0:T(8,128)(2,1)S(1)}, u32[]{:S(2)}, u32[]{:S(2)}) %collective-permute-start.25) | collective-permute-done | bytes 327712 | tf_op jit(solution)/shard_map/ppermute | solution.py:193
  175.0 0.1 add_convert_fusion.6
  175.1 0.9 pad_maximum_fusion
  175.9 33.8 %all-gather.2.cloned.1.call-done = bf16[2,1024,768]{2,1,0:T(8,128)(2,1)} async-done(((bf16[2,256,768]{2,1,0:T(8,128)(2,1)}), bf16[2,1024,768]{2,1,0:T(8,128)(2,1)}) %all-gather.2.cloned.1.call-update) | async-done | bytes 3145744 | tf_op jit(solution)/shard_map/all_gather | solution.py:220
  209.8 3.8 %copy.10 = bf16[2,1024,768]{2,1,0:T(8,128)(2,1)} copy(bf16[2,1024,768]{2,1,0:T(8,128)(2,1)} %all-gather.2.cloned.1.call-done) | data formatting | bytes 6291456
  (27 shorter events, 0.4 us)
Async XLA Ops:
  7.2 56.1 %copy-start = (bf16[1280,768]{1,0:T(8,128)(2,1)S(1)}, bf16[1280,768]{1,0:T(8,128)(2,1)}, u32[]{:S(2)}) copy-start(bf16[1280,768]{1,0:T(8,128)(2,1)} %param.7) | copy-start | bytes 5898244
  7.2 202.6 %all-gather.2.cloned.1.call-start = ((), (), s32[]{:S(2)}) async-start(), calls=%async_computation | async-start | bytes 3932160 | tf_op jit(solution)/shard_map/all_gather | solution.py:220
  7.2 22.1 %collective-permute-start = (bf16[256,1280]{1,0:T(8,128)(2,1)}, bf16[256,1280]{1,0:T(8,128)(2,1)S(1)}, u32[]{:S(2)}, u32[]{:S(2)}) collective-permute-start(bf16[256,1280]{1,0:T(8,128)(2,1)} %param.6), channel_id=1, source_target_pairs={{12,0},{13,4},{2,10},{3,14},{28,16},{29,20},{18,26},{19,30}} | collective-permute-start | bytes 1966088 | tf_op jit(solution)/shard_map/ppermute | solution.py:32
  29.3 7.2 %collective-permute-start.1 = (bf16[256,1280]{1,0:T(8,128)(2,1)}, bf16[256,1280]{1,0:T(8,128)(2,1)S(1)}, u32[]{:S(2)}, u32[]{:S(2)}) collective-permute-start(bf16[256,1280]{1,0:T(8,128)(2,1)} %param.6), channel_id=1, source_target_pairs={{8,1},{9,5},{6,11},{7,15},{24,17},{25,21},{22,27},{23,31}} | collective-permute-start | bytes 1966088 | tf_op jit(solution)/shard_map/ppermute | solution.py:32
  30.0 10.6 %collective-permute-start.10 = (bf16[256,1280]{1,0:T(8,128)(2,1)S(1)}, bf16[256,1280]{1,0:T(8,128)(2,1)}, u32[]{:S(2)}, u32[]{:S(2)}) collective-permute-start(bf16[256,1280]{1,0:T(8,128)(2,1)S(1)} %collective-permute-done), channel_id=1, source_target_pairs={{0,2},{4,6},{10,8},{14,12},{16,18},{20,22},{26,24},{30,28}} | collective-permute-start | bytes 1966088 | tf_op jit(solution)/shard_map/ppermute | solution.py:36
  36.4 13.6 %copy-start.2 = (bf16[1280,768]{1,0:T(8,128)(2,1)S(1)}, bf16[1280,768]{1,0:T(8,128)(2,1)}, u32[]{:S(2)}) copy-start(bf16[1280,768]{1,0:T(8,128)(2,1)} %param.9) | copy-start | bytes 5898244
  36.4 15.1 %collective-permute-start.6 = (bf16[256,1280]{1,0:T(8,128)(2,1)S(1)}, bf16[256,1280]{1,0:T(8,128)(2,1)}, u32[]{:S(2)}, u32[]{:S(2)}) collective-permute-start(bf16[256,1280]{1,0:T(8,128)(2,1)S(1)} %collective-permute-done.1), channel_id=1, source_target_pairs={{1,3},{5,7},{11,9},{15,13},{17,19},{21,23},{27,25},{31,29}} | collective-permute-start | bytes 1966088 | tf_op jit(solution)/shard_map/ppermute | solution.py:36
  41.5 21.7 %collective-permute-start.11 = (bf16[256,1280]{1,0:T(8,128)(2,1)}, bf16[256,1280]{1,0:T(8,128)(2,1)}, u32[]{:S(2)}, u32[]{:S(2)}) collective-permute-start(bf16[256,1280]{1,0:T(8,128)(2,1)} %broadcast_select_fusion.2), channel_id=1, source_target_pairs={{0,1},{2,3},{4,5},{6,7},{8,9},{10,11},{12,13},{14,15},{16,17},{18,... | collective-permute-start | bytes 1966088 | tf_op jit(solution)/shard_map/ppermute | solution.py:39
  48.8 13.1 %collective-permute-start.2 = (bf16[256,1280]{1,0:T(8,128)(2,1)}, bf16[256,1280]{1,0:T(8,128)(2,1)S(1)}, u32[]{:S(2)}, u32[]{:S(2)}) collective-permute-start(bf16[256,1280]{1,0:T(8,128)(2,1)} %param.6), channel_id=1, source_target_pairs={{4,0},{1,4},{14,10},{11,14},{20,16},{17,20},{30,26},{27,30}} | collective-permute-start | bytes 1966088 | tf_op jit(solution)/shard_map/ppermute | solution.py:32
  51.6 22.4 %collective-permute-start.7 = (bf16[256,1280]{1,0:T(8,128)(2,1)S(1)}, bf16[256,1280]{1,0:T(8,128)(2,1)S(1)}, u32[]{:S(2)}, u32[]{:S(2)}) collective-permute-start(bf16[256,1280]{1,0:T(8,128)(2,1)S(1)} %broadcast_select_fusion.4), channel_id=1, source_target_pairs={{1,0},{3,2},{5,4},{7,6},{9,8},{11,10},{13,12},{15,14},{17,16},{19,... | collective-permute-start | bytes 1966088 | tf_op jit(solution)/shard_map/ppermute | solution.py:39
  61.9 20.5 %collective-permute-start.3 = (bf16[256,1280]{1,0:T(8,128)(2,1)}, bf16[256,1280]{1,0:T(8,128)(2,1)S(1)}, u32[]{:S(2)}, u32[]{:S(2)}) collective-permute-start(bf16[256,1280]{1,0:T(8,128)(2,1)} %param.6), channel_id=1, source_target_pairs={{0,1},{5,5},{10,11},{15,15},{16,17},{21,21},{26,27},{31,31}} | collective-permute-start | bytes 1966088 | tf_op jit(solution)/shard_map/ppermute | solution.py:32
  65.1 12.0 %collective-permute-start.12 = (f16[256,768]{1,0:T(8,128)(2,1)S(1)}, f16[256,768]{1,0:T(8,128)(2,1)S(1)}, u32[]{:S(2)}, u32[]{:S(2)}) collective-permute-start(f16[256,768]{1,0:T(8,128)(2,1)S(1)} %fusion.9), channel_id=1, source_target_pairs={{0,4},{12,8},{1,5},{13,9},{2,6},{14,10},{3,7},{15,11},{16,20},{28,... | collective-permute-start | bytes 1179656 | tf_op jit(solution)/shard_map/ppermute | solution.py:60
  67.8 15.3 %collective-permute-start.8 = (bf16[256,1280]{1,0:T(8,128)(2,1)S(1)}, bf16[256,1280]{1,0:T(8,128)(2,1)S(1)}, u32[]{:S(2)}, u32[]{:S(2)}) collective-permute-start(bf16[256,1280]{1,0:T(8,128)(2,1)S(1)} %collective-permute-done.2), channel_id=1, source_target_pairs={{0,2},{4,6},{10,8},{14,12},{16,18},{20,22},{26,24},{30,28}} | collective-permute-start | bytes 1966088 | tf_op jit(solution)/shard_map/ppermute | solution.py:36
  72.7 21.3 %collective-permute-start.17 = (f16[256,1536]{1,0:T(8,128)(2,1)S(1)}, f16[256,1536]{1,0:T(8,128)(2,1)S(1)}, u32[]{:S(2)}, u32[]{:S(2)}) collective-permute-start(f16[256,1536]{1,0:T(8,128)(2,1)S(1)} %fusion.3), channel_id=1, source_target_pairs={{0,4},{12,8},{1,5},{13,9},{2,6},{14,10},{3,7},{15,11},{16,20},{28,... | collective-permute-start | bytes 2359304 | tf_op jit(solution)/shard_map/ppermute | solution.py:60
  77.3 27.6 %collective-permute-start.13 = (f16[256,768]{1,0:T(8,128)(2,1)S(1)}, f16[256,768]{1,0:T(8,128)(2,1)S(1)}, u32[]{:S(2)}, u32[]{:S(2)}) collective-permute-start(f16[256,768]{1,0:T(8,128)(2,1)S(1)} %fusion.11), channel_id=1, source_target_pairs={{0,4},{4,8},{1,5},{5,9},{2,6},{6,10},{3,7},{7,11},{16,20},{20,24},... | collective-permute-start | bytes 1179656 | tf_op jit(solution)/shard_map/ppermute | solution.py:62
  81.7 23.2 %collective-permute-start.15 = (f16[256,768]{1,0:T(8,128)(2,1)S(1)}, f16[256,768]{1,0:T(8,128)(2,1)S(1)}, u32[]{:S(2)}, u32[]{:S(2)}) collective-permute-start(f16[256,768]{1,0:T(8,128)(2,1)S(1)} %fusion.11), channel_id=1, source_target_pairs={{12,8},{8,4},{13,9},{9,5},{14,10},{10,6},{15,11},{11,7},{28,24},{2... | collective-permute-start | bytes 1179656 | tf_op jit(solution)/shard_map/ppermute | solution.py:63
  82.4 16.3 %collective-permute-start.4 = (bf16[256,1280]{1,0:T(8,128)(2,1)S(1)}, bf16[256,1280]{1,0:T(8,128)(2,1)S(1)}, u32[]{:S(2)}, u32[]{:S(2)}) collective-permute-start(bf16[256,1280]{1,0:T(8,128)(2,1)S(1)} %collective-permute-done.3), channel_id=1, source_target_pairs={{1,3},{5,7},{11,9},{15,13},{17,19},{21,23},{27,25},{31,29}} | collective-permute-start | bytes 1966088 | tf_op jit(solution)/shard_map/ppermute | solution.py:36
  86.5 13.0 %collective-permute-start.9 = (bf16[256,1280]{1,0:T(8,128)(2,1)S(1)}, bf16[256,1280]{1,0:T(8,128)(2,1)S(1)}, u32[]{:S(2)}, u32[]{:S(2)}) collective-permute-start(bf16[256,1280]{1,0:T(8,128)(2,1)S(1)} %broadcast_select_fusion.3), channel_id=1, source_target_pairs={{0,1},{2,3},{4,5},{6,7},{8,9},{10,11},{12,13},{14,15},{16,17},{18,... | collective-permute-start | bytes 1966088 | tf_op jit(solution)/shard_map/ppermute | solution.py:39
  94.3 24.9 %collective-permute-start.18 = (f16[256,1536]{1,0:T(8,128)(2,1)S(1)}, f16[256,1536]{1,0:T(8,128)(2,1)S(1)}, u32[]{:S(2)}, u32[]{:S(2)}) collective-permute-start(f16[256,1536]{1,0:T(8,128)(2,1)S(1)} %fusion.10), channel_id=1, source_target_pairs={{0,4},{4,8},{1,5},{5,9},{2,6},{6,10},{3,7},{7,11},{16,20},{20,24},... | collective-permute-start | bytes 2359304 | tf_op jit(solution)/shard_map/ppermute | solution.py:62
  98.8 20.5 %collective-permute-start.20 = (f16[256,1536]{1,0:T(8,128)(2,1)S(1)}, f16[256,1536]{1,0:T(8,128)(2,1)S(1)}, u32[]{:S(2)}, u32[]{:S(2)}) collective-permute-start(f16[256,1536]{1,0:T(8,128)(2,1)S(1)} %fusion.10), channel_id=1, source_target_pairs={{12,8},{8,4},{13,9},{9,5},{14,10},{10,6},{15,11},{11,7},{28,24},{2... | collective-permute-start | bytes 2359304 | tf_op jit(solution)/shard_map/ppermute | solution.py:63
  99.6 26.2 %collective-permute-start.5 = (bf16[256,1280]{1,0:T(8,128)(2,1)S(1)}, bf16[256,1280]{1,0:T(8,128)(2,1)S(1)}, u32[]{:S(2)}, u32[]{:S(2)}) collective-permute-start(bf16[256,1280]{1,0:T(8,128)(2,1)S(1)} %broadcast_select_fusion.5), channel_id=1, source_target_pairs={{1,0},{3,2},{5,4},{7,6},{9,8},{11,10},{13,12},{15,14},{17,16},{19,... | collective-permute-start | bytes 1966088 | tf_op jit(solution)/shard_map/ppermute | solution.py:39
  105.3 24.5 %collective-permute-start.14 = (f16[256,768]{1,0:T(8,128)(2,1)S(1)}, f16[256,768]{1,0:T(8,128)(2,1)S(1)}, u32[]{:S(2)}, u32[]{:S(2)}) collective-permute-start(f16[256,768]{1,0:T(8,128)(2,1)S(1)} %get-tuple-element.22), channel_id=1, source_target_pairs={{0,4},{4,8},{8,12},{1,5},{5,9},{9,13},{2,6},{6,10},{10,14},{3,7},{... | collective-permute-start | bytes 1179656 | tf_op jit(solution)/shard_map/ppermute | solution.py:66
  107.8 22.0 %collective-permute-start.16 = (f16[256,768]{1,0:T(8,128)(2,1)S(1)}, f16[256,768]{1,0:T(8,128)(2,1)S(1)}, u32[]{:S(2)}, u32[]{:S(2)}) collective-permute-start(f16[256,768]{1,0:T(8,128)(2,1)S(1)} %get-tuple-element.23), channel_id=1, source_target_pairs={{12,8},{8,4},{4,0},{13,9},{9,5},{5,1},{14,10},{10,6},{6,2},{15,11}... | collective-permute-start | bytes 1179656 | tf_op jit(solution)/shard_map/ppermute | solution.py:67
  119.8 21.9 %collective-permute-start.19 = (f16[256,1536]{1,0:T(8,128)(2,1)S(1)}, f16[256,1536]{1,0:T(8,128)(2,1)S(1)}, u32[]{:S(2)}, u32[]{:S(2)}) collective-permute-start(f16[256,1536]{1,0:T(8,128)(2,1)S(1)} %get-tuple-element.20), channel_id=1, source_target_pairs={{0,4},{4,8},{8,12},{1,5},{5,9},{9,13},{2,6},{6,10},{10,14},{3,7},{... | collective-permute-start | bytes 2359304 | tf_op jit(solution)/shard_map/ppermute | solution.py:66
  124.3 17.5 %collective-permute-start.21 = (f16[256,1536]{1,0:T(8,128)(2,1)S(1)}, f16[256,1536]{1,0:T(8,128)(2,1)S(1)}, u32[]{:S(2)}, u32[]{:S(2)}) collective-permute-start(f16[256,1536]{1,0:T(8,128)(2,1)S(1)} %get-tuple-element.21), channel_id=1, source_target_pairs={{12,8},{8,4},{4,0},{13,9},{9,5},{5,1},{14,10},{10,6},{6,2},{15,11}... | collective-permute-start | bytes 2359304 | tf_op jit(solution)/shard_map/ppermute | solution.py:67
  144.6 1.1 copy-start.1
  155.9 2.2 collective-permute-start.22
  156.0 3.0 %collective-permute-start.24 = (bf16[256,1280]{1,0:T(8,128)(2,1)S(1)}, bf16[256,1280]{1,0:T(8,128)(2,1)S(1)}, u32[]{:S(2)}, u32[]{:S(2)}) collective-permute-start(bf16[256,1280]{1,0:T(8,128)(2,1)S(1)} %get-tuple-element.16), channel_id=1, source_target_pairs={{0,1},{1,0},{2,3},{3,2},{4,5},{5,4},{6,7},{7,6},{8,9},{9,8},{10,11... | collective-permute-start | bytes 1966088 | tf_op jit(solution)/shard_map/ppermute | solution.py:183
  158.1 10.6 %collective-permute-start.23 = (bf16[256,640]{1,0:T(8,128)(2,1)S(1)}, bf16[256,640]{1,0:T(8,128)(2,1)S(1)}, u32[]{:S(2)}, u32[]{:S(2)}) collective-permute-start(bf16[256,640]{1,0:T(8,128)(2,1)S(1)} %add_convert_fusion.9), channel_id=1, source_target_pairs={{0,2},{1,3},{2,0},{3,1},{4,6},{5,7},{6,4},{7,5},{8,10},{9,11},{10,... | collective-permute-start | bytes 983048 | tf_op jit(solution)/shard_map/ppermute | solution.py:193
  159.1 15.9 %collective-permute-start.25 = (bf16[256,640]{1,0:T(8,128)(2,1)S(1)}, bf16[256,640]{1,0:T(8,128)(2,1)S(1)}, u32[]{:S(2)}, u32[]{:S(2)}) collective-permute-start(bf16[256,640]{1,0:T(8,128)(2,1)S(1)} %add_convert_fusion.7), channel_id=1, source_target_pairs={{0,2},{1,3},{2,0},{3,1},{4,6},{5,7},{6,4},{7,5},{8,10},{9,11},{10,... | collective-permute-start | bytes 983048 | tf_op jit(solution)/shard_map/ppermute | solution.py:193
Sparse Core Ops, SparseCore 0:
  144.6 65.0 all-gather.1

commit v9 on v6

--- a/solution.py
+++ b/solution.py
@@ -17,6 +17,10 @@
 def spread_features(hidden):
     features = lax.all_gather(hidden, "tensor", axis=1, tiled=True)
     return lax.all_to_all(features, "patch", split_axis=1, concat_axis=0, tiled=True)
+
+
+def after(value, *earlier):
+    return lax.optimization_barrier((value, *earlier))[0] if earlier else value
 
 
 def spread_in_pairs(hidden):
@@ -50,33 +54,53 @@
 
 def sum_in_pairs(far, near, weight):
     patch, core = lax.axis_index("patch"), lax.axis_index("tensor") % 2
+    is_end = (patch == 0) | (patch == 3)
 
     def project(features):
         product = (jnp.dot(features, weight, preferred_element_type=F32) * LIFT).astype(F16)
         return product.reshape(2, features.shape[0] // 2, weight.shape[1])
 
-    far, near = project(far), project(near)
-
-    def mine(slab, step):
-        slab = jnp.clip(slab, 0, 3)
-        place = (slab % 2) ^ core
-        part = lax.dynamic_index_in_dim(far, place, 0, keepdims=False)
-        if step == 3:
-            other = lax.dynamic_index_in_dim(near, place, 0, keepdims=False)
-            part = jnp.where(slab // 2 == patch // 2, other, part)
-        return part
-
-    up = down = None
-    for step in range(1, 4):
-        send_up, send_down = mine(4 - step + patch, step), mine(step - 4 + patch, step)
-        if step > 1:
-            send_up = (send_up.astype(F32) + up.astype(F32)).astype(F16)
-            send_down = (send_down.astype(F32) + down.astype(F32)).astype(F16)
-        up = lax.ppermute(send_up, "patch", [(i, i + 1) for i in range(step)])
-        down = lax.ppermute(send_down, "patch", [(3 - i, 2 - i) for i in range(step)])
-    own = lax.dynamic_index_in_dim(near, (patch % 2) ^ core, 0, keepdims=False)
+    def slab(pair, odd):
+        return lax.dynamic_index_in_dim(pair, odd ^ core, 0, keepdims=False)
+
+    def plus(part, got):
+        return (part.astype(F32) + got.astype(F32)).astype(F16)
+
+    far, near = project(far), lax.optimization_barrier(project(near))
+    outermost, inner = slab(far, 1 - patch // 2), slab(far, patch // 2)
+    own, mate = slab(near, patch % 2), slab(near, 1 - patch % 2)
+    first = lax.ppermute(outermost, "patch", [(0, 1), (3, 2)])
+    second = jnp.where(is_end, inner, plus(outermost, first))
+    up = lax.ppermute(second, "patch", [(0, 1), (1, 2)])
+    down = lax.ppermute(second, "patch", [(3, 2), (2, 1)])
+    third_up = plus(jnp.where(patch == 1, inner, mate), up)
+    third_down = plus(jnp.where(patch == 2, inner, mate), down)
+    up = lax.ppermute(third_up, "patch", [(0, 1), (1, 2), (2, 3)])
+    down = lax.ppermute(third_down, "patch", [(3, 2), (2, 1), (1, 0)])
     total = own.astype(F32) + (up.astype(F32) + down.astype(F32))
     return (total * (1.0 / LIFT)).astype(BF16)
+
+
+class PairGather:
+    def __init__(self, own):
+        self.own = own
+        self.mate = lax.ppermute(own, "patch", [(0, 1), (1, 0), (2, 3), (3, 2)])
+        self.across = lax.ppermute(own, "patch", [(1, 2), (2, 1)])
+
+    def into(self, whole, index, *earlier):
+        patch = lax.axis_index("patch")
+        rows = self.own.shape[0]
+        is_inner = (patch == 1) | (patch == 2)
+        outward = [(1, 0), (2, 3)]
+        across_mate = lax.ppermute(self.mate, "patch", [(1, 2), (2, 1)])
+        far_inner = jnp.where(is_inner, self.across, lax.ppermute(self.across, "patch", outward))
+        last = lax.ppermute(after(across_mate, *earlier), "patch", outward)
+        far_outer = jnp.where(is_inner, across_mate, last)
+        low = patch < 2
+        slabs = (patch, patch ^ 1, jnp.where(low, 2, 1), jnp.where(low, 3, 0))
+        for slab, block in zip(slabs, (self.own, self.mate, far_inner, far_outer)):
+            whole = lax.dynamic_update_slice(whole, block[None], (index, slab * rows, 0))
+        return whole
 
 
 def sum_own_slab(features, weight, patches):
@@ -105,7 +129,7 @@
     return (total * (1.0 / LIFT)).astype(BF16)
 
 
-def attend_and_project(patches, heads, chips, chunks, place_ref, query_ref, stale_ref, fresh_ref, w_ref, *out_refs):
+def attend_and_project(patches, heads, chips, chunks, place_ref, query_ref, stale_ref, key_ref, value_ref, w_ref, *out_refs):
     *out_refs, sums = out_refs
     send_refs, keep_refs = out_refs[:chunks], out_refs[chunks:]
     me = place_ref[0]
@@ -118,8 +142,8 @@
     for h in range(heads):
         columns = slice(h * HEAD_DIM, (h + 1) * HEAD_DIM)
         query = query_ref[:, columns]
-        keys = [fresh_ref[0, :, columns]] + [stale_ref[0, pl.ds(start, rows), columns] for start in starts]
-        values = [fresh_ref[1, :, columns]] + [stale_ref[1, pl.ds(start, rows), columns] for start in starts]
+        keys = [key_ref[:, columns]] + [stale_ref[0, pl.ds(start, rows), columns] for start in starts]
+        values = [value_ref[:, columns]] + [stale_ref[1, pl.ds(start, rows), columns] for start in starts]
         scores = [lax.dot_general(query, key, dims, preferred_element_type=F32) * scale for key in keys]
         top = functools.reduce(jnp.maximum, [jnp.max(s, axis=-1, keepdims=True) for s in scores])
         total = mixed = None
@@ -153,7 +177,7 @@
                 keep_refs[c][:, there] = sums[:, pl.ds(ours, part)]
 
 
-def attend(query, stale_kv, fresh_kv, w_out, patches, ranks):
+def attend(query, stale_kv, key_new, value_new, w_out, patches, ranks):
     rows, depth = query.shape
     tokens, model = stale_kv.shape[1], w_out.shape[1]
     rank = lax.axis_index("tensor").astype(jnp.int32)
@@ -176,7 +200,8 @@
             in_specs=[
                 pl.BlockSpec((rows, block), lambda h, p: (0, h)),
                 pl.BlockSpec((2, tokens, block), lambda h, p: (0, 0, h)),
-                pl.BlockSpec((2, rows, block), lambda h, p: (0, 0, h)),
+                pl.BlockSpec((rows, block), lambda h, p: (0, h)),
+                pl.BlockSpec((rows, block), lambda h, p: (0, h)),
                 pl.BlockSpec((block, model), lambda h, p: (h, 0)),
             ],
             out_specs=[pl.BlockSpec((rows, chips * part), lambda h, p: (0, 0))] * (2 * chunks),
@@ -188,10 +213,10 @@
             bytes_accessed=4 * tokens * depth + 2 * depth * model + 6 * rows * chips * width,
             transcendentals=rows * tokens * (depth // HEAD_DIM),
         ),
-    )(place, query, stale_kv, fresh_kv, w_out)
+    )(place, query, stale_kv, key_new, value_new, w_out)
     across = [(r, r ^ 1) for r in range(ranks)]
     got = [lax.ppermute(send, "tensor", across) for send in results[:chunks]]
-    pieces = []
+    pieces, sends = [], []
     for mine, theirs in zip(results[chunks:], got):
 
         def summed(j):
@@ -200,21 +225,23 @@
         arrived = []
         for hop in range(1, chips):
             pairs = [(r, (r + 2 * hop) % ranks) for r in range(ranks)]
-            arrived.append(lax.ppermute(summed(hop - 1).astype(BF16), "tensor", pairs))
+            sends.append(summed(hop - 1).astype(BF16))
+            arrived.append(lax.ppermute(sends[-1], "tensor", pairs))
         total = summed(chips - 1)
         for piece in arrived:
             total = total + piece.astype(F32)
         pieces.append(total.astype(BF16))
-    return jnp.concatenate(pieces, axis=1)
+    return jnp.concatenate(pieces, axis=1), sends
 
 
 def make_shards(patches, ranks):
     def shards(hidden_in, w_query, w_key, w_value, w_out, stale_kv):
         rows = hidden_in.shape[0]
         me = lax.axis_index("patch")
-        own_stale = lax.dynamic_slice_in_dim(stale_kv, me * rows, rows, 1).astype(F32)
+        own_stale = lax.dynamic_slice_in_dim(stale_kv, me * rows, rows, 1)
+        in_pairs = patches == ranks == 4
         w_both = jnp.concatenate([w_key, w_value], axis=1)
-        if patches == ranks == 4:
+        if in_pairs:
             far, near = spread_in_pairs(hidden_in)
             both = sum_in_pairs(far, near, w_both)
             query = sum_in_pairs(far, near, w_query)
@@ -222,13 +249,24 @@
             features = spread_features(hidden_in)
             both = sum_own_slab(features, w_both, patches)
             query = sum_own_slab(features, w_query, patches)
+
+        def refresh(fresh, stale):
+            fresh = lax.reduce_precision(fresh.astype(F32), 8, 7)
+            stale = stale.astype(F32)
+            return (stale + lax.reduce_precision(fresh - stale, 8, 7)).astype(BF16)
+
         width = w_key.shape[1]
-        fresh = lax.reduce_precision(both.astype(F32), 8, 7)
-        fresh = jnp.stack([fresh[:, :width], fresh[:, width:]])
-        delta = lax.reduce_precision(fresh - own_stale, 8, 7)
-        own_new = (own_stale + delta).astype(BF16)
-        refreshed = lax.all_gather(own_new, "patch", axis=1, tiled=True)
-        attended = attend(query, stale_kv, own_new, w_out, patches, ranks)
+        key_new = refresh(both[:, :width], own_stale[0])
+        value_new = refresh(both[:, width:], own_stale[1])
+        if in_pairs:
+            keys, values = PairGather(after(key_new, query)), PairGather(after(value_new, query))
+            query = after(query, keys.mate, keys.across)
+        attended, sent = attend(query, stale_kv, key_new, value_new, w_out, patches, ranks)
+        if in_pairs:
+            refreshed = keys.into(jnp.zeros_like(stale_kv), 0, *sent)
+            refreshed = values.into(refreshed, 1, *sent)
+        else:
+            refreshed = lax.all_gather(jnp.stack([key_new, value_new]), "patch", axis=1, tiled=True)
         return (attended, refreshed)
 
     return shards

time: 253 us -> 208 us (0.82)
  the two profiles are of different devices: /device:TPU:8 before, /device:TPU:0 now
where the time goes in v9:
time: 208 us
  waiting for transfers between devices  96.3 us (46%)
  starting transfers between devices  69.9 us (34%)
  local copies, waits for them, and re-layouts  12.6 us (6%)
  Pallas kernels  10.9 us (5%)
  other arithmetic  9.9 us (5%)
  matrix products  6.77 us (3%)
    ppermute x2, waiting for transfers between devices, sum_in_pairs(): down = lax.ppermute(third_down, 'patch', [(3, 2), (2, 1), (1, 0)])  14.8 us
    ppermute x2, waiting for transfers between devices, sum_in_pairs(): first = lax.ppermute(outermost, 'patch', [(0, 1), (3, 2)])  14.6 us
    ppermute x2, waiting for transfers between devices, __init__(): self.mate = lax.ppermute(own, 'patch', [(0, 1), (1, 0), (2, 3), (3, 2)])  13.3 us
    ppermute x2, waiting for transfers between devices, into(): last = lax.ppermute(after(across_mate, *earlier), 'patch', outward)  12.5 us
    ppermute x2, starting transfers between devices, sum_in_pairs(): up = lax.ppermute(third_up, 'patch', [(0, 1), (1, 2), (2, 3)])  11.6 us
    ppermute x2, waiting for transfers between devices, sum_in_pairs(): up = lax.ppermute(second, 'patch', [(0, 1), (1, 2)])  11.6 us
    ppermute x2, waiting for transfers between devices, both_slabs(): other = lax.ppermute(held, 'tensor', across)  11.2 us
    pallas_call x1, Pallas kernels, attend(): pl.pallas_call(functools.partial(attend_and_project, patches, heads, chip...  10.9 us
  transfers between devices with their start and end apart: 33, of which 17 were waited for; matrix products, arithmetic and copies ran while one was open for 10% of the time, Pallas kernels for 0%

profile of v9, /device:TPU:0, one launch (start us, length us, event | category | flops | bytes accessed | tf_op | source)
XLA Modules:
  0.0 207.6 jit_solution(4923383703044437682)
XLA Ops:
  0.6 1.3 fusion.16
  1.9 3.0 %collective-permute-start.1 = (bf16[128,1280]{1,0:T(8,128)(2,1)S(1)}, bf16[128,1280]{1,0:T(8,128)(2,1)}, u32[]{:S(2)}, u32[]{:S(2)}) collective-permute-start(bf16[128,1280]{1,0:T(8,128)(2,1)S(1)} %get-tuple-element.30), channel_id=1, source_target_pairs={{0,2},{1,3},{2,0},{3,1},{4,6},{5,7},{6,4},{7,5},{8,10},{9,11},{10,... | collective-permute-start | bytes 983048 | tf_op jit(solution)/shard_map/ppermute | solution.py:31
  4.9 1.3 collective-permute-start.5
  6.2 0.7 collective-permute-start
  6.9 5.8 %collective-permute-done.1 = bf16[128,1280]{1,0:T(8,128)(2,1)} collective-permute-done((bf16[128,1280]{1,0:T(8,128)(2,1)S(1)}, bf16[128,1280]{1,0:T(8,128)(2,1)}, u32[]{:S(2)}, u32[]{:S(2)}) %collective-permute-start.1) | collective-permute-done | bytes 327712 | tf_op jit(solution)/shard_map/ppermute | solution.py:31
  12.7 4.7 %collective-permute-start.6 = (bf16[128,1280]{1,0:T(8,128)(2,1)}, bf16[128,1280]{1,0:T(8,128)(2,1)S(1)}, u32[]{:S(2)}, u32[]{:S(2)}) collective-permute-start(bf16[128,1280]{1,0:T(8,128)(2,1)} %collective-permute-done.1), channel_id=1, source_target_pairs={{0,8},{1,12},{4,9},{5,13},{10,2},{11,6},{14,3},{15,7},{16,24},{17,... | collective-permute-start | bytes 983048 | tf_op jit(solution)/shard_map/ppermute | solution.py:41
  17.5 3.0 %constant_dynamic-update-slice_fusion.1 = bf16[1280,1536]{1,0:T(8,128)(2,1)} fusion(bf16[1280,768]{1,0:T(8,128)(2,1)} %param.8), kind=kLoop, calls=%fused_computation.60 | loop fusion | bytes 3932160
  20.5 3.0 %constant_dynamic-update-slice_fusion = bf16[1280,1536]{1,0:T(8,128)(2,1)} fusion(bf16[1280,1536]{1,0:T(8,128)(2,1)} %constant_dynamic-update-slice_fusion.1, bf16[1280,768]{1,0:T(8,128)(2,1)} %param.9), kind=kLoop, calls=%fused_computation.59 | loop fusion | bytes 3932160 | tf_op jit(solution)/shard_map/concatenate | solution.py:243
  23.5 0.7 collective-permute-start.2
  24.2 0.6 collective-permute-done.5
  24.8 0.7 collective-permute-done.6
  25.6 8.6 %collective-permute-start.7 = (bf16[128,1280]{1,0:T(8,128)(2,1)S(1)}, bf16[128,1280]{1,0:T(8,128)(2,1)S(1)}, u32[]{:S(2)}, u32[]{:S(2)}) collective-permute-start(bf16[128,1280]{1,0:T(8,128)(2,1)S(1)} %broadcast_select_fusion.2), channel_id=1, source_target_pairs={{0,2},{1,3},{2,0},{3,1},{4,6},{5,7},{6,4},{7,5},{8,10},{9,11},{10,... | collective-permute-start | bytes 983048 | tf_op jit(solution)/shard_map/ppermute | solution.py:45
  34.3 7.8 %collective-permute-done.7 = bf16[128,1280]{1,0:T(8,128)(2,1)S(1)} collective-permute-done((bf16[128,1280]{1,0:T(8,128)(2,1)S(1)}, bf16[128,1280]{1,0:T(8,128)(2,1)S(1)}, u32[]{:S(2)}, u32[]{:S(2)}) %collective-permute-start.7) | collective-permute-done | bytes 327712 | tf_op jit(solution)/shard_map/ppermute | solution.py:45
  42.4 3.3 %collective-permute-done.3 = bf16[128,1280]{1,0:T(8,128)(2,1)S(1)} collective-permute-done((bf16[128,1280]{1,0:T(8,128)(2,1)S(1)}, bf16[128,1280]{1,0:T(8,128)(2,1)S(1)}, u32[]{:S(2)}, u32[]{:S(2)}) %collective-permute-start.3) | collective-permute-done | bytes 327712 | tf_op jit(solution)/shard_map/ppermute | solution.py:45
  45.9 2.2 %fusion.1 = f16[512,1536]{1,0:T(8,128)(2,1)S(1)} fusion(bf16[1280,1536]{1,0:T(8,128)(2,1)S(1)} %copy-done.8, bf16[256,1280]{1,0:T(8,128)(2,1)S(1)} %collective-permute-done.8, bf16[128,1280]{1,0:T(8,128)(2,1)S(1)} %get-tuple-element.29, bf16[128,1280]{1,0:T(8,128)(2,1)S(1)} %get-tuple-element.28), kind=kOutput, calls=%fused_computation.3 | convolution fusion | flops 2018770944 | bytes 6815744 | tf_op jit(solution)/shard_map/dot_general | solution.py:60
  48.2 5.1 %collective-permute-start.14 = (f16[256,1536]{1,0:T(8,128)(2,1)S(1)}, f16[256,1536]{1,0:T(8,128)(2,1)S(1)}, u32[]{:S(2)}, u32[]{:S(2)}) collective-permute-start(f16[256,1536]{1,0:T(8,128)(2,1)S(1)} %dynamic-slice_bitcast_fusion), channel_id=1, source_target_pairs={{0,4},{12,8},{1,5},{13,9},{2,6},{14,10},{3,7},{15,11},{16,20},{28,... | collective-permute-start | bytes 2359304 | tf_op jit(solution)/shard_map/ppermute | solution.py:72
  53.4 1.2 multiply_convert_fusion
  54.7 1.3 collective-permute-start.9
  56.0 1.2 multiply_convert_fusion.1
  57.2 14.0 %collective-permute-done.14 = f16[256,1536]{1,0:T(8,128)(2,1)S(1)} collective-permute-done((f16[256,1536]{1,0:T(8,128)(2,1)S(1)}, f16[256,1536]{1,0:T(8,128)(2,1)S(1)}, u32[]{:S(2)}, u32[]{:S(2)}) %collective-permute-start.14) | collective-permute-done | bytes 786464 | tf_op jit(solution)/shard_map/ppermute | solution.py:72
  71.2 0.4 fusion.8
  71.6 4.4 %collective-permute-start.15 = (f16[256,1536]{1,0:T(8,128)(2,1)S(1)}, f16[256,1536]{1,0:T(8,128)(2,1)S(1)}, u32[]{:S(2)}, u32[]{:S(2)}) collective-permute-start(f16[256,1536]{1,0:T(8,128)(2,1)S(1)} %fusion.8), channel_id=1, source_target_pairs={{0,4},{4,8},{1,5},{5,9},{2,6},{6,10},{3,7},{7,11},{16,20},{20,24},... | collective-permute-start | bytes 2359304 | tf_op jit(solution)/shard_map/ppermute | solution.py:74
  76.1 0.7 collective-permute-start.17
  76.8 2.2 %fusion = f16[512,1536]{1,0:T(8,128)(2,1)S(1)} fusion(bf16[1280,1536]{1,0:T(8,128)(2,1)S(1)} %copy-done.8, bf16[256,1280]{1,0:T(8,128)(2,1)S(1)} %collective-permute-done.4, bf16[128,1280]{1,0:T(8,128)(2,1)S(1)} %get-tuple-element.27, bf16[128,1280]{1,0:T(8,128)(2,1)S(1)} %get-tuple-element.26), kind=kOutput, calls=%fused_computation.2 | convolution fusion | flops 2018770944 | bytes 6815744 | tf_op jit(solution)/shard_map/dot_general | solution.py:60
  79.0 0.6 collective-permute-done.9
  79.8 4.4 %collective-permute-start.10 = (f16[256,768]{1,0:T(8,128)(2,1)S(1)}, f16[256,768]{1,0:T(8,128)(2,1)S(1)}, u32[]{:S(2)}, u32[]{:S(2)}) collective-permute-start(f16[256,768]{1,0:T(8,128)(2,1)S(1)} %fusion.11), channel_id=1, source_target_pairs={{0,4},{4,8},{1,5},{5,9},{2,6},{6,10},{3,7},{7,11},{16,20},{20,24},... | collective-permute-start | bytes 1179656 | tf_op jit(solution)/shard_map/ppermute | solution.py:74
  84.2 0.7 collective-permute-start.12
  84.9 11.6 %collective-permute-done.15 = f16[256,1536]{1,0:T(8,128)(2,1)S(1)} collective-permute-done((f16[256,1536]{1,0:T(8,128)(2,1)S(1)}, f16[256,1536]{1,0:T(8,128)(2,1)S(1)}, u32[]{:S(2)}, u32[]{:S(2)}) %collective-permute-start.15) | collective-permute-done | bytes 786464 | tf_op jit(solution)/shard_map/ppermute | solution.py:74
  96.5 1.8 add_convert_fusion.1
  98.2 1.3 collective-permute-start.18
  99.5 6.3 %collective-permute-start.16 = (f16[256,1536]{1,0:T(8,128)(2,1)}, f16[256,1536]{1,0:T(8,128)(2,1)}, u32[]{:S(2)}, u32[]{:S(2)}) collective-permute-start(f16[256,1536]{1,0:T(8,128)(2,1)} %get-tuple-element.22), channel_id=1, source_target_pairs={{0,4},{4,8},{8,12},{1,5},{5,9},{9,13},{2,6},{6,10},{10,14},{3,7},{... | collective-permute-start | bytes 2359304 | tf_op jit(solution)/shard_map/ppermute | solution.py:78
  105.8 1.1 add_convert_fusion.4
  106.8 1.3 collective-permute-start.13
  108.1 5.3 %collective-permute-start.11 = (f16[256,768]{1,0:T(8,128)(2,1)S(1)}, f16[256,768]{1,0:T(8,128)(2,1)}, u32[]{:S(2)}, u32[]{:S(2)}) collective-permute-start(f16[256,768]{1,0:T(8,128)(2,1)S(1)} %get-tuple-element.24), channel_id=1, source_target_pairs={{0,4},{4,8},{8,12},{1,5},{5,9},{9,13},{2,6},{6,10},{10,14},{3,7},{... | collective-permute-start | bytes 1179656 | tf_op jit(solution)/shard_map/ppermute | solution.py:78
  113.4 14.8 %collective-permute-done.13 = f16[256,768]{1,0:T(8,128)(2,1)S(1)} collective-permute-done((f16[256,768]{1,0:T(8,128)(2,1)}, f16[256,768]{1,0:T(8,128)(2,1)S(1)}, u32[]{:S(2)}, u32[]{:S(2)}) %collective-permute-start.13) | collective-permute-done | bytes 393248 | tf_op jit(solution)/shard_map/ppermute | solution.py:79
  128.2 1.5 collective-permute-done.11
  129.8 1.2 fusion.10.query_ref
  130.9 1.9 fusion.3
  132.9 1.4 fusion.7
  134.3 2.7 %collective-permute-start.19 = (bf16[256,768]{1,0:T(8,128)(2,1)S(1)}, bf16[256,768]{1,0:T(8,128)(2,1)S(1)}, u32[]{:S(2)}, u32[]{:S(2)}) collective-permute-start(bf16[256,768]{1,0:T(8,128)(2,1)S(1)} %get-tuple-element.11.key_ref), channel_id=1, source_target_pairs={{0,4},{4,0},{8,12},{12,8},{1,5},{5,1},{9,13},{13,9},{2,6},{6,2},{1... | collective-permute-start | bytes 1179656 | tf_op jit(solution)/shard_map/ppermute | solution.py:87
  137.0 1.4 collective-permute-start.20
  138.5 6.1 %collective-permute-done.19 = bf16[256,768]{1,0:T(8,128)(2,1)S(1)} collective-permute-done((bf16[256,768]{1,0:T(8,128)(2,1)S(1)}, bf16[256,768]{1,0:T(8,128)(2,1)S(1)}, u32[]{:S(2)}, u32[]{:S(2)}) %collective-permute-start.19) | collective-permute-done | bytes 393248 | tf_op jit(solution)/shard_map/ppermute | solution.py:87
  144.6 10.9 %shard_map.77 = (bf16[256,1280]{1,0:T(8,128)(2,1)S(1)}, bf16[256,1280]{1,0:T(8,128)(2,1)}, f32[256,1280]{1,0:T(8,128)S(1)}, f32[256,1280]{1,0:T(8,128)S(1)}) custom-call(s32[5]{0:T(128)S(1)} %stack.23.place_ref, bf16[256,768]{1,0:T(8,128)(2,1)S(1)} %fusion.10.query_ref, bf16[2,1024,768]{2,1,0:T(8,128)(2,1)} %stale_ref.1, ...), custom_call_target="tpu_custom_call" | custom-call | flops 2818572288 | bytes 14942208 | tf_op jit(solution)/shard_map/pallas_call | solution.py:193
  155.5 1.1 copy-done.1
  156.6 1.1 copy-done.3
  157.7 0.8 copy-done.5
  158.6 3.7 %collective-permute-start.28 = (bf16[256,768]{1,0:T(8,128)(2,1)S(1)}, bf16[256,768]{1,0:T(8,128)(2,1)S(1)}, u32[]{:S(2)}, u32[]{:S(2)}) collective-permute-start(bf16[256,768]{1,0:T(8,128)(2,1)S(1)} %get-tuple-element.18.value_ref), channel_id=1, source_target_pairs={{0,4},{4,0},{8,12},{12,8},{1,5},{5,1},{9,13},{13,9},{2,6},{6,2},{1... | collective-permute-start | bytes 1179656 | tf_op jit(solution)/shard_map/ppermute | solution.py:87
  162.3 0.7 collective-permute-start.29
  163.0 0.3 collective-permute-start.21
  163.6 1.4 collective-permute-start.25
  165.0 7.2 %collective-permute-done.28 = bf16[256,768]{1,0:T(8,128)(2,1)S(1)} collective-permute-done((bf16[256,768]{1,0:T(8,128)(2,1)S(1)}, bf16[256,768]{1,0:T(8,128)(2,1)S(1)}, u32[]{:S(2)}, u32[]{:S(2)}) %collective-permute-start.28) | collective-permute-done | bytes 393248 | tf_op jit(solution)/shard_map/ppermute | solution.py:87
  172.3 0.7 collective-permute-start.26
  173.0 1.3 collective-permute-start.30
  174.3 0.7 collective-permute-start.31
  175.1 2.2 %collective-permute-start.24 = (bf16[256,640]{1,0:T(8,128)(2,1)S(1)}, bf16[256,640]{1,0:T(8,128)(2,1)S(1)}, u32[]{:S(2)}, u32[]{:S(2)}) collective-permute-start(bf16[256,640]{1,0:T(8,128)(2,1)S(1)} %add_convert_fusion.7), channel_id=1, source_target_pairs={{0,2},{1,3},{2,0},{3,1},{4,6},{5,7},{6,4},{7,5},{8,10},{9,11},{10,... | collective-permute-start | bytes 983048 | tf_op jit(solution)/shard_map/ppermute | solution.py:229
  177.4 3.3 %collective-permute-done.25 = bf16[256,768]{1,0:T(8,128)(2,1)S(1)} collective-permute-done((bf16[256,768]{1,0:T(8,128)(2,1)}, bf16[256,768]{1,0:T(8,128)(2,1)S(1)}, u32[]{:S(2)}, u32[]{:S(2)}) %collective-permute-start.25) | collective-permute-done | bytes 393248 | tf_op jit(solution)/shard_map/ppermute | solution.py:96
  180.7 2.2 %collective-permute-start.22 = (bf16[256,640]{1,0:T(8,128)(2,1)S(1)}, bf16[256,640]{1,0:T(8,128)(2,1)S(1)}, u32[]{:S(2)}, u32[]{:S(2)}) collective-permute-start(bf16[256,640]{1,0:T(8,128)(2,1)S(1)} %add_convert_fusion.9), channel_id=1, source_target_pairs={{0,2},{1,3},{2,0},{3,1},{4,6},{5,7},{6,4},{7,5},{8,10},{9,11},{10,... | collective-permute-start | bytes 983048 | tf_op jit(solution)/shard_map/ppermute | solution.py:229
  183.0 1.3 collective-permute-start.27
  184.3 1.3 collective-permute-start.32
  186.0 6.0 %collective-permute-done.22 = bf16[256,640]{1,0:T(8,128)(2,1)S(1)} collective-permute-done((bf16[256,640]{1,0:T(8,128)(2,1)S(1)}, bf16[256,640]{1,0:T(8,128)(2,1)S(1)}, u32[]{:S(2)}, u32[]{:S(2)}) %collective-permute-start.22) | collective-permute-done | bytes 327712 | tf_op jit(solution)/shard_map/ppermute | solution.py:229
  192.1 0.9 pad_maximum_fusion.4
  193.0 5.9 %collective-permute-done.27 = bf16[256,768]{1,0:T(8,128)(2,1)S(1)} collective-permute-done((bf16[256,768]{1,0:T(8,128)(2,1)S(1)}, bf16[256,768]{1,0:T(8,128)(2,1)S(1)}, u32[]{:S(2)}, u32[]{:S(2)}) %collective-permute-start.27) | collective-permute-done | bytes 393248 | tf_op jit(solution)/shard_map/ppermute | solution.py:97
  199.1 6.7 %collective-permute-done.32 = bf16[256,768]{1,0:T(8,128)(2,1)S(1)} collective-permute-done((bf16[256,768]{1,0:T(8,128)(2,1)S(1)}, bf16[256,768]{1,0:T(8,128)(2,1)S(1)}, u32[]{:S(2)}, u32[]{:S(2)}) %collective-permute-start.32) | collective-permute-done | bytes 393248 | tf_op jit(solution)/shard_map/ppermute | solution.py:97
  205.9 1.7 copy-done.6
  (62 shorter events, 2.5 us)
Async XLA Ops:
  0.6 52.8 %copy-start = (bf16[1280,768]{1,0:T(8,128)(2,1)S(1)}, bf16[1280,768]{1,0:T(8,128)(2,1)}, u32[]{:S(2)}) copy-start(bf16[1280,768]{1,0:T(8,128)(2,1)} %param.7) | copy-start | bytes 5898244
  1.9 10.8 %collective-permute-start.1 = (bf16[128,1280]{1,0:T(8,128)(2,1)S(1)}, bf16[128,1280]{1,0:T(8,128)(2,1)}, u32[]{:S(2)}, u32[]{:S(2)}) collective-permute-start(bf16[128,1280]{1,0:T(8,128)(2,1)S(1)} %get-tuple-element.30), channel_id=1, source_target_pairs={{0,2},{1,3},{2,0},{3,1},{4,6},{5,7},{6,4},{7,5},{8,10},{9,11},{10,... | collective-permute-start | bytes 983048 | tf_op jit(solution)/shard_map/ppermute | solution.py:31
  4.9 19.9 %collective-permute-start.5 = (bf16[128,1280]{1,0:T(8,128)(2,1)S(1)}, bf16[128,1280]{1,0:T(8,128)(2,1)S(1)}, u32[]{:S(2)}, u32[]{:S(2)}) collective-permute-start(bf16[128,1280]{1,0:T(8,128)(2,1)S(1)} %get-tuple-element.31), channel_id=1, source_target_pairs={{2,10},{3,14},{6,11},{7,15},{8,0},{9,4},{12,1},{13,5},{18,26},{19,... | collective-permute-start | bytes 983048 | tf_op jit(solution)/shard_map/ppermute | solution.py:41
  6.2 28.0 %collective-permute-start = (bf16[128,1280]{1,0:T(8,128)(2,1)S(1)}, bf16[128,1280]{1,0:T(8,128)(2,1)S(1)}, u32[]{:S(2)}, u32[]{:S(2)}) collective-permute-start(bf16[128,1280]{1,0:T(8,128)(2,1)S(1)} %get-tuple-element.31), channel_id=1, source_target_pairs={{0,0},{1,4},{4,1},{5,5},{10,10},{11,14},{14,11},{15,15},{16,16},{1... | collective-permute-start | bytes 983048 | tf_op jit(solution)/shard_map/ppermute | solution.py:41
  12.7 12.8 %collective-permute-start.6 = (bf16[128,1280]{1,0:T(8,128)(2,1)}, bf16[128,1280]{1,0:T(8,128)(2,1)S(1)}, u32[]{:S(2)}, u32[]{:S(2)}) collective-permute-start(bf16[128,1280]{1,0:T(8,128)(2,1)} %collective-permute-done.1), channel_id=1, source_target_pairs={{0,8},{1,12},{4,9},{5,13},{10,2},{11,6},{14,3},{15,7},{16,24},{17,... | collective-permute-start | bytes 983048 | tf_op jit(solution)/shard_map/ppermute | solution.py:41
  23.5 10.7 %collective-permute-start.2 = (bf16[128,1280]{1,0:T(8,128)(2,1)}, bf16[128,1280]{1,0:T(8,128)(2,1)S(1)}, u32[]{:S(2)}, u32[]{:S(2)}) collective-permute-start(bf16[128,1280]{1,0:T(8,128)(2,1)} %collective-permute-done.1), channel_id=1, source_target_pairs={{2,2},{3,6},{6,3},{7,7},{8,8},{9,12},{12,9},{13,13},{18,18},{19,22... | collective-permute-start | bytes 983048 | tf_op jit(solution)/shard_map/ppermute | solution.py:41
  25.6 16.6 %collective-permute-start.7 = (bf16[128,1280]{1,0:T(8,128)(2,1)S(1)}, bf16[128,1280]{1,0:T(8,128)(2,1)S(1)}, u32[]{:S(2)}, u32[]{:S(2)}) collective-permute-start(bf16[128,1280]{1,0:T(8,128)(2,1)S(1)} %broadcast_select_fusion.2), channel_id=1, source_target_pairs={{0,2},{1,3},{2,0},{3,1},{4,6},{5,7},{6,4},{7,5},{8,10},{9,11},{10,... | collective-permute-start | bytes 983048 | tf_op jit(solution)/shard_map/ppermute | solution.py:45
  34.2 11.5 %collective-permute-start.3 = (bf16[128,1280]{1,0:T(8,128)(2,1)S(1)}, bf16[128,1280]{1,0:T(8,128)(2,1)S(1)}, u32[]{:S(2)}, u32[]{:S(2)}) collective-permute-start(bf16[128,1280]{1,0:T(8,128)(2,1)S(1)} %broadcast_select_fusion.5), channel_id=1, source_target_pairs={{0,2},{1,3},{2,0},{3,1},{4,6},{5,7},{6,4},{7,5},{8,10},{9,11},{10,... | collective-permute-start | bytes 983048 | tf_op jit(solution)/shard_map/ppermute | solution.py:45
  42.2 3.7 %copy-start.8 = (bf16[1280,1536]{1,0:T(8,128)(2,1)S(1)}, bf16[1280,1536]{1,0:T(8,128)(2,1)}, u32[]{:S(2)}) copy-start(bf16[1280,1536]{1,0:T(8,128)(2,1)} %constant_dynamic-update-slice_fusion) | copy-start | bytes 11796484
  42.3 3.6 %collective-permute-start.8 = (bf16[256,1280]{1,0:T(8,128)(2,1)S(1)}, bf16[256,1280]{1,0:T(8,128)(2,1)S(1)}, u32[]{:S(2)}, u32[]{:S(2)}) collective-permute-start(bf16[256,1280]{1,0:T(8,128)(2,1)S(1)} %pad_maximum_fusion.3), channel_id=1, source_target_pairs={{0,1},{1,0},{2,3},{3,2},{4,5},{5,4},{6,7},{7,6},{8,9},{9,8},{10,11... | collective-permute-start | bytes 1966088 | tf_op jit(solution)/shard_map/ppermute | solution.py:49
  45.8 10.2 %collective-permute-start.4 = (bf16[256,1280]{1,0:T(8,128)(2,1)S(1)}, bf16[256,1280]{1,0:T(8,128)(2,1)S(1)}, u32[]{:S(2)}, u32[]{:S(2)}) collective-permute-start(bf16[256,1280]{1,0:T(8,128)(2,1)S(1)} %pad_maximum_fusion.2), channel_id=1, source_target_pairs={{0,1},{1,0},{2,3},{3,2},{4,5},{5,4},{6,7},{7,6},{8,9},{9,8},{10,11... | collective-permute-start | bytes 1966088 | tf_op jit(solution)/shard_map/ppermute | solution.py:49
  48.2 22.9 %collective-permute-start.14 = (f16[256,1536]{1,0:T(8,128)(2,1)S(1)}, f16[256,1536]{1,0:T(8,128)(2,1)S(1)}, u32[]{:S(2)}, u32[]{:S(2)}) collective-permute-start(f16[256,1536]{1,0:T(8,128)(2,1)S(1)} %dynamic-slice_bitcast_fusion), channel_id=1, source_target_pairs={{0,4},{12,8},{1,5},{13,9},{2,6},{14,10},{3,7},{15,11},{16,20},{28,... | collective-permute-start | bytes 2359304 | tf_op jit(solution)/shard_map/ppermute | solution.py:72
  54.7 24.9 %collective-permute-start.9 = (f16[256,768]{1,0:T(8,128)(2,1)S(1)}, f16[256,768]{1,0:T(8,128)(2,1)S(1)}, u32[]{:S(2)}, u32[]{:S(2)}) collective-permute-start(f16[256,768]{1,0:T(8,128)(2,1)S(1)} %dynamic-slice_bitcast_fusion.3), channel_id=1, source_target_pairs={{0,4},{12,8},{1,5},{13,9},{2,6},{14,10},{3,7},{15,11},{16,20},{28,... | collective-permute-start | bytes 1179656 | tf_op jit(solution)/shard_map/ppermute | solution.py:72
  71.6 24.8 %collective-permute-start.15 = (f16[256,1536]{1,0:T(8,128)(2,1)S(1)}, f16[256,1536]{1,0:T(8,128)(2,1)S(1)}, u32[]{:S(2)}, u32[]{:S(2)}) collective-permute-start(f16[256,1536]{1,0:T(8,128)(2,1)S(1)} %fusion.8), channel_id=1, source_target_pairs={{0,4},{4,8},{1,5},{5,9},{2,6},{6,10},{3,7},{7,11},{16,20},{20,24},... | collective-permute-start | bytes 2359304 | tf_op jit(solution)/shard_map/ppermute | solution.py:74
  76.1 20.4 %collective-permute-start.17 = (f16[256,1536]{1,0:T(8,128)(2,1)S(1)}, f16[256,1536]{1,0:T(8,128)(2,1)S(1)}, u32[]{:S(2)}, u32[]{:S(2)}) collective-permute-start(f16[256,1536]{1,0:T(8,128)(2,1)S(1)} %fusion.8), channel_id=1, source_target_pairs={{12,8},{8,4},{13,9},{9,5},{14,10},{10,6},{15,11},{11,7},{28,24},{2... | collective-permute-start | bytes 2359304 | tf_op jit(solution)/shard_map/ppermute | solution.py:75
  79.0 19.2 %copy-start.7 = (f16[512,1536]{1,0:T(8,128)(2,1)}, f16[512,1536]{1,0:T(8,128)(2,1)S(1)}, u32[]{:S(2)}) copy-start(f16[512,1536]{1,0:T(8,128)(2,1)S(1)} %fusion) | copy-start | bytes 4718596
  79.8 26.0 %collective-permute-start.10 = (f16[256,768]{1,0:T(8,128)(2,1)S(1)}, f16[256,768]{1,0:T(8,128)(2,1)S(1)}, u32[]{:S(2)}, u32[]{:S(2)}) collective-permute-start(f16[256,768]{1,0:T(8,128)(2,1)S(1)} %fusion.11), channel_id=1, source_target_pairs={{0,4},{4,8},{1,5},{5,9},{2,6},{6,10},{3,7},{7,11},{16,20},{20,24},... | collective-permute-start | bytes 1179656 | tf_op jit(solution)/shard_map/ppermute | solution.py:74
  84.2 21.6 %collective-permute-start.12 = (f16[256,768]{1,0:T(8,128)(2,1)S(1)}, f16[256,768]{1,0:T(8,128)(2,1)S(1)}, u32[]{:S(2)}, u32[]{:S(2)}) collective-permute-start(f16[256,768]{1,0:T(8,128)(2,1)S(1)} %fusion.11), channel_id=1, source_target_pairs={{12,8},{8,4},{13,9},{9,5},{14,10},{10,6},{15,11},{11,7},{28,24},{2... | collective-permute-start | bytes 1179656 | tf_op jit(solution)/shard_map/ppermute | solution.py:75
  98.2 32.7 %collective-permute-start.18 = (f16[256,1536]{1,0:T(8,128)(2,1)}, f16[256,1536]{1,0:T(8,128)(2,1)}, u32[]{:S(2)}, u32[]{:S(2)}) collective-permute-start(f16[256,1536]{1,0:T(8,128)(2,1)} %get-tuple-element.23), channel_id=1, source_target_pairs={{12,8},{8,4},{4,0},{13,9},{9,5},{5,1},{14,10},{10,6},{6,2},{15,11}... | collective-permute-start | bytes 2359304 | tf_op jit(solution)/shard_map/ppermute | solution.py:79
  99.5 31.4 %collective-permute-start.16 = (f16[256,1536]{1,0:T(8,128)(2,1)}, f16[256,1536]{1,0:T(8,128)(2,1)}, u32[]{:S(2)}, u32[]{:S(2)}) collective-permute-start(f16[256,1536]{1,0:T(8,128)(2,1)} %get-tuple-element.22), channel_id=1, source_target_pairs={{0,4},{4,8},{8,12},{1,5},{5,9},{9,13},{2,6},{6,10},{10,14},{3,7},{... | collective-permute-start | bytes 2359304 | tf_op jit(solution)/shard_map/ppermute | solution.py:78
  106.8 21.4 %collective-permute-start.13 = (f16[256,768]{1,0:T(8,128)(2,1)}, f16[256,768]{1,0:T(8,128)(2,1)S(1)}, u32[]{:S(2)}, u32[]{:S(2)}) collective-permute-start(f16[256,768]{1,0:T(8,128)(2,1)} %get-tuple-element.25), channel_id=1, source_target_pairs={{12,8},{8,4},{4,0},{13,9},{9,5},{5,1},{14,10},{10,6},{6,2},{15,11}... | collective-permute-start | bytes 1179656 | tf_op jit(solution)/shard_map/ppermute | solution.py:79
  108.1 21.6 %collective-permute-start.11 = (f16[256,768]{1,0:T(8,128)(2,1)S(1)}, f16[256,768]{1,0:T(8,128)(2,1)}, u32[]{:S(2)}, u32[]{:S(2)}) collective-permute-start(f16[256,768]{1,0:T(8,128)(2,1)S(1)} %get-tuple-element.24), channel_id=1, source_target_pairs={{0,4},{4,8},{8,12},{1,5},{5,9},{9,13},{2,6},{6,10},{10,14},{3,7},{... | collective-permute-start | bytes 1179656 | tf_op jit(solution)/shard_map/ppermute | solution.py:78
  134.3 10.3 %collective-permute-start.19 = (bf16[256,768]{1,0:T(8,128)(2,1)S(1)}, bf16[256,768]{1,0:T(8,128)(2,1)S(1)}, u32[]{:S(2)}, u32[]{:S(2)}) collective-permute-start(bf16[256,768]{1,0:T(8,128)(2,1)S(1)} %get-tuple-element.11.key_ref), channel_id=1, source_target_pairs={{0,4},{4,0},{8,12},{12,8},{1,5},{5,1},{9,13},{13,9},{2,6},{6,2},{1... | collective-permute-start | bytes 1179656 | tf_op jit(solution)/shard_map/ppermute | solution.py:87
  137.0 7.6 %collective-permute-start.20 = (bf16[256,768]{1,0:T(8,128)(2,1)S(1)}, bf16[256,768]{1,0:T(8,128)(2,1)}, u32[]{:S(2)}, u32[]{:S(2)}) collective-permute-start(bf16[256,768]{1,0:T(8,128)(2,1)S(1)} %get-tuple-element.11.key_ref), channel_id=1, source_target_pairs={{4,8},{8,4},{5,9},{9,5},{6,10},{10,6},{7,11},{11,7},{20,24},{24,20... | collective-permute-start | bytes 1179656 | tf_op jit(solution)/shard_map/ppermute | solution.py:88
  144.6 11.0 %copy-start.9 = (bf16[256,768]{1,0:T(8,128)(2,1)}, bf16[256,768]{1,0:T(8,128)(2,1)S(1)}, u32[]{:S(2)}) copy-start(bf16[256,768]{1,0:T(8,128)(2,1)S(1)} %collective-permute-done.19) | copy-start | bytes 1179652
  155.5 1.1 copy-start.1
  156.6 1.1 copy-start.3
  157.7 0.8 copy-start.5
  158.5 15.7 %collective-permute-start.23 = (bf16[256,1280]{1,0:T(8,128)(2,1)}, bf16[256,1280]{1,0:T(8,128)(2,1)S(1)}, u32[]{:S(2)}, u32[]{:S(2)}) collective-permute-start(bf16[256,1280]{1,0:T(8,128)(2,1)} %get-tuple-element.16), channel_id=1, source_target_pairs={{0,1},{1,0},{2,3},{3,2},{4,5},{5,4},{6,7},{7,6},{8,9},{9,8},{10,11... | collective-permute-start | bytes 1966088 | tf_op jit(solution)/shard_map/ppermute | solution.py:218
  158.6 13.7 %collective-permute-start.28 = (bf16[256,768]{1,0:T(8,128)(2,1)S(1)}, bf16[256,768]{1,0:T(8,128)(2,1)S(1)}, u32[]{:S(2)}, u32[]{:S(2)}) collective-permute-start(bf16[256,768]{1,0:T(8,128)(2,1)S(1)} %get-tuple-element.18.value_ref), channel_id=1, source_target_pairs={{0,4},{4,0},{8,12},{12,8},{1,5},{5,1},{9,13},{13,9},{2,6},{6,2},{1... | collective-permute-start | bytes 1179656 | tf_op jit(solution)/shard_map/ppermute | solution.py:87
  162.3 10.7 %collective-permute-start.29 = (bf16[256,768]{1,0:T(8,128)(2,1)S(1)}, bf16[256,768]{1,0:T(8,128)(2,1)S(1)}, u32[]{:S(2)}, u32[]{:S(2)}) collective-permute-start(bf16[256,768]{1,0:T(8,128)(2,1)S(1)} %get-tuple-element.18.value_ref), channel_id=1, source_target_pairs={{4,8},{8,4},{5,9},{9,5},{6,10},{10,6},{7,11},{11,7},{20,24},{24,20... | collective-permute-start | bytes 1179656 | tf_op jit(solution)/shard_map/ppermute | solution.py:88
  163.0 2.0 copy-start.10
  163.0 12.0 %copy-start.4 = (f32[256,1280]{1,0:T(8,128)S(1)}, f32[256,1280]{1,0:T(8,128)}, u32[]{:S(2)}) copy-start(f32[256,1280]{1,0:T(8,128)} %copy-done.3) | copy-start | bytes 3932164
  163.0 12.0 %collective-permute-start.21 = (bf16[256,1280]{1,0:T(8,128)(2,1)}, bf16[256,1280]{1,0:T(8,128)(2,1)S(1)}, u32[]{:S(2)}, u32[]{:S(2)}) collective-permute-start(bf16[256,1280]{1,0:T(8,128)(2,1)} %copy-done.5), channel_id=1, source_target_pairs={{0,1},{1,0},{2,3},{3,2},{4,5},{5,4},{6,7},{7,6},{8,9},{9,8},{10,11... | collective-permute-start | bytes 1966088 | tf_op jit(solution)/shard_map/ppermute | solution.py:218
  163.5 13.8 %copy-start.2 = (f32[256,1280]{1,0:T(8,128)S(1)}, f32[256,1280]{1,0:T(8,128)}, u32[]{:S(2)}) copy-start(f32[256,1280]{1,0:T(8,128)} %copy-done.1) | copy-start | bytes 3932164
  163.6 17.1 %collective-permute-start.25 = (bf16[256,768]{1,0:T(8,128)(2,1)}, bf16[256,768]{1,0:T(8,128)(2,1)S(1)}, u32[]{:S(2)}, u32[]{:S(2)}) collective-permute-start(bf16[256,768]{1,0:T(8,128)(2,1)} %collective-permute-done.20), channel_id=1, source_target_pairs={{4,0},{8,12},{5,1},{9,13},{6,2},{10,14},{7,3},{11,15},{20,16},{24,... | collective-permute-start | bytes 1179656 | tf_op jit(solution)/shard_map/ppermute | solution.py:96
  172.3 10.7 %collective-permute-start.26 = (bf16[256,768]{1,0:T(8,128)(2,1)S(1)}, bf16[256,768]{1,0:T(8,128)(2,1)S(1)}, u32[]{:S(2)}, u32[]{:S(2)}) collective-permute-start(bf16[256,768]{1,0:T(8,128)(2,1)S(1)} %copy-done.10), channel_id=1, source_target_pairs={{4,8},{8,4},{5,9},{9,5},{6,10},{10,6},{7,11},{11,7},{20,24},{24,20... | collective-permute-start | bytes 1179656 | tf_op jit(solution)/shard_map/ppermute | solution.py:95
  173.0 26.0 %collective-permute-start.30 = (bf16[256,768]{1,0:T(8,128)(2,1)S(1)}, bf16[256,768]{1,0:T(8,128)(2,1)S(1)}, u32[]{:S(2)}, u32[]{:S(2)}) collective-permute-start(bf16[256,768]{1,0:T(8,128)(2,1)S(1)} %collective-permute-done.29), channel_id=1, source_target_pairs={{4,0},{8,12},{5,1},{9,13},{6,2},{10,14},{7,3},{11,15},{20,16},{24,... | collective-permute-start | bytes 1179656 | tf_op jit(solution)/shard_map/ppermute | solution.py:96
  174.3 10.0 %collective-permute-start.31 = (bf16[256,768]{1,0:T(8,128)(2,1)S(1)}, bf16[256,768]{1,0:T(8,128)(2,1)S(1)}, u32[]{:S(2)}, u32[]{:S(2)}) collective-permute-start(bf16[256,768]{1,0:T(8,128)(2,1)S(1)} %collective-permute-done.28), channel_id=1, source_target_pairs={{4,8},{8,4},{5,9},{9,5},{6,10},{10,6},{7,11},{11,7},{20,24},{24,20... | collective-permute-start | bytes 1179656 | tf_op jit(solution)/shard_map/ppermute | solution.py:95
  175.1 10.8 %collective-permute-start.24 = (bf16[256,640]{1,0:T(8,128)(2,1)S(1)}, bf16[256,640]{1,0:T(8,128)(2,1)S(1)}, u32[]{:S(2)}, u32[]{:S(2)}) collective-permute-start(bf16[256,640]{1,0:T(8,128)(2,1)S(1)} %add_convert_fusion.7), channel_id=1, source_target_pairs={{0,2},{1,3},{2,0},{3,1},{4,6},{5,7},{6,4},{7,5},{8,10},{9,11},{10,... | collective-permute-start | bytes 983048 | tf_op jit(solution)/shard_map/ppermute | solution.py:229
  180.7 11.3 %collective-permute-start.22 = (bf16[256,640]{1,0:T(8,128)(2,1)S(1)}, bf16[256,640]{1,0:T(8,128)(2,1)S(1)}, u32[]{:S(2)}, u32[]{:S(2)}) collective-permute-start(bf16[256,640]{1,0:T(8,128)(2,1)S(1)} %add_convert_fusion.9), channel_id=1, source_target_pairs={{0,2},{1,3},{2,0},{3,1},{4,6},{5,7},{6,4},{7,5},{8,10},{9,11},{10,... | collective-permute-start | bytes 983048 | tf_op jit(solution)/shard_map/ppermute | solution.py:229
  183.0 15.8 %collective-permute-start.27 = (bf16[256,768]{1,0:T(8,128)(2,1)S(1)}, bf16[256,768]{1,0:T(8,128)(2,1)S(1)}, u32[]{:S(2)}, u32[]{:S(2)}) collective-permute-start(bf16[256,768]{1,0:T(8,128)(2,1)S(1)} %collective-permute-done.26), channel_id=1, source_target_pairs={{4,0},{8,12},{5,1},{9,13},{6,2},{10,14},{7,3},{11,15},{20,16},{24,... | collective-permute-start | bytes 1179656 | tf_op jit(solution)/shard_map/ppermute | solution.py:97
  184.3 21.5 %collective-permute-start.32 = (bf16[256,768]{1,0:T(8,128)(2,1)S(1)}, bf16[256,768]{1,0:T(8,128)(2,1)S(1)}, u32[]{:S(2)}, u32[]{:S(2)}) collective-permute-start(bf16[256,768]{1,0:T(8,128)(2,1)S(1)} %collective-permute-done.31), channel_id=1, source_target_pairs={{4,0},{8,12},{5,1},{9,13},{6,2},{10,14},{7,3},{11,15},{20,16},{24,... | collective-permute-start | bytes 1179656 | tf_op jit(solution)/shard_map/ppermute | solution.py:97
  205.9 1.7 copy-start.6

commit v10 on v9

--- a/solution.py
+++ b/solution.py
@@ -177,7 +177,7 @@
                 keep_refs[c][:, there] = sums[:, pl.ds(ours, part)]
 
 
-def attend(query, stale_kv, key_new, value_new, w_out, patches, ranks):
+def attend(query, stale_kv, key_new, value_new, w_out, patches, ranks, *earlier):
     rows, depth = query.shape
     tokens, model = stale_kv.shape[1], w_out.shape[1]
     rank = lax.axis_index("tensor").astype(jnp.int32)
@@ -215,7 +215,7 @@
         ),
     )(place, query, stale_kv, key_new, value_new, w_out)
     across = [(r, r ^ 1) for r in range(ranks)]
-    got = [lax.ppermute(send, "tensor", across) for send in results[:chunks]]
+    got = [lax.ppermute(after(send, *earlier), "tensor", across) for send in results[:chunks]]
     pieces, sends = [], []
     for mine, theirs in zip(results[chunks:], got):
 
@@ -260,8 +260,10 @@
         value_new = refresh(both[:, width:], own_stale[1])
         if in_pairs:
             keys, values = PairGather(after(key_new, query)), PairGather(after(value_new, query))
-            query = after(query, keys.mate, keys.across)
-        attended, sent = attend(query, stale_kv, key_new, value_new, w_out, patches, ranks)
+            first_hop = (keys.mate, keys.across, values.mate, values.across)
+        else:
+            first_hop = ()
+        attended, sent = attend(query, stale_kv, key_new, value_new, w_out, patches, ranks, *first_hop)
         if in_pairs:
             refreshed = keys.into(jnp.zeros_like(stale_kv), 0, *sent)
             refreshed = values.into(refreshed, 1, *sent)

time: 208 us -> 199 us (0.957)
  waiting for transfers between devices: 96.3 us -> 84.6 us
  local copies, waits for them, and re-layouts: 12.6 us -> 15.4 us
    ppermute x2, waiting for transfers between devices: 13.3 us -> 0.01 us  [__init__(): self.mate = lax.ppermute(own, 'patch', [(0, 1), (1, 0), (2, 3), (3, 2)])]
    ppermute x2, waiting for transfers between devices: 3.32 us -> 6.7 us  [into(): lax.ppermute(self.across, 'patch', outward)]
    ppermute x2, waiting for transfers between devices: 6.22 us -> 3.2 us  [attend(): arrived.append(lax.ppermute(sends[-1], 'tensor', pairs))]
  transfers between devices with their start and end apart: 33 -> 33, of which waited for: 17 -> 14; matrix products, arithmetic and copies ran while one was open for 10% -> 11% of each run, Pallas kernels for 0% -> 6%
where the time goes in v10:
time: 199 us; the launch traced here: 198 us
  waiting for transfers between devices  84.6 us (43%)
  starting transfers between devices  69.3 us (35%)
  local copies, waits for them, and re-layouts  15.4 us (8%)
  Pallas kernels  10.9 us (5%)
  other arithmetic  9.9 us (5%)
  matrix products  6.77 us (3%)
    ppermute x2, waiting for transfers between devices, sum_in_pairs(): down = lax.ppermute(third_down, 'patch', [(3, 2), (2, 1), (1, 0)])  14.8 us
    ppermute x2, waiting for transfers between devices, sum_in_pairs(): first = lax.ppermute(outermost, 'patch', [(0, 1), (3, 2)])  14.6 us
    ppermute x2, waiting for transfers between devices, into(): last = lax.ppermute(after(across_mate, *earlier), 'patch', outward)  13.8 us
    ppermute x2, starting transfers between devices, sum_in_pairs(): up = lax.ppermute(third_up, 'patch', [(0, 1), (1, 2), (2, 3)])  11.6 us
    ppermute x2, waiting for transfers between devices, sum_in_pairs(): up = lax.ppermute(second, 'patch', [(0, 1), (1, 2)])  11.6 us
    ppermute x2, waiting for transfers between devices, both_slabs(): other = lax.ppermute(held, 'tensor', across)  11.2 us
    pallas_call x1, Pallas kernels, attend(): pl.pallas_call(functools.partial(attend_and_project, patches, heads, chip...  10.9 us
    ppermute x2, starting transfers between devices, sum_in_pairs(): up = lax.ppermute(second, 'patch', [(0, 1), (1, 2)])  8.85 us
  transfers between devices with their start and end apart: 33, of which 14 were waited for; matrix products, arithmetic and copies ran while one was open for 11% of the time, Pallas kernels for 6%

profile of v10, /device:TPU:0, one launch (start us, length us, event | category | flops | bytes accessed | tf_op | source)
XLA Modules:
  0.0 198.1 jit_solution(16984065676874906739)
XLA Ops:
  0.6 1.3 fusion.16
  1.9 3.0 %collective-permute-start.1 = (bf16[128,1280]{1,0:T(8,128)(2,1)S(1)}, bf16[128,1280]{1,0:T(8,128)(2,1)}, u32[]{:S(2)}, u32[]{:S(2)}) collective-permute-start(bf16[128,1280]{1,0:T(8,128)(2,1)S(1)} %get-tuple-element.32), channel_id=1, source_target_pairs={{0,2},{1,3},{2,0},{3,1},{4,6},{5,7},{6,4},{7,5},{8,10},{9,11},{10,... | collective-permute-start | bytes 983048 | tf_op jit(solution)/shard_map/ppermute | solution.py:31
  4.9 1.3 collective-permute-start.5
  6.2 0.7 collective-permute-start
  6.9 5.8 %collective-permute-done.1 = bf16[128,1280]{1,0:T(8,128)(2,1)} collective-permute-done((bf16[128,1280]{1,0:T(8,128)(2,1)S(1)}, bf16[128,1280]{1,0:T(8,128)(2,1)}, u32[]{:S(2)}, u32[]{:S(2)}) %collective-permute-start.1) | collective-permute-done | bytes 327712 | tf_op jit(solution)/shard_map/ppermute | solution.py:31
  12.7 4.7 %collective-permute-start.6 = (bf16[128,1280]{1,0:T(8,128)(2,1)}, bf16[128,1280]{1,0:T(8,128)(2,1)S(1)}, u32[]{:S(2)}, u32[]{:S(2)}) collective-permute-start(bf16[128,1280]{1,0:T(8,128)(2,1)} %collective-permute-done.1), channel_id=1, source_target_pairs={{0,8},{1,12},{4,9},{5,13},{10,2},{11,6},{14,3},{15,7},{16,24},{17,... | collective-permute-start | bytes 983048 | tf_op jit(solution)/shard_map/ppermute | solution.py:41
  17.5 3.0 %constant_dynamic-update-slice_fusion.1 = bf16[1280,1536]{1,0:T(8,128)(2,1)} fusion(bf16[1280,768]{1,0:T(8,128)(2,1)} %param.8), kind=kLoop, calls=%fused_computation.60 | loop fusion | bytes 3932160
  20.5 3.0 %constant_dynamic-update-slice_fusion = bf16[1280,1536]{1,0:T(8,128)(2,1)} fusion(bf16[1280,1536]{1,0:T(8,128)(2,1)} %constant_dynamic-update-slice_fusion.1, bf16[1280,768]{1,0:T(8,128)(2,1)} %param.9), kind=kLoop, calls=%fused_computation.59 | loop fusion | bytes 3932160 | tf_op jit(solution)/shard_map/concatenate | solution.py:243
  23.5 0.7 collective-permute-start.2
  24.2 0.6 collective-permute-done.5
  24.8 0.7 collective-permute-done.6
  25.6 8.6 %collective-permute-start.7 = (bf16[128,1280]{1,0:T(8,128)(2,1)S(1)}, bf16[128,1280]{1,0:T(8,128)(2,1)S(1)}, u32[]{:S(2)}, u32[]{:S(2)}) collective-permute-start(bf16[128,1280]{1,0:T(8,128)(2,1)S(1)} %broadcast_select_fusion.2), channel_id=1, source_target_pairs={{0,2},{1,3},{2,0},{3,1},{4,6},{5,7},{6,4},{7,5},{8,10},{9,11},{10,... | collective-permute-start | bytes 983048 | tf_op jit(solution)/shard_map/ppermute | solution.py:45
  34.3 7.8 %collective-permute-done.7 = bf16[128,1280]{1,0:T(8,128)(2,1)S(1)} collective-permute-done((bf16[128,1280]{1,0:T(8,128)(2,1)S(1)}, bf16[128,1280]{1,0:T(8,128)(2,1)S(1)}, u32[]{:S(2)}, u32[]{:S(2)}) %collective-permute-start.7) | collective-permute-done | bytes 327712 | tf_op jit(solution)/shard_map/ppermute | solution.py:45
  42.4 3.3 %collective-permute-done.3 = bf16[128,1280]{1,0:T(8,128)(2,1)S(1)} collective-permute-done((bf16[128,1280]{1,0:T(8,128)(2,1)S(1)}, bf16[128,1280]{1,0:T(8,128)(2,1)S(1)}, u32[]{:S(2)}, u32[]{:S(2)}) %collective-permute-start.3) | collective-permute-done | bytes 327712 | tf_op jit(solution)/shard_map/ppermute | solution.py:45
  45.9 2.2 %fusion.1 = f16[512,1536]{1,0:T(8,128)(2,1)S(1)} fusion(bf16[1280,1536]{1,0:T(8,128)(2,1)S(1)} %copy-done.8, bf16[256,1280]{1,0:T(8,128)(2,1)S(1)} %collective-permute-done.8, bf16[128,1280]{1,0:T(8,128)(2,1)S(1)} %get-tuple-element.31, bf16[128,1280]{1,0:T(8,128)(2,1)S(1)} %get-tuple-element.30), kind=kOutput, calls=%fused_computation.3 | convolution fusion | flops 2018770944 | bytes 6815744 | tf_op jit(solution)/shard_map/dot_general | solution.py:60
  48.2 5.1 %collective-permute-start.14 = (f16[256,1536]{1,0:T(8,128)(2,1)S(1)}, f16[256,1536]{1,0:T(8,128)(2,1)S(1)}, u32[]{:S(2)}, u32[]{:S(2)}) collective-permute-start(f16[256,1536]{1,0:T(8,128)(2,1)S(1)} %dynamic-slice_bitcast_fusion), channel_id=1, source_target_pairs={{0,4},{12,8},{1,5},{13,9},{2,6},{14,10},{3,7},{15,11},{16,20},{28,... | collective-permute-start | bytes 2359304 | tf_op jit(solution)/shard_map/ppermute | solution.py:72
  53.4 1.2 multiply_convert_fusion
  54.7 1.3 collective-permute-start.9
  56.0 1.2 multiply_convert_fusion.1
  57.2 14.0 %collective-permute-done.14 = f16[256,1536]{1,0:T(8,128)(2,1)S(1)} collective-permute-done((f16[256,1536]{1,0:T(8,128)(2,1)S(1)}, f16[256,1536]{1,0:T(8,128)(2,1)S(1)}, u32[]{:S(2)}, u32[]{:S(2)}) %collective-permute-start.14) | collective-permute-done | bytes 786464 | tf_op jit(solution)/shard_map/ppermute | solution.py:72
  71.6 4.4 %collective-permute-start.15 = (f16[256,1536]{1,0:T(8,128)(2,1)S(1)}, f16[256,1536]{1,0:T(8,128)(2,1)S(1)}, u32[]{:S(2)}, u32[]{:S(2)}) collective-permute-start(f16[256,1536]{1,0:T(8,128)(2,1)S(1)} %fusion.8), channel_id=1, source_target_pairs={{0,4},{4,8},{1,5},{5,9},{2,6},{6,10},{3,7},{7,11},{16,20},{20,24},... | collective-permute-start | bytes 2359304 | tf_op jit(solution)/shard_map/ppermute | solution.py:74
  76.1 0.7 collective-permute-start.17
  76.8 2.2 %fusion = f16[512,1536]{1,0:T(8,128)(2,1)S(1)} fusion(bf16[1280,1536]{1,0:T(8,128)(2,1)S(1)} %copy-done.8, bf16[256,1280]{1,0:T(8,128)(2,1)S(1)} %collective-permute-done.4, bf16[128,1280]{1,0:T(8,128)(2,1)S(1)} %get-tuple-element.29, bf16[128,1280]{1,0:T(8,128)(2,1)S(1)} %get-tuple-element.28), kind=kOutput, calls=%fused_computation.2 | convolution fusion | flops 2018770944 | bytes 6815744 | tf_op jit(solution)/shard_map/dot_general | solution.py:60
  79.0 0.6 collective-permute-done.9
  79.8 4.4 %collective-permute-start.10 = (f16[256,768]{1,0:T(8,128)(2,1)S(1)}, f16[256,768]{1,0:T(8,128)(2,1)S(1)}, u32[]{:S(2)}, u32[]{:S(2)}) collective-permute-start(f16[256,768]{1,0:T(8,128)(2,1)S(1)} %fusion.11), channel_id=1, source_target_pairs={{0,4},{4,8},{1,5},{5,9},{2,6},{6,10},{3,7},{7,11},{16,20},{20,24},... | collective-permute-start | bytes 1179656 | tf_op jit(solution)/shard_map/ppermute | solution.py:74
  84.2 0.7 collective-permute-start.12
  84.9 11.6 %collective-permute-done.15 = f16[256,1536]{1,0:T(8,128)(2,1)S(1)} collective-permute-done((f16[256,1536]{1,0:T(8,128)(2,1)S(1)}, f16[256,1536]{1,0:T(8,128)(2,1)S(1)}, u32[]{:S(2)}, u32[]{:S(2)}) %collective-permute-start.15) | collective-permute-done | bytes 786464 | tf_op jit(solution)/shard_map/ppermute | solution.py:74
  96.5 1.8 add_convert_fusion.1
  98.2 1.3 collective-permute-start.18
  99.5 6.3 %collective-permute-start.16 = (f16[256,1536]{1,0:T(8,128)(2,1)}, f16[256,1536]{1,0:T(8,128)(2,1)}, u32[]{:S(2)}, u32[]{:S(2)}) collective-permute-start(f16[256,1536]{1,0:T(8,128)(2,1)} %get-tuple-element.24), channel_id=1, source_target_pairs={{0,4},{4,8},{8,12},{1,5},{5,9},{9,13},{2,6},{6,10},{10,14},{3,7},{... | collective-permute-start | bytes 2359304 | tf_op jit(solution)/shard_map/ppermute | solution.py:78
  105.8 1.1 add_convert_fusion.4
  106.8 1.3 collective-permute-start.13
  108.1 5.3 %collective-permute-start.11 = (f16[256,768]{1,0:T(8,128)(2,1)S(1)}, f16[256,768]{1,0:T(8,128)(2,1)}, u32[]{:S(2)}, u32[]{:S(2)}) collective-permute-start(f16[256,768]{1,0:T(8,128)(2,1)S(1)} %get-tuple-element.26), channel_id=1, source_target_pairs={{0,4},{4,8},{8,12},{1,5},{5,9},{9,13},{2,6},{6,10},{10,14},{3,7},{... | collective-permute-start | bytes 1179656 | tf_op jit(solution)/shard_map/ppermute | solution.py:78
  113.4 14.8 %collective-permute-done.13 = f16[256,768]{1,0:T(8,128)(2,1)S(1)} collective-permute-done((f16[256,768]{1,0:T(8,128)(2,1)}, f16[256,768]{1,0:T(8,128)(2,1)S(1)}, u32[]{:S(2)}, u32[]{:S(2)}) %collective-permute-start.13) | collective-permute-done | bytes 393248 | tf_op jit(solution)/shard_map/ppermute | solution.py:79
  128.2 1.5 collective-permute-done.11
  129.8 1.2 fusion.10.query_ref
  130.9 1.9 fusion.3
  132.9 1.4 fusion.7
  134.3 2.7 %collective-permute-start.19 = (bf16[256,768]{1,0:T(8,128)(2,1)S(1)}, bf16[256,768]{1,0:T(8,128)(2,1)}, u32[]{:S(2)}, u32[]{:S(2)}) collective-permute-start(bf16[256,768]{1,0:T(8,128)(2,1)S(1)} %get-tuple-element.14.key_ref), channel_id=1, source_target_pairs={{0,4},{4,0},{8,12},{12,8},{1,5},{5,1},{9,13},{13,9},{2,6},{6,2},{1... | collective-permute-start | bytes 1179656 | tf_op jit(solution)/shard_map/ppermute | solution.py:87
  137.0 1.4 collective-permute-start.20
  138.4 2.9 %collective-permute-start.21 = (bf16[256,768]{1,0:T(8,128)(2,1)S(1)}, bf16[256,768]{1,0:T(8,128)(2,1)}, u32[]{:S(2)}, u32[]{:S(2)}) collective-permute-start(bf16[256,768]{1,0:T(8,128)(2,1)S(1)} %get-tuple-element.15.value_ref), channel_id=1, source_target_pairs={{0,4},{4,0},{8,12},{12,8},{1,5},{5,1},{9,13},{13,9},{2,6},{6,2},{1... | collective-permute-start | bytes 1179656 | tf_op jit(solution)/shard_map/ppermute | solution.py:87
  141.3 0.9 collective-permute-start.22
  142.3 10.9 %shard_map.77 = (bf16[256,1280]{1,0:T(8,128)(2,1)S(1)}, bf16[256,1280]{1,0:T(8,128)(2,1)}, f32[256,1280]{1,0:T(8,128)S(1)}, f32[256,1280]{1,0:T(8,128)S(1)}) custom-call(s32[5]{0:T(128)S(1)} %stack.23.place_ref, bf16[256,768]{1,0:T(8,128)(2,1)S(1)} %fusion.10.query_ref, bf16[2,1024,768]{2,1,0:T(8,128)(2,1)} %stale_ref.1, ...), custom_call_target="tpu_custom_call" | custom-call | flops 2818572288 | bytes 14942208 | tf_op jit(solution)/shard_map/pallas_call | solution.py:193
  153.2 1.1 copy-done.1
  154.3 1.1 copy-done.3
  155.4 0.8 copy-done.5
  156.3 0.7 copy-done.9
  157.0 0.5 collective-permute-start.23
  157.8 1.4 collective-permute-start.27
  159.2 0.7 collective-permute-start.28
  159.9 1.3 collective-permute-start.30
  161.2 1.0 bitcast_dynamic-update-slice_fusion.6
  162.3 0.7 collective-permute-start.31
  163.1 2.2 %collective-permute-start.26 = (bf16[256,640]{1,0:T(8,128)(2,1)S(1)}, bf16[256,640]{1,0:T(8,128)(2,1)S(1)}, u32[]{:S(2)}, u32[]{:S(2)}) collective-permute-start(bf16[256,640]{1,0:T(8,128)(2,1)S(1)} %add_convert_fusion.7), channel_id=1, source_target_pairs={{0,2},{1,3},{2,0},{3,1},{4,6},{5,7},{6,4},{7,5},{8,10},{9,11},{10,... | collective-permute-start | bytes 983048 | tf_op jit(solution)/shard_map/ppermute | solution.py:229
  165.3 6.7 %collective-permute-done.27 = bf16[256,768]{1,0:T(8,128)(2,1)S(1)} collective-permute-done((bf16[256,768]{1,0:T(8,128)(2,1)}, bf16[256,768]{1,0:T(8,128)(2,1)S(1)}, u32[]{:S(2)}, u32[]{:S(2)}) %collective-permute-start.27) | collective-permute-done | bytes 393248 | tf_op jit(solution)/shard_map/ppermute | solution.py:96
  172.0 2.1 %collective-permute-start.24 = (bf16[256,640]{1,0:T(8,128)(2,1)S(1)}, bf16[256,640]{1,0:T(8,128)(2,1)S(1)}, u32[]{:S(2)}, u32[]{:S(2)}) collective-permute-start(bf16[256,640]{1,0:T(8,128)(2,1)S(1)} %add_convert_fusion.9), channel_id=1, source_target_pairs={{0,2},{1,3},{2,0},{3,1},{4,6},{5,7},{6,4},{7,5},{8,10},{9,11},{10,... | collective-permute-start | bytes 983048 | tf_op jit(solution)/shard_map/ppermute | solution.py:229
  174.2 1.3 collective-permute-start.29
  175.5 1.3 collective-permute-start.32
  177.0 3.2 %collective-permute-done.24 = bf16[256,640]{1,0:T(8,128)(2,1)S(1)} collective-permute-done((bf16[256,640]{1,0:T(8,128)(2,1)S(1)}, bf16[256,640]{1,0:T(8,128)(2,1)S(1)}, u32[]{:S(2)}, u32[]{:S(2)}) %collective-permute-start.24) | collective-permute-done | bytes 327712 | tf_op jit(solution)/shard_map/ppermute | solution.py:229
  180.3 0.9 pad_maximum_fusion.4
  181.2 7.7 %collective-permute-done.29 = bf16[256,768]{1,0:T(8,128)(2,1)S(1)} collective-permute-done((bf16[256,768]{1,0:T(8,128)(2,1)S(1)}, bf16[256,768]{1,0:T(8,128)(2,1)S(1)}, u32[]{:S(2)}, u32[]{:S(2)}) %collective-permute-start.29) | collective-permute-done | bytes 393248 | tf_op jit(solution)/shard_map/ppermute | solution.py:97
  189.0 1.0 bitcast_dynamic-update-slice_fusion.2
  190.1 6.2 %collective-permute-done.32 = bf16[256,768]{1,0:T(8,128)(2,1)S(1)} collective-permute-done((bf16[256,768]{1,0:T(8,128)(2,1)S(1)}, bf16[256,768]{1,0:T(8,128)(2,1)S(1)}, u32[]{:S(2)}, u32[]{:S(2)}) %collective-permute-start.32) | collective-permute-done | bytes 393248 | tf_op jit(solution)/shard_map/ppermute | solution.py:97
  196.4 1.7 copy-done.6
  (62 shorter events, 2.6 us)
Async XLA Ops:
  0.6 52.8 %copy-start = (bf16[1280,768]{1,0:T(8,128)(2,1)S(1)}, bf16[1280,768]{1,0:T(8,128)(2,1)}, u32[]{:S(2)}) copy-start(bf16[1280,768]{1,0:T(8,128)(2,1)} %param.7) | copy-start | bytes 5898244
  1.9 10.8 %collective-permute-start.1 = (bf16[128,1280]{1,0:T(8,128)(2,1)S(1)}, bf16[128,1280]{1,0:T(8,128)(2,1)}, u32[]{:S(2)}, u32[]{:S(2)}) collective-permute-start(bf16[128,1280]{1,0:T(8,128)(2,1)S(1)} %get-tuple-element.32), channel_id=1, source_target_pairs={{0,2},{1,3},{2,0},{3,1},{4,6},{5,7},{6,4},{7,5},{8,10},{9,11},{10,... | collective-permute-start | bytes 983048 | tf_op jit(solution)/shard_map/ppermute | solution.py:31
  4.9 19.9 %collective-permute-start.5 = (bf16[128,1280]{1,0:T(8,128)(2,1)S(1)}, bf16[128,1280]{1,0:T(8,128)(2,1)S(1)}, u32[]{:S(2)}, u32[]{:S(2)}) collective-permute-start(bf16[128,1280]{1,0:T(8,128)(2,1)S(1)} %get-tuple-element.33), channel_id=1, source_target_pairs={{2,10},{3,14},{6,11},{7,15},{8,0},{9,4},{12,1},{13,5},{18,26},{19,... | collective-permute-start | bytes 983048 | tf_op jit(solution)/shard_map/ppermute | solution.py:41
  6.2 28.0 %collective-permute-start = (bf16[128,1280]{1,0:T(8,128)(2,1)S(1)}, bf16[128,1280]{1,0:T(8,128)(2,1)S(1)}, u32[]{:S(2)}, u32[]{:S(2)}) collective-permute-start(bf16[128,1280]{1,0:T(8,128)(2,1)S(1)} %get-tuple-element.33), channel_id=1, source_target_pairs={{0,0},{1,4},{4,1},{5,5},{10,10},{11,14},{14,11},{15,15},{16,16},{1... | collective-permute-start | bytes 983048 | tf_op jit(solution)/shard_map/ppermute | solution.py:41
  12.7 12.8 %collective-permute-start.6 = (bf16[128,1280]{1,0:T(8,128)(2,1)}, bf16[128,1280]{1,0:T(8,128)(2,1)S(1)}, u32[]{:S(2)}, u32[]{:S(2)}) collective-permute-start(bf16[128,1280]{1,0:T(8,128)(2,1)} %collective-permute-done.1), channel_id=1, source_target_pairs={{0,8},{1,12},{4,9},{5,13},{10,2},{11,6},{14,3},{15,7},{16,24},{17,... | collective-permute-start | bytes 983048 | tf_op jit(solution)/shard_map/ppermute | solution.py:41
  23.5 10.7 %collective-permute-start.2 = (bf16[128,1280]{1,0:T(8,128)(2,1)}, bf16[128,1280]{1,0:T(8,128)(2,1)S(1)}, u32[]{:S(2)}, u32[]{:S(2)}) collective-permute-start(bf16[128,1280]{1,0:T(8,128)(2,1)} %collective-permute-done.1), channel_id=1, source_target_pairs={{2,2},{3,6},{6,3},{7,7},{8,8},{9,12},{12,9},{13,13},{18,18},{19,22... | collective-permute-start | bytes 983048 | tf_op jit(solution)/shard_map/ppermute | solution.py:41
  25.6 16.6 %collective-permute-start.7 = (bf16[128,1280]{1,0:T(8,128)(2,1)S(1)}, bf16[128,1280]{1,0:T(8,128)(2,1)S(1)}, u32[]{:S(2)}, u32[]{:S(2)}) collective-permute-start(bf16[128,1280]{1,0:T(8,128)(2,1)S(1)} %broadcast_select_fusion.2), channel_id=1, source_target_pairs={{0,2},{1,3},{2,0},{3,1},{4,6},{5,7},{6,4},{7,5},{8,10},{9,11},{10,... | collective-permute-start | bytes 983048 | tf_op jit(solution)/shard_map/ppermute | solution.py:45
  34.2 11.5 %collective-permute-start.3 = (bf16[128,1280]{1,0:T(8,128)(2,1)S(1)}, bf16[128,1280]{1,0:T(8,128)(2,1)S(1)}, u32[]{:S(2)}, u32[]{:S(2)}) collective-permute-start(bf16[128,1280]{1,0:T(8,128)(2,1)S(1)} %broadcast_select_fusion.5), channel_id=1, source_target_pairs={{0,2},{1,3},{2,0},{3,1},{4,6},{5,7},{6,4},{7,5},{8,10},{9,11},{10,... | collective-permute-start | bytes 983048 | tf_op jit(solution)/shard_map/ppermute | solution.py:45
  42.2 3.7 %copy-start.8 = (bf16[1280,1536]{1,0:T(8,128)(2,1)S(1)}, bf16[1280,1536]{1,0:T(8,128)(2,1)}, u32[]{:S(2)}) copy-start(bf16[1280,1536]{1,0:T(8,128)(2,1)} %constant_dynamic-update-slice_fusion) | copy-start | bytes 11796484
  42.3 3.6 %collective-permute-start.8 = (bf16[256,1280]{1,0:T(8,128)(2,1)S(1)}, bf16[256,1280]{1,0:T(8,128)(2,1)S(1)}, u32[]{:S(2)}, u32[]{:S(2)}) collective-permute-start(bf16[256,1280]{1,0:T(8,128)(2,1)S(1)} %pad_maximum_fusion.3), channel_id=1, source_target_pairs={{0,1},{1,0},{2,3},{3,2},{4,5},{5,4},{6,7},{7,6},{8,9},{9,8},{10,11... | collective-permute-start | bytes 1966088 | tf_op jit(solution)/shard_map/ppermute | solution.py:49
  45.8 10.2 %collective-permute-start.4 = (bf16[256,1280]{1,0:T(8,128)(2,1)S(1)}, bf16[256,1280]{1,0:T(8,128)(2,1)S(1)}, u32[]{:S(2)}, u32[]{:S(2)}) collective-permute-start(bf16[256,1280]{1,0:T(8,128)(2,1)S(1)} %pad_maximum_fusion.2), channel_id=1, source_target_pairs={{0,1},{1,0},{2,3},{3,2},{4,5},{5,4},{6,7},{7,6},{8,9},{9,8},{10,11... | collective-permute-start | bytes 1966088 | tf_op jit(solution)/shard_map/ppermute | solution.py:49
  48.2 22.9 %collective-permute-start.14 = (f16[256,1536]{1,0:T(8,128)(2,1)S(1)}, f16[256,1536]{1,0:T(8,128)(2,1)S(1)}, u32[]{:S(2)}, u32[]{:S(2)}) collective-permute-start(f16[256,1536]{1,0:T(8,128)(2,1)S(1)} %dynamic-slice_bitcast_fusion), channel_id=1, source_target_pairs={{0,4},{12,8},{1,5},{13,9},{2,6},{14,10},{3,7},{15,11},{16,20},{28,... | collective-permute-start | bytes 2359304 | tf_op jit(solution)/shard_map/ppermute | solution.py:72
  54.7 24.9 %collective-permute-start.9 = (f16[256,768]{1,0:T(8,128)(2,1)S(1)}, f16[256,768]{1,0:T(8,128)(2,1)S(1)}, u32[]{:S(2)}, u32[]{:S(2)}) collective-permute-start(f16[256,768]{1,0:T(8,128)(2,1)S(1)} %dynamic-slice_bitcast_fusion.3), channel_id=1, source_target_pairs={{0,4},{12,8},{1,5},{13,9},{2,6},{14,10},{3,7},{15,11},{16,20},{28,... | collective-permute-start | bytes 1179656 | tf_op jit(solution)/shard_map/ppermute | solution.py:72
  71.6 24.8 %collective-permute-start.15 = (f16[256,1536]{1,0:T(8,128)(2,1)S(1)}, f16[256,1536]{1,0:T(8,128)(2,1)S(1)}, u32[]{:S(2)}, u32[]{:S(2)}) collective-permute-start(f16[256,1536]{1,0:T(8,128)(2,1)S(1)} %fusion.8), channel_id=1, source_target_pairs={{0,4},{4,8},{1,5},{5,9},{2,6},{6,10},{3,7},{7,11},{16,20},{20,24},... | collective-permute-start | bytes 2359304 | tf_op jit(solution)/shard_map/ppermute | solution.py:74
  76.1 20.4 %collective-permute-start.17 = (f16[256,1536]{1,0:T(8,128)(2,1)S(1)}, f16[256,1536]{1,0:T(8,128)(2,1)S(1)}, u32[]{:S(2)}, u32[]{:S(2)}) collective-permute-start(f16[256,1536]{1,0:T(8,128)(2,1)S(1)} %fusion.8), channel_id=1, source_target_pairs={{12,8},{8,4},{13,9},{9,5},{14,10},{10,6},{15,11},{11,7},{28,24},{2... | collective-permute-start | bytes 2359304 | tf_op jit(solution)/shard_map/ppermute | solution.py:75
  79.0 19.2 %copy-start.7 = (f16[512,1536]{1,0:T(8,128)(2,1)}, f16[512,1536]{1,0:T(8,128)(2,1)S(1)}, u32[]{:S(2)}) copy-start(f16[512,1536]{1,0:T(8,128)(2,1)S(1)} %fusion) | copy-start | bytes 4718596
  79.8 26.0 %collective-permute-start.10 = (f16[256,768]{1,0:T(8,128)(2,1)S(1)}, f16[256,768]{1,0:T(8,128)(2,1)S(1)}, u32[]{:S(2)}, u32[]{:S(2)}) collective-permute-start(f16[256,768]{1,0:T(8,128)(2,1)S(1)} %fusion.11), channel_id=1, source_target_pairs={{0,4},{4,8},{1,5},{5,9},{2,6},{6,10},{3,7},{7,11},{16,20},{20,24},... | collective-permute-start | bytes 1179656 | tf_op jit(solution)/shard_map/ppermute | solution.py:74
  84.2 21.6 %collective-permute-start.12 = (f16[256,768]{1,0:T(8,128)(2,1)S(1)}, f16[256,768]{1,0:T(8,128)(2,1)S(1)}, u32[]{:S(2)}, u32[]{:S(2)}) collective-permute-start(f16[256,768]{1,0:T(8,128)(2,1)S(1)} %fusion.11), channel_id=1, source_target_pairs={{12,8},{8,4},{13,9},{9,5},{14,10},{10,6},{15,11},{11,7},{28,24},{2... | collective-permute-start | bytes 1179656 | tf_op jit(solution)/shard_map/ppermute | solution.py:75
  98.2 32.7 %collective-permute-start.18 = (f16[256,1536]{1,0:T(8,128)(2,1)}, f16[256,1536]{1,0:T(8,128)(2,1)}, u32[]{:S(2)}, u32[]{:S(2)}) collective-permute-start(f16[256,1536]{1,0:T(8,128)(2,1)} %get-tuple-element.25), channel_id=1, source_target_pairs={{12,8},{8,4},{4,0},{13,9},{9,5},{5,1},{14,10},{10,6},{6,2},{15,11}... | collective-permute-start | bytes 2359304 | tf_op jit(solution)/shard_map/ppermute | solution.py:79
  99.5 31.4 %collective-permute-start.16 = (f16[256,1536]{1,0:T(8,128)(2,1)}, f16[256,1536]{1,0:T(8,128)(2,1)}, u32[]{:S(2)}, u32[]{:S(2)}) collective-permute-start(f16[256,1536]{1,0:T(8,128)(2,1)} %get-tuple-element.24), channel_id=1, source_target_pairs={{0,4},{4,8},{8,12},{1,5},{5,9},{9,13},{2,6},{6,10},{10,14},{3,7},{... | collective-permute-start | bytes 2359304 | tf_op jit(solution)/shard_map/ppermute | solution.py:78
  106.8 21.4 %collective-permute-start.13 = (f16[256,768]{1,0:T(8,128)(2,1)}, f16[256,768]{1,0:T(8,128)(2,1)S(1)}, u32[]{:S(2)}, u32[]{:S(2)}) collective-permute-start(f16[256,768]{1,0:T(8,128)(2,1)} %get-tuple-element.27), channel_id=1, source_target_pairs={{12,8},{8,4},{4,0},{13,9},{9,5},{5,1},{14,10},{10,6},{6,2},{15,11}... | collective-permute-start | bytes 1179656 | tf_op jit(solution)/shard_map/ppermute | solution.py:79
  108.1 21.6 %collective-permute-start.11 = (f16[256,768]{1,0:T(8,128)(2,1)S(1)}, f16[256,768]{1,0:T(8,128)(2,1)}, u32[]{:S(2)}, u32[]{:S(2)}) collective-permute-start(f16[256,768]{1,0:T(8,128)(2,1)S(1)} %get-tuple-element.26), channel_id=1, source_target_pairs={{0,4},{4,8},{8,12},{1,5},{5,9},{9,13},{2,6},{6,10},{10,14},{3,7},{... | collective-permute-start | bytes 1179656 | tf_op jit(solution)/shard_map/ppermute | solution.py:78
  134.3 21.9 %collective-permute-start.19 = (bf16[256,768]{1,0:T(8,128)(2,1)S(1)}, bf16[256,768]{1,0:T(8,128)(2,1)}, u32[]{:S(2)}, u32[]{:S(2)}) collective-permute-start(bf16[256,768]{1,0:T(8,128)(2,1)S(1)} %get-tuple-element.14.key_ref), channel_id=1, source_target_pairs={{0,4},{4,0},{8,12},{12,8},{1,5},{5,1},{9,13},{13,9},{2,6},{6,2},{1... | collective-permute-start | bytes 1179656 | tf_op jit(solution)/shard_map/ppermute | solution.py:87
  137.0 19.3 %collective-permute-start.20 = (bf16[256,768]{1,0:T(8,128)(2,1)S(1)}, bf16[256,768]{1,0:T(8,128)(2,1)}, u32[]{:S(2)}, u32[]{:S(2)}) collective-permute-start(bf16[256,768]{1,0:T(8,128)(2,1)S(1)} %get-tuple-element.14.key_ref), channel_id=1, source_target_pairs={{4,8},{8,4},{5,9},{9,5},{6,10},{10,6},{7,11},{11,7},{20,24},{24,20... | collective-permute-start | bytes 1179656 | tf_op jit(solution)/shard_map/ppermute | solution.py:88
  138.4 17.9 %collective-permute-start.21 = (bf16[256,768]{1,0:T(8,128)(2,1)S(1)}, bf16[256,768]{1,0:T(8,128)(2,1)}, u32[]{:S(2)}, u32[]{:S(2)}) collective-permute-start(bf16[256,768]{1,0:T(8,128)(2,1)S(1)} %get-tuple-element.15.value_ref), channel_id=1, source_target_pairs={{0,4},{4,0},{8,12},{12,8},{1,5},{5,1},{9,13},{13,9},{2,6},{6,2},{1... | collective-permute-start | bytes 1179656 | tf_op jit(solution)/shard_map/ppermute | solution.py:87
  141.3 14.9 %collective-permute-start.22 = (bf16[256,768]{1,0:T(8,128)(2,1)S(1)}, bf16[256,768]{1,0:T(8,128)(2,1)S(1)}, u32[]{:S(2)}, u32[]{:S(2)}) collective-permute-start(bf16[256,768]{1,0:T(8,128)(2,1)S(1)} %get-tuple-element.15.value_ref), channel_id=1, source_target_pairs={{4,8},{8,4},{5,9},{9,5},{6,10},{10,6},{7,11},{11,7},{20,24},{24,20... | collective-permute-start | bytes 1179656 | tf_op jit(solution)/shard_map/ppermute | solution.py:88
  153.2 1.1 copy-start.1
  154.3 1.1 copy-start.3
  155.4 0.8 copy-start.5
  156.3 0.7 copy-start.9
  157.0 5.2 %collective-permute-start.25 = (bf16[256,1280]{1,0:T(8,128)(2,1)}, bf16[256,1280]{1,0:T(8,128)(2,1)S(1)}, u32[]{:S(2)}, u32[]{:S(2)}) collective-permute-start(bf16[256,1280]{1,0:T(8,128)(2,1)} %get-tuple-element.19), channel_id=1, source_target_pairs={{0,1},{1,0},{2,3},{3,2},{4,5},{5,4},{6,7},{7,6},{8,9},{9,8},{10,11... | collective-permute-start | bytes 1966088 | tf_op jit(solution)/shard_map/ppermute | solution.py:218
  157.0 2.9 %copy-start.10 = (bf16[256,768]{1,0:T(8,128)(2,1)S(1)}, bf16[256,768]{1,0:T(8,128)(2,1)}, u32[]{:S(2)}) copy-start(bf16[256,768]{1,0:T(8,128)(2,1)} %copy-done.9) | copy-start | bytes 1179652
  157.0 5.9 %copy-start.4 = (f32[256,1280]{1,0:T(8,128)S(1)}, f32[256,1280]{1,0:T(8,128)}, u32[]{:S(2)}) copy-start(f32[256,1280]{1,0:T(8,128)} %copy-done.3) | copy-start | bytes 3932164
  157.0 6.0 %collective-permute-start.23 = (bf16[256,1280]{1,0:T(8,128)(2,1)}, bf16[256,1280]{1,0:T(8,128)(2,1)S(1)}, u32[]{:S(2)}, u32[]{:S(2)}) collective-permute-start(bf16[256,1280]{1,0:T(8,128)(2,1)} %copy-done.5), channel_id=1, source_target_pairs={{0,1},{1,0},{2,3},{3,2},{4,5},{5,4},{6,7},{7,6},{8,9},{9,8},{10,11... | collective-permute-start | bytes 1966088 | tf_op jit(solution)/shard_map/ppermute | solution.py:218
  157.7 7.5 %copy-start.2 = (f32[256,1280]{1,0:T(8,128)S(1)}, f32[256,1280]{1,0:T(8,128)}, u32[]{:S(2)}) copy-start(f32[256,1280]{1,0:T(8,128)} %copy-done.1) | copy-start | bytes 3932164
  157.8 14.2 %collective-permute-start.27 = (bf16[256,768]{1,0:T(8,128)(2,1)}, bf16[256,768]{1,0:T(8,128)(2,1)S(1)}, u32[]{:S(2)}, u32[]{:S(2)}) collective-permute-start(bf16[256,768]{1,0:T(8,128)(2,1)} %collective-permute-done.20), channel_id=1, source_target_pairs={{4,0},{8,12},{5,1},{9,13},{6,2},{10,14},{7,3},{11,15},{20,16},{24,... | collective-permute-start | bytes 1179656 | tf_op jit(solution)/shard_map/ppermute | solution.py:96
  159.2 15.0 %collective-permute-start.28 = (bf16[256,768]{1,0:T(8,128)(2,1)}, bf16[256,768]{1,0:T(8,128)(2,1)S(1)}, u32[]{:S(2)}, u32[]{:S(2)}) collective-permute-start(bf16[256,768]{1,0:T(8,128)(2,1)} %collective-permute-done.19), channel_id=1, source_target_pairs={{4,8},{8,4},{5,9},{9,5},{6,10},{10,6},{7,11},{11,7},{20,24},{24,20... | collective-permute-start | bytes 1179656 | tf_op jit(solution)/shard_map/ppermute | solution.py:95
  159.9 30.1 %collective-permute-start.30 = (bf16[256,768]{1,0:T(8,128)(2,1)S(1)}, bf16[256,768]{1,0:T(8,128)(2,1)S(1)}, u32[]{:S(2)}, u32[]{:S(2)}) collective-permute-start(bf16[256,768]{1,0:T(8,128)(2,1)S(1)} %copy-done.10), channel_id=1, source_target_pairs={{4,0},{8,12},{5,1},{9,13},{6,2},{10,14},{7,3},{11,15},{20,16},{24,... | collective-permute-start | bytes 1179656 | tf_op jit(solution)/shard_map/ppermute | solution.py:96
  162.3 13.3 %collective-permute-start.31 = (bf16[256,768]{1,0:T(8,128)(2,1)}, bf16[256,768]{1,0:T(8,128)(2,1)S(1)}, u32[]{:S(2)}, u32[]{:S(2)}) collective-permute-start(bf16[256,768]{1,0:T(8,128)(2,1)} %collective-permute-done.21), channel_id=1, source_target_pairs={{4,8},{8,4},{5,9},{9,5},{6,10},{10,6},{7,11},{11,7},{20,24},{24,20... | collective-permute-start | bytes 1179656 | tf_op jit(solution)/shard_map/ppermute | solution.py:95
  163.1 13.8 %collective-permute-start.26 = (bf16[256,640]{1,0:T(8,128)(2,1)S(1)}, bf16[256,640]{1,0:T(8,128)(2,1)S(1)}, u32[]{:S(2)}, u32[]{:S(2)}) collective-permute-start(bf16[256,640]{1,0:T(8,128)(2,1)S(1)} %add_convert_fusion.7), channel_id=1, source_target_pairs={{0,2},{1,3},{2,0},{3,1},{4,6},{5,7},{6,4},{7,5},{8,10},{9,11},{10,... | collective-permute-start | bytes 983048 | tf_op jit(solution)/shard_map/ppermute | solution.py:229
  172.0 8.2 %collective-permute-start.24 = (bf16[256,640]{1,0:T(8,128)(2,1)S(1)}, bf16[256,640]{1,0:T(8,128)(2,1)S(1)}, u32[]{:S(2)}, u32[]{:S(2)}) collective-permute-start(bf16[256,640]{1,0:T(8,128)(2,1)S(1)} %add_convert_fusion.9), channel_id=1, source_target_pairs={{0,2},{1,3},{2,0},{3,1},{4,6},{5,7},{6,4},{7,5},{8,10},{9,11},{10,... | collective-permute-start | bytes 983048 | tf_op jit(solution)/shard_map/ppermute | solution.py:229
  174.2 14.6 %collective-permute-start.29 = (bf16[256,768]{1,0:T(8,128)(2,1)S(1)}, bf16[256,768]{1,0:T(8,128)(2,1)S(1)}, u32[]{:S(2)}, u32[]{:S(2)}) collective-permute-start(bf16[256,768]{1,0:T(8,128)(2,1)S(1)} %collective-permute-done.28), channel_id=1, source_target_pairs={{4,0},{8,12},{5,1},{9,13},{6,2},{10,14},{7,3},{11,15},{20,16},{24,... | collective-permute-start | bytes 1179656 | tf_op jit(solution)/shard_map/ppermute | solution.py:97
  175.5 20.8 %collective-permute-start.32 = (bf16[256,768]{1,0:T(8,128)(2,1)S(1)}, bf16[256,768]{1,0:T(8,128)(2,1)S(1)}, u32[]{:S(2)}, u32[]{:S(2)}) collective-permute-start(bf16[256,768]{1,0:T(8,128)(2,1)S(1)} %collective-permute-done.31), channel_id=1, source_target_pairs={{4,0},{8,12},{5,1},{9,13},{6,2},{10,14},{7,3},{11,15},{20,16},{24,... | collective-permute-start | bytes 1179656 | tf_op jit(solution)/shard_map/ppermute | solution.py:97
  196.4 1.7 copy-start.6

commit v11 on v10

--- a/solution.py
+++ b/solution.py
@@ -77,8 +77,7 @@
     third_down = plus(jnp.where(patch == 2, inner, mate), down)
     up = lax.ppermute(third_up, "patch", [(0, 1), (1, 2), (2, 3)])
     down = lax.ppermute(third_down, "patch", [(3, 2), (2, 1), (1, 0)])
-    total = own.astype(F32) + (up.astype(F32) + down.astype(F32))
-    return (total * (1.0 / LIFT)).astype(BF16)
+    return own, up, down
 
 
 class PairGather:
@@ -244,22 +243,28 @@
         if in_pairs:
             far, near = spread_in_pairs(hidden_in)
             both = sum_in_pairs(far, near, w_both)
-            query = sum_in_pairs(far, near, w_query)
+            query_own, *query_got = sum_in_pairs(far, near, w_query)
         else:
             features = spread_features(hidden_in)
-            both = sum_own_slab(features, w_both, patches)
+            both = (sum_own_slab(features, w_both, patches),)
             query = sum_own_slab(features, w_query, patches)
 
-        def refresh(fresh, stale):
-            fresh = lax.reduce_precision(fresh.astype(F32), 8, 7)
+        def total(parts, factor):
+            return functools.reduce(jnp.add, [part.astype(F32) for part in parts]) * factor
+
+        def refresh(parts, factor, stale):
+            fresh = lax.reduce_precision(total(parts, factor), 8, 7)
             stale = stale.astype(F32)
             return (stale + lax.reduce_precision(fresh - stale, 8, 7)).astype(BF16)
 
         width = w_key.shape[1]
-        key_new = refresh(both[:, :width], own_stale[0])
-        value_new = refresh(both[:, width:], own_stale[1])
+        factor = 1.0 / LIFT if in_pairs else 1.0
+        key_new = refresh([part[:, :width] for part in both], factor, own_stale[0])
+        value_new = refresh([part[:, width:] for part in both], factor, own_stale[1])
         if in_pairs:
-            keys, values = PairGather(after(key_new, query)), PairGather(after(value_new, query))
+            *query_got, key_new, value_new = lax.optimization_barrier((*query_got, key_new, value_new))
+            query = total((query_own, *query_got), factor).astype(BF16)
+            keys, values = PairGather(key_new), PairGather(value_new)
             first_hop = (keys.mate, keys.across, values.mate, values.across)
         else:
             first_hop = ()

time: 199 us -> 188 us (0.945)
  local copies, waits for them, and re-layouts: 15.4 us -> 9.06 us
  waiting for transfers between devices: 84.6 us -> 79.7 us
  starting transfers between devices: 69.3 us -> 72.2 us
  other arithmetic: 9.9 us -> 7.29 us
    ppermute x2, waiting for transfers between devices: 11.2 us -> 1.62 us  [both_slabs(): other = lax.ppermute(held, 'tensor', across)]
    ppermute x2, waiting for transfers between devices: 14.8 us -> 5.67 us  [sum_in_pairs(): down = lax.ppermute(third_down, 'patch', [(3, 2), (2, 1), (1, 0)])]
    ppermute x2, waiting for transfers between devices: 1.54 us -> 8.84 us  [sum_in_pairs(): up = lax.ppermute(third_up, 'patch', [(0, 1), (1, 2), (2, 3)])]
    ppermute x4, waiting for transfers between devices: 1.36 us -> 7.73 us  [along(): return lax.ppermute(block, ('patch', 'tensor'), pairs)]
    ppermute x2, starting transfers between devices: 6.46 us -> 10.1 us  [sum_in_pairs(): first = lax.ppermute(outermost, 'patch', [(0, 1), (3, 2)])]
    convert_element_type x2 -> x1, other arithmetic: 3.11 us -> 0.18 us  [shards(): query = total((query_own, *query_got), factor).astype(BF16)]
    concatenate x1, local copies, waits for them, and re-layouts: 3.03 us -> 0.15 us  [shards(): w_both = jnp.concatenate([w_key, w_value], axis=1)]
    ppermute x2, starting transfers between devices: 11.6 us -> 9.47 us  [sum_in_pairs(): up = lax.ppermute(third_up, 'patch', [(0, 1), (1, 2), (2, 3)])]
  transfers between devices with their start and end apart: 33 -> 33, of which waited for: 14 -> 15; matrix products, arithmetic and copies ran while one was open for 11% -> 9% of each run, Pallas kernels for 6% -> 6%
where the time goes in v11:
time: 188 us; the launch traced here: 187 us
  waiting for transfers between devices  79.7 us (42%)
  starting transfers between devices  72.2 us (38%)
  Pallas kernels  10.9 us (6%)
  local copies, waits for them, and re-layouts  9.06 us (5%)
  other arithmetic  7.29 us (4%)
  matrix products  6.77 us (4%)
    ppermute x2, waiting for transfers between devices, into(): last = lax.ppermute(after(across_mate, *earlier), 'patch', outward)  14.4 us
    ppermute x2, waiting for transfers between devices, sum_in_pairs(): first = lax.ppermute(outermost, 'patch', [(0, 1), (3, 2)])  13.1 us
    ppermute x2, waiting for transfers between devices, sum_in_pairs(): up = lax.ppermute(second, 'patch', [(0, 1), (1, 2)])  11.2 us
    pallas_call x1, Pallas kernels, attend(): pl.pallas_call(functools.partial(attend_and_project, patches, heads, chip...  10.9 us
    ppermute x2, starting transfers between devices, both_slabs(): other = lax.ppermute(held, 'tensor', across)  10.5 us
    ppermute x2, starting transfers between devices, sum_in_pairs(): first = lax.ppermute(outermost, 'patch', [(0, 1), (3, 2)])  10.1 us
    ppermute x2, starting transfers between devices, sum_in_pairs(): up = lax.ppermute(third_up, 'patch', [(0, 1), (1, 2), (2, 3)])  9.47 us
    ppermute x2, starting transfers between devices, sum_in_pairs(): up = lax.ppermute(second, 'patch', [(0, 1), (1, 2)])  9.45 us
  transfers between devices with their start and end apart: 33, of which 15 were waited for; matrix products, arithmetic and copies ran while one was open for 9% of the time, Pallas kernels for 6%

profile of v11, /device:TPU:0, one launch (start us, length us, event | category | flops | bytes accessed | tf_op | source)
XLA Modules:
  0.0 187.2 jit_solution(15077187485404543278)
XLA Ops:
  0.6 1.3 fusion.15
  1.9 3.0 %collective-permute-start.1 = (bf16[128,1280]{1,0:T(8,128)(2,1)S(1)}, bf16[128,1280]{1,0:T(8,128)(2,1)S(1)}, u32[]{:S(2)}, u32[]{:S(2)}) collective-permute-start(bf16[128,1280]{1,0:T(8,128)(2,1)S(1)} %get-tuple-element.36), channel_id=1, source_target_pairs={{0,2},{1,3},{2,0},{3,1},{4,6},{5,7},{6,4},{7,5},{8,10},{9,11},{10,... | collective-permute-start | bytes 983048 | tf_op jit(solution)/shard_map/ppermute | solution.py:31
  4.9 1.3 collective-permute-start.5
  6.2 6.4 %collective-permute-done.1 = bf16[128,1280]{1,0:T(8,128)(2,1)S(1)} collective-permute-done((bf16[128,1280]{1,0:T(8,128)(2,1)S(1)}, bf16[128,1280]{1,0:T(8,128)(2,1)S(1)}, u32[]{:S(2)}, u32[]{:S(2)}) %collective-permute-start.1) | collective-permute-done | bytes 327712 | tf_op jit(solution)/shard_map/ppermute | solution.py:31
  12.6 4.8 %collective-permute-start.6 = (bf16[128,1280]{1,0:T(8,128)(2,1)S(1)}, bf16[128,1280]{1,0:T(8,128)(2,1)S(1)}, u32[]{:S(2)}, u32[]{:S(2)}) collective-permute-start(bf16[128,1280]{1,0:T(8,128)(2,1)S(1)} %collective-permute-done.1), channel_id=1, source_target_pairs={{0,8},{1,12},{4,9},{5,13},{10,2},{11,6},{14,3},{15,7},{16,24},{17,... | collective-permute-start | bytes 983048 | tf_op jit(solution)/shard_map/ppermute | solution.py:41
  17.4 7.4 %collective-permute-done.5 = bf16[128,1280]{1,0:T(8,128)(2,1)S(1)} collective-permute-done((bf16[128,1280]{1,0:T(8,128)(2,1)S(1)}, bf16[128,1280]{1,0:T(8,128)(2,1)S(1)}, u32[]{:S(2)}, u32[]{:S(2)}) %collective-permute-start.5) | collective-permute-done | bytes 327712 | tf_op jit(solution)/shard_map/ppermute | solution.py:41
  24.8 0.3 collective-permute-done.6
  25.2 8.7 %collective-permute-start.7 = (bf16[128,1280]{1,0:T(8,128)(2,1)S(1)}, bf16[128,1280]{1,0:T(8,128)(2,1)S(1)}, u32[]{:S(2)}, u32[]{:S(2)}) collective-permute-start(bf16[128,1280]{1,0:T(8,128)(2,1)S(1)} %broadcast_select_fusion.2), channel_id=1, source_target_pairs={{0,2},{1,3},{2,0},{3,1},{4,6},{5,7},{6,4},{7,5},{8,10},{9,11},{10,... | collective-permute-start | bytes 983048 | tf_op jit(solution)/shard_map/ppermute | solution.py:45
  33.9 0.7 collective-permute-start
  34.7 1.7 constant_dynamic-update-slice_fusion.1
  36.5 0.8 collective-permute-start.2
  37.3 1.6 collective-permute-done.7
  39.0 0.3 collective-permute-start.8
  39.6 1.8 collective-permute-start.3
  41.4 2.2 %fusion.1 = f16[512,1536]{1,0:T(8,128)(2,1)S(1)} fusion(bf16[1280,1536]{1,0:T(8,128)(2,1)S(1)} %constant_dynamic-update-slice_fusion, bf16[256,1280]{1,0:T(8,128)(2,1)S(1)} %collective-permute-done.8, bf16[128,1280]{1,0:T(8,128)(2,1)S(1)} %get-tuple-element.35, bf16[128,1280]{1,0:T(8,128)(2,1)S(1)} %get-tuple-element.34), kind=kOutput, calls=%fused_computation.3 | convolution fusion | flops 2018770944 | bytes 6815744 | tf_op jit(solution)/shard_map/dot_general | solution.py:60
  43.8 6.2 %collective-permute-start.14 = (f16[256,1536]{1,0:T(8,128)(2,1)S(1)}, f16[256,1536]{1,0:T(8,128)(2,1)S(1)}, u32[]{:S(2)}, u32[]{:S(2)}) collective-permute-start(f16[256,1536]{1,0:T(8,128)(2,1)S(1)} %dynamic-slice_bitcast_fusion), channel_id=1, source_target_pairs={{0,4},{12,8},{1,5},{13,9},{2,6},{14,10},{3,7},{15,11},{16,20},{28,... | collective-permute-start | bytes 2359304 | tf_op jit(solution)/shard_map/ppermute | solution.py:72
  50.2 1.2 multiply_convert_fusion
  51.5 3.9 %collective-permute-start.9 = (f16[256,768]{1,0:T(8,128)(2,1)S(1)}, f16[256,768]{1,0:T(8,128)(2,1)S(1)}, u32[]{:S(2)}, u32[]{:S(2)}) collective-permute-start(f16[256,768]{1,0:T(8,128)(2,1)S(1)} %dynamic-slice_bitcast_fusion.4), channel_id=1, source_target_pairs={{0,4},{12,8},{1,5},{13,9},{2,6},{14,10},{3,7},{15,11},{16,20},{28,... | collective-permute-start | bytes 1179656 | tf_op jit(solution)/shard_map/ppermute | solution.py:72
  55.4 12.5 %collective-permute-done.14 = f16[256,1536]{1,0:T(8,128)(2,1)S(1)} collective-permute-done((f16[256,1536]{1,0:T(8,128)(2,1)S(1)}, f16[256,1536]{1,0:T(8,128)(2,1)S(1)}, u32[]{:S(2)}, u32[]{:S(2)}) %collective-permute-start.14) | collective-permute-done | bytes 786464 | tf_op jit(solution)/shard_map/ppermute | solution.py:72
  67.9 0.4 fusion.6
  68.3 4.4 %collective-permute-start.15 = (f16[256,1536]{1,0:T(8,128)(2,1)S(1)}, f16[256,1536]{1,0:T(8,128)(2,1)S(1)}, u32[]{:S(2)}, u32[]{:S(2)}) collective-permute-start(f16[256,1536]{1,0:T(8,128)(2,1)S(1)} %fusion.6), channel_id=1, source_target_pairs={{0,4},{4,8},{1,5},{5,9},{2,6},{6,10},{3,7},{7,11},{16,20},{20,24},... | collective-permute-start | bytes 2359304 | tf_op jit(solution)/shard_map/ppermute | solution.py:74
  72.8 0.7 collective-permute-start.17
  73.5 2.2 %fusion = f16[512,1536]{1,0:T(8,128)(2,1)S(1)} fusion(bf16[1280,1536]{1,0:T(8,128)(2,1)S(1)} %constant_dynamic-update-slice_fusion, bf16[256,1280]{1,0:T(8,128)(2,1)S(1)} %collective-permute-done.4, bf16[128,1280]{1,0:T(8,128)(2,1)S(1)} %get-tuple-element.33, bf16[128,1280]{1,0:T(8,128)(2,1)S(1)} %get-tuple-element.32), kind=kOutput, calls=%fused_computation.2 | convolution fusion | flops 2018770944 | bytes 6815744 | tf_op jit(solution)/shard_map/dot_general | solution.py:60
  75.7 0.6 collective-permute-done.9
  76.5 0.7 collective-permute-start.12
  77.2 5.0 %collective-permute-start.10 = (f16[256,768]{1,0:T(8,128)(2,1)S(1)}, f16[256,768]{1,0:T(8,128)(2,1)S(1)}, u32[]{:S(2)}, u32[]{:S(2)}) collective-permute-start(f16[256,768]{1,0:T(8,128)(2,1)S(1)} %fusion.10), channel_id=1, source_target_pairs={{0,4},{4,8},{1,5},{5,9},{2,6},{6,10},{3,7},{7,11},{16,20},{20,24},... | collective-permute-start | bytes 1179656 | tf_op jit(solution)/shard_map/ppermute | solution.py:74
  82.2 11.0 %collective-permute-done.15 = f16[256,1536]{1,0:T(8,128)(2,1)S(1)} collective-permute-done((f16[256,1536]{1,0:T(8,128)(2,1)S(1)}, f16[256,1536]{1,0:T(8,128)(2,1)S(1)}, u32[]{:S(2)}, u32[]{:S(2)}) %collective-permute-start.15) | collective-permute-done | bytes 786464 | tf_op jit(solution)/shard_map/ppermute | solution.py:74
  93.2 0.6 add_convert_fusion.1
  93.8 1.3 collective-permute-start.18
  95.1 5.1 %collective-permute-start.16 = (f16[256,1536]{1,0:T(8,128)(2,1)S(1)}, f16[256,1536]{1,0:T(8,128)(2,1)S(1)}, u32[]{:S(2)}, u32[]{:S(2)}) collective-permute-start(f16[256,1536]{1,0:T(8,128)(2,1)S(1)} %get-tuple-element.28), channel_id=1, source_target_pairs={{0,4},{4,8},{8,12},{1,5},{5,9},{9,13},{2,6},{6,10},{10,14},{3,7},{... | collective-permute-start | bytes 2359304 | tf_op jit(solution)/shard_map/ppermute | solution.py:78
  100.1 1.2 multiply_convert_fusion.1
  101.3 0.3 collective-permute-done.10
  101.6 0.3 add_convert_fusion.3
  101.9 4.4 %collective-permute-start.11 = (f16[256,768]{1,0:T(8,128)(2,1)S(1)}, f16[256,768]{1,0:T(8,128)(2,1)S(1)}, u32[]{:S(2)}, u32[]{:S(2)}) collective-permute-start(f16[256,768]{1,0:T(8,128)(2,1)S(1)} %get-tuple-element.31), channel_id=1, source_target_pairs={{0,4},{4,8},{8,12},{1,5},{5,9},{9,13},{2,6},{6,10},{10,14},{3,7},{... | collective-permute-start | bytes 1179656 | tf_op jit(solution)/shard_map/ppermute | solution.py:78
  106.3 1.3 collective-permute-start.13
  107.8 5.7 %collective-permute-done.18 = f16[256,1536]{1,0:T(8,128)(2,1)S(1)} collective-permute-done((f16[256,1536]{1,0:T(8,128)(2,1)S(1)}, f16[256,1536]{1,0:T(8,128)(2,1)S(1)}, u32[]{:S(2)}, u32[]{:S(2)}) %collective-permute-start.18) | collective-permute-done | bytes 786464 | tf_op jit(solution)/shard_map/ppermute | solution.py:79
  113.4 5.0 %collective-permute-done.16 = f16[256,1536]{1,0:T(8,128)(2,1)S(1)} collective-permute-done((f16[256,1536]{1,0:T(8,128)(2,1)S(1)}, f16[256,1536]{1,0:T(8,128)(2,1)S(1)}, u32[]{:S(2)}, u32[]{:S(2)}) %collective-permute-start.16) | collective-permute-done | bytes 786464 | tf_op jit(solution)/shard_map/ppermute | solution.py:78
  118.5 1.8 fusion.5
  120.2 3.8 %collective-permute-done.11 = f16[256,768]{1,0:T(8,128)(2,1)S(1)} collective-permute-done((f16[256,768]{1,0:T(8,128)(2,1)S(1)}, f16[256,768]{1,0:T(8,128)(2,1)S(1)}, u32[]{:S(2)}, u32[]{:S(2)}) %collective-permute-start.11) | collective-permute-done | bytes 393248 | tf_op jit(solution)/shard_map/ppermute | solution.py:78
  124.0 2.6 %collective-permute-start.19 = (bf16[256,768]{1,0:T(8,128)(2,1)S(1)}, bf16[256,768]{1,0:T(8,128)(2,1)S(1)}, u32[]{:S(2)}, u32[]{:S(2)}) collective-permute-start(bf16[256,768]{1,0:T(8,128)(2,1)S(1)} %get-tuple-element.16.key_ref), channel_id=1, source_target_pairs={{0,4},{4,0},{8,12},{12,8},{1,5},{5,1},{9,13},{13,9},{2,6},{6,2},{1... | collective-permute-start | bytes 1179656 | tf_op jit(solution)/shard_map/ppermute | solution.py:86
  126.6 0.7 collective-permute-start.20
  127.3 2.7 %collective-permute-start.21 = (bf16[256,768]{1,0:T(8,128)(2,1)S(1)}, bf16[256,768]{1,0:T(8,128)(2,1)S(1)}, u32[]{:S(2)}, u32[]{:S(2)}) collective-permute-start(bf16[256,768]{1,0:T(8,128)(2,1)S(1)} %get-tuple-element.17.value_ref), channel_id=1, source_target_pairs={{0,4},{4,0},{8,12},{12,8},{1,5},{5,1},{9,13},{13,9},{2,6},{6,2},{1... | collective-permute-start | bytes 1179656 | tf_op jit(solution)/shard_map/ppermute | solution.py:86
  129.9 0.9 collective-permute-start.22
  131.0 10.9 %shard_map.77 = (bf16[256,1280]{1,0:T(8,128)(2,1)S(1)}, bf16[256,1280]{1,0:T(8,128)(2,1)}, f32[256,1280]{1,0:T(8,128)S(1)}, f32[256,1280]{1,0:T(8,128)S(1)}) custom-call(s32[5]{0:T(128)S(1)} %stack.23.place_ref, bf16[256,768]{1,0:T(8,128)(2,1)S(1)} %fusion.9.query_ref, bf16[2,1024,768]{2,1,0:T(8,128)(2,1)} %stale_ref.1, ...), custom_call_target="tpu_custom_call" | custom-call | flops 2818572288 | bytes 14942208 | tf_op jit(solution)/shard_map/pallas_call | solution.py:192
  141.9 1.1 copy-done.1
  143.0 1.1 copy-done.3
  144.1 0.8 copy-done.7
  145.3 0.6 collective-permute-start.23
  146.3 1.4 collective-permute-start.27
  147.7 0.7 collective-permute-start.28
  148.4 1.3 collective-permute-start.30
  149.8 0.7 collective-permute-start.31
  150.5 1.0 add_convert_fusion.7
  151.5 1.9 collective-permute-start.26
  153.5 6.9 %collective-permute-done.27 = bf16[256,768]{1,0:T(8,128)(2,1)S(1)} collective-permute-done((bf16[256,768]{1,0:T(8,128)(2,1)S(1)}, bf16[256,768]{1,0:T(8,128)(2,1)S(1)}, u32[]{:S(2)}, u32[]{:S(2)}) %collective-permute-start.27) | collective-permute-done | bytes 393248 | tf_op jit(solution)/shard_map/ppermute | solution.py:95
  160.4 1.8 collective-permute-start.24
  162.3 1.3 collective-permute-start.29
  163.6 1.3 collective-permute-start.32
  164.9 1.1 add_convert_fusion.6
  166.0 3.7 %collective-permute-done.24 = bf16[256,640]{1,0:T(8,128)(2,1)S(1)} collective-permute-done((bf16[256,640]{1,0:T(8,128)(2,1)S(1)}, bf16[256,640]{1,0:T(8,128)(2,1)S(1)}, u32[]{:S(2)}, u32[]{:S(2)}) %collective-permute-start.24) | collective-permute-done | bytes 327712 | tf_op jit(solution)/shard_map/ppermute | solution.py:228
  169.9 0.9 pad_maximum_fusion.4
  170.8 6.5 %collective-permute-done.29 = bf16[256,768]{1,0:T(8,128)(2,1)S(1)} collective-permute-done((bf16[256,768]{1,0:T(8,128)(2,1)S(1)}, bf16[256,768]{1,0:T(8,128)(2,1)S(1)}, u32[]{:S(2)}, u32[]{:S(2)}) %collective-permute-start.29) | collective-permute-done | bytes 393248 | tf_op jit(solution)/shard_map/ppermute | solution.py:96
  177.6 7.9 %collective-permute-done.32 = bf16[256,768]{1,0:T(8,128)(2,1)S(1)} collective-permute-done((bf16[256,768]{1,0:T(8,128)(2,1)S(1)}, bf16[256,768]{1,0:T(8,128)(2,1)S(1)}, u32[]{:S(2)}, u32[]{:S(2)}) %collective-permute-start.32) | collective-permute-done | bytes 393248 | tf_op jit(solution)/shard_map/ppermute | solution.py:96
  185.6 1.7 copy-done.5
  (74 shorter events, 2.8 us)
Async XLA Ops:
  0.6 49.6 %copy-start = (bf16[1280,768]{1,0:T(8,128)(2,1)S(1)}, bf16[1280,768]{1,0:T(8,128)(2,1)}, u32[]{:S(2)}) copy-start(bf16[1280,768]{1,0:T(8,128)(2,1)} %param.7) | copy-start | bytes 5898244
  1.9 10.7 %collective-permute-start.1 = (bf16[128,1280]{1,0:T(8,128)(2,1)S(1)}, bf16[128,1280]{1,0:T(8,128)(2,1)S(1)}, u32[]{:S(2)}, u32[]{:S(2)}) collective-permute-start(bf16[128,1280]{1,0:T(8,128)(2,1)S(1)} %get-tuple-element.36), channel_id=1, source_target_pairs={{0,2},{1,3},{2,0},{3,1},{4,6},{5,7},{6,4},{7,5},{8,10},{9,11},{10,... | collective-permute-start | bytes 983048 | tf_op jit(solution)/shard_map/ppermute | solution.py:31
  4.9 19.9 %collective-permute-start.5 = (bf16[128,1280]{1,0:T(8,128)(2,1)S(1)}, bf16[128,1280]{1,0:T(8,128)(2,1)S(1)}, u32[]{:S(2)}, u32[]{:S(2)}) collective-permute-start(bf16[128,1280]{1,0:T(8,128)(2,1)S(1)} %get-tuple-element.37), channel_id=1, source_target_pairs={{2,10},{3,14},{6,11},{7,15},{8,0},{9,4},{12,1},{13,5},{18,26},{19,... | collective-permute-start | bytes 983048 | tf_op jit(solution)/shard_map/ppermute | solution.py:41
  12.6 12.2 %copy-start.15 = (bf16[128,1280]{1,0:T(8,128)(2,1)}, bf16[128,1280]{1,0:T(8,128)(2,1)S(1)}, u32[]{:S(2)}) copy-start(bf16[128,1280]{1,0:T(8,128)(2,1)S(1)} %collective-permute-done.1) | copy-start | bytes 983044
  12.6 12.5 %collective-permute-start.6 = (bf16[128,1280]{1,0:T(8,128)(2,1)S(1)}, bf16[128,1280]{1,0:T(8,128)(2,1)S(1)}, u32[]{:S(2)}, u32[]{:S(2)}) collective-permute-start(bf16[128,1280]{1,0:T(8,128)(2,1)S(1)} %collective-permute-done.1), channel_id=1, source_target_pairs={{0,8},{1,12},{4,9},{5,13},{10,2},{11,6},{14,3},{15,7},{16,24},{17,... | collective-permute-start | bytes 983048 | tf_op jit(solution)/shard_map/ppermute | solution.py:41
  25.2 13.7 %collective-permute-start.7 = (bf16[128,1280]{1,0:T(8,128)(2,1)S(1)}, bf16[128,1280]{1,0:T(8,128)(2,1)S(1)}, u32[]{:S(2)}, u32[]{:S(2)}) collective-permute-start(bf16[128,1280]{1,0:T(8,128)(2,1)S(1)} %broadcast_select_fusion.2), channel_id=1, source_target_pairs={{0,2},{1,3},{2,0},{3,1},{4,6},{5,7},{6,4},{7,5},{8,10},{9,11},{10,... | collective-permute-start | bytes 983048 | tf_op jit(solution)/shard_map/ppermute | solution.py:45
  33.9 5.6 %collective-permute-start = (bf16[128,1280]{1,0:T(8,128)(2,1)S(1)}, bf16[128,1280]{1,0:T(8,128)(2,1)S(1)}, u32[]{:S(2)}, u32[]{:S(2)}) collective-permute-start(bf16[128,1280]{1,0:T(8,128)(2,1)S(1)} %get-tuple-element.37), channel_id=1, source_target_pairs={{0,0},{1,4},{4,1},{5,5},{10,10},{11,14},{14,11},{15,15},{16,16},{1... | collective-permute-start | bytes 983048 | tf_op jit(solution)/shard_map/ppermute | solution.py:41
  34.7 1.8 copy-start.16
  36.5 2.9 %copy-start.6 = (bf16[1280,768]{1,0:T(8,128)(2,1)S(1)}, bf16[1280,768]{1,0:T(8,128)(2,1)}, u32[]{:S(2)}) copy-start(bf16[1280,768]{1,0:T(8,128)(2,1)} %param.9) | copy-start | bytes 5898244
  36.5 3.0 %collective-permute-start.2 = (bf16[128,1280]{1,0:T(8,128)(2,1)S(1)}, bf16[128,1280]{1,0:T(8,128)(2,1)S(1)}, u32[]{:S(2)}, u32[]{:S(2)}) collective-permute-start(bf16[128,1280]{1,0:T(8,128)(2,1)S(1)} %copy-done.16), channel_id=1, source_target_pairs={{2,2},{3,6},{6,3},{7,7},{8,8},{9,12},{12,9},{13,13},{18,18},{19,22... | collective-permute-start | bytes 983048 | tf_op jit(solution)/shard_map/ppermute | solution.py:41
  39.0 2.4 %collective-permute-start.8 = (bf16[256,1280]{1,0:T(8,128)(2,1)S(1)}, bf16[256,1280]{1,0:T(8,128)(2,1)S(1)}, u32[]{:S(2)}, u32[]{:S(2)}) collective-permute-start(bf16[256,1280]{1,0:T(8,128)(2,1)S(1)} %pad_maximum_fusion.3), channel_id=1, source_target_pairs={{0,1},{1,0},{2,3},{3,2},{4,5},{5,4},{6,7},{7,6},{8,9},{9,8},{10,11... | collective-permute-start | bytes 1966088 | tf_op jit(solution)/shard_map/ppermute | solution.py:49
  39.6 10.4 %collective-permute-start.3 = (bf16[128,1280]{1,0:T(8,128)(2,1)S(1)}, bf16[128,1280]{1,0:T(8,128)(2,1)S(1)}, u32[]{:S(2)}, u32[]{:S(2)}) collective-permute-start(bf16[128,1280]{1,0:T(8,128)(2,1)S(1)} %broadcast_select_fusion.5), channel_id=1, source_target_pairs={{0,2},{1,3},{2,0},{3,1},{4,6},{5,7},{6,4},{7,5},{8,10},{9,11},{10,... | collective-permute-start | bytes 983048 | tf_op jit(solution)/shard_map/ppermute | solution.py:45
  43.8 24.1 %collective-permute-start.14 = (f16[256,1536]{1,0:T(8,128)(2,1)S(1)}, f16[256,1536]{1,0:T(8,128)(2,1)S(1)}, u32[]{:S(2)}, u32[]{:S(2)}) collective-permute-start(f16[256,1536]{1,0:T(8,128)(2,1)S(1)} %dynamic-slice_bitcast_fusion), channel_id=1, source_target_pairs={{0,4},{12,8},{1,5},{13,9},{2,6},{14,10},{3,7},{15,11},{16,20},{28,... | collective-permute-start | bytes 2359304 | tf_op jit(solution)/shard_map/ppermute | solution.py:72
  50.1 23.4 %collective-permute-start.4 = (bf16[256,1280]{1,0:T(8,128)(2,1)S(1)}, bf16[256,1280]{1,0:T(8,128)(2,1)S(1)}, u32[]{:S(2)}, u32[]{:S(2)}) collective-permute-start(bf16[256,1280]{1,0:T(8,128)(2,1)S(1)} %pad_maximum_fusion.2), channel_id=1, source_target_pairs={{0,1},{1,0},{2,3},{3,2},{4,5},{5,4},{6,7},{7,6},{8,9},{9,8},{10,11... | collective-permute-start | bytes 1966088 | tf_op jit(solution)/shard_map/ppermute | solution.py:49
  51.5 24.8 %collective-permute-start.9 = (f16[256,768]{1,0:T(8,128)(2,1)S(1)}, f16[256,768]{1,0:T(8,128)(2,1)S(1)}, u32[]{:S(2)}, u32[]{:S(2)}) collective-permute-start(f16[256,768]{1,0:T(8,128)(2,1)S(1)} %dynamic-slice_bitcast_fusion.4), channel_id=1, source_target_pairs={{0,4},{12,8},{1,5},{13,9},{2,6},{14,10},{3,7},{15,11},{16,20},{28,... | collective-permute-start | bytes 1179656 | tf_op jit(solution)/shard_map/ppermute | solution.py:72
  68.3 24.8 %collective-permute-start.15 = (f16[256,1536]{1,0:T(8,128)(2,1)S(1)}, f16[256,1536]{1,0:T(8,128)(2,1)S(1)}, u32[]{:S(2)}, u32[]{:S(2)}) collective-permute-start(f16[256,1536]{1,0:T(8,128)(2,1)S(1)} %fusion.6), channel_id=1, source_target_pairs={{0,4},{4,8},{1,5},{5,9},{2,6},{6,10},{3,7},{7,11},{16,20},{20,24},... | collective-permute-start | bytes 2359304 | tf_op jit(solution)/shard_map/ppermute | solution.py:74
  72.8 20.4 %collective-permute-start.17 = (f16[256,1536]{1,0:T(8,128)(2,1)S(1)}, f16[256,1536]{1,0:T(8,128)(2,1)S(1)}, u32[]{:S(2)}, u32[]{:S(2)}) collective-permute-start(f16[256,1536]{1,0:T(8,128)(2,1)S(1)} %fusion.6), channel_id=1, source_target_pairs={{12,8},{8,4},{13,9},{9,5},{14,10},{10,6},{15,11},{11,7},{28,24},{2... | collective-permute-start | bytes 2359304 | tf_op jit(solution)/shard_map/ppermute | solution.py:75
  76.5 24.8 %collective-permute-start.12 = (f16[256,768]{1,0:T(8,128)(2,1)S(1)}, f16[256,768]{1,0:T(8,128)(2,1)S(1)}, u32[]{:S(2)}, u32[]{:S(2)}) collective-permute-start(f16[256,768]{1,0:T(8,128)(2,1)S(1)} %fusion.10), channel_id=1, source_target_pairs={{12,8},{8,4},{13,9},{9,5},{14,10},{10,6},{15,11},{11,7},{28,24},{2... | collective-permute-start | bytes 1179656 | tf_op jit(solution)/shard_map/ppermute | solution.py:75
  77.2 24.4 %collective-permute-start.10 = (f16[256,768]{1,0:T(8,128)(2,1)S(1)}, f16[256,768]{1,0:T(8,128)(2,1)S(1)}, u32[]{:S(2)}, u32[]{:S(2)}) collective-permute-start(f16[256,768]{1,0:T(8,128)(2,1)S(1)} %fusion.10), channel_id=1, source_target_pairs={{0,4},{4,8},{1,5},{5,9},{2,6},{6,10},{3,7},{7,11},{16,20},{20,24},... | collective-permute-start | bytes 1179656 | tf_op jit(solution)/shard_map/ppermute | solution.py:74
  93.8 19.7 %collective-permute-start.18 = (f16[256,1536]{1,0:T(8,128)(2,1)S(1)}, f16[256,1536]{1,0:T(8,128)(2,1)S(1)}, u32[]{:S(2)}, u32[]{:S(2)}) collective-permute-start(f16[256,1536]{1,0:T(8,128)(2,1)S(1)} %get-tuple-element.29), channel_id=1, source_target_pairs={{12,8},{8,4},{4,0},{13,9},{9,5},{5,1},{14,10},{10,6},{6,2},{15,11}... | collective-permute-start | bytes 2359304 | tf_op jit(solution)/shard_map/ppermute | solution.py:79
  95.1 23.4 %collective-permute-start.16 = (f16[256,1536]{1,0:T(8,128)(2,1)S(1)}, f16[256,1536]{1,0:T(8,128)(2,1)S(1)}, u32[]{:S(2)}, u32[]{:S(2)}) collective-permute-start(f16[256,1536]{1,0:T(8,128)(2,1)S(1)} %get-tuple-element.28), channel_id=1, source_target_pairs={{0,4},{4,8},{8,12},{1,5},{5,9},{9,13},{2,6},{6,10},{10,14},{3,7},{... | collective-permute-start | bytes 2359304 | tf_op jit(solution)/shard_map/ppermute | solution.py:78
  101.9 22.1 %collective-permute-start.11 = (f16[256,768]{1,0:T(8,128)(2,1)S(1)}, f16[256,768]{1,0:T(8,128)(2,1)S(1)}, u32[]{:S(2)}, u32[]{:S(2)}) collective-permute-start(f16[256,768]{1,0:T(8,128)(2,1)S(1)} %get-tuple-element.31), channel_id=1, source_target_pairs={{0,4},{4,8},{8,12},{1,5},{5,9},{9,13},{2,6},{6,10},{10,14},{3,7},{... | collective-permute-start | bytes 1179656 | tf_op jit(solution)/shard_map/ppermute | solution.py:78
  106.3 17.7 %collective-permute-start.13 = (f16[256,768]{1,0:T(8,128)(2,1)S(1)}, f16[256,768]{1,0:T(8,128)(2,1)S(1)}, u32[]{:S(2)}, u32[]{:S(2)}) collective-permute-start(f16[256,768]{1,0:T(8,128)(2,1)S(1)} %get-tuple-element.30), channel_id=1, source_target_pairs={{12,8},{8,4},{4,0},{13,9},{9,5},{5,1},{14,10},{10,6},{6,2},{15,11}... | collective-permute-start | bytes 1179656 | tf_op jit(solution)/shard_map/ppermute | solution.py:79
  124.0 20.1 %collective-permute-start.19 = (bf16[256,768]{1,0:T(8,128)(2,1)S(1)}, bf16[256,768]{1,0:T(8,128)(2,1)S(1)}, u32[]{:S(2)}, u32[]{:S(2)}) collective-permute-start(bf16[256,768]{1,0:T(8,128)(2,1)S(1)} %get-tuple-element.16.key_ref), channel_id=1, source_target_pairs={{0,4},{4,0},{8,12},{12,8},{1,5},{5,1},{9,13},{13,9},{2,6},{6,2},{1... | collective-permute-start | bytes 1179656 | tf_op jit(solution)/shard_map/ppermute | solution.py:86
  126.6 17.5 %collective-permute-start.20 = (bf16[256,768]{1,0:T(8,128)(2,1)S(1)}, bf16[256,768]{1,0:T(8,128)(2,1)S(1)}, u32[]{:S(2)}, u32[]{:S(2)}) collective-permute-start(bf16[256,768]{1,0:T(8,128)(2,1)S(1)} %get-tuple-element.16.key_ref), channel_id=1, source_target_pairs={{4,8},{8,4},{5,9},{9,5},{6,10},{10,6},{7,11},{11,7},{20,24},{24,20... | collective-permute-start | bytes 1179656 | tf_op jit(solution)/shard_map/ppermute | solution.py:87
  127.3 16.8 %collective-permute-start.21 = (bf16[256,768]{1,0:T(8,128)(2,1)S(1)}, bf16[256,768]{1,0:T(8,128)(2,1)S(1)}, u32[]{:S(2)}, u32[]{:S(2)}) collective-permute-start(bf16[256,768]{1,0:T(8,128)(2,1)S(1)} %get-tuple-element.17.value_ref), channel_id=1, source_target_pairs={{0,4},{4,0},{8,12},{12,8},{1,5},{5,1},{9,13},{13,9},{2,6},{6,2},{1... | collective-permute-start | bytes 1179656 | tf_op jit(solution)/shard_map/ppermute | solution.py:86
  129.9 14.2 %collective-permute-start.22 = (bf16[256,768]{1,0:T(8,128)(2,1)S(1)}, bf16[256,768]{1,0:T(8,128)(2,1)S(1)}, u32[]{:S(2)}, u32[]{:S(2)}) collective-permute-start(bf16[256,768]{1,0:T(8,128)(2,1)S(1)} %get-tuple-element.17.value_ref), channel_id=1, source_target_pairs={{4,8},{8,4},{5,9},{9,5},{6,10},{10,6},{7,11},{11,7},{20,24},{24,20... | collective-permute-start | bytes 1179656 | tf_op jit(solution)/shard_map/ppermute | solution.py:87
  141.9 1.1 copy-start.1
  143.0 1.1 copy-start.3
  144.1 0.9 copy-start.11
  144.1 1.0 copy-start.13
  144.1 1.1 copy-start.9
  144.1 0.8 copy-start.7
  145.3 4.5 %collective-permute-start.25 = (bf16[256,1280]{1,0:T(8,128)(2,1)}, bf16[256,1280]{1,0:T(8,128)(2,1)}, u32[]{:S(2)}, u32[]{:S(2)}) collective-permute-start(bf16[256,1280]{1,0:T(8,128)(2,1)} %get-tuple-element.23), channel_id=1, source_target_pairs={{0,1},{1,0},{2,3},{3,2},{4,5},{5,4},{6,7},{7,6},{8,9},{9,8},{10,11... | collective-permute-start | bytes 1966088 | tf_op jit(solution)/shard_map/ppermute | solution.py:217
  145.3 1.0 copy-start.14
  145.3 2.4 %copy-start.12 = (bf16[256,768]{1,0:T(8,128)(2,1)S(1)}, bf16[256,768]{1,0:T(8,128)(2,1)}, u32[]{:S(2)}) copy-start(bf16[256,768]{1,0:T(8,128)(2,1)} %copy-done.11) | copy-start | bytes 1179652
  145.3 3.1 %copy-start.8 = (bf16[256,768]{1,0:T(8,128)(2,1)S(1)}, bf16[256,768]{1,0:T(8,128)(2,1)}, u32[]{:S(2)}) copy-start(bf16[256,768]{1,0:T(8,128)(2,1)} %copy-done.7) | copy-start | bytes 1179652
  145.3 4.5 %copy-start.10 = (bf16[256,768]{1,0:T(8,128)(2,1)S(1)}, bf16[256,768]{1,0:T(8,128)(2,1)}, u32[]{:S(2)}) copy-start(bf16[256,768]{1,0:T(8,128)(2,1)} %copy-done.9) | copy-start | bytes 1179652
  145.3 5.2 %copy-start.4 = (f32[256,1280]{1,0:T(8,128)S(1)}, f32[256,1280]{1,0:T(8,128)}, u32[]{:S(2)}) copy-start(f32[256,1280]{1,0:T(8,128)} %copy-done.3) | copy-start | bytes 3932164
  145.3 6.2 %collective-permute-start.23 = (bf16[256,1280]{1,0:T(8,128)(2,1)S(1)}, bf16[256,1280]{1,0:T(8,128)(2,1)S(1)}, u32[]{:S(2)}, u32[]{:S(2)}) collective-permute-start(bf16[256,1280]{1,0:T(8,128)(2,1)S(1)} %get-tuple-element.20), channel_id=1, source_target_pairs={{0,1},{1,0},{2,3},{3,2},{4,5},{5,4},{6,7},{7,6},{8,9},{9,8},{10,11... | collective-permute-start | bytes 1966088 | tf_op jit(solution)/shard_map/ppermute | solution.py:217
  146.1 7.3 %copy-start.2 = (f32[256,1280]{1,0:T(8,128)S(1)}, f32[256,1280]{1,0:T(8,128)}, u32[]{:S(2)}) copy-start(f32[256,1280]{1,0:T(8,128)} %copy-done.1) | copy-start | bytes 3932164
  146.3 14.1 %collective-permute-start.27 = (bf16[256,768]{1,0:T(8,128)(2,1)S(1)}, bf16[256,768]{1,0:T(8,128)(2,1)S(1)}, u32[]{:S(2)}, u32[]{:S(2)}) collective-permute-start(bf16[256,768]{1,0:T(8,128)(2,1)S(1)} %copy-done.14), channel_id=1, source_target_pairs={{4,0},{8,12},{5,1},{9,13},{6,2},{10,14},{7,3},{11,15},{20,16},{24,... | collective-permute-start | bytes 1179656 | tf_op jit(solution)/shard_map/ppermute | solution.py:95
  147.7 14.6 %collective-permute-start.28 = (bf16[256,768]{1,0:T(8,128)(2,1)S(1)}, bf16[256,768]{1,0:T(8,128)(2,1)S(1)}, u32[]{:S(2)}, u32[]{:S(2)}) collective-permute-start(bf16[256,768]{1,0:T(8,128)(2,1)S(1)} %copy-done.12), channel_id=1, source_target_pairs={{4,8},{8,4},{5,9},{9,5},{6,10},{10,6},{7,11},{11,7},{20,24},{24,20... | collective-permute-start | bytes 1179656 | tf_op jit(solution)/shard_map/ppermute | solution.py:94
  148.4 29.1 %collective-permute-start.30 = (bf16[256,768]{1,0:T(8,128)(2,1)S(1)}, bf16[256,768]{1,0:T(8,128)(2,1)S(1)}, u32[]{:S(2)}, u32[]{:S(2)}) collective-permute-start(bf16[256,768]{1,0:T(8,128)(2,1)S(1)} %copy-done.8), channel_id=1, source_target_pairs={{4,0},{8,12},{5,1},{9,13},{6,2},{10,14},{7,3},{11,15},{20,16},{24,... | collective-permute-start | bytes 1179656 | tf_op jit(solution)/shard_map/ppermute | solution.py:95
  149.8 13.9 %collective-permute-start.31 = (bf16[256,768]{1,0:T(8,128)(2,1)S(1)}, bf16[256,768]{1,0:T(8,128)(2,1)S(1)}, u32[]{:S(2)}, u32[]{:S(2)}) collective-permute-start(bf16[256,768]{1,0:T(8,128)(2,1)S(1)} %copy-done.10), channel_id=1, source_target_pairs={{4,8},{8,4},{5,9},{9,5},{6,10},{10,6},{7,11},{11,7},{20,24},{24,20... | collective-permute-start | bytes 1179656 | tf_op jit(solution)/shard_map/ppermute | solution.py:94
  151.5 13.4 %collective-permute-start.26 = (bf16[256,640]{1,0:T(8,128)(2,1)S(1)}, bf16[256,640]{1,0:T(8,128)(2,1)S(1)}, u32[]{:S(2)}, u32[]{:S(2)}) collective-permute-start(bf16[256,640]{1,0:T(8,128)(2,1)S(1)} %add_convert_fusion.7), channel_id=1, source_target_pairs={{0,2},{1,3},{2,0},{3,1},{4,6},{5,7},{6,4},{7,5},{8,10},{9,11},{10,... | collective-permute-start | bytes 983048 | tf_op jit(solution)/shard_map/ppermute | solution.py:228
  160.4 9.3 %collective-permute-start.24 = (bf16[256,640]{1,0:T(8,128)(2,1)S(1)}, bf16[256,640]{1,0:T(8,128)(2,1)S(1)}, u32[]{:S(2)}, u32[]{:S(2)}) collective-permute-start(bf16[256,640]{1,0:T(8,128)(2,1)S(1)} %add_convert_fusion.9), channel_id=1, source_target_pairs={{0,2},{1,3},{2,0},{3,1},{4,6},{5,7},{6,4},{7,5},{8,10},{9,11},{10,... | collective-permute-start | bytes 983048 | tf_op jit(solution)/shard_map/ppermute | solution.py:228
  162.3 14.9 %collective-permute-start.29 = (bf16[256,768]{1,0:T(8,128)(2,1)S(1)}, bf16[256,768]{1,0:T(8,128)(2,1)S(1)}, u32[]{:S(2)}, u32[]{:S(2)}) collective-permute-start(bf16[256,768]{1,0:T(8,128)(2,1)S(1)} %collective-permute-done.28), channel_id=1, source_target_pairs={{4,0},{8,12},{5,1},{9,13},{6,2},{10,14},{7,3},{11,15},{20,16},{24,... | collective-permute-start | bytes 1179656 | tf_op jit(solution)/shard_map/ppermute | solution.py:96
  163.6 21.8 %collective-permute-start.32 = (bf16[256,768]{1,0:T(8,128)(2,1)S(1)}, bf16[256,768]{1,0:T(8,128)(2,1)S(1)}, u32[]{:S(2)}, u32[]{:S(2)}) collective-permute-start(bf16[256,768]{1,0:T(8,128)(2,1)S(1)} %collective-permute-done.31), channel_id=1, source_target_pairs={{4,0},{8,12},{5,1},{9,13},{6,2},{10,14},{7,3},{11,15},{20,16},{24,... | collective-permute-start | bytes 1179656 | tf_op jit(solution)/shard_map/ppermute | solution.py:96
  185.6 1.7 copy-start.5

commit v12 on v11

--- a/solution.py
+++ b/solution.py
@@ -206,7 +206,7 @@
             out_specs=[pl.BlockSpec((rows, chips * part), lambda h, p: (0, 0))] * (2 * chunks),
             scratch_shapes=[pltpu.VMEM((rows, model), F32)],
         ),
-        compiler_params=pltpu.CompilerParams(vmem_limit_bytes=48 * 2**20),
+        compiler_params=pltpu.CompilerParams(vmem_limit_bytes=60 * 2**20),
         cost_estimate=pl.CostEstimate(
             flops=4 * rows * tokens * depth + 2 * rows * depth * model,
             bytes_accessed=4 * tokens * depth + 2 * depth * model + 6 * rows * chips * width,

time: 188 us -> 188 us (level)
    unnamed x35 -> x27, local copies, waits for them, and re-layouts: 6.87 us -> 4.29 us
  transfers between devices with their start and end apart: 33 -> 33, of which waited for: 15 -> 16; matrix products, arithmetic and copies ran while one was open for 9% -> 10% of each run, Pallas kernels for 6% -> 7%
where the time goes in v12:
time: 188 us
  waiting for transfers between devices  80.2 us (43%)
  starting transfers between devices  71.9 us (38%)
  Pallas kernels  12.3 us (7%)
  local copies, waits for them, and re-layouts  8.14 us (4%)
  other arithmetic  7 us (4%)
  matrix products  6.77 us (4%)
    ppermute x2, waiting for transfers between devices, into(): last = lax.ppermute(after(across_mate, *earlier), 'patch', outward)  15.1 us
    ppermute x2, waiting for transfers between devices, sum_in_pairs(): first = lax.ppermute(outermost, 'patch', [(0, 1), (3, 2)])  13.7 us
    pallas_call x1, Pallas kernels, attend(): pl.pallas_call(functools.partial(attend_and_project, patches, heads, chip...  12.3 us
    ppermute x2, waiting for transfers between devices, sum_in_pairs(): up = lax.ppermute(second, 'patch', [(0, 1), (1, 2)])  11.2 us
    ppermute x2, starting transfers between devices, both_slabs(): other = lax.ppermute(held, 'tensor', across)  9.97 us
    ppermute x2, starting transfers between devices, sum_in_pairs(): first = lax.ppermute(outermost, 'patch', [(0, 1), (3, 2)])  9.91 us
    ppermute x2, waiting for transfers between devices, sum_in_pairs(): up = lax.ppermute(third_up, 'patch', [(0, 1), (1, 2), (2, 3)])  9.53 us
    ppermute x2, starting transfers between devices, sum_in_pairs(): up = lax.ppermute(third_up, 'patch', [(0, 1), (1, 2), (2, 3)])  9.47 us
  transfers between devices with their start and end apart: 33, of which 16 were waited for; matrix products, arithmetic and copies ran while one was open for 10% of the time, Pallas kernels for 7%

profile of v12, /device:TPU:0, one launch (start us, length us, event | category | flops | bytes accessed | tf_op | source)
XLA Modules:
  0.0 187.6 jit_solution(8990276613089324709)
XLA Ops:
  0.6 1.3 fusion.15
  1.9 3.0 %collective-permute-start.1 = (bf16[128,1280]{1,0:T(8,128)(2,1)S(1)}, bf16[128,1280]{1,0:T(8,128)(2,1)S(1)}, u32[]{:S(2)}, u32[]{:S(2)}) collective-permute-start(bf16[128,1280]{1,0:T(8,128)(2,1)S(1)} %get-tuple-element.36), channel_id=1, source_target_pairs={{0,2},{1,3},{2,0},{3,1},{4,6},{5,7},{6,4},{7,5},{8,10},{9,11},{10,... | collective-permute-start | bytes 983048 | tf_op jit(solution)/shard_map/ppermute | solution.py:31
  4.9 1.3 collective-permute-start.5
  6.2 6.4 %collective-permute-done.1 = bf16[128,1280]{1,0:T(8,128)(2,1)S(1)} collective-permute-done((bf16[128,1280]{1,0:T(8,128)(2,1)S(1)}, bf16[128,1280]{1,0:T(8,128)(2,1)S(1)}, u32[]{:S(2)}, u32[]{:S(2)}) %collective-permute-start.1) | collective-permute-done | bytes 327712 | tf_op jit(solution)/shard_map/ppermute | solution.py:31
  12.6 4.8 %collective-permute-start.6 = (bf16[128,1280]{1,0:T(8,128)(2,1)S(1)}, bf16[128,1280]{1,0:T(8,128)(2,1)S(1)}, u32[]{:S(2)}, u32[]{:S(2)}) collective-permute-start(bf16[128,1280]{1,0:T(8,128)(2,1)S(1)} %collective-permute-done.1), channel_id=1, source_target_pairs={{0,8},{1,12},{4,9},{5,13},{10,2},{11,6},{14,3},{15,7},{16,24},{17,... | collective-permute-start | bytes 983048 | tf_op jit(solution)/shard_map/ppermute | solution.py:41
  17.4 7.4 %collective-permute-done.5 = bf16[128,1280]{1,0:T(8,128)(2,1)S(1)} collective-permute-done((bf16[128,1280]{1,0:T(8,128)(2,1)S(1)}, bf16[128,1280]{1,0:T(8,128)(2,1)S(1)}, u32[]{:S(2)}, u32[]{:S(2)}) %collective-permute-start.5) | collective-permute-done | bytes 327712 | tf_op jit(solution)/shard_map/ppermute | solution.py:41
  24.8 0.3 collective-permute-done.6
  25.2 8.7 %collective-permute-start.7 = (bf16[128,1280]{1,0:T(8,128)(2,1)S(1)}, bf16[128,1280]{1,0:T(8,128)(2,1)S(1)}, u32[]{:S(2)}, u32[]{:S(2)}) collective-permute-start(bf16[128,1280]{1,0:T(8,128)(2,1)S(1)} %broadcast_select_fusion.2), channel_id=1, source_target_pairs={{0,2},{1,3},{2,0},{3,1},{4,6},{5,7},{6,4},{7,5},{8,10},{9,11},{10,... | collective-permute-start | bytes 983048 | tf_op jit(solution)/shard_map/ppermute | solution.py:45
  33.9 0.7 collective-permute-start
  34.6 0.7 stack.23.place_ref
  35.3 1.7 constant_dynamic-update-slice_fusion.1
  37.0 0.8 collective-permute-start.2
  37.9 1.1 collective-permute-done.7
  39.0 0.9 collective-permute-start.8
  40.1 1.3 collective-permute-start.3
  41.4 0.2 collective-permute-done.8
  41.6 2.2 %fusion.1 = f16[512,1536]{1,0:T(8,128)(2,1)S(1)} fusion(bf16[1280,1536]{1,0:T(8,128)(2,1)S(1)} %constant_dynamic-update-slice_fusion, bf16[256,1280]{1,0:T(8,128)(2,1)S(1)} %collective-permute-done.8, bf16[128,1280]{1,0:T(8,128)(2,1)S(1)} %get-tuple-element.35, bf16[128,1280]{1,0:T(8,128)(2,1)S(1)} %get-tuple-element.34), kind=kOutput, calls=%fused_computation.3 | convolution fusion | flops 2018770944 | bytes 6815744 | tf_op jit(solution)/shard_map/dot_general | solution.py:60
  44.0 6.5 %collective-permute-start.14 = (f16[256,1536]{1,0:T(8,128)(2,1)S(1)}, f16[256,1536]{1,0:T(8,128)(2,1)S(1)}, u32[]{:S(2)}, u32[]{:S(2)}) collective-permute-start(f16[256,1536]{1,0:T(8,128)(2,1)S(1)} %dynamic-slice_bitcast_fusion), channel_id=1, source_target_pairs={{0,4},{12,8},{1,5},{13,9},{2,6},{14,10},{3,7},{15,11},{16,20},{28,... | collective-permute-start | bytes 2359304 | tf_op jit(solution)/shard_map/ppermute | solution.py:72
  50.8 1.2 multiply_convert_fusion
  52.1 3.4 %collective-permute-start.9 = (f16[256,768]{1,0:T(8,128)(2,1)S(1)}, f16[256,768]{1,0:T(8,128)(2,1)S(1)}, u32[]{:S(2)}, u32[]{:S(2)}) collective-permute-start(f16[256,768]{1,0:T(8,128)(2,1)S(1)} %dynamic-slice_bitcast_fusion.4), channel_id=1, source_target_pairs={{0,4},{12,8},{1,5},{13,9},{2,6},{14,10},{3,7},{15,11},{16,20},{28,... | collective-permute-start | bytes 1179656 | tf_op jit(solution)/shard_map/ppermute | solution.py:72
  55.4 13.0 %collective-permute-done.14 = f16[256,1536]{1,0:T(8,128)(2,1)S(1)} collective-permute-done((f16[256,1536]{1,0:T(8,128)(2,1)S(1)}, f16[256,1536]{1,0:T(8,128)(2,1)S(1)}, u32[]{:S(2)}, u32[]{:S(2)}) %collective-permute-start.14) | collective-permute-done | bytes 786464 | tf_op jit(solution)/shard_map/ppermute | solution.py:72
  68.5 0.4 fusion.6
  68.9 4.4 %collective-permute-start.15 = (f16[256,1536]{1,0:T(8,128)(2,1)S(1)}, f16[256,1536]{1,0:T(8,128)(2,1)S(1)}, u32[]{:S(2)}, u32[]{:S(2)}) collective-permute-start(f16[256,1536]{1,0:T(8,128)(2,1)S(1)} %fusion.6), channel_id=1, source_target_pairs={{0,4},{4,8},{1,5},{5,9},{2,6},{6,10},{3,7},{7,11},{16,20},{20,24},... | collective-permute-start | bytes 2359304 | tf_op jit(solution)/shard_map/ppermute | solution.py:74
  73.3 0.7 collective-permute-start.17
  74.1 2.2 %fusion = f16[512,1536]{1,0:T(8,128)(2,1)S(1)} fusion(bf16[1280,1536]{1,0:T(8,128)(2,1)S(1)} %constant_dynamic-update-slice_fusion, bf16[256,1280]{1,0:T(8,128)(2,1)S(1)} %collective-permute-done.4, bf16[128,1280]{1,0:T(8,128)(2,1)S(1)} %get-tuple-element.33, bf16[128,1280]{1,0:T(8,128)(2,1)S(1)} %get-tuple-element.32), kind=kOutput, calls=%fused_computation.2 | convolution fusion | flops 2018770944 | bytes 6815744 | tf_op jit(solution)/shard_map/dot_general | solution.py:60
  76.3 0.6 collective-permute-done.9
  77.1 0.7 collective-permute-start.12
  77.8 5.0 %collective-permute-start.10 = (f16[256,768]{1,0:T(8,128)(2,1)S(1)}, f16[256,768]{1,0:T(8,128)(2,1)S(1)}, u32[]{:S(2)}, u32[]{:S(2)}) collective-permute-start(f16[256,768]{1,0:T(8,128)(2,1)S(1)} %fusion.10), channel_id=1, source_target_pairs={{0,4},{4,8},{1,5},{5,9},{2,6},{6,10},{3,7},{7,11},{16,20},{20,24},... | collective-permute-start | bytes 1179656 | tf_op jit(solution)/shard_map/ppermute | solution.py:74
  82.8 11.0 %collective-permute-done.15 = f16[256,1536]{1,0:T(8,128)(2,1)S(1)} collective-permute-done((f16[256,1536]{1,0:T(8,128)(2,1)S(1)}, f16[256,1536]{1,0:T(8,128)(2,1)S(1)}, u32[]{:S(2)}, u32[]{:S(2)}) %collective-permute-start.15) | collective-permute-done | bytes 786464 | tf_op jit(solution)/shard_map/ppermute | solution.py:74
  93.7 0.6 add_convert_fusion.1
  94.3 1.3 collective-permute-start.18
  95.6 5.1 %collective-permute-start.16 = (f16[256,1536]{1,0:T(8,128)(2,1)S(1)}, f16[256,1536]{1,0:T(8,128)(2,1)S(1)}, u32[]{:S(2)}, u32[]{:S(2)}) collective-permute-start(f16[256,1536]{1,0:T(8,128)(2,1)S(1)} %get-tuple-element.28), channel_id=1, source_target_pairs={{0,4},{4,8},{8,12},{1,5},{5,9},{9,13},{2,6},{6,10},{10,14},{3,7},{... | collective-permute-start | bytes 2359304 | tf_op jit(solution)/shard_map/ppermute | solution.py:78
  100.7 1.2 multiply_convert_fusion.1
  101.9 0.3 collective-permute-done.10
  102.2 0.3 add_convert_fusion.3
  102.5 4.4 %collective-permute-start.11 = (f16[256,768]{1,0:T(8,128)(2,1)S(1)}, f16[256,768]{1,0:T(8,128)(2,1)S(1)}, u32[]{:S(2)}, u32[]{:S(2)}) collective-permute-start(f16[256,768]{1,0:T(8,128)(2,1)S(1)} %get-tuple-element.31), channel_id=1, source_target_pairs={{0,4},{4,8},{8,12},{1,5},{5,9},{9,13},{2,6},{6,10},{10,14},{3,7},{... | collective-permute-start | bytes 1179656 | tf_op jit(solution)/shard_map/ppermute | solution.py:78
  106.9 1.3 collective-permute-start.13
  108.4 3.9 %collective-permute-done.18 = f16[256,1536]{1,0:T(8,128)(2,1)S(1)} collective-permute-done((f16[256,1536]{1,0:T(8,128)(2,1)S(1)}, f16[256,1536]{1,0:T(8,128)(2,1)S(1)}, u32[]{:S(2)}, u32[]{:S(2)}) %collective-permute-start.18) | collective-permute-done | bytes 786464 | tf_op jit(solution)/shard_map/ppermute | solution.py:79
  112.3 6.7 %collective-permute-done.16 = f16[256,1536]{1,0:T(8,128)(2,1)S(1)} collective-permute-done((f16[256,1536]{1,0:T(8,128)(2,1)S(1)}, f16[256,1536]{1,0:T(8,128)(2,1)S(1)}, u32[]{:S(2)}, u32[]{:S(2)}) %collective-permute-start.16) | collective-permute-done | bytes 786464 | tf_op jit(solution)/shard_map/ppermute | solution.py:78
  119.0 2.6 %fusion.5 = (bf16[256,768]{1,0:T(8,128)(2,1)S(1)}, bf16[256,768]{1,0:T(8,128)(2,1)}) fusion(f16[256,1536]{1,0:T(8,128)(2,1)S(1)} %collective-permute-done.18, f16[256,1536]{1,0:T(8,128)(2,1)S(1)} %collective-permute-done.16, f16[256,1536]{1,0:T(8,128)(2,1)S(1)} %dynamic-slice_bitcast_fusion.1, bf16[2,1024,768]{2,1,0:T(8,128)(2,1)} %stale_ref.1, ...), kind=kLoop, calls=%fused_computation.18 | loop fusion | flops 4718592 | bytes 3932168 | tf_op jit(solution)/shard_map/convert_element_type | solution.py:258
  121.6 2.8 %collective-permute-done.11 = f16[256,768]{1,0:T(8,128)(2,1)S(1)} collective-permute-done((f16[256,768]{1,0:T(8,128)(2,1)S(1)}, f16[256,768]{1,0:T(8,128)(2,1)S(1)}, u32[]{:S(2)}, u32[]{:S(2)}) %collective-permute-start.11) | collective-permute-done | bytes 393248 | tf_op jit(solution)/shard_map/ppermute | solution.py:78
  124.4 2.5 %collective-permute-start.19 = (bf16[256,768]{1,0:T(8,128)(2,1)}, bf16[256,768]{1,0:T(8,128)(2,1)S(1)}, u32[]{:S(2)}, u32[]{:S(2)}) collective-permute-start(bf16[256,768]{1,0:T(8,128)(2,1)} %get-tuple-element.16.key_ref), channel_id=1, source_target_pairs={{0,4},{4,0},{8,12},{12,8},{1,5},{5,1},{9,13},{13,9},{2,6},{6,2},{1... | collective-permute-start | bytes 1179656 | tf_op jit(solution)/shard_map/ppermute | solution.py:86
  126.9 0.7 collective-permute-start.20
  127.6 3.0 %collective-permute-start.21 = (bf16[256,768]{1,0:T(8,128)(2,1)S(1)}, bf16[256,768]{1,0:T(8,128)(2,1)S(1)}, u32[]{:S(2)}, u32[]{:S(2)}) collective-permute-start(bf16[256,768]{1,0:T(8,128)(2,1)S(1)} %get-tuple-element.17.value_ref), channel_id=1, source_target_pairs={{0,4},{4,0},{8,12},{12,8},{1,5},{5,1},{9,13},{13,9},{2,6},{6,2},{1... | collective-permute-start | bytes 1179656 | tf_op jit(solution)/shard_map/ppermute | solution.py:86
  130.6 0.9 collective-permute-start.22
  131.5 1.0 fusion.9.query_ref
  132.5 12.3 %shard_map.77 = (bf16[256,1280]{1,0:T(8,128)(2,1)}, bf16[256,1280]{1,0:T(8,128)(2,1)}, f32[256,1280]{1,0:T(8,128)}, f32[256,1280]{1,0:T(8,128)}) custom-call(s32[5]{0:T(128)} %stack.23.place_ref, bf16[256,768]{1,0:T(8,128)(2,1)} %fusion.9.query_ref, bf16[2,1024,768]{2,1,0:T(8,128)(2,1)} %stale_ref.1, bf16[256,768]{1,0:T(8,128)(2,1)} %get-tuple-element.16.key_ref, ...), custom_call_target="tpu_custom_call" | custom-call | flops 2818572288 | bytes 14942208 | tf_op jit(solution)/shard_map/pallas_call | solution.py:192
  144.8 0.7 copy-done.7
  145.7 0.5 collective-permute-start.23
  146.4 1.1 bitcast_dynamic-update-slice_fusion.7
  147.6 1.3 collective-permute-start.27
  148.9 0.7 collective-permute-start.28
  149.6 1.3 collective-permute-start.30
  150.9 0.7 collective-permute-start.31
  151.7 1.8 collective-permute-start.26
  153.6 7.8 %collective-permute-done.27 = bf16[256,768]{1,0:T(8,128)(2,1)S(1)} collective-permute-done((bf16[256,768]{1,0:T(8,128)(2,1)S(1)}, bf16[256,768]{1,0:T(8,128)(2,1)S(1)}, u32[]{:S(2)}, u32[]{:S(2)}) %collective-permute-start.27) | collective-permute-done | bytes 393248 | tf_op jit(solution)/shard_map/ppermute | solution.py:95
  161.4 1.7 collective-permute-start.24
  163.3 1.3 collective-permute-start.29
  164.6 1.3 collective-permute-start.32
  166.0 3.5 %collective-permute-done.24 = bf16[256,640]{1,0:T(8,128)(2,1)S(1)} collective-permute-done((bf16[256,640]{1,0:T(8,128)(2,1)S(1)}, bf16[256,640]{1,0:T(8,128)(2,1)S(1)}, u32[]{:S(2)}, u32[]{:S(2)}) %collective-permute-start.24) | collective-permute-done | bytes 327712 | tf_op jit(solution)/shard_map/ppermute | solution.py:228
  169.6 0.9 pad_maximum_fusion.4
  170.5 7.8 %collective-permute-done.29 = bf16[256,768]{1,0:T(8,128)(2,1)S(1)} collective-permute-done((bf16[256,768]{1,0:T(8,128)(2,1)S(1)}, bf16[256,768]{1,0:T(8,128)(2,1)S(1)}, u32[]{:S(2)}, u32[]{:S(2)}) %collective-permute-start.29) | collective-permute-done | bytes 393248 | tf_op jit(solution)/shard_map/ppermute | solution.py:96
  178.6 7.3 %collective-permute-done.32 = bf16[256,768]{1,0:T(8,128)(2,1)S(1)} collective-permute-done((bf16[256,768]{1,0:T(8,128)(2,1)S(1)}, bf16[256,768]{1,0:T(8,128)(2,1)S(1)}, u32[]{:S(2)}, u32[]{:S(2)}) %collective-permute-start.32) | collective-permute-done | bytes 393248 | tf_op jit(solution)/shard_map/ppermute | solution.py:96
  186.0 1.7 copy-done.3
  (66 shorter events, 2.4 us)
Async XLA Ops:
  0.6 50.1 %copy-start = (bf16[1280,768]{1,0:T(8,128)(2,1)S(1)}, bf16[1280,768]{1,0:T(8,128)(2,1)}, u32[]{:S(2)}) copy-start(bf16[1280,768]{1,0:T(8,128)(2,1)} %param.7) | copy-start | bytes 5898244
  1.9 10.7 %collective-permute-start.1 = (bf16[128,1280]{1,0:T(8,128)(2,1)S(1)}, bf16[128,1280]{1,0:T(8,128)(2,1)S(1)}, u32[]{:S(2)}, u32[]{:S(2)}) collective-permute-start(bf16[128,1280]{1,0:T(8,128)(2,1)S(1)} %get-tuple-element.36), channel_id=1, source_target_pairs={{0,2},{1,3},{2,0},{3,1},{4,6},{5,7},{6,4},{7,5},{8,10},{9,11},{10,... | collective-permute-start | bytes 983048 | tf_op jit(solution)/shard_map/ppermute | solution.py:31
  4.9 19.9 %collective-permute-start.5 = (bf16[128,1280]{1,0:T(8,128)(2,1)S(1)}, bf16[128,1280]{1,0:T(8,128)(2,1)S(1)}, u32[]{:S(2)}, u32[]{:S(2)}) collective-permute-start(bf16[128,1280]{1,0:T(8,128)(2,1)S(1)} %get-tuple-element.37), channel_id=1, source_target_pairs={{2,10},{3,14},{6,11},{7,15},{8,0},{9,4},{12,1},{13,5},{18,26},{19,... | collective-permute-start | bytes 983048 | tf_op jit(solution)/shard_map/ppermute | solution.py:41
  12.6 12.2 %copy-start.11 = (bf16[128,1280]{1,0:T(8,128)(2,1)}, bf16[128,1280]{1,0:T(8,128)(2,1)S(1)}, u32[]{:S(2)}) copy-start(bf16[128,1280]{1,0:T(8,128)(2,1)S(1)} %collective-permute-done.1) | copy-start | bytes 983044
  12.6 12.5 %collective-permute-start.6 = (bf16[128,1280]{1,0:T(8,128)(2,1)S(1)}, bf16[128,1280]{1,0:T(8,128)(2,1)S(1)}, u32[]{:S(2)}, u32[]{:S(2)}) collective-permute-start(bf16[128,1280]{1,0:T(8,128)(2,1)S(1)} %collective-permute-done.1), channel_id=1, source_target_pairs={{0,8},{1,12},{4,9},{5,13},{10,2},{11,6},{14,3},{15,7},{16,24},{17,... | collective-permute-start | bytes 983048 | tf_op jit(solution)/shard_map/ppermute | solution.py:41
  25.2 13.7 %collective-permute-start.7 = (bf16[128,1280]{1,0:T(8,128)(2,1)S(1)}, bf16[128,1280]{1,0:T(8,128)(2,1)S(1)}, u32[]{:S(2)}, u32[]{:S(2)}) collective-permute-start(bf16[128,1280]{1,0:T(8,128)(2,1)S(1)} %broadcast_select_fusion.2), channel_id=1, source_target_pairs={{0,2},{1,3},{2,0},{3,1},{4,6},{5,7},{6,4},{7,5},{8,10},{9,11},{10,... | collective-permute-start | bytes 983048 | tf_op jit(solution)/shard_map/ppermute | solution.py:45
  33.9 6.2 %collective-permute-start = (bf16[128,1280]{1,0:T(8,128)(2,1)S(1)}, bf16[128,1280]{1,0:T(8,128)(2,1)S(1)}, u32[]{:S(2)}, u32[]{:S(2)}) collective-permute-start(bf16[128,1280]{1,0:T(8,128)(2,1)S(1)} %get-tuple-element.37), channel_id=1, source_target_pairs={{0,0},{1,4},{4,1},{5,5},{10,10},{11,14},{14,11},{15,15},{16,16},{1... | collective-permute-start | bytes 983048 | tf_op jit(solution)/shard_map/ppermute | solution.py:41
  35.3 1.8 copy-start.12
  37.0 2.9 %copy-start.4 = (bf16[1280,768]{1,0:T(8,128)(2,1)S(1)}, bf16[1280,768]{1,0:T(8,128)(2,1)}, u32[]{:S(2)}) copy-start(bf16[1280,768]{1,0:T(8,128)(2,1)} %param.9) | copy-start | bytes 5898244
  37.0 3.0 %collective-permute-start.2 = (bf16[128,1280]{1,0:T(8,128)(2,1)S(1)}, bf16[128,1280]{1,0:T(8,128)(2,1)S(1)}, u32[]{:S(2)}, u32[]{:S(2)}) collective-permute-start(bf16[128,1280]{1,0:T(8,128)(2,1)S(1)} %copy-done.12), channel_id=1, source_target_pairs={{2,2},{3,6},{6,3},{7,7},{8,8},{9,12},{12,9},{13,13},{18,18},{19,22... | collective-permute-start | bytes 983048 | tf_op jit(solution)/shard_map/ppermute | solution.py:41
  39.0 2.6 %collective-permute-start.8 = (bf16[256,1280]{1,0:T(8,128)(2,1)S(1)}, bf16[256,1280]{1,0:T(8,128)(2,1)S(1)}, u32[]{:S(2)}, u32[]{:S(2)}) collective-permute-start(bf16[256,1280]{1,0:T(8,128)(2,1)S(1)} %pad_maximum_fusion.3), channel_id=1, source_target_pairs={{0,1},{1,0},{2,3},{3,2},{4,5},{5,4},{6,7},{7,6},{8,9},{9,8},{10,11... | collective-permute-start | bytes 1966088 | tf_op jit(solution)/shard_map/ppermute | solution.py:49
  40.1 10.4 %collective-permute-start.3 = (bf16[128,1280]{1,0:T(8,128)(2,1)S(1)}, bf16[128,1280]{1,0:T(8,128)(2,1)S(1)}, u32[]{:S(2)}, u32[]{:S(2)}) collective-permute-start(bf16[128,1280]{1,0:T(8,128)(2,1)S(1)} %broadcast_select_fusion.5), channel_id=1, source_target_pairs={{0,2},{1,3},{2,0},{3,1},{4,6},{5,7},{6,4},{7,5},{8,10},{9,11},{10,... | collective-permute-start | bytes 983048 | tf_op jit(solution)/shard_map/ppermute | solution.py:45
  44.0 24.5 %collective-permute-start.14 = (f16[256,1536]{1,0:T(8,128)(2,1)S(1)}, f16[256,1536]{1,0:T(8,128)(2,1)S(1)}, u32[]{:S(2)}, u32[]{:S(2)}) collective-permute-start(f16[256,1536]{1,0:T(8,128)(2,1)S(1)} %dynamic-slice_bitcast_fusion), channel_id=1, source_target_pairs={{0,4},{12,8},{1,5},{13,9},{2,6},{14,10},{3,7},{15,11},{16,20},{28,... | collective-permute-start | bytes 2359304 | tf_op jit(solution)/shard_map/ppermute | solution.py:72
  50.7 23.4 %collective-permute-start.4 = (bf16[256,1280]{1,0:T(8,128)(2,1)S(1)}, bf16[256,1280]{1,0:T(8,128)(2,1)S(1)}, u32[]{:S(2)}, u32[]{:S(2)}) collective-permute-start(bf16[256,1280]{1,0:T(8,128)(2,1)S(1)} %pad_maximum_fusion.2), channel_id=1, source_target_pairs={{0,1},{1,0},{2,3},{3,2},{4,5},{5,4},{6,7},{7,6},{8,9},{9,8},{10,11... | collective-permute-start | bytes 1966088 | tf_op jit(solution)/shard_map/ppermute | solution.py:49
  52.1 24.8 %collective-permute-start.9 = (f16[256,768]{1,0:T(8,128)(2,1)S(1)}, f16[256,768]{1,0:T(8,128)(2,1)S(1)}, u32[]{:S(2)}, u32[]{:S(2)}) collective-permute-start(f16[256,768]{1,0:T(8,128)(2,1)S(1)} %dynamic-slice_bitcast_fusion.4), channel_id=1, source_target_pairs={{0,4},{12,8},{1,5},{13,9},{2,6},{14,10},{3,7},{15,11},{16,20},{28,... | collective-permute-start | bytes 1179656 | tf_op jit(solution)/shard_map/ppermute | solution.py:72
  68.9 24.8 %collective-permute-start.15 = (f16[256,1536]{1,0:T(8,128)(2,1)S(1)}, f16[256,1536]{1,0:T(8,128)(2,1)S(1)}, u32[]{:S(2)}, u32[]{:S(2)}) collective-permute-start(f16[256,1536]{1,0:T(8,128)(2,1)S(1)} %fusion.6), channel_id=1, source_target_pairs={{0,4},{4,8},{1,5},{5,9},{2,6},{6,10},{3,7},{7,11},{16,20},{20,24},... | collective-permute-start | bytes 2359304 | tf_op jit(solution)/shard_map/ppermute | solution.py:74
  73.3 20.4 %collective-permute-start.17 = (f16[256,1536]{1,0:T(8,128)(2,1)S(1)}, f16[256,1536]{1,0:T(8,128)(2,1)S(1)}, u32[]{:S(2)}, u32[]{:S(2)}) collective-permute-start(f16[256,1536]{1,0:T(8,128)(2,1)S(1)} %fusion.6), channel_id=1, source_target_pairs={{12,8},{8,4},{13,9},{9,5},{14,10},{10,6},{15,11},{11,7},{28,24},{2... | collective-permute-start | bytes 2359304 | tf_op jit(solution)/shard_map/ppermute | solution.py:75
  77.1 24.8 %collective-permute-start.12 = (f16[256,768]{1,0:T(8,128)(2,1)S(1)}, f16[256,768]{1,0:T(8,128)(2,1)S(1)}, u32[]{:S(2)}, u32[]{:S(2)}) collective-permute-start(f16[256,768]{1,0:T(8,128)(2,1)S(1)} %fusion.10), channel_id=1, source_target_pairs={{12,8},{8,4},{13,9},{9,5},{14,10},{10,6},{15,11},{11,7},{28,24},{2... | collective-permute-start | bytes 1179656 | tf_op jit(solution)/shard_map/ppermute | solution.py:75
  77.8 24.4 %collective-permute-start.10 = (f16[256,768]{1,0:T(8,128)(2,1)S(1)}, f16[256,768]{1,0:T(8,128)(2,1)S(1)}, u32[]{:S(2)}, u32[]{:S(2)}) collective-permute-start(f16[256,768]{1,0:T(8,128)(2,1)S(1)} %fusion.10), channel_id=1, source_target_pairs={{0,4},{4,8},{1,5},{5,9},{2,6},{6,10},{3,7},{7,11},{16,20},{20,24},... | collective-permute-start | bytes 1179656 | tf_op jit(solution)/shard_map/ppermute | solution.py:74
  94.3 18.0 %collective-permute-start.18 = (f16[256,1536]{1,0:T(8,128)(2,1)S(1)}, f16[256,1536]{1,0:T(8,128)(2,1)S(1)}, u32[]{:S(2)}, u32[]{:S(2)}) collective-permute-start(f16[256,1536]{1,0:T(8,128)(2,1)S(1)} %get-tuple-element.29), channel_id=1, source_target_pairs={{12,8},{8,4},{4,0},{13,9},{9,5},{5,1},{14,10},{10,6},{6,2},{15,11}... | collective-permute-start | bytes 2359304 | tf_op jit(solution)/shard_map/ppermute | solution.py:79
  95.6 23.4 %collective-permute-start.16 = (f16[256,1536]{1,0:T(8,128)(2,1)S(1)}, f16[256,1536]{1,0:T(8,128)(2,1)S(1)}, u32[]{:S(2)}, u32[]{:S(2)}) collective-permute-start(f16[256,1536]{1,0:T(8,128)(2,1)S(1)} %get-tuple-element.28), channel_id=1, source_target_pairs={{0,4},{4,8},{8,12},{1,5},{5,9},{9,13},{2,6},{6,10},{10,14},{3,7},{... | collective-permute-start | bytes 2359304 | tf_op jit(solution)/shard_map/ppermute | solution.py:78
  102.5 21.9 %collective-permute-start.11 = (f16[256,768]{1,0:T(8,128)(2,1)S(1)}, f16[256,768]{1,0:T(8,128)(2,1)S(1)}, u32[]{:S(2)}, u32[]{:S(2)}) collective-permute-start(f16[256,768]{1,0:T(8,128)(2,1)S(1)} %get-tuple-element.31), channel_id=1, source_target_pairs={{0,4},{4,8},{8,12},{1,5},{5,9},{9,13},{2,6},{6,10},{10,14},{3,7},{... | collective-permute-start | bytes 1179656 | tf_op jit(solution)/shard_map/ppermute | solution.py:78
  106.9 17.5 %collective-permute-start.13 = (f16[256,768]{1,0:T(8,128)(2,1)S(1)}, f16[256,768]{1,0:T(8,128)(2,1)S(1)}, u32[]{:S(2)}, u32[]{:S(2)}) collective-permute-start(f16[256,768]{1,0:T(8,128)(2,1)S(1)} %get-tuple-element.30), channel_id=1, source_target_pairs={{12,8},{8,4},{4,0},{13,9},{9,5},{5,1},{14,10},{10,6},{6,2},{15,11}... | collective-permute-start | bytes 1179656 | tf_op jit(solution)/shard_map/ppermute | solution.py:79
  121.6 10.9 %copy-start.1 = (bf16[256,768]{1,0:T(8,128)(2,1)}, bf16[256,768]{1,0:T(8,128)(2,1)S(1)}, u32[]{:S(2)}) copy-start(bf16[256,768]{1,0:T(8,128)(2,1)S(1)} %get-tuple-element.17.value_ref) | copy-start | bytes 1179652
  124.4 20.4 %collective-permute-start.19 = (bf16[256,768]{1,0:T(8,128)(2,1)}, bf16[256,768]{1,0:T(8,128)(2,1)S(1)}, u32[]{:S(2)}, u32[]{:S(2)}) collective-permute-start(bf16[256,768]{1,0:T(8,128)(2,1)} %get-tuple-element.16.key_ref), channel_id=1, source_target_pairs={{0,4},{4,0},{8,12},{12,8},{1,5},{5,1},{9,13},{13,9},{2,6},{6,2},{1... | collective-permute-start | bytes 1179656 | tf_op jit(solution)/shard_map/ppermute | solution.py:86
  126.9 17.9 %collective-permute-start.20 = (bf16[256,768]{1,0:T(8,128)(2,1)}, bf16[256,768]{1,0:T(8,128)(2,1)S(1)}, u32[]{:S(2)}, u32[]{:S(2)}) collective-permute-start(bf16[256,768]{1,0:T(8,128)(2,1)} %get-tuple-element.16.key_ref), channel_id=1, source_target_pairs={{4,8},{8,4},{5,9},{9,5},{6,10},{10,6},{7,11},{11,7},{20,24},{24,20... | collective-permute-start | bytes 1179656 | tf_op jit(solution)/shard_map/ppermute | solution.py:87
  127.6 17.2 %collective-permute-start.21 = (bf16[256,768]{1,0:T(8,128)(2,1)S(1)}, bf16[256,768]{1,0:T(8,128)(2,1)S(1)}, u32[]{:S(2)}, u32[]{:S(2)}) collective-permute-start(bf16[256,768]{1,0:T(8,128)(2,1)S(1)} %get-tuple-element.17.value_ref), channel_id=1, source_target_pairs={{0,4},{4,0},{8,12},{12,8},{1,5},{5,1},{9,13},{13,9},{2,6},{6,2},{1... | collective-permute-start | bytes 1179656 | tf_op jit(solution)/shard_map/ppermute | solution.py:86
  130.6 14.2 %collective-permute-start.22 = (bf16[256,768]{1,0:T(8,128)(2,1)S(1)}, bf16[256,768]{1,0:T(8,128)(2,1)S(1)}, u32[]{:S(2)}, u32[]{:S(2)}) collective-permute-start(bf16[256,768]{1,0:T(8,128)(2,1)S(1)} %get-tuple-element.17.value_ref), channel_id=1, source_target_pairs={{4,8},{8,4},{5,9},{9,5},{6,10},{10,6},{7,11},{11,7},{20,24},{24,20... | collective-permute-start | bytes 1179656 | tf_op jit(solution)/shard_map/ppermute | solution.py:87
  144.8 0.7 copy-start.7
  144.8 0.9 copy-start.9
  145.7 5.2 %collective-permute-start.25 = (bf16[256,1280]{1,0:T(8,128)(2,1)}, bf16[256,1280]{1,0:T(8,128)(2,1)S(1)}, u32[]{:S(2)}, u32[]{:S(2)}) collective-permute-start(bf16[256,1280]{1,0:T(8,128)(2,1)} %get-tuple-element.23), channel_id=1, source_target_pairs={{0,1},{1,0},{2,3},{3,2},{4,5},{5,4},{6,7},{7,6},{8,9},{9,8},{10,11... | collective-permute-start | bytes 1966088 | tf_op jit(solution)/shard_map/ppermute | solution.py:217
  145.7 1.9 copy-start.10
  145.7 3.2 %copy-start.8 = (bf16[256,768]{1,0:T(8,128)(2,1)S(1)}, bf16[256,768]{1,0:T(8,128)(2,1)}, u32[]{:S(2)}) copy-start(bf16[256,768]{1,0:T(8,128)(2,1)} %copy-done.7) | copy-start | bytes 1179652
  145.7 5.9 %copy-start.6 = (f32[256,1280]{1,0:T(8,128)S(1)}, f32[256,1280]{1,0:T(8,128)}, u32[]{:S(2)}) copy-start(f32[256,1280]{1,0:T(8,128)} %get-tuple-element.21) | copy-start | bytes 3932164
  145.7 6.0 %collective-permute-start.23 = (bf16[256,1280]{1,0:T(8,128)(2,1)}, bf16[256,1280]{1,0:T(8,128)(2,1)S(1)}, u32[]{:S(2)}, u32[]{:S(2)}) collective-permute-start(bf16[256,1280]{1,0:T(8,128)(2,1)} %get-tuple-element.20), channel_id=1, source_target_pairs={{0,1},{1,0},{2,3},{3,2},{4,5},{5,4},{6,7},{7,6},{8,9},{9,8},{10,11... | collective-permute-start | bytes 1966088 | tf_op jit(solution)/shard_map/ppermute | solution.py:217
  146.4 7.1 %copy-start.5 = (f32[256,1280]{1,0:T(8,128)S(1)}, f32[256,1280]{1,0:T(8,128)}, u32[]{:S(2)}) copy-start(f32[256,1280]{1,0:T(8,128)} %get-tuple-element.18) | copy-start | bytes 3932164
  147.6 13.9 %collective-permute-start.27 = (bf16[256,768]{1,0:T(8,128)(2,1)S(1)}, bf16[256,768]{1,0:T(8,128)(2,1)S(1)}, u32[]{:S(2)}, u32[]{:S(2)}) collective-permute-start(bf16[256,768]{1,0:T(8,128)(2,1)S(1)} %copy-done.10), channel_id=1, source_target_pairs={{4,0},{8,12},{5,1},{9,13},{6,2},{10,14},{7,3},{11,15},{20,16},{24,... | collective-permute-start | bytes 1179656 | tf_op jit(solution)/shard_map/ppermute | solution.py:95
  148.9 14.4 %collective-permute-start.28 = (bf16[256,768]{1,0:T(8,128)(2,1)S(1)}, bf16[256,768]{1,0:T(8,128)(2,1)S(1)}, u32[]{:S(2)}, u32[]{:S(2)}) collective-permute-start(bf16[256,768]{1,0:T(8,128)(2,1)S(1)} %copy-done.8), channel_id=1, source_target_pairs={{4,8},{8,4},{5,9},{9,5},{6,10},{10,6},{7,11},{11,7},{20,24},{24,20... | collective-permute-start | bytes 1179656 | tf_op jit(solution)/shard_map/ppermute | solution.py:94
  149.6 28.9 %collective-permute-start.30 = (bf16[256,768]{1,0:T(8,128)(2,1)S(1)}, bf16[256,768]{1,0:T(8,128)(2,1)S(1)}, u32[]{:S(2)}, u32[]{:S(2)}) collective-permute-start(bf16[256,768]{1,0:T(8,128)(2,1)S(1)} %collective-permute-done.22), channel_id=1, source_target_pairs={{4,0},{8,12},{5,1},{9,13},{6,2},{10,14},{7,3},{11,15},{20,16},{24,... | collective-permute-start | bytes 1179656 | tf_op jit(solution)/shard_map/ppermute | solution.py:95
  150.9 13.7 %collective-permute-start.31 = (bf16[256,768]{1,0:T(8,128)(2,1)S(1)}, bf16[256,768]{1,0:T(8,128)(2,1)S(1)}, u32[]{:S(2)}, u32[]{:S(2)}) collective-permute-start(bf16[256,768]{1,0:T(8,128)(2,1)S(1)} %collective-permute-done.21), channel_id=1, source_target_pairs={{4,8},{8,4},{5,9},{9,5},{6,10},{10,6},{7,11},{11,7},{20,24},{24,20... | collective-permute-start | bytes 1179656 | tf_op jit(solution)/shard_map/ppermute | solution.py:94
  151.7 14.2 %collective-permute-start.26 = (bf16[256,640]{1,0:T(8,128)(2,1)S(1)}, bf16[256,640]{1,0:T(8,128)(2,1)S(1)}, u32[]{:S(2)}, u32[]{:S(2)}) collective-permute-start(bf16[256,640]{1,0:T(8,128)(2,1)S(1)} %add_convert_fusion.7), channel_id=1, source_target_pairs={{0,2},{1,3},{2,0},{3,1},{4,6},{5,7},{6,4},{7,5},{8,10},{9,11},{10,... | collective-permute-start | bytes 983048 | tf_op jit(solution)/shard_map/ppermute | solution.py:228
  161.4 8.1 %collective-permute-start.24 = (bf16[256,640]{1,0:T(8,128)(2,1)S(1)}, bf16[256,640]{1,0:T(8,128)(2,1)S(1)}, u32[]{:S(2)}, u32[]{:S(2)}) collective-permute-start(bf16[256,640]{1,0:T(8,128)(2,1)S(1)} %add_convert_fusion.9), channel_id=1, source_target_pairs={{0,2},{1,3},{2,0},{3,1},{4,6},{5,7},{6,4},{7,5},{8,10},{9,11},{10,... | collective-permute-start | bytes 983048 | tf_op jit(solution)/shard_map/ppermute | solution.py:228
  163.3 15.0 %collective-permute-start.29 = (bf16[256,768]{1,0:T(8,128)(2,1)S(1)}, bf16[256,768]{1,0:T(8,128)(2,1)S(1)}, u32[]{:S(2)}, u32[]{:S(2)}) collective-permute-start(bf16[256,768]{1,0:T(8,128)(2,1)S(1)} %collective-permute-done.28), channel_id=1, source_target_pairs={{4,0},{8,12},{5,1},{9,13},{6,2},{10,14},{7,3},{11,15},{20,16},{24,... | collective-permute-start | bytes 1179656 | tf_op jit(solution)/shard_map/ppermute | solution.py:96
  164.6 21.3 %collective-permute-start.32 = (bf16[256,768]{1,0:T(8,128)(2,1)S(1)}, bf16[256,768]{1,0:T(8,128)(2,1)S(1)}, u32[]{:S(2)}, u32[]{:S(2)}) collective-permute-start(bf16[256,768]{1,0:T(8,128)(2,1)S(1)} %collective-permute-done.31), channel_id=1, source_target_pairs={{4,0},{8,12},{5,1},{9,13},{6,2},{10,14},{7,3},{11,15},{20,16},{24,... | collective-permute-start | bytes 1179656 | tf_op jit(solution)/shard_map/ppermute | solution.py:96
  166.0 12.3 %copy-start.2 = (bf16[256,768]{1,0:T(8,128)(2,1)S(1)}, bf16[256,768]{1,0:T(8,128)(2,1)}, u32[]{:S(2)}) copy-start(bf16[256,768]{1,0:T(8,128)(2,1)} %copy-done.1) | copy-start | bytes 1179652
  186.0 1.7 copy-start.3

commit v13 on v11

--- a/solution.py
+++ b/solution.py
@@ -73,11 +73,12 @@
     second = jnp.where(is_end, inner, plus(outermost, first))
     up = lax.ppermute(second, "patch", [(0, 1), (1, 2)])
     down = lax.ppermute(second, "patch", [(3, 2), (2, 1)])
+    hop = (up, down)
     third_up = plus(jnp.where(patch == 1, inner, mate), up)
     third_down = plus(jnp.where(patch == 2, inner, mate), down)
     up = lax.ppermute(third_up, "patch", [(0, 1), (1, 2), (2, 3)])
     down = lax.ppermute(third_down, "patch", [(3, 2), (2, 1), (1, 0)])
-    return own, up, down
+    return (own, up, down), hop
 
 
 class PairGather:
@@ -242,8 +243,8 @@
         w_both = jnp.concatenate([w_key, w_value], axis=1)
         if in_pairs:
             far, near = spread_in_pairs(hidden_in)
-            both = sum_in_pairs(far, near, w_both)
-            query_own, *query_got = sum_in_pairs(far, near, w_query)
+            both, _ = sum_in_pairs(far, near, w_both)
+            query_parts, query_hop = sum_in_pairs(far, near, w_query)
         else:
             features = spread_features(hidden_in)
             both = (sum_own_slab(features, w_both, patches),)
@@ -262,8 +263,8 @@
         key_new = refresh([part[:, :width] for part in both], factor, own_stale[0])
         value_new = refresh([part[:, width:] for part in both], factor, own_stale[1])
         if in_pairs:
-            *query_got, key_new, value_new = lax.optimization_barrier((*query_got, key_new, value_new))
-            query = total((query_own, *query_got), factor).astype(BF16)
+            key_new, value_new, *_ = lax.optimization_barrier((key_new, value_new, *query_hop))
+            query = total(query_parts, factor).astype(BF16)
             keys, values = PairGather(key_new), PairGather(value_new)
             first_hop = (keys.mate, keys.across, values.mate, values.across)
         else:

time: 188 us -> 185 us (0.984)
  waiting for transfers between devices: 79.7 us -> 77.7 us
    ppermute x2, waiting for transfers between devices: 8.84 us -> 3.98 us  [sum_in_pairs(): up = lax.ppermute(third_up, 'patch', [(0, 1), (1, 2), (2, 3)])]
where the time goes in v13:
time: 185 us; the launch traced here: 184 us
  waiting for transfers between devices  77.7 us (42%)
  starting transfers between devices  70.7 us (38%)
  Pallas kernels  10.9 us (6%)
  local copies, waits for them, and re-layouts  9.42 us (5%)
  other arithmetic  7.29 us (4%)
  matrix products  6.77 us (4%)
    ppermute x2, waiting for transfers between devices, into(): last = lax.ppermute(after(across_mate, *earlier), 'patch', outward)  14.5 us
    ppermute x2, waiting for transfers between devices, sum_in_pairs(): first = lax.ppermute(outermost, 'patch', [(0, 1), (3, 2)])  13.1 us
    ppermute x2, waiting for transfers between devices, sum_in_pairs(): up = lax.ppermute(second, 'patch', [(0, 1), (1, 2)])  11.8 us
    pallas_call x1, Pallas kernels, attend(): pl.pallas_call(functools.partial(attend_and_project, patches, heads, chip...  10.9 us
    ppermute x2, starting transfers between devices, both_slabs(): other = lax.ppermute(held, 'tensor', across)  10.5 us
    ppermute x2, starting transfers between devices, sum_in_pairs(): first = lax.ppermute(outermost, 'patch', [(0, 1), (3, 2)])  10.1 us
    ppermute x2, starting transfers between devices, sum_in_pairs(): up = lax.ppermute(third_up, 'patch', [(0, 1), (1, 2), (2, 3)])  10.1 us
    ppermute x2, starting transfers between devices, sum_in_pairs(): up = lax.ppermute(second, 'patch', [(0, 1), (1, 2)])  8.85 us
  transfers between devices with their start and end apart: 33, of which 15 were waited for; matrix products, arithmetic and copies ran while one was open for 9% of the time, Pallas kernels for 6%

profile of v13, /device:TPU:0, one launch (start us, length us, event | category | flops | bytes accessed | tf_op | source)
XLA Modules:
  0.0 184.2 jit_solution(3917299987048729970)
XLA Ops:
  0.6 1.3 fusion.15
  1.9 3.0 %collective-permute-start.1 = (bf16[128,1280]{1,0:T(8,128)(2,1)S(1)}, bf16[128,1280]{1,0:T(8,128)(2,1)S(1)}, u32[]{:S(2)}, u32[]{:S(2)}) collective-permute-start(bf16[128,1280]{1,0:T(8,128)(2,1)S(1)} %get-tuple-element.32), channel_id=1, source_target_pairs={{0,2},{1,3},{2,0},{3,1},{4,6},{5,7},{6,4},{7,5},{8,10},{9,11},{10,... | collective-permute-start | bytes 983048 | tf_op jit(solution)/shard_map/ppermute | solution.py:31
  4.9 1.3 collective-permute-start.5
  6.2 6.4 %collective-permute-done.1 = bf16[128,1280]{1,0:T(8,128)(2,1)S(1)} collective-permute-done((bf16[128,1280]{1,0:T(8,128)(2,1)S(1)}, bf16[128,1280]{1,0:T(8,128)(2,1)S(1)}, u32[]{:S(2)}, u32[]{:S(2)}) %collective-permute-start.1) | collective-permute-done | bytes 327712 | tf_op jit(solution)/shard_map/ppermute | solution.py:31
  12.6 4.8 %collective-permute-start.6 = (bf16[128,1280]{1,0:T(8,128)(2,1)S(1)}, bf16[128,1280]{1,0:T(8,128)(2,1)S(1)}, u32[]{:S(2)}, u32[]{:S(2)}) collective-permute-start(bf16[128,1280]{1,0:T(8,128)(2,1)S(1)} %collective-permute-done.1), channel_id=1, source_target_pairs={{0,8},{1,12},{4,9},{5,13},{10,2},{11,6},{14,3},{15,7},{16,24},{17,... | collective-permute-start | bytes 983048 | tf_op jit(solution)/shard_map/ppermute | solution.py:41
  17.4 7.4 %collective-permute-done.5 = bf16[128,1280]{1,0:T(8,128)(2,1)S(1)} collective-permute-done((bf16[128,1280]{1,0:T(8,128)(2,1)S(1)}, bf16[128,1280]{1,0:T(8,128)(2,1)S(1)}, u32[]{:S(2)}, u32[]{:S(2)}) %collective-permute-start.5) | collective-permute-done | bytes 327712 | tf_op jit(solution)/shard_map/ppermute | solution.py:41
  24.8 0.3 collective-permute-done.6
  25.2 8.7 %collective-permute-start.7 = (bf16[128,1280]{1,0:T(8,128)(2,1)S(1)}, bf16[128,1280]{1,0:T(8,128)(2,1)S(1)}, u32[]{:S(2)}, u32[]{:S(2)}) collective-permute-start(bf16[128,1280]{1,0:T(8,128)(2,1)S(1)} %broadcast_select_fusion.2), channel_id=1, source_target_pairs={{0,2},{1,3},{2,0},{3,1},{4,6},{5,7},{6,4},{7,5},{8,10},{9,11},{10,... | collective-permute-start | bytes 983048 | tf_op jit(solution)/shard_map/ppermute | solution.py:45
  33.9 0.7 collective-permute-start
  34.7 1.7 constant_dynamic-update-slice_fusion.1
  36.5 0.8 collective-permute-start.2
  37.3 1.6 collective-permute-done.7
  39.0 0.3 collective-permute-start.8
  39.6 1.8 %collective-permute-start.3 = (bf16[128,1280]{1,0:T(8,128)(2,1)S(1)}, bf16[128,1280]{1,0:T(8,128)(2,1)S(1)}, u32[]{:S(2)}, u32[]{:S(2)}) collective-permute-start(bf16[128,1280]{1,0:T(8,128)(2,1)S(1)} %broadcast_select_fusion.5), channel_id=1, source_target_pairs={{0,2},{1,3},{2,0},{3,1},{4,6},{5,7},{6,4},{7,5},{8,10},{9,11},{10,... | collective-permute-start | bytes 983048 | tf_op jit(solution)/shard_map/ppermute | solution.py:45
  41.4 2.2 %fusion.1 = f16[512,1536]{1,0:T(8,128)(2,1)S(1)} fusion(bf16[1280,1536]{1,0:T(8,128)(2,1)S(1)} %constant_dynamic-update-slice_fusion, bf16[256,1280]{1,0:T(8,128)(2,1)S(1)} %collective-permute-done.8, bf16[128,1280]{1,0:T(8,128)(2,1)S(1)} %get-tuple-element.31, bf16[128,1280]{1,0:T(8,128)(2,1)S(1)} %get-tuple-element.30), kind=kOutput, calls=%fused_computation.3 | convolution fusion | flops 2018770944 | bytes 6815744 | tf_op jit(solution)/shard_map/dot_general | solution.py:60
  43.8 6.2 %collective-permute-start.14 = (f16[256,1536]{1,0:T(8,128)(2,1)S(1)}, f16[256,1536]{1,0:T(8,128)(2,1)S(1)}, u32[]{:S(2)}, u32[]{:S(2)}) collective-permute-start(f16[256,1536]{1,0:T(8,128)(2,1)S(1)} %dynamic-slice_bitcast_fusion), channel_id=1, source_target_pairs={{0,4},{12,8},{1,5},{13,9},{2,6},{14,10},{3,7},{15,11},{16,20},{28,... | collective-permute-start | bytes 2359304 | tf_op jit(solution)/shard_map/ppermute | solution.py:72
  50.2 1.2 multiply_convert_fusion
  51.5 3.9 %collective-permute-start.9 = (f16[256,768]{1,0:T(8,128)(2,1)S(1)}, f16[256,768]{1,0:T(8,128)(2,1)S(1)}, u32[]{:S(2)}, u32[]{:S(2)}) collective-permute-start(f16[256,768]{1,0:T(8,128)(2,1)S(1)} %dynamic-slice_bitcast_fusion.4), channel_id=1, source_target_pairs={{0,4},{12,8},{1,5},{13,9},{2,6},{14,10},{3,7},{15,11},{16,20},{28,... | collective-permute-start | bytes 1179656 | tf_op jit(solution)/shard_map/ppermute | solution.py:72
  55.4 12.5 %collective-permute-done.14 = f16[256,1536]{1,0:T(8,128)(2,1)S(1)} collective-permute-done((f16[256,1536]{1,0:T(8,128)(2,1)S(1)}, f16[256,1536]{1,0:T(8,128)(2,1)S(1)}, u32[]{:S(2)}, u32[]{:S(2)}) %collective-permute-start.14) | collective-permute-done | bytes 786464 | tf_op jit(solution)/shard_map/ppermute | solution.py:72
  67.9 0.4 fusion.6
  68.3 4.4 %collective-permute-start.15 = (f16[256,1536]{1,0:T(8,128)(2,1)S(1)}, f16[256,1536]{1,0:T(8,128)(2,1)S(1)}, u32[]{:S(2)}, u32[]{:S(2)}) collective-permute-start(f16[256,1536]{1,0:T(8,128)(2,1)S(1)} %fusion.6), channel_id=1, source_target_pairs={{0,4},{4,8},{1,5},{5,9},{2,6},{6,10},{3,7},{7,11},{16,20},{20,24},... | collective-permute-start | bytes 2359304 | tf_op jit(solution)/shard_map/ppermute | solution.py:74
  72.8 0.7 collective-permute-start.17
  73.5 2.2 %fusion = f16[512,1536]{1,0:T(8,128)(2,1)S(1)} fusion(bf16[1280,1536]{1,0:T(8,128)(2,1)S(1)} %constant_dynamic-update-slice_fusion, bf16[256,1280]{1,0:T(8,128)(2,1)S(1)} %collective-permute-done.4, bf16[128,1280]{1,0:T(8,128)(2,1)S(1)} %get-tuple-element.29, bf16[128,1280]{1,0:T(8,128)(2,1)S(1)} %get-tuple-element.28), kind=kOutput, calls=%fused_computation.2 | convolution fusion | flops 2018770944 | bytes 6815744 | tf_op jit(solution)/shard_map/dot_general | solution.py:60
  75.7 0.6 collective-permute-done.9
  76.5 4.4 %collective-permute-start.10 = (f16[256,768]{1,0:T(8,128)(2,1)S(1)}, f16[256,768]{1,0:T(8,128)(2,1)S(1)}, u32[]{:S(2)}, u32[]{:S(2)}) collective-permute-start(f16[256,768]{1,0:T(8,128)(2,1)S(1)} %fusion.10), channel_id=1, source_target_pairs={{0,4},{4,8},{1,5},{5,9},{2,6},{6,10},{3,7},{7,11},{16,20},{20,24},... | collective-permute-start | bytes 1179656 | tf_op jit(solution)/shard_map/ppermute | solution.py:74
  80.9 0.7 collective-permute-start.12
  81.6 11.6 %collective-permute-done.15 = f16[256,1536]{1,0:T(8,128)(2,1)S(1)} collective-permute-done((f16[256,1536]{1,0:T(8,128)(2,1)S(1)}, f16[256,1536]{1,0:T(8,128)(2,1)S(1)}, u32[]{:S(2)}, u32[]{:S(2)}) %collective-permute-start.15) | collective-permute-done | bytes 786464 | tf_op jit(solution)/shard_map/ppermute | solution.py:74
  93.2 0.6 add_convert_fusion.1
  93.8 1.3 collective-permute-start.18
  95.1 5.1 %collective-permute-start.16 = (f16[256,1536]{1,0:T(8,128)(2,1)S(1)}, f16[256,1536]{1,0:T(8,128)(2,1)S(1)}, u32[]{:S(2)}, u32[]{:S(2)}) collective-permute-start(f16[256,1536]{1,0:T(8,128)(2,1)S(1)} %get-tuple-element.24), channel_id=1, source_target_pairs={{0,4},{4,8},{8,12},{1,5},{5,9},{9,13},{2,6},{6,10},{10,14},{3,7},{... | collective-permute-start | bytes 2359304 | tf_op jit(solution)/shard_map/ppermute | solution.py:79
  100.1 1.2 multiply_convert_fusion.1
  101.6 0.3 add_convert_fusion.4
  101.9 1.3 collective-permute-start.13
  103.2 5.0 %collective-permute-start.11 = (f16[256,768]{1,0:T(8,128)(2,1)S(1)}, f16[256,768]{1,0:T(8,128)(2,1)S(1)}, u32[]{:S(2)}, u32[]{:S(2)}) collective-permute-start(f16[256,768]{1,0:T(8,128)(2,1)S(1)} %get-tuple-element.26), channel_id=1, source_target_pairs={{0,4},{4,8},{8,12},{1,5},{5,9},{9,13},{2,6},{6,10},{10,14},{3,7},{... | collective-permute-start | bytes 1179656 | tf_op jit(solution)/shard_map/ppermute | solution.py:79
  108.4 6.1 %collective-permute-done.18 = f16[256,1536]{1,0:T(8,128)(2,1)S(1)} collective-permute-done((f16[256,1536]{1,0:T(8,128)(2,1)S(1)}, f16[256,1536]{1,0:T(8,128)(2,1)S(1)}, u32[]{:S(2)}, u32[]{:S(2)}) %collective-permute-start.18) | collective-permute-done | bytes 786464 | tf_op jit(solution)/shard_map/ppermute | solution.py:80
  114.5 4.0 %collective-permute-done.16 = f16[256,1536]{1,0:T(8,128)(2,1)S(1)} collective-permute-done((f16[256,1536]{1,0:T(8,128)(2,1)S(1)}, f16[256,1536]{1,0:T(8,128)(2,1)S(1)}, u32[]{:S(2)}, u32[]{:S(2)}) %collective-permute-start.16) | collective-permute-done | bytes 786464 | tf_op jit(solution)/shard_map/ppermute | solution.py:79
  118.5 1.8 fusion.5
  120.2 2.5 %collective-permute-start.19 = (bf16[256,768]{1,0:T(8,128)(2,1)S(1)}, bf16[256,768]{1,0:T(8,128)(2,1)S(1)}, u32[]{:S(2)}, u32[]{:S(2)}) collective-permute-start(bf16[256,768]{1,0:T(8,128)(2,1)S(1)} %get-tuple-element.12.key_ref), channel_id=1, source_target_pairs={{0,4},{4,0},{8,12},{12,8},{1,5},{5,1},{9,13},{13,9},{2,6},{6,2},{1... | collective-permute-start | bytes 1179656 | tf_op jit(solution)/shard_map/ppermute | solution.py:87
  122.8 0.7 collective-permute-start.20
  123.4 2.9 %collective-permute-start.21 = (bf16[256,768]{1,0:T(8,128)(2,1)S(1)}, bf16[256,768]{1,0:T(8,128)(2,1)S(1)}, u32[]{:S(2)}, u32[]{:S(2)}) collective-permute-start(bf16[256,768]{1,0:T(8,128)(2,1)S(1)} %get-tuple-element.13.value_ref), channel_id=1, source_target_pairs={{0,4},{4,0},{8,12},{12,8},{1,5},{5,1},{9,13},{13,9},{2,6},{6,2},{1... | collective-permute-start | bytes 1179656 | tf_op jit(solution)/shard_map/ppermute | solution.py:87
  126.4 0.9 collective-permute-start.22
  127.4 10.9 %shard_map.77 = (bf16[256,1280]{1,0:T(8,128)(2,1)S(1)}, bf16[256,1280]{1,0:T(8,128)(2,1)}, f32[256,1280]{1,0:T(8,128)S(1)}, f32[256,1280]{1,0:T(8,128)S(1)}) custom-call(s32[5]{0:T(128)S(1)} %stack.23.place_ref, bf16[256,768]{1,0:T(8,128)(2,1)S(1)} %fusion.9.query_ref, bf16[2,1024,768]{2,1,0:T(8,128)(2,1)} %stale_ref.1, ...), custom_call_target="tpu_custom_call" | custom-call | flops 2818572288 | bytes 14942208 | tf_op jit(solution)/shard_map/pallas_call | solution.py:193
  138.4 1.1 copy-done.1
  139.5 1.1 copy-done.3
  140.6 0.3 collective-permute-done.21
  140.9 0.7 copy-done.7
  141.6 0.7 copy-done.9
  142.4 0.6 collective-permute-start.23
  143.4 1.4 collective-permute-start.27
  144.8 0.7 collective-permute-start.28
  145.5 1.3 collective-permute-start.30
  146.9 0.7 collective-permute-start.31
  147.6 1.0 add_convert_fusion.7
  148.6 0.4 collective-permute-start.26
  149.1 8.3 %collective-permute-done.27 = bf16[256,768]{1,0:T(8,128)(2,1)S(1)} collective-permute-done((bf16[256,768]{1,0:T(8,128)(2,1)S(1)}, bf16[256,768]{1,0:T(8,128)(2,1)S(1)}, u32[]{:S(2)}, u32[]{:S(2)}) %collective-permute-start.27) | collective-permute-done | bytes 393248 | tf_op jit(solution)/shard_map/ppermute | solution.py:96
  157.4 1.5 collective-permute-start.24
  159.0 1.3 collective-permute-start.29
  160.3 1.3 collective-permute-start.32
  161.6 1.1 add_convert_fusion.6
  162.7 3.8 %collective-permute-done.24 = bf16[256,640]{1,0:T(8,128)(2,1)S(1)} collective-permute-done((bf16[256,640]{1,0:T(8,128)(2,1)S(1)}, bf16[256,640]{1,0:T(8,128)(2,1)S(1)}, u32[]{:S(2)}, u32[]{:S(2)}) %collective-permute-start.24) | collective-permute-done | bytes 327712 | tf_op jit(solution)/shard_map/ppermute | solution.py:229
  166.7 0.9 pad_maximum_fusion.4
  167.6 6.6 %collective-permute-done.29 = bf16[256,768]{1,0:T(8,128)(2,1)S(1)} collective-permute-done((bf16[256,768]{1,0:T(8,128)(2,1)S(1)}, bf16[256,768]{1,0:T(8,128)(2,1)S(1)}, u32[]{:S(2)}, u32[]{:S(2)}) %collective-permute-start.29) | collective-permute-done | bytes 393248 | tf_op jit(solution)/shard_map/ppermute | solution.py:97
  174.5 7.9 %collective-permute-done.32 = bf16[256,768]{1,0:T(8,128)(2,1)S(1)} collective-permute-done((bf16[256,768]{1,0:T(8,128)(2,1)S(1)}, bf16[256,768]{1,0:T(8,128)(2,1)S(1)}, u32[]{:S(2)}, u32[]{:S(2)}) %collective-permute-start.32) | collective-permute-done | bytes 393248 | tf_op jit(solution)/shard_map/ppermute | solution.py:97
  182.5 1.7 copy-done.5
  (74 shorter events, 2.8 us)
Async XLA Ops:
  0.6 49.6 %copy-start = (bf16[1280,768]{1,0:T(8,128)(2,1)S(1)}, bf16[1280,768]{1,0:T(8,128)(2,1)}, u32[]{:S(2)}) copy-start(bf16[1280,768]{1,0:T(8,128)(2,1)} %param.7) | copy-start | bytes 5898244
  1.9 10.7 %collective-permute-start.1 = (bf16[128,1280]{1,0:T(8,128)(2,1)S(1)}, bf16[128,1280]{1,0:T(8,128)(2,1)S(1)}, u32[]{:S(2)}, u32[]{:S(2)}) collective-permute-start(bf16[128,1280]{1,0:T(8,128)(2,1)S(1)} %get-tuple-element.32), channel_id=1, source_target_pairs={{0,2},{1,3},{2,0},{3,1},{4,6},{5,7},{6,4},{7,5},{8,10},{9,11},{10,... | collective-permute-start | bytes 983048 | tf_op jit(solution)/shard_map/ppermute | solution.py:31
  4.9 19.9 %collective-permute-start.5 = (bf16[128,1280]{1,0:T(8,128)(2,1)S(1)}, bf16[128,1280]{1,0:T(8,128)(2,1)S(1)}, u32[]{:S(2)}, u32[]{:S(2)}) collective-permute-start(bf16[128,1280]{1,0:T(8,128)(2,1)S(1)} %get-tuple-element.33), channel_id=1, source_target_pairs={{2,10},{3,14},{6,11},{7,15},{8,0},{9,4},{12,1},{13,5},{18,26},{19,... | collective-permute-start | bytes 983048 | tf_op jit(solution)/shard_map/ppermute | solution.py:41
  12.6 12.2 %copy-start.15 = (bf16[128,1280]{1,0:T(8,128)(2,1)}, bf16[128,1280]{1,0:T(8,128)(2,1)S(1)}, u32[]{:S(2)}) copy-start(bf16[128,1280]{1,0:T(8,128)(2,1)S(1)} %collective-permute-done.1) | copy-start | bytes 983044
  12.6 12.5 %collective-permute-start.6 = (bf16[128,1280]{1,0:T(8,128)(2,1)S(1)}, bf16[128,1280]{1,0:T(8,128)(2,1)S(1)}, u32[]{:S(2)}, u32[]{:S(2)}) collective-permute-start(bf16[128,1280]{1,0:T(8,128)(2,1)S(1)} %collective-permute-done.1), channel_id=1, source_target_pairs={{0,8},{1,12},{4,9},{5,13},{10,2},{11,6},{14,3},{15,7},{16,24},{17,... | collective-permute-start | bytes 983048 | tf_op jit(solution)/shard_map/ppermute | solution.py:41
  25.2 13.7 %collective-permute-start.7 = (bf16[128,1280]{1,0:T(8,128)(2,1)S(1)}, bf16[128,1280]{1,0:T(8,128)(2,1)S(1)}, u32[]{:S(2)}, u32[]{:S(2)}) collective-permute-start(bf16[128,1280]{1,0:T(8,128)(2,1)S(1)} %broadcast_select_fusion.2), channel_id=1, source_target_pairs={{0,2},{1,3},{2,0},{3,1},{4,6},{5,7},{6,4},{7,5},{8,10},{9,11},{10,... | collective-permute-start | bytes 983048 | tf_op jit(solution)/shard_map/ppermute | solution.py:45
  33.9 5.6 %collective-permute-start = (bf16[128,1280]{1,0:T(8,128)(2,1)S(1)}, bf16[128,1280]{1,0:T(8,128)(2,1)S(1)}, u32[]{:S(2)}, u32[]{:S(2)}) collective-permute-start(bf16[128,1280]{1,0:T(8,128)(2,1)S(1)} %get-tuple-element.33), channel_id=1, source_target_pairs={{0,0},{1,4},{4,1},{5,5},{10,10},{11,14},{14,11},{15,15},{16,16},{1... | collective-permute-start | bytes 983048 | tf_op jit(solution)/shard_map/ppermute | solution.py:41
  34.7 1.8 copy-start.16
  36.5 2.9 %copy-start.6 = (bf16[1280,768]{1,0:T(8,128)(2,1)S(1)}, bf16[1280,768]{1,0:T(8,128)(2,1)}, u32[]{:S(2)}) copy-start(bf16[1280,768]{1,0:T(8,128)(2,1)} %param.9) | copy-start | bytes 5898244
  36.5 3.0 %collective-permute-start.2 = (bf16[128,1280]{1,0:T(8,128)(2,1)S(1)}, bf16[128,1280]{1,0:T(8,128)(2,1)S(1)}, u32[]{:S(2)}, u32[]{:S(2)}) collective-permute-start(bf16[128,1280]{1,0:T(8,128)(2,1)S(1)} %copy-done.16), channel_id=1, source_target_pairs={{2,2},{3,6},{6,3},{7,7},{8,8},{9,12},{12,9},{13,13},{18,18},{19,22... | collective-permute-start | bytes 983048 | tf_op jit(solution)/shard_map/ppermute | solution.py:41
  39.0 2.4 %collective-permute-start.8 = (bf16[256,1280]{1,0:T(8,128)(2,1)S(1)}, bf16[256,1280]{1,0:T(8,128)(2,1)S(1)}, u32[]{:S(2)}, u32[]{:S(2)}) collective-permute-start(bf16[256,1280]{1,0:T(8,128)(2,1)S(1)} %pad_maximum_fusion.3), channel_id=1, source_target_pairs={{0,1},{1,0},{2,3},{3,2},{4,5},{5,4},{6,7},{7,6},{8,9},{9,8},{10,11... | collective-permute-start | bytes 1966088 | tf_op jit(solution)/shard_map/ppermute | solution.py:49
  39.6 10.4 %collective-permute-start.3 = (bf16[128,1280]{1,0:T(8,128)(2,1)S(1)}, bf16[128,1280]{1,0:T(8,128)(2,1)S(1)}, u32[]{:S(2)}, u32[]{:S(2)}) collective-permute-start(bf16[128,1280]{1,0:T(8,128)(2,1)S(1)} %broadcast_select_fusion.5), channel_id=1, source_target_pairs={{0,2},{1,3},{2,0},{3,1},{4,6},{5,7},{6,4},{7,5},{8,10},{9,11},{10,... | collective-permute-start | bytes 983048 | tf_op jit(solution)/shard_map/ppermute | solution.py:45
  43.8 24.1 %collective-permute-start.14 = (f16[256,1536]{1,0:T(8,128)(2,1)S(1)}, f16[256,1536]{1,0:T(8,128)(2,1)S(1)}, u32[]{:S(2)}, u32[]{:S(2)}) collective-permute-start(f16[256,1536]{1,0:T(8,128)(2,1)S(1)} %dynamic-slice_bitcast_fusion), channel_id=1, source_target_pairs={{0,4},{12,8},{1,5},{13,9},{2,6},{14,10},{3,7},{15,11},{16,20},{28,... | collective-permute-start | bytes 2359304 | tf_op jit(solution)/shard_map/ppermute | solution.py:72
  50.1 23.4 %collective-permute-start.4 = (bf16[256,1280]{1,0:T(8,128)(2,1)S(1)}, bf16[256,1280]{1,0:T(8,128)(2,1)S(1)}, u32[]{:S(2)}, u32[]{:S(2)}) collective-permute-start(bf16[256,1280]{1,0:T(8,128)(2,1)S(1)} %pad_maximum_fusion.2), channel_id=1, source_target_pairs={{0,1},{1,0},{2,3},{3,2},{4,5},{5,4},{6,7},{7,6},{8,9},{9,8},{10,11... | collective-permute-start | bytes 1966088 | tf_op jit(solution)/shard_map/ppermute | solution.py:49
  51.5 24.8 %collective-permute-start.9 = (f16[256,768]{1,0:T(8,128)(2,1)S(1)}, f16[256,768]{1,0:T(8,128)(2,1)S(1)}, u32[]{:S(2)}, u32[]{:S(2)}) collective-permute-start(f16[256,768]{1,0:T(8,128)(2,1)S(1)} %dynamic-slice_bitcast_fusion.4), channel_id=1, source_target_pairs={{0,4},{12,8},{1,5},{13,9},{2,6},{14,10},{3,7},{15,11},{16,20},{28,... | collective-permute-start | bytes 1179656 | tf_op jit(solution)/shard_map/ppermute | solution.py:72
  68.3 24.8 %collective-permute-start.15 = (f16[256,1536]{1,0:T(8,128)(2,1)S(1)}, f16[256,1536]{1,0:T(8,128)(2,1)S(1)}, u32[]{:S(2)}, u32[]{:S(2)}) collective-permute-start(f16[256,1536]{1,0:T(8,128)(2,1)S(1)} %fusion.6), channel_id=1, source_target_pairs={{0,4},{4,8},{1,5},{5,9},{2,6},{6,10},{3,7},{7,11},{16,20},{20,24},... | collective-permute-start | bytes 2359304 | tf_op jit(solution)/shard_map/ppermute | solution.py:74
  72.8 20.4 %collective-permute-start.17 = (f16[256,1536]{1,0:T(8,128)(2,1)S(1)}, f16[256,1536]{1,0:T(8,128)(2,1)S(1)}, u32[]{:S(2)}, u32[]{:S(2)}) collective-permute-start(f16[256,1536]{1,0:T(8,128)(2,1)S(1)} %fusion.6), channel_id=1, source_target_pairs={{12,8},{8,4},{13,9},{9,5},{14,10},{10,6},{15,11},{11,7},{28,24},{2... | collective-permute-start | bytes 2359304 | tf_op jit(solution)/shard_map/ppermute | solution.py:75
  76.5 25.1 %collective-permute-start.10 = (f16[256,768]{1,0:T(8,128)(2,1)S(1)}, f16[256,768]{1,0:T(8,128)(2,1)S(1)}, u32[]{:S(2)}, u32[]{:S(2)}) collective-permute-start(f16[256,768]{1,0:T(8,128)(2,1)S(1)} %fusion.10), channel_id=1, source_target_pairs={{0,4},{4,8},{1,5},{5,9},{2,6},{6,10},{3,7},{7,11},{16,20},{20,24},... | collective-permute-start | bytes 1179656 | tf_op jit(solution)/shard_map/ppermute | solution.py:74
  80.9 20.7 %collective-permute-start.12 = (f16[256,768]{1,0:T(8,128)(2,1)S(1)}, f16[256,768]{1,0:T(8,128)(2,1)S(1)}, u32[]{:S(2)}, u32[]{:S(2)}) collective-permute-start(f16[256,768]{1,0:T(8,128)(2,1)S(1)} %fusion.10), channel_id=1, source_target_pairs={{12,8},{8,4},{13,9},{9,5},{14,10},{10,6},{15,11},{11,7},{28,24},{2... | collective-permute-start | bytes 1179656 | tf_op jit(solution)/shard_map/ppermute | solution.py:75
  93.8 20.7 %collective-permute-start.18 = (f16[256,1536]{1,0:T(8,128)(2,1)S(1)}, f16[256,1536]{1,0:T(8,128)(2,1)S(1)}, u32[]{:S(2)}, u32[]{:S(2)}) collective-permute-start(f16[256,1536]{1,0:T(8,128)(2,1)S(1)} %get-tuple-element.25), channel_id=1, source_target_pairs={{12,8},{8,4},{4,0},{13,9},{9,5},{5,1},{14,10},{10,6},{6,2},{15,11}... | collective-permute-start | bytes 2359304 | tf_op jit(solution)/shard_map/ppermute | solution.py:80
  95.1 23.4 %collective-permute-start.16 = (f16[256,1536]{1,0:T(8,128)(2,1)S(1)}, f16[256,1536]{1,0:T(8,128)(2,1)S(1)}, u32[]{:S(2)}, u32[]{:S(2)}) collective-permute-start(f16[256,1536]{1,0:T(8,128)(2,1)S(1)} %get-tuple-element.24), channel_id=1, source_target_pairs={{0,4},{4,8},{8,12},{1,5},{5,9},{9,13},{2,6},{6,10},{10,14},{3,7},{... | collective-permute-start | bytes 2359304 | tf_op jit(solution)/shard_map/ppermute | solution.py:79
  101.9 24.5 %collective-permute-start.13 = (f16[256,768]{1,0:T(8,128)(2,1)S(1)}, f16[256,768]{1,0:T(8,128)(2,1)S(1)}, u32[]{:S(2)}, u32[]{:S(2)}) collective-permute-start(f16[256,768]{1,0:T(8,128)(2,1)S(1)} %get-tuple-element.27), channel_id=1, source_target_pairs={{12,8},{8,4},{4,0},{13,9},{9,5},{5,1},{14,10},{10,6},{6,2},{15,11}... | collective-permute-start | bytes 1179656 | tf_op jit(solution)/shard_map/ppermute | solution.py:80
  103.2 24.0 %collective-permute-start.11 = (f16[256,768]{1,0:T(8,128)(2,1)S(1)}, f16[256,768]{1,0:T(8,128)(2,1)S(1)}, u32[]{:S(2)}, u32[]{:S(2)}) collective-permute-start(f16[256,768]{1,0:T(8,128)(2,1)S(1)} %get-tuple-element.26), channel_id=1, source_target_pairs={{0,4},{4,8},{8,12},{1,5},{5,9},{9,13},{2,6},{6,10},{10,14},{3,7},{... | collective-permute-start | bytes 1179656 | tf_op jit(solution)/shard_map/ppermute | solution.py:79
  120.2 20.3 %collective-permute-start.19 = (bf16[256,768]{1,0:T(8,128)(2,1)S(1)}, bf16[256,768]{1,0:T(8,128)(2,1)S(1)}, u32[]{:S(2)}, u32[]{:S(2)}) collective-permute-start(bf16[256,768]{1,0:T(8,128)(2,1)S(1)} %get-tuple-element.12.key_ref), channel_id=1, source_target_pairs={{0,4},{4,0},{8,12},{12,8},{1,5},{5,1},{9,13},{13,9},{2,6},{6,2},{1... | collective-permute-start | bytes 1179656 | tf_op jit(solution)/shard_map/ppermute | solution.py:87
  122.8 17.8 %collective-permute-start.20 = (bf16[256,768]{1,0:T(8,128)(2,1)S(1)}, bf16[256,768]{1,0:T(8,128)(2,1)S(1)}, u32[]{:S(2)}, u32[]{:S(2)}) collective-permute-start(bf16[256,768]{1,0:T(8,128)(2,1)S(1)} %get-tuple-element.12.key_ref), channel_id=1, source_target_pairs={{4,8},{8,4},{5,9},{9,5},{6,10},{10,6},{7,11},{11,7},{20,24},{24,20... | collective-permute-start | bytes 1179656 | tf_op jit(solution)/shard_map/ppermute | solution.py:88
  123.4 17.4 %collective-permute-start.21 = (bf16[256,768]{1,0:T(8,128)(2,1)S(1)}, bf16[256,768]{1,0:T(8,128)(2,1)S(1)}, u32[]{:S(2)}, u32[]{:S(2)}) collective-permute-start(bf16[256,768]{1,0:T(8,128)(2,1)S(1)} %get-tuple-element.13.value_ref), channel_id=1, source_target_pairs={{0,4},{4,0},{8,12},{12,8},{1,5},{5,1},{9,13},{13,9},{2,6},{6,2},{1... | collective-permute-start | bytes 1179656 | tf_op jit(solution)/shard_map/ppermute | solution.py:87
  126.4 14.5 %collective-permute-start.22 = (bf16[256,768]{1,0:T(8,128)(2,1)S(1)}, bf16[256,768]{1,0:T(8,128)(2,1)S(1)}, u32[]{:S(2)}, u32[]{:S(2)}) collective-permute-start(bf16[256,768]{1,0:T(8,128)(2,1)S(1)} %get-tuple-element.13.value_ref), channel_id=1, source_target_pairs={{4,8},{8,4},{5,9},{9,5},{6,10},{10,6},{7,11},{11,7},{20,24},{24,20... | collective-permute-start | bytes 1179656 | tf_op jit(solution)/shard_map/ppermute | solution.py:88
  138.4 1.1 copy-start.1
  139.5 1.1 copy-start.3
  140.5 1.1 copy-start.11
  140.5 1.1 copy-start.13
  140.9 0.7 copy-start.7
  141.6 0.7 copy-start.9
  142.4 4.5 %collective-permute-start.25 = (bf16[256,1280]{1,0:T(8,128)(2,1)}, bf16[256,1280]{1,0:T(8,128)(2,1)}, u32[]{:S(2)}, u32[]{:S(2)}) collective-permute-start(bf16[256,1280]{1,0:T(8,128)(2,1)} %get-tuple-element.19), channel_id=1, source_target_pairs={{0,1},{1,0},{2,3},{3,2},{4,5},{5,4},{6,7},{7,6},{8,9},{9,8},{10,11... | collective-permute-start | bytes 1966088 | tf_op jit(solution)/shard_map/ppermute | solution.py:218
  142.4 1.0 copy-start.14
  142.4 2.4 %copy-start.12 = (bf16[256,768]{1,0:T(8,128)(2,1)S(1)}, bf16[256,768]{1,0:T(8,128)(2,1)}, u32[]{:S(2)}) copy-start(bf16[256,768]{1,0:T(8,128)(2,1)} %copy-done.11) | copy-start | bytes 1179652
  142.4 3.1 %copy-start.10 = (bf16[256,768]{1,0:T(8,128)(2,1)S(1)}, bf16[256,768]{1,0:T(8,128)(2,1)}, u32[]{:S(2)}) copy-start(bf16[256,768]{1,0:T(8,128)(2,1)} %copy-done.9) | copy-start | bytes 1179652
  142.4 4.5 %copy-start.8 = (bf16[256,768]{1,0:T(8,128)(2,1)S(1)}, bf16[256,768]{1,0:T(8,128)(2,1)}, u32[]{:S(2)}) copy-start(bf16[256,768]{1,0:T(8,128)(2,1)} %copy-done.7) | copy-start | bytes 1179652
  142.4 5.2 %copy-start.4 = (f32[256,1280]{1,0:T(8,128)S(1)}, f32[256,1280]{1,0:T(8,128)}, u32[]{:S(2)}) copy-start(f32[256,1280]{1,0:T(8,128)} %copy-done.3) | copy-start | bytes 3932164
  142.4 6.2 %collective-permute-start.23 = (bf16[256,1280]{1,0:T(8,128)(2,1)S(1)}, bf16[256,1280]{1,0:T(8,128)(2,1)S(1)}, u32[]{:S(2)}, u32[]{:S(2)}) collective-permute-start(bf16[256,1280]{1,0:T(8,128)(2,1)S(1)} %get-tuple-element.16), channel_id=1, source_target_pairs={{0,1},{1,0},{2,3},{3,2},{4,5},{5,4},{6,7},{7,6},{8,9},{9,8},{10,11... | collective-permute-start | bytes 1966088 | tf_op jit(solution)/shard_map/ppermute | solution.py:218
  143.2 5.8 %copy-start.2 = (f32[256,1280]{1,0:T(8,128)S(1)}, f32[256,1280]{1,0:T(8,128)}, u32[]{:S(2)}) copy-start(f32[256,1280]{1,0:T(8,128)} %copy-done.1) | copy-start | bytes 3932164
  143.4 14.0 %collective-permute-start.27 = (bf16[256,768]{1,0:T(8,128)(2,1)S(1)}, bf16[256,768]{1,0:T(8,128)(2,1)S(1)}, u32[]{:S(2)}, u32[]{:S(2)}) collective-permute-start(bf16[256,768]{1,0:T(8,128)(2,1)S(1)} %copy-done.14), channel_id=1, source_target_pairs={{4,0},{8,12},{5,1},{9,13},{6,2},{10,14},{7,3},{11,15},{20,16},{24,... | collective-permute-start | bytes 1179656 | tf_op jit(solution)/shard_map/ppermute | solution.py:96
  144.8 14.2 %collective-permute-start.28 = (bf16[256,768]{1,0:T(8,128)(2,1)S(1)}, bf16[256,768]{1,0:T(8,128)(2,1)S(1)}, u32[]{:S(2)}, u32[]{:S(2)}) collective-permute-start(bf16[256,768]{1,0:T(8,128)(2,1)S(1)} %copy-done.12), channel_id=1, source_target_pairs={{4,8},{8,4},{5,9},{9,5},{6,10},{10,6},{7,11},{11,7},{20,24},{24,20... | collective-permute-start | bytes 1179656 | tf_op jit(solution)/shard_map/ppermute | solution.py:95
  145.5 28.9 %collective-permute-start.30 = (bf16[256,768]{1,0:T(8,128)(2,1)S(1)}, bf16[256,768]{1,0:T(8,128)(2,1)S(1)}, u32[]{:S(2)}, u32[]{:S(2)}) collective-permute-start(bf16[256,768]{1,0:T(8,128)(2,1)S(1)} %copy-done.10), channel_id=1, source_target_pairs={{4,0},{8,12},{5,1},{9,13},{6,2},{10,14},{7,3},{11,15},{20,16},{24,... | collective-permute-start | bytes 1179656 | tf_op jit(solution)/shard_map/ppermute | solution.py:96
  146.9 13.5 %collective-permute-start.31 = (bf16[256,768]{1,0:T(8,128)(2,1)S(1)}, bf16[256,768]{1,0:T(8,128)(2,1)S(1)}, u32[]{:S(2)}, u32[]{:S(2)}) collective-permute-start(bf16[256,768]{1,0:T(8,128)(2,1)S(1)} %copy-done.8), channel_id=1, source_target_pairs={{4,8},{8,4},{5,9},{9,5},{6,10},{10,6},{7,11},{11,7},{20,24},{24,20... | collective-permute-start | bytes 1179656 | tf_op jit(solution)/shard_map/ppermute | solution.py:95
  148.6 13.0 %collective-permute-start.26 = (bf16[256,640]{1,0:T(8,128)(2,1)S(1)}, bf16[256,640]{1,0:T(8,128)(2,1)S(1)}, u32[]{:S(2)}, u32[]{:S(2)}) collective-permute-start(bf16[256,640]{1,0:T(8,128)(2,1)S(1)} %add_convert_fusion.7), channel_id=1, source_target_pairs={{0,2},{1,3},{2,0},{3,1},{4,6},{5,7},{6,4},{7,5},{8,10},{9,11},{10,... | collective-permute-start | bytes 983048 | tf_op jit(solution)/shard_map/ppermute | solution.py:229
  157.4 9.2 %collective-permute-start.24 = (bf16[256,640]{1,0:T(8,128)(2,1)S(1)}, bf16[256,640]{1,0:T(8,128)(2,1)S(1)}, u32[]{:S(2)}, u32[]{:S(2)}) collective-permute-start(bf16[256,640]{1,0:T(8,128)(2,1)S(1)} %add_convert_fusion.9), channel_id=1, source_target_pairs={{0,2},{1,3},{2,0},{3,1},{4,6},{5,7},{6,4},{7,5},{8,10},{9,11},{10,... | collective-permute-start | bytes 983048 | tf_op jit(solution)/shard_map/ppermute | solution.py:229
  159.0 15.2 %collective-permute-start.29 = (bf16[256,768]{1,0:T(8,128)(2,1)S(1)}, bf16[256,768]{1,0:T(8,128)(2,1)S(1)}, u32[]{:S(2)}, u32[]{:S(2)}) collective-permute-start(bf16[256,768]{1,0:T(8,128)(2,1)S(1)} %collective-permute-done.28), channel_id=1, source_target_pairs={{4,0},{8,12},{5,1},{9,13},{6,2},{10,14},{7,3},{11,15},{20,16},{24,... | collective-permute-start | bytes 1179656 | tf_op jit(solution)/shard_map/ppermute | solution.py:97
  160.3 22.1 %collective-permute-start.32 = (bf16[256,768]{1,0:T(8,128)(2,1)S(1)}, bf16[256,768]{1,0:T(8,128)(2,1)S(1)}, u32[]{:S(2)}, u32[]{:S(2)}) collective-permute-start(bf16[256,768]{1,0:T(8,128)(2,1)S(1)} %collective-permute-done.31), channel_id=1, source_target_pairs={{4,0},{8,12},{5,1},{9,13},{6,2},{10,14},{7,3},{11,15},{20,16},{24,... | collective-permute-start | bytes 1179656 | tf_op jit(solution)/shard_map/ppermute | solution.py:97
  182.5 1.7 copy-start.5

commit v14 on v13

--- a/solution.py
+++ b/solution.py
@@ -207,7 +207,7 @@
             out_specs=[pl.BlockSpec((rows, chips * part), lambda h, p: (0, 0))] * (2 * chunks),
             scratch_shapes=[pltpu.VMEM((rows, model), F32)],
         ),
-        compiler_params=pltpu.CompilerParams(vmem_limit_bytes=48 * 2**20),
+        compiler_params=pltpu.CompilerParams(vmem_limit_bytes=60 * 2**20),
         cost_estimate=pl.CostEstimate(
             flops=4 * rows * tokens * depth + 2 * rows * depth * model,
             bytes_accessed=4 * tokens * depth + 2 * depth * model + 6 * rows * chips * width,
@@ -271,8 +271,8 @@
             first_hop = ()
         attended, sent = attend(query, stale_kv, key_new, value_new, w_out, patches, ranks, *first_hop)
         if in_pairs:
-            refreshed = keys.into(jnp.zeros_like(stale_kv), 0, *sent)
-            refreshed = values.into(refreshed, 1, *sent)
+            refreshed = keys.into(jnp.zeros_like(stale_kv), 0, *sent[:1])
+            refreshed = values.into(refreshed, 1, *sent[:1])
         else:
             refreshed = lax.all_gather(jnp.stack([key_new, value_new]), "patch", axis=1, tiled=True)
         return (attended, refreshed)

time: 185 us -> 185 us (level)
  waiting for transfers between devices: 77.7 us -> 80.6 us
  starting transfers between devices: 70.7 us -> 68.6 us
    unnamed x35 -> x27, local copies, waits for them, and re-layouts: 7.24 us -> 4.29 us
  transfers between devices with their start and end apart: 33 -> 33, of which waited for: 15 -> 15; matrix products, arithmetic and copies ran while one was open for 9% -> 10% of each run, Pallas kernels for 6% -> 7%
where the time goes in v14:
time: 185 us
  waiting for transfers between devices  80.6 us (44%)
  starting transfers between devices  68.6 us (37%)
  Pallas kernels  12.3 us (7%)
  local copies, waits for them, and re-layouts  8.14 us (4%)
  other arithmetic  6.9 us (4%)
  matrix products  6.77 us (4%)
    ppermute x2, waiting for transfers between devices, into(): last = lax.ppermute(after(across_mate, *earlier), 'patch', outward)  15.1 us
    ppermute x2, waiting for transfers between devices, sum_in_pairs(): first = lax.ppermute(outermost, 'patch', [(0, 1), (3, 2)])  13.7 us
    pallas_call x1, Pallas kernels, attend(): pl.pallas_call(functools.partial(attend_and_project, patches, heads, chip...  12.3 us
    ppermute x2, waiting for transfers between devices, sum_in_pairs(): up = lax.ppermute(second, 'patch', [(0, 1), (1, 2)])  11.8 us
    ppermute x2, starting transfers between devices, sum_in_pairs(): up = lax.ppermute(third_up, 'patch', [(0, 1), (1, 2), (2, 3)])  10.1 us
    ppermute x2, starting transfers between devices, both_slabs(): other = lax.ppermute(held, 'tensor', across)  9.97 us
    ppermute x2, starting transfers between devices, sum_in_pairs(): first = lax.ppermute(outermost, 'patch', [(0, 1), (3, 2)])  9.91 us
    ppermute x2, waiting for transfers between devices, into(): lax.ppermute(self.across, 'patch', outward)  9.55 us
  transfers between devices with their start and end apart: 33, of which 15 were waited for; matrix products, arithmetic and copies ran while one was open for 10% of the time, Pallas kernels for 7%

profile of v14, /device:TPU:0, one launch (start us, length us, event | category | flops | bytes accessed | tf_op | source)
XLA Modules:
  0.0 184.6 jit_solution(14309405955200475847)
XLA Ops:
  0.6 1.3 fusion.15
  1.9 3.0 %collective-permute-start.1 = (bf16[128,1280]{1,0:T(8,128)(2,1)S(1)}, bf16[128,1280]{1,0:T(8,128)(2,1)S(1)}, u32[]{:S(2)}, u32[]{:S(2)}) collective-permute-start(bf16[128,1280]{1,0:T(8,128)(2,1)S(1)} %get-tuple-element.32), channel_id=1, source_target_pairs={{0,2},{1,3},{2,0},{3,1},{4,6},{5,7},{6,4},{7,5},{8,10},{9,11},{10,... | collective-permute-start | bytes 983048 | tf_op jit(solution)/shard_map/ppermute | solution.py:31
  4.9 1.3 collective-permute-start.5
  6.2 6.4 %collective-permute-done.1 = bf16[128,1280]{1,0:T(8,128)(2,1)S(1)} collective-permute-done((bf16[128,1280]{1,0:T(8,128)(2,1)S(1)}, bf16[128,1280]{1,0:T(8,128)(2,1)S(1)}, u32[]{:S(2)}, u32[]{:S(2)}) %collective-permute-start.1) | collective-permute-done | bytes 327712 | tf_op jit(solution)/shard_map/ppermute | solution.py:31
  12.6 4.8 %collective-permute-start.6 = (bf16[128,1280]{1,0:T(8,128)(2,1)S(1)}, bf16[128,1280]{1,0:T(8,128)(2,1)S(1)}, u32[]{:S(2)}, u32[]{:S(2)}) collective-permute-start(bf16[128,1280]{1,0:T(8,128)(2,1)S(1)} %collective-permute-done.1), channel_id=1, source_target_pairs={{0,8},{1,12},{4,9},{5,13},{10,2},{11,6},{14,3},{15,7},{16,24},{17,... | collective-permute-start | bytes 983048 | tf_op jit(solution)/shard_map/ppermute | solution.py:41
  17.4 7.4 %collective-permute-done.5 = bf16[128,1280]{1,0:T(8,128)(2,1)S(1)} collective-permute-done((bf16[128,1280]{1,0:T(8,128)(2,1)S(1)}, bf16[128,1280]{1,0:T(8,128)(2,1)S(1)}, u32[]{:S(2)}, u32[]{:S(2)}) %collective-permute-start.5) | collective-permute-done | bytes 327712 | tf_op jit(solution)/shard_map/ppermute | solution.py:41
  24.8 0.3 collective-permute-done.6
  25.2 8.7 %collective-permute-start.7 = (bf16[128,1280]{1,0:T(8,128)(2,1)S(1)}, bf16[128,1280]{1,0:T(8,128)(2,1)S(1)}, u32[]{:S(2)}, u32[]{:S(2)}) collective-permute-start(bf16[128,1280]{1,0:T(8,128)(2,1)S(1)} %broadcast_select_fusion.2), channel_id=1, source_target_pairs={{0,2},{1,3},{2,0},{3,1},{4,6},{5,7},{6,4},{7,5},{8,10},{9,11},{10,... | collective-permute-start | bytes 983048 | tf_op jit(solution)/shard_map/ppermute | solution.py:45
  33.9 0.7 collective-permute-start
  34.6 0.7 stack.23.place_ref
  35.3 1.7 constant_dynamic-update-slice_fusion.1
  37.0 0.8 collective-permute-start.2
  37.9 1.1 collective-permute-done.7
  39.0 0.9 collective-permute-start.8
  40.1 1.3 collective-permute-start.3
  41.4 0.2 collective-permute-done.8
  41.6 2.2 %fusion.1 = f16[512,1536]{1,0:T(8,128)(2,1)S(1)} fusion(bf16[1280,1536]{1,0:T(8,128)(2,1)S(1)} %constant_dynamic-update-slice_fusion, bf16[256,1280]{1,0:T(8,128)(2,1)S(1)} %collective-permute-done.8, bf16[128,1280]{1,0:T(8,128)(2,1)S(1)} %get-tuple-element.31, bf16[128,1280]{1,0:T(8,128)(2,1)S(1)} %get-tuple-element.30), kind=kOutput, calls=%fused_computation.3 | convolution fusion | flops 2018770944 | bytes 6815744 | tf_op jit(solution)/shard_map/dot_general | solution.py:60
  44.0 6.5 %collective-permute-start.14 = (f16[256,1536]{1,0:T(8,128)(2,1)S(1)}, f16[256,1536]{1,0:T(8,128)(2,1)S(1)}, u32[]{:S(2)}, u32[]{:S(2)}) collective-permute-start(f16[256,1536]{1,0:T(8,128)(2,1)S(1)} %dynamic-slice_bitcast_fusion), channel_id=1, source_target_pairs={{0,4},{12,8},{1,5},{13,9},{2,6},{14,10},{3,7},{15,11},{16,20},{28,... | collective-permute-start | bytes 2359304 | tf_op jit(solution)/shard_map/ppermute | solution.py:72
  50.8 1.2 multiply_convert_fusion
  52.1 3.4 %collective-permute-start.9 = (f16[256,768]{1,0:T(8,128)(2,1)S(1)}, f16[256,768]{1,0:T(8,128)(2,1)S(1)}, u32[]{:S(2)}, u32[]{:S(2)}) collective-permute-start(f16[256,768]{1,0:T(8,128)(2,1)S(1)} %dynamic-slice_bitcast_fusion.4), channel_id=1, source_target_pairs={{0,4},{12,8},{1,5},{13,9},{2,6},{14,10},{3,7},{15,11},{16,20},{28,... | collective-permute-start | bytes 1179656 | tf_op jit(solution)/shard_map/ppermute | solution.py:72
  55.4 13.0 %collective-permute-done.14 = f16[256,1536]{1,0:T(8,128)(2,1)S(1)} collective-permute-done((f16[256,1536]{1,0:T(8,128)(2,1)S(1)}, f16[256,1536]{1,0:T(8,128)(2,1)S(1)}, u32[]{:S(2)}, u32[]{:S(2)}) %collective-permute-start.14) | collective-permute-done | bytes 786464 | tf_op jit(solution)/shard_map/ppermute | solution.py:72
  68.5 0.4 fusion.6
  68.9 4.4 %collective-permute-start.15 = (f16[256,1536]{1,0:T(8,128)(2,1)S(1)}, f16[256,1536]{1,0:T(8,128)(2,1)S(1)}, u32[]{:S(2)}, u32[]{:S(2)}) collective-permute-start(f16[256,1536]{1,0:T(8,128)(2,1)S(1)} %fusion.6), channel_id=1, source_target_pairs={{0,4},{4,8},{1,5},{5,9},{2,6},{6,10},{3,7},{7,11},{16,20},{20,24},... | collective-permute-start | bytes 2359304 | tf_op jit(solution)/shard_map/ppermute | solution.py:74
  73.3 0.7 collective-permute-start.17
  74.1 2.2 %fusion = f16[512,1536]{1,0:T(8,128)(2,1)S(1)} fusion(bf16[1280,1536]{1,0:T(8,128)(2,1)S(1)} %constant_dynamic-update-slice_fusion, bf16[256,1280]{1,0:T(8,128)(2,1)S(1)} %collective-permute-done.4, bf16[128,1280]{1,0:T(8,128)(2,1)S(1)} %get-tuple-element.29, bf16[128,1280]{1,0:T(8,128)(2,1)S(1)} %get-tuple-element.28), kind=kOutput, calls=%fused_computation.2 | convolution fusion | flops 2018770944 | bytes 6815744 | tf_op jit(solution)/shard_map/dot_general | solution.py:60
  76.3 0.6 collective-permute-done.9
  76.9 0.2 fusion.10
  77.1 4.4 %collective-permute-start.10 = (f16[256,768]{1,0:T(8,128)(2,1)S(1)}, f16[256,768]{1,0:T(8,128)(2,1)S(1)}, u32[]{:S(2)}, u32[]{:S(2)}) collective-permute-start(f16[256,768]{1,0:T(8,128)(2,1)S(1)} %fusion.10), channel_id=1, source_target_pairs={{0,4},{4,8},{1,5},{5,9},{2,6},{6,10},{3,7},{7,11},{16,20},{20,24},... | collective-permute-start | bytes 1179656 | tf_op jit(solution)/shard_map/ppermute | solution.py:74
  81.5 0.7 collective-permute-start.12
  82.2 11.6 %collective-permute-done.15 = f16[256,1536]{1,0:T(8,128)(2,1)S(1)} collective-permute-done((f16[256,1536]{1,0:T(8,128)(2,1)S(1)}, f16[256,1536]{1,0:T(8,128)(2,1)S(1)}, u32[]{:S(2)}, u32[]{:S(2)}) %collective-permute-start.15) | collective-permute-done | bytes 786464 | tf_op jit(solution)/shard_map/ppermute | solution.py:74
  93.7 0.6 add_convert_fusion.1
  94.3 1.3 collective-permute-start.18
  95.6 5.1 %collective-permute-start.16 = (f16[256,1536]{1,0:T(8,128)(2,1)S(1)}, f16[256,1536]{1,0:T(8,128)(2,1)S(1)}, u32[]{:S(2)}, u32[]{:S(2)}) collective-permute-start(f16[256,1536]{1,0:T(8,128)(2,1)S(1)} %get-tuple-element.24), channel_id=1, source_target_pairs={{0,4},{4,8},{8,12},{1,5},{5,9},{9,13},{2,6},{6,10},{10,14},{3,7},{... | collective-permute-start | bytes 2359304 | tf_op jit(solution)/shard_map/ppermute | solution.py:79
  100.7 1.2 multiply_convert_fusion.1
  101.9 0.3 collective-permute-done.10
  102.2 0.3 add_convert_fusion.4
  102.5 1.3 collective-permute-start.13
  103.8 5.0 %collective-permute-start.11 = (f16[256,768]{1,0:T(8,128)(2,1)S(1)}, f16[256,768]{1,0:T(8,128)(2,1)S(1)}, u32[]{:S(2)}, u32[]{:S(2)}) collective-permute-start(f16[256,768]{1,0:T(8,128)(2,1)S(1)} %get-tuple-element.26), channel_id=1, source_target_pairs={{0,4},{4,8},{8,12},{1,5},{5,9},{9,13},{2,6},{6,10},{10,14},{3,7},{... | collective-permute-start | bytes 1179656 | tf_op jit(solution)/shard_map/ppermute | solution.py:79
  109.0 5.3 %collective-permute-done.18 = f16[256,1536]{1,0:T(8,128)(2,1)S(1)} collective-permute-done((f16[256,1536]{1,0:T(8,128)(2,1)S(1)}, f16[256,1536]{1,0:T(8,128)(2,1)S(1)}, u32[]{:S(2)}, u32[]{:S(2)}) %collective-permute-start.18) | collective-permute-done | bytes 786464 | tf_op jit(solution)/shard_map/ppermute | solution.py:80
  114.3 4.8 %collective-permute-done.16 = f16[256,1536]{1,0:T(8,128)(2,1)S(1)} collective-permute-done((f16[256,1536]{1,0:T(8,128)(2,1)S(1)}, f16[256,1536]{1,0:T(8,128)(2,1)S(1)}, u32[]{:S(2)}, u32[]{:S(2)}) %collective-permute-start.16) | collective-permute-done | bytes 786464 | tf_op jit(solution)/shard_map/ppermute | solution.py:79
  119.0 2.5 %fusion.5 = (bf16[256,768]{1,0:T(8,128)(2,1)S(1)}, bf16[256,768]{1,0:T(8,128)(2,1)}) fusion(f16[256,1536]{1,0:T(8,128)(2,1)S(1)} %collective-permute-done.18, f16[256,1536]{1,0:T(8,128)(2,1)S(1)} %collective-permute-done.16, f16[256,1536]{1,0:T(8,128)(2,1)S(1)} %dynamic-slice_bitcast_fusion.1, bf16[2,1024,768]{2,1,0:T(8,128)(2,1)} %stale_ref.1, ...), kind=kLoop, calls=%fused_computation.18 | loop fusion | flops 4718592 | bytes 3932168 | tf_op jit(solution)/shard_map/convert_element_type | solution.py:259
  121.5 2.5 %collective-permute-start.19 = (bf16[256,768]{1,0:T(8,128)(2,1)}, bf16[256,768]{1,0:T(8,128)(2,1)S(1)}, u32[]{:S(2)}, u32[]{:S(2)}) collective-permute-start(bf16[256,768]{1,0:T(8,128)(2,1)} %get-tuple-element.12.key_ref), channel_id=1, source_target_pairs={{0,4},{4,0},{8,12},{12,8},{1,5},{5,1},{9,13},{13,9},{2,6},{6,2},{1... | collective-permute-start | bytes 1179656 | tf_op jit(solution)/shard_map/ppermute | solution.py:87
  124.0 0.7 collective-permute-start.20
  124.7 2.9 %collective-permute-start.21 = (bf16[256,768]{1,0:T(8,128)(2,1)S(1)}, bf16[256,768]{1,0:T(8,128)(2,1)S(1)}, u32[]{:S(2)}, u32[]{:S(2)}) collective-permute-start(bf16[256,768]{1,0:T(8,128)(2,1)S(1)} %get-tuple-element.13.value_ref), channel_id=1, source_target_pairs={{0,4},{4,0},{8,12},{12,8},{1,5},{5,1},{9,13},{13,9},{2,6},{6,2},{1... | collective-permute-start | bytes 1179656 | tf_op jit(solution)/shard_map/ppermute | solution.py:87
  127.6 0.9 collective-permute-start.22
  128.5 0.9 fusion.9.query_ref
  129.4 12.3 %shard_map.77 = (bf16[256,1280]{1,0:T(8,128)(2,1)}, bf16[256,1280]{1,0:T(8,128)(2,1)}, f32[256,1280]{1,0:T(8,128)}, f32[256,1280]{1,0:T(8,128)}) custom-call(s32[5]{0:T(128)} %stack.23.place_ref, bf16[256,768]{1,0:T(8,128)(2,1)} %fusion.9.query_ref, bf16[2,1024,768]{2,1,0:T(8,128)(2,1)} %stale_ref.1, bf16[256,768]{1,0:T(8,128)(2,1)} %get-tuple-element.12.key_ref, ...), custom_call_target="tpu_custom_call" | custom-call | flops 2818572288 | bytes 14942208 | tf_op jit(solution)/shard_map/pallas_call | solution.py:193
  141.8 0.7 copy-done.7
  142.7 0.5 collective-permute-start.23
  143.2 0.2 broadcast_in_dim.27
  143.4 1.1 bitcast_dynamic-update-slice_fusion.7
  144.5 1.3 collective-permute-start.27
  145.8 0.7 collective-permute-start.28
  146.5 1.3 collective-permute-start.30
  147.9 0.7 collective-permute-start.31
  148.8 9.5 %collective-permute-done.27 = bf16[256,768]{1,0:T(8,128)(2,1)S(1)} collective-permute-done((bf16[256,768]{1,0:T(8,128)(2,1)S(1)}, bf16[256,768]{1,0:T(8,128)(2,1)S(1)}, u32[]{:S(2)}, u32[]{:S(2)}) %collective-permute-start.27) | collective-permute-done | bytes 393248 | tf_op jit(solution)/shard_map/ppermute | solution.py:96
  158.4 0.2 collective-permute-start.24
  158.7 1.3 collective-permute-start.29
  160.0 1.3 collective-permute-start.32
  161.5 5.0 %collective-permute-done.24 = bf16[256,640]{1,0:T(8,128)(2,1)S(1)} collective-permute-done((bf16[256,640]{1,0:T(8,128)(2,1)S(1)}, bf16[256,640]{1,0:T(8,128)(2,1)S(1)}, u32[]{:S(2)}, u32[]{:S(2)}) %collective-permute-start.24) | collective-permute-done | bytes 327712 | tf_op jit(solution)/shard_map/ppermute | solution.py:229
  166.6 0.9 pad_maximum_fusion.4
  167.5 7.8 %collective-permute-done.29 = bf16[256,768]{1,0:T(8,128)(2,1)S(1)} collective-permute-done((bf16[256,768]{1,0:T(8,128)(2,1)S(1)}, bf16[256,768]{1,0:T(8,128)(2,1)S(1)}, u32[]{:S(2)}, u32[]{:S(2)}) %collective-permute-start.29) | collective-permute-done | bytes 393248 | tf_op jit(solution)/shard_map/ppermute | solution.py:97
  175.6 7.3 %collective-permute-done.32 = bf16[256,768]{1,0:T(8,128)(2,1)S(1)} collective-permute-done((bf16[256,768]{1,0:T(8,128)(2,1)S(1)}, bf16[256,768]{1,0:T(8,128)(2,1)S(1)}, u32[]{:S(2)}, u32[]{:S(2)}) %collective-permute-start.32) | collective-permute-done | bytes 393248 | tf_op jit(solution)/shard_map/ppermute | solution.py:97
  183.0 1.7 copy-done.3
  (66 shorter events, 2.1 us)
Async XLA Ops:
  0.6 50.1 %copy-start = (bf16[1280,768]{1,0:T(8,128)(2,1)S(1)}, bf16[1280,768]{1,0:T(8,128)(2,1)}, u32[]{:S(2)}) copy-start(bf16[1280,768]{1,0:T(8,128)(2,1)} %param.7) | copy-start | bytes 5898244
  1.9 10.7 %collective-permute-start.1 = (bf16[128,1280]{1,0:T(8,128)(2,1)S(1)}, bf16[128,1280]{1,0:T(8,128)(2,1)S(1)}, u32[]{:S(2)}, u32[]{:S(2)}) collective-permute-start(bf16[128,1280]{1,0:T(8,128)(2,1)S(1)} %get-tuple-element.32), channel_id=1, source_target_pairs={{0,2},{1,3},{2,0},{3,1},{4,6},{5,7},{6,4},{7,5},{8,10},{9,11},{10,... | collective-permute-start | bytes 983048 | tf_op jit(solution)/shard_map/ppermute | solution.py:31
  4.9 19.9 %collective-permute-start.5 = (bf16[128,1280]{1,0:T(8,128)(2,1)S(1)}, bf16[128,1280]{1,0:T(8,128)(2,1)S(1)}, u32[]{:S(2)}, u32[]{:S(2)}) collective-permute-start(bf16[128,1280]{1,0:T(8,128)(2,1)S(1)} %get-tuple-element.33), channel_id=1, source_target_pairs={{2,10},{3,14},{6,11},{7,15},{8,0},{9,4},{12,1},{13,5},{18,26},{19,... | collective-permute-start | bytes 983048 | tf_op jit(solution)/shard_map/ppermute | solution.py:41
  12.6 12.2 %copy-start.11 = (bf16[128,1280]{1,0:T(8,128)(2,1)}, bf16[128,1280]{1,0:T(8,128)(2,1)S(1)}, u32[]{:S(2)}) copy-start(bf16[128,1280]{1,0:T(8,128)(2,1)S(1)} %collective-permute-done.1) | copy-start | bytes 983044
  12.6 12.5 %collective-permute-start.6 = (bf16[128,1280]{1,0:T(8,128)(2,1)S(1)}, bf16[128,1280]{1,0:T(8,128)(2,1)S(1)}, u32[]{:S(2)}, u32[]{:S(2)}) collective-permute-start(bf16[128,1280]{1,0:T(8,128)(2,1)S(1)} %collective-permute-done.1), channel_id=1, source_target_pairs={{0,8},{1,12},{4,9},{5,13},{10,2},{11,6},{14,3},{15,7},{16,24},{17,... | collective-permute-start | bytes 983048 | tf_op jit(solution)/shard_map/ppermute | solution.py:41
  25.2 13.7 %collective-permute-start.7 = (bf16[128,1280]{1,0:T(8,128)(2,1)S(1)}, bf16[128,1280]{1,0:T(8,128)(2,1)S(1)}, u32[]{:S(2)}, u32[]{:S(2)}) collective-permute-start(bf16[128,1280]{1,0:T(8,128)(2,1)S(1)} %broadcast_select_fusion.2), channel_id=1, source_target_pairs={{0,2},{1,3},{2,0},{3,1},{4,6},{5,7},{6,4},{7,5},{8,10},{9,11},{10,... | collective-permute-start | bytes 983048 | tf_op jit(solution)/shard_map/ppermute | solution.py:45
  33.9 6.2 %collective-permute-start = (bf16[128,1280]{1,0:T(8,128)(2,1)S(1)}, bf16[128,1280]{1,0:T(8,128)(2,1)S(1)}, u32[]{:S(2)}, u32[]{:S(2)}) collective-permute-start(bf16[128,1280]{1,0:T(8,128)(2,1)S(1)} %get-tuple-element.33), channel_id=1, source_target_pairs={{0,0},{1,4},{4,1},{5,5},{10,10},{11,14},{14,11},{15,15},{16,16},{1... | collective-permute-start | bytes 983048 | tf_op jit(solution)/shard_map/ppermute | solution.py:41
  35.3 1.8 copy-start.12
  37.0 2.9 %copy-start.4 = (bf16[1280,768]{1,0:T(8,128)(2,1)S(1)}, bf16[1280,768]{1,0:T(8,128)(2,1)}, u32[]{:S(2)}) copy-start(bf16[1280,768]{1,0:T(8,128)(2,1)} %param.9) | copy-start | bytes 5898244
  37.0 3.0 %collective-permute-start.2 = (bf16[128,1280]{1,0:T(8,128)(2,1)S(1)}, bf16[128,1280]{1,0:T(8,128)(2,1)S(1)}, u32[]{:S(2)}, u32[]{:S(2)}) collective-permute-start(bf16[128,1280]{1,0:T(8,128)(2,1)S(1)} %copy-done.12), channel_id=1, source_target_pairs={{2,2},{3,6},{6,3},{7,7},{8,8},{9,12},{12,9},{13,13},{18,18},{19,22... | collective-permute-start | bytes 983048 | tf_op jit(solution)/shard_map/ppermute | solution.py:41
  39.0 2.6 %collective-permute-start.8 = (bf16[256,1280]{1,0:T(8,128)(2,1)S(1)}, bf16[256,1280]{1,0:T(8,128)(2,1)S(1)}, u32[]{:S(2)}, u32[]{:S(2)}) collective-permute-start(bf16[256,1280]{1,0:T(8,128)(2,1)S(1)} %pad_maximum_fusion.3), channel_id=1, source_target_pairs={{0,1},{1,0},{2,3},{3,2},{4,5},{5,4},{6,7},{7,6},{8,9},{9,8},{10,11... | collective-permute-start | bytes 1966088 | tf_op jit(solution)/shard_map/ppermute | solution.py:49
  40.1 10.4 %collective-permute-start.3 = (bf16[128,1280]{1,0:T(8,128)(2,1)S(1)}, bf16[128,1280]{1,0:T(8,128)(2,1)S(1)}, u32[]{:S(2)}, u32[]{:S(2)}) collective-permute-start(bf16[128,1280]{1,0:T(8,128)(2,1)S(1)} %broadcast_select_fusion.5), channel_id=1, source_target_pairs={{0,2},{1,3},{2,0},{3,1},{4,6},{5,7},{6,4},{7,5},{8,10},{9,11},{10,... | collective-permute-start | bytes 983048 | tf_op jit(solution)/shard_map/ppermute | solution.py:45
  44.0 24.5 %collective-permute-start.14 = (f16[256,1536]{1,0:T(8,128)(2,1)S(1)}, f16[256,1536]{1,0:T(8,128)(2,1)S(1)}, u32[]{:S(2)}, u32[]{:S(2)}) collective-permute-start(f16[256,1536]{1,0:T(8,128)(2,1)S(1)} %dynamic-slice_bitcast_fusion), channel_id=1, source_target_pairs={{0,4},{12,8},{1,5},{13,9},{2,6},{14,10},{3,7},{15,11},{16,20},{28,... | collective-permute-start | bytes 2359304 | tf_op jit(solution)/shard_map/ppermute | solution.py:72
  50.7 23.4 %collective-permute-start.4 = (bf16[256,1280]{1,0:T(8,128)(2,1)S(1)}, bf16[256,1280]{1,0:T(8,128)(2,1)S(1)}, u32[]{:S(2)}, u32[]{:S(2)}) collective-permute-start(bf16[256,1280]{1,0:T(8,128)(2,1)S(1)} %pad_maximum_fusion.2), channel_id=1, source_target_pairs={{0,1},{1,0},{2,3},{3,2},{4,5},{5,4},{6,7},{7,6},{8,9},{9,8},{10,11... | collective-permute-start | bytes 1966088 | tf_op jit(solution)/shard_map/ppermute | solution.py:49
  52.1 24.8 %collective-permute-start.9 = (f16[256,768]{1,0:T(8,128)(2,1)S(1)}, f16[256,768]{1,0:T(8,128)(2,1)S(1)}, u32[]{:S(2)}, u32[]{:S(2)}) collective-permute-start(f16[256,768]{1,0:T(8,128)(2,1)S(1)} %dynamic-slice_bitcast_fusion.4), channel_id=1, source_target_pairs={{0,4},{12,8},{1,5},{13,9},{2,6},{14,10},{3,7},{15,11},{16,20},{28,... | collective-permute-start | bytes 1179656 | tf_op jit(solution)/shard_map/ppermute | solution.py:72
  68.9 24.8 %collective-permute-start.15 = (f16[256,1536]{1,0:T(8,128)(2,1)S(1)}, f16[256,1536]{1,0:T(8,128)(2,1)S(1)}, u32[]{:S(2)}, u32[]{:S(2)}) collective-permute-start(f16[256,1536]{1,0:T(8,128)(2,1)S(1)} %fusion.6), channel_id=1, source_target_pairs={{0,4},{4,8},{1,5},{5,9},{2,6},{6,10},{3,7},{7,11},{16,20},{20,24},... | collective-permute-start | bytes 2359304 | tf_op jit(solution)/shard_map/ppermute | solution.py:74
  73.3 20.4 %collective-permute-start.17 = (f16[256,1536]{1,0:T(8,128)(2,1)S(1)}, f16[256,1536]{1,0:T(8,128)(2,1)S(1)}, u32[]{:S(2)}, u32[]{:S(2)}) collective-permute-start(f16[256,1536]{1,0:T(8,128)(2,1)S(1)} %fusion.6), channel_id=1, source_target_pairs={{12,8},{8,4},{13,9},{9,5},{14,10},{10,6},{15,11},{11,7},{28,24},{2... | collective-permute-start | bytes 2359304 | tf_op jit(solution)/shard_map/ppermute | solution.py:75
  77.1 25.1 %collective-permute-start.10 = (f16[256,768]{1,0:T(8,128)(2,1)S(1)}, f16[256,768]{1,0:T(8,128)(2,1)S(1)}, u32[]{:S(2)}, u32[]{:S(2)}) collective-permute-start(f16[256,768]{1,0:T(8,128)(2,1)S(1)} %fusion.10), channel_id=1, source_target_pairs={{0,4},{4,8},{1,5},{5,9},{2,6},{6,10},{3,7},{7,11},{16,20},{20,24},... | collective-permute-start | bytes 1179656 | tf_op jit(solution)/shard_map/ppermute | solution.py:74
  81.5 20.7 %collective-permute-start.12 = (f16[256,768]{1,0:T(8,128)(2,1)S(1)}, f16[256,768]{1,0:T(8,128)(2,1)S(1)}, u32[]{:S(2)}, u32[]{:S(2)}) collective-permute-start(f16[256,768]{1,0:T(8,128)(2,1)S(1)} %fusion.10), channel_id=1, source_target_pairs={{12,8},{8,4},{13,9},{9,5},{14,10},{10,6},{15,11},{11,7},{28,24},{2... | collective-permute-start | bytes 1179656 | tf_op jit(solution)/shard_map/ppermute | solution.py:75
  94.3 19.9 %collective-permute-start.18 = (f16[256,1536]{1,0:T(8,128)(2,1)S(1)}, f16[256,1536]{1,0:T(8,128)(2,1)S(1)}, u32[]{:S(2)}, u32[]{:S(2)}) collective-permute-start(f16[256,1536]{1,0:T(8,128)(2,1)S(1)} %get-tuple-element.25), channel_id=1, source_target_pairs={{12,8},{8,4},{4,0},{13,9},{9,5},{5,1},{14,10},{10,6},{6,2},{15,11}... | collective-permute-start | bytes 2359304 | tf_op jit(solution)/shard_map/ppermute | solution.py:80
  95.6 23.4 %collective-permute-start.16 = (f16[256,1536]{1,0:T(8,128)(2,1)S(1)}, f16[256,1536]{1,0:T(8,128)(2,1)S(1)}, u32[]{:S(2)}, u32[]{:S(2)}) collective-permute-start(f16[256,1536]{1,0:T(8,128)(2,1)S(1)} %get-tuple-element.24), channel_id=1, source_target_pairs={{0,4},{4,8},{8,12},{1,5},{5,9},{9,13},{2,6},{6,10},{10,14},{3,7},{... | collective-permute-start | bytes 2359304 | tf_op jit(solution)/shard_map/ppermute | solution.py:79
  102.5 25.1 %collective-permute-start.13 = (f16[256,768]{1,0:T(8,128)(2,1)S(1)}, f16[256,768]{1,0:T(8,128)(2,1)S(1)}, u32[]{:S(2)}, u32[]{:S(2)}) collective-permute-start(f16[256,768]{1,0:T(8,128)(2,1)S(1)} %get-tuple-element.27), channel_id=1, source_target_pairs={{12,8},{8,4},{4,0},{13,9},{9,5},{5,1},{14,10},{10,6},{6,2},{15,11}... | collective-permute-start | bytes 1179656 | tf_op jit(solution)/shard_map/ppermute | solution.py:80
  103.8 24.7 %collective-permute-start.11 = (f16[256,768]{1,0:T(8,128)(2,1)S(1)}, f16[256,768]{1,0:T(8,128)(2,1)S(1)}, u32[]{:S(2)}, u32[]{:S(2)}) collective-permute-start(f16[256,768]{1,0:T(8,128)(2,1)S(1)} %get-tuple-element.26), channel_id=1, source_target_pairs={{0,4},{4,8},{8,12},{1,5},{5,9},{9,13},{2,6},{6,10},{10,14},{3,7},{... | collective-permute-start | bytes 1179656 | tf_op jit(solution)/shard_map/ppermute | solution.py:79
  121.5 7.9 %copy-start.1 = (bf16[256,768]{1,0:T(8,128)(2,1)}, bf16[256,768]{1,0:T(8,128)(2,1)S(1)}, u32[]{:S(2)}) copy-start(bf16[256,768]{1,0:T(8,128)(2,1)S(1)} %get-tuple-element.13.value_ref) | copy-start | bytes 1179652
  121.5 20.2 %collective-permute-start.19 = (bf16[256,768]{1,0:T(8,128)(2,1)}, bf16[256,768]{1,0:T(8,128)(2,1)S(1)}, u32[]{:S(2)}, u32[]{:S(2)}) collective-permute-start(bf16[256,768]{1,0:T(8,128)(2,1)} %get-tuple-element.12.key_ref), channel_id=1, source_target_pairs={{0,4},{4,0},{8,12},{12,8},{1,5},{5,1},{9,13},{13,9},{2,6},{6,2},{1... | collective-permute-start | bytes 1179656 | tf_op jit(solution)/shard_map/ppermute | solution.py:87
  124.0 17.7 %collective-permute-start.20 = (bf16[256,768]{1,0:T(8,128)(2,1)}, bf16[256,768]{1,0:T(8,128)(2,1)S(1)}, u32[]{:S(2)}, u32[]{:S(2)}) collective-permute-start(bf16[256,768]{1,0:T(8,128)(2,1)} %get-tuple-element.12.key_ref), channel_id=1, source_target_pairs={{4,8},{8,4},{5,9},{9,5},{6,10},{10,6},{7,11},{11,7},{20,24},{24,20... | collective-permute-start | bytes 1179656 | tf_op jit(solution)/shard_map/ppermute | solution.py:88
  124.7 17.1 %collective-permute-start.21 = (bf16[256,768]{1,0:T(8,128)(2,1)S(1)}, bf16[256,768]{1,0:T(8,128)(2,1)S(1)}, u32[]{:S(2)}, u32[]{:S(2)}) collective-permute-start(bf16[256,768]{1,0:T(8,128)(2,1)S(1)} %get-tuple-element.13.value_ref), channel_id=1, source_target_pairs={{0,4},{4,0},{8,12},{12,8},{1,5},{5,1},{9,13},{13,9},{2,6},{6,2},{1... | collective-permute-start | bytes 1179656 | tf_op jit(solution)/shard_map/ppermute | solution.py:87
  127.6 14.2 %collective-permute-start.22 = (bf16[256,768]{1,0:T(8,128)(2,1)S(1)}, bf16[256,768]{1,0:T(8,128)(2,1)S(1)}, u32[]{:S(2)}, u32[]{:S(2)}) collective-permute-start(bf16[256,768]{1,0:T(8,128)(2,1)S(1)} %get-tuple-element.13.value_ref), channel_id=1, source_target_pairs={{4,8},{8,4},{5,9},{9,5},{6,10},{10,6},{7,11},{11,7},{20,24},{24,20... | collective-permute-start | bytes 1179656 | tf_op jit(solution)/shard_map/ppermute | solution.py:88
  141.8 0.7 copy-start.7
  141.8 0.9 copy-start.9
  142.7 5.2 %collective-permute-start.25 = (bf16[256,1280]{1,0:T(8,128)(2,1)}, bf16[256,1280]{1,0:T(8,128)(2,1)S(1)}, u32[]{:S(2)}, u32[]{:S(2)}) collective-permute-start(bf16[256,1280]{1,0:T(8,128)(2,1)} %get-tuple-element.19), channel_id=1, source_target_pairs={{0,1},{1,0},{2,3},{3,2},{4,5},{5,4},{6,7},{7,6},{8,9},{9,8},{10,11... | collective-permute-start | bytes 1966088 | tf_op jit(solution)/shard_map/ppermute | solution.py:218
  142.7 1.9 %copy-start.10 = (bf16[256,768]{1,0:T(8,128)(2,1)S(1)}, bf16[256,768]{1,0:T(8,128)(2,1)}, u32[]{:S(2)}) copy-start(bf16[256,768]{1,0:T(8,128)(2,1)} %copy-done.9) | copy-start | bytes 1179652
  142.7 3.2 %copy-start.8 = (bf16[256,768]{1,0:T(8,128)(2,1)S(1)}, bf16[256,768]{1,0:T(8,128)(2,1)}, u32[]{:S(2)}) copy-start(bf16[256,768]{1,0:T(8,128)(2,1)} %copy-done.7) | copy-start | bytes 1179652
  142.7 5.9 %copy-start.6 = (f32[256,1280]{1,0:T(8,128)S(1)}, f32[256,1280]{1,0:T(8,128)}, u32[]{:S(2)}) copy-start(f32[256,1280]{1,0:T(8,128)} %get-tuple-element.17) | copy-start | bytes 3932164
  142.7 6.0 %collective-permute-start.23 = (bf16[256,1280]{1,0:T(8,128)(2,1)}, bf16[256,1280]{1,0:T(8,128)(2,1)S(1)}, u32[]{:S(2)}, u32[]{:S(2)}) collective-permute-start(bf16[256,1280]{1,0:T(8,128)(2,1)} %get-tuple-element.16), channel_id=1, source_target_pairs={{0,1},{1,0},{2,3},{3,2},{4,5},{5,4},{6,7},{7,6},{8,9},{9,8},{10,11... | collective-permute-start | bytes 1966088 | tf_op jit(solution)/shard_map/ppermute | solution.py:218
  143.4 5.4 %copy-start.5 = (f32[256,1280]{1,0:T(8,128)S(1)}, f32[256,1280]{1,0:T(8,128)}, u32[]{:S(2)}) copy-start(f32[256,1280]{1,0:T(8,128)} %get-tuple-element.14) | copy-start | bytes 3932164
  144.5 13.9 %collective-permute-start.27 = (bf16[256,768]{1,0:T(8,128)(2,1)S(1)}, bf16[256,768]{1,0:T(8,128)(2,1)S(1)}, u32[]{:S(2)}, u32[]{:S(2)}) collective-permute-start(bf16[256,768]{1,0:T(8,128)(2,1)S(1)} %copy-done.10), channel_id=1, source_target_pairs={{4,0},{8,12},{5,1},{9,13},{6,2},{10,14},{7,3},{11,15},{20,16},{24,... | collective-permute-start | bytes 1179656 | tf_op jit(solution)/shard_map/ppermute | solution.py:96
  145.8 12.8 %collective-permute-start.28 = (bf16[256,768]{1,0:T(8,128)(2,1)S(1)}, bf16[256,768]{1,0:T(8,128)(2,1)S(1)}, u32[]{:S(2)}, u32[]{:S(2)}) collective-permute-start(bf16[256,768]{1,0:T(8,128)(2,1)S(1)} %copy-done.8), channel_id=1, source_target_pairs={{4,8},{8,4},{5,9},{9,5},{6,10},{10,6},{7,11},{11,7},{20,24},{24,20... | collective-permute-start | bytes 1179656 | tf_op jit(solution)/shard_map/ppermute | solution.py:95
  146.5 28.9 %collective-permute-start.30 = (bf16[256,768]{1,0:T(8,128)(2,1)S(1)}, bf16[256,768]{1,0:T(8,128)(2,1)S(1)}, u32[]{:S(2)}, u32[]{:S(2)}) collective-permute-start(bf16[256,768]{1,0:T(8,128)(2,1)S(1)} %collective-permute-done.22), channel_id=1, source_target_pairs={{4,0},{8,12},{5,1},{9,13},{6,2},{10,14},{7,3},{11,15},{20,16},{24,... | collective-permute-start | bytes 1179656 | tf_op jit(solution)/shard_map/ppermute | solution.py:96
  147.9 12.1 %collective-permute-start.31 = (bf16[256,768]{1,0:T(8,128)(2,1)S(1)}, bf16[256,768]{1,0:T(8,128)(2,1)S(1)}, u32[]{:S(2)}, u32[]{:S(2)}) collective-permute-start(bf16[256,768]{1,0:T(8,128)(2,1)S(1)} %collective-permute-done.21), channel_id=1, source_target_pairs={{4,8},{8,4},{5,9},{9,5},{6,10},{10,6},{7,11},{11,7},{20,24},{24,20... | collective-permute-start | bytes 1179656 | tf_op jit(solution)/shard_map/ppermute | solution.py:95
  148.7 12.6 %collective-permute-start.26 = (bf16[256,640]{1,0:T(8,128)(2,1)S(1)}, bf16[256,640]{1,0:T(8,128)(2,1)S(1)}, u32[]{:S(2)}, u32[]{:S(2)}) collective-permute-start(bf16[256,640]{1,0:T(8,128)(2,1)S(1)} %add_convert_fusion.7), channel_id=1, source_target_pairs={{0,2},{1,3},{2,0},{3,1},{4,6},{5,7},{6,4},{7,5},{8,10},{9,11},{10,... | collective-permute-start | bytes 983048 | tf_op jit(solution)/shard_map/ppermute | solution.py:229
  158.4 8.1 %collective-permute-start.24 = (bf16[256,640]{1,0:T(8,128)(2,1)S(1)}, bf16[256,640]{1,0:T(8,128)(2,1)S(1)}, u32[]{:S(2)}, u32[]{:S(2)}) collective-permute-start(bf16[256,640]{1,0:T(8,128)(2,1)S(1)} %add_convert_fusion.9), channel_id=1, source_target_pairs={{0,2},{1,3},{2,0},{3,1},{4,6},{5,7},{6,4},{7,5},{8,10},{9,11},{10,... | collective-permute-start | bytes 983048 | tf_op jit(solution)/shard_map/ppermute | solution.py:229
  158.7 16.6 %collective-permute-start.29 = (bf16[256,768]{1,0:T(8,128)(2,1)S(1)}, bf16[256,768]{1,0:T(8,128)(2,1)S(1)}, u32[]{:S(2)}, u32[]{:S(2)}) collective-permute-start(bf16[256,768]{1,0:T(8,128)(2,1)S(1)} %collective-permute-done.28), channel_id=1, source_target_pairs={{4,0},{8,12},{5,1},{9,13},{6,2},{10,14},{7,3},{11,15},{20,16},{24,... | collective-permute-start | bytes 1179656 | tf_op jit(solution)/shard_map/ppermute | solution.py:97
  160.0 22.8 %collective-permute-start.32 = (bf16[256,768]{1,0:T(8,128)(2,1)S(1)}, bf16[256,768]{1,0:T(8,128)(2,1)S(1)}, u32[]{:S(2)}, u32[]{:S(2)}) collective-permute-start(bf16[256,768]{1,0:T(8,128)(2,1)S(1)} %collective-permute-done.31), channel_id=1, source_target_pairs={{4,0},{8,12},{5,1},{9,13},{6,2},{10,14},{7,3},{11,15},{20,16},{24,... | collective-permute-start | bytes 1179656 | tf_op jit(solution)/shard_map/ppermute | solution.py:97
  161.4 13.9 %copy-start.2 = (bf16[256,768]{1,0:T(8,128)(2,1)S(1)}, bf16[256,768]{1,0:T(8,128)(2,1)}, u32[]{:S(2)}) copy-start(bf16[256,768]{1,0:T(8,128)(2,1)} %copy-done.1) | copy-start | bytes 1179652
  182.9 1.7 copy-start.3

commit v15 on v14

--- a/solution.py
+++ b/solution.py
@@ -188,7 +188,7 @@
     place = jnp.stack([me] + [2 * c + 1 - core for c in order] + [2 * c + core for c in order])
     heads = 2 if depth % (2 * HEAD_DIM) == 0 else 1
     block = heads * HEAD_DIM
-    chunks = 2 if width % (2 * 128) == 0 else 1
+    chunks = 1
     part = width // chunks
     results = pl.pallas_call(
         functools.partial(attend_and_project, patches, heads, chips, chunks),

time: 185 us -> 186 us (level)
    ppermute x2, waiting for transfers between devices: 15.1 us -> 22.5 us  [into(): last = lax.ppermute(after(across_mate, *earlier), 'patch', outward)]
    ppermute x2 -> x1, waiting for transfers between devices: 5.01 us -> 0.01 us  [attend(): arrived.append(lax.ppermute(sends[-1], 'tensor', pairs))]
    unnamed x27 -> x33, local copies, waits for them, and re-layouts: 4.29 us -> 4.07 us
  transfers between devices with their start and end apart: 33 -> 31, of which waited for: 15 -> 14; matrix products, arithmetic and copies ran while one was open for 10% -> 9% of each run, Pallas kernels for 7% -> 7%
where the time goes in v15:
time: 186 us
  waiting for transfers between devices  81.5 us (44%)
  starting transfers between devices  68.6 us (37%)
  Pallas kernels  12.3 us (7%)
  local copies, waits for them, and re-layouts  7.88 us (4%)
  other arithmetic  7.13 us (4%)
  matrix products  6.77 us (4%)
    ppermute x2, waiting for transfers between devices, into(): last = lax.ppermute(after(across_mate, *earlier), 'patch', outward)  22.5 us
    ppermute x2, waiting for transfers between devices, sum_in_pairs(): first = lax.ppermute(outermost, 'patch', [(0, 1), (3, 2)])  13.6 us
    pallas_call x1, Pallas kernels, attend(): pl.pallas_call(functools.partial(attend_and_project, patches, heads, chip...  12.3 us
    ppermute x2, waiting for transfers between devices, sum_in_pairs(): up = lax.ppermute(second, 'patch', [(0, 1), (1, 2)])  11.8 us
    ppermute x2, starting transfers between devices, sum_in_pairs(): up = lax.ppermute(third_up, 'patch', [(0, 1), (1, 2), (2, 3)])  10.1 us
    ppermute x2, starting transfers between devices, both_slabs(): other = lax.ppermute(held, 'tensor', across)  10.1 us
    ppermute x2, starting transfers between devices, sum_in_pairs(): first = lax.ppermute(outermost, 'patch', [(0, 1), (3, 2)])  9.99 us
    ppermute x2, starting transfers between devices, sum_in_pairs(): up = lax.ppermute(second, 'patch', [(0, 1), (1, 2)])  8.85 us
  transfers between devices with their start and end apart: 31, of which 14 were waited for; matrix products, arithmetic and copies ran while one was open for 9% of the time, Pallas kernels for 7%

profile of v15, /device:TPU:0, one launch (start us, length us, event | category | flops | bytes accessed | tf_op | source)
XLA Modules:
  0.0 185.5 jit_solution(16879623912445540791)
XLA Ops:
  0.6 1.3 fusion.15
  1.9 3.0 %collective-permute-start.1 = (bf16[128,1280]{1,0:T(8,128)(2,1)S(1)}, bf16[128,1280]{1,0:T(8,128)(2,1)S(1)}, u32[]{:S(2)}, u32[]{:S(2)}) collective-permute-start(bf16[128,1280]{1,0:T(8,128)(2,1)S(1)} %get-tuple-element.26), channel_id=1, source_target_pairs={{0,2},{1,3},{2,0},{3,1},{4,6},{5,7},{6,4},{7,5},{8,10},{9,11},{10,... | collective-permute-start | bytes 983048 | tf_op jit(solution)/shard_map/ppermute | solution.py:31
  4.9 1.3 collective-permute-start.5
  6.2 6.4 %collective-permute-done.1 = bf16[128,1280]{1,0:T(8,128)(2,1)S(1)} collective-permute-done((bf16[128,1280]{1,0:T(8,128)(2,1)S(1)}, bf16[128,1280]{1,0:T(8,128)(2,1)S(1)}, u32[]{:S(2)}, u32[]{:S(2)}) %collective-permute-start.1) | collective-permute-done | bytes 327712 | tf_op jit(solution)/shard_map/ppermute | solution.py:31
  12.6 4.8 %collective-permute-start.6 = (bf16[128,1280]{1,0:T(8,128)(2,1)S(1)}, bf16[128,1280]{1,0:T(8,128)(2,1)S(1)}, u32[]{:S(2)}, u32[]{:S(2)}) collective-permute-start(bf16[128,1280]{1,0:T(8,128)(2,1)S(1)} %collective-permute-done.1), channel_id=1, source_target_pairs={{0,8},{1,12},{4,9},{5,13},{10,2},{11,6},{14,3},{15,7},{16,24},{17,... | collective-permute-start | bytes 983048 | tf_op jit(solution)/shard_map/ppermute | solution.py:41
  17.4 7.4 %collective-permute-done.5 = bf16[128,1280]{1,0:T(8,128)(2,1)S(1)} collective-permute-done((bf16[128,1280]{1,0:T(8,128)(2,1)S(1)}, bf16[128,1280]{1,0:T(8,128)(2,1)S(1)}, u32[]{:S(2)}, u32[]{:S(2)}) %collective-permute-start.5) | collective-permute-done | bytes 327712 | tf_op jit(solution)/shard_map/ppermute | solution.py:41
  24.8 0.3 collective-permute-done.6
  25.2 8.7 %collective-permute-start.7 = (bf16[128,1280]{1,0:T(8,128)(2,1)S(1)}, bf16[128,1280]{1,0:T(8,128)(2,1)S(1)}, u32[]{:S(2)}, u32[]{:S(2)}) collective-permute-start(bf16[128,1280]{1,0:T(8,128)(2,1)S(1)} %broadcast_select_fusion.2), channel_id=1, source_target_pairs={{0,2},{1,3},{2,0},{3,1},{4,6},{5,7},{6,4},{7,5},{8,10},{9,11},{10,... | collective-permute-start | bytes 983048 | tf_op jit(solution)/shard_map/ppermute | solution.py:45
  33.9 0.7 collective-permute-start
  34.6 0.6 stack.23.place_ref
  35.2 1.7 constant_dynamic-update-slice_fusion.1
  37.0 0.8 collective-permute-start.2
  37.8 1.1 collective-permute-done.7
  39.0 0.8 collective-permute-start.8
  39.8 0.1 constant_dynamic-update-slice_fusion
  40.1 1.4 collective-permute-start.3
  41.6 2.2 %fusion.1 = f16[512,1536]{1,0:T(8,128)(2,1)S(1)} fusion(bf16[1280,1536]{1,0:T(8,128)(2,1)S(1)} %constant_dynamic-update-slice_fusion, bf16[256,1280]{1,0:T(8,128)(2,1)S(1)} %collective-permute-done.8, bf16[128,1280]{1,0:T(8,128)(2,1)S(1)} %get-tuple-element.25, bf16[128,1280]{1,0:T(8,128)(2,1)S(1)} %get-tuple-element.24), kind=kOutput, calls=%fused_computation.3 | convolution fusion | flops 2018770944 | bytes 6815744 | tf_op jit(solution)/shard_map/dot_general | solution.py:60
  43.9 6.5 %collective-permute-start.14 = (f16[256,1536]{1,0:T(8,128)(2,1)S(1)}, f16[256,1536]{1,0:T(8,128)(2,1)S(1)}, u32[]{:S(2)}, u32[]{:S(2)}) collective-permute-start(f16[256,1536]{1,0:T(8,128)(2,1)S(1)} %dynamic-slice_bitcast_fusion), channel_id=1, source_target_pairs={{0,4},{12,8},{1,5},{13,9},{2,6},{14,10},{3,7},{15,11},{16,20},{28,... | collective-permute-start | bytes 2359304 | tf_op jit(solution)/shard_map/ppermute | solution.py:72
  50.7 1.2 multiply_convert_fusion
  52.0 3.4 %collective-permute-start.9 = (f16[256,768]{1,0:T(8,128)(2,1)S(1)}, f16[256,768]{1,0:T(8,128)(2,1)S(1)}, u32[]{:S(2)}, u32[]{:S(2)}) collective-permute-start(f16[256,768]{1,0:T(8,128)(2,1)S(1)} %dynamic-slice_bitcast_fusion.4), channel_id=1, source_target_pairs={{0,4},{12,8},{1,5},{13,9},{2,6},{14,10},{3,7},{15,11},{16,20},{28,... | collective-permute-start | bytes 1179656 | tf_op jit(solution)/shard_map/ppermute | solution.py:72
  55.4 13.0 %collective-permute-done.14 = f16[256,1536]{1,0:T(8,128)(2,1)S(1)} collective-permute-done((f16[256,1536]{1,0:T(8,128)(2,1)S(1)}, f16[256,1536]{1,0:T(8,128)(2,1)S(1)}, u32[]{:S(2)}, u32[]{:S(2)}) %collective-permute-start.14) | collective-permute-done | bytes 786464 | tf_op jit(solution)/shard_map/ppermute | solution.py:72
  68.4 0.4 fusion.6
  68.8 4.4 %collective-permute-start.15 = (f16[256,1536]{1,0:T(8,128)(2,1)S(1)}, f16[256,1536]{1,0:T(8,128)(2,1)S(1)}, u32[]{:S(2)}, u32[]{:S(2)}) collective-permute-start(f16[256,1536]{1,0:T(8,128)(2,1)S(1)} %fusion.6), channel_id=1, source_target_pairs={{0,4},{4,8},{1,5},{5,9},{2,6},{6,10},{3,7},{7,11},{16,20},{20,24},... | collective-permute-start | bytes 2359304 | tf_op jit(solution)/shard_map/ppermute | solution.py:74
  73.3 0.7 collective-permute-start.17
  74.0 2.2 %fusion = f16[512,1536]{1,0:T(8,128)(2,1)S(1)} fusion(bf16[1280,1536]{1,0:T(8,128)(2,1)S(1)} %constant_dynamic-update-slice_fusion, bf16[256,1280]{1,0:T(8,128)(2,1)S(1)} %collective-permute-done.4, bf16[128,1280]{1,0:T(8,128)(2,1)S(1)} %get-tuple-element.23, bf16[128,1280]{1,0:T(8,128)(2,1)S(1)} %get-tuple-element.22), kind=kOutput, calls=%fused_computation.2 | convolution fusion | flops 2018770944 | bytes 6815744 | tf_op jit(solution)/shard_map/dot_general | solution.py:60
  76.2 0.6 collective-permute-done.9
  76.8 0.2 fusion.10
  77.0 4.4 %collective-permute-start.10 = (f16[256,768]{1,0:T(8,128)(2,1)S(1)}, f16[256,768]{1,0:T(8,128)(2,1)S(1)}, u32[]{:S(2)}, u32[]{:S(2)}) collective-permute-start(f16[256,768]{1,0:T(8,128)(2,1)S(1)} %fusion.10), channel_id=1, source_target_pairs={{0,4},{4,8},{1,5},{5,9},{2,6},{6,10},{3,7},{7,11},{16,20},{20,24},... | collective-permute-start | bytes 1179656 | tf_op jit(solution)/shard_map/ppermute | solution.py:74
  81.4 0.7 collective-permute-start.12
  82.1 11.6 %collective-permute-done.15 = f16[256,1536]{1,0:T(8,128)(2,1)S(1)} collective-permute-done((f16[256,1536]{1,0:T(8,128)(2,1)S(1)}, f16[256,1536]{1,0:T(8,128)(2,1)S(1)}, u32[]{:S(2)}, u32[]{:S(2)}) %collective-permute-start.15) | collective-permute-done | bytes 786464 | tf_op jit(solution)/shard_map/ppermute | solution.py:74
  93.7 0.6 add_convert_fusion.1
  94.2 1.3 collective-permute-start.18
  95.5 5.1 %collective-permute-start.16 = (f16[256,1536]{1,0:T(8,128)(2,1)S(1)}, f16[256,1536]{1,0:T(8,128)(2,1)S(1)}, u32[]{:S(2)}, u32[]{:S(2)}) collective-permute-start(f16[256,1536]{1,0:T(8,128)(2,1)S(1)} %get-tuple-element.18), channel_id=1, source_target_pairs={{0,4},{4,8},{8,12},{1,5},{5,9},{9,13},{2,6},{6,10},{10,14},{3,7},{... | collective-permute-start | bytes 2359304 | tf_op jit(solution)/shard_map/ppermute | solution.py:79
  100.6 1.2 multiply_convert_fusion.1
  101.8 0.3 collective-permute-done.10
  102.1 0.3 add_convert_fusion.6
  102.4 1.3 collective-permute-start.13
  103.7 5.0 %collective-permute-start.11 = (f16[256,768]{1,0:T(8,128)(2,1)S(1)}, f16[256,768]{1,0:T(8,128)(2,1)S(1)}, u32[]{:S(2)}, u32[]{:S(2)}) collective-permute-start(f16[256,768]{1,0:T(8,128)(2,1)S(1)} %get-tuple-element.20), channel_id=1, source_target_pairs={{0,4},{4,8},{8,12},{1,5},{5,9},{9,13},{2,6},{6,10},{10,14},{3,7},{... | collective-permute-start | bytes 1179656 | tf_op jit(solution)/shard_map/ppermute | solution.py:79
  108.9 5.5 %collective-permute-done.18 = f16[256,1536]{1,0:T(8,128)(2,1)S(1)} collective-permute-done((f16[256,1536]{1,0:T(8,128)(2,1)S(1)}, f16[256,1536]{1,0:T(8,128)(2,1)S(1)}, u32[]{:S(2)}, u32[]{:S(2)}) %collective-permute-start.18) | collective-permute-done | bytes 786464 | tf_op jit(solution)/shard_map/ppermute | solution.py:80
  114.4 4.6 %collective-permute-done.16 = f16[256,1536]{1,0:T(8,128)(2,1)S(1)} collective-permute-done((f16[256,1536]{1,0:T(8,128)(2,1)S(1)}, f16[256,1536]{1,0:T(8,128)(2,1)S(1)}, u32[]{:S(2)}, u32[]{:S(2)}) %collective-permute-start.16) | collective-permute-done | bytes 786464 | tf_op jit(solution)/shard_map/ppermute | solution.py:79
  118.9 2.5 %fusion.5 = (bf16[256,768]{1,0:T(8,128)(2,1)S(1)}, bf16[256,768]{1,0:T(8,128)(2,1)}) fusion(f16[256,1536]{1,0:T(8,128)(2,1)S(1)} %collective-permute-done.18, f16[256,1536]{1,0:T(8,128)(2,1)S(1)} %collective-permute-done.16, f16[256,1536]{1,0:T(8,128)(2,1)S(1)} %dynamic-slice_bitcast_fusion.1, bf16[2,1024,768]{2,1,0:T(8,128)(2,1)} %stale_ref.1, ...), kind=kLoop, calls=%fused_computation.20 | loop fusion | flops 4718592 | bytes 3932168 | tf_op jit(solution)/shard_map/convert_element_type | solution.py:259
  121.5 2.5 %collective-permute-start.19 = (bf16[256,768]{1,0:T(8,128)(2,1)}, bf16[256,768]{1,0:T(8,128)(2,1)S(1)}, u32[]{:S(2)}, u32[]{:S(2)}) collective-permute-start(bf16[256,768]{1,0:T(8,128)(2,1)} %get-tuple-element.9.key_ref), channel_id=1, source_target_pairs={{0,4},{4,0},{8,12},{12,8},{1,5},{5,1},{9,13},{13,9},{2,6},{6,2},{1... | collective-permute-start | bytes 1179656 | tf_op jit(solution)/shard_map/ppermute | solution.py:87
  123.9 0.7 collective-permute-start.20
  124.6 2.9 %collective-permute-start.21 = (bf16[256,768]{1,0:T(8,128)(2,1)S(1)}, bf16[256,768]{1,0:T(8,128)(2,1)S(1)}, u32[]{:S(2)}, u32[]{:S(2)}) collective-permute-start(bf16[256,768]{1,0:T(8,128)(2,1)S(1)} %get-tuple-element.10.value_ref), channel_id=1, source_target_pairs={{0,4},{4,0},{8,12},{12,8},{1,5},{5,1},{9,13},{13,9},{2,6},{6,2},{1... | collective-permute-start | bytes 1179656 | tf_op jit(solution)/shard_map/ppermute | solution.py:87
  127.5 0.9 collective-permute-start.22
  128.4 1.0 fusion.9.query_ref
  129.4 12.3 %shard_map.77 = (bf16[256,2560]{1,0:T(8,128)(2,1)}, f32[256,2560]{1,0:T(8,128)}) custom-call(s32[5]{0:T(128)} %stack.23.place_ref, bf16[256,768]{1,0:T(8,128)(2,1)} %fusion.9.query_ref, bf16[2,1024,768]{2,1,0:T(8,128)(2,1)} %stale_ref.1, bf16[256,768]{1,0:T(8,128)(2,1)} %get-tuple-element.9.key_ref, bf16[256,768]{1,0:T(8,128)(2,1)} %copy-done.1, ...), custom_call_target="tpu_custom_call" | custom-call | flops 2818572288 | bytes 14942208 | tf_op jit(solution)/shard_map/pallas_call | solution.py:193
  141.7 0.7 copy-done.12
  142.7 0.8 copy-done.8
  143.5 0.2 broadcast_in_dim.27
  143.7 1.2 bitcast_dynamic-update-slice_fusion.7
  144.9 1.3 collective-permute-start.25
  146.2 0.7 collective-permute-start.26
  146.9 1.3 collective-permute-start.28
  148.2 0.7 collective-permute-start.29
  148.9 0.2 add_convert_fusion.4
  149.1 1.4 collective-permute-start.27
  150.6 8.1 %collective-permute-done.25 = bf16[256,768]{1,0:T(8,128)(2,1)S(1)} collective-permute-done((bf16[256,768]{1,0:T(8,128)(2,1)S(1)}, bf16[256,768]{1,0:T(8,128)(2,1)S(1)}, u32[]{:S(2)}, u32[]{:S(2)}) %collective-permute-start.25) | collective-permute-done | bytes 393248 | tf_op jit(solution)/shard_map/ppermute | solution.py:96
  158.8 0.6 collective-permute-start.24
  159.4 1.3 collective-permute-start.30
  160.7 14.8 %collective-permute-done.27 = bf16[256,768]{1,0:T(8,128)(2,1)S(1)} collective-permute-done((bf16[256,768]{1,0:T(8,128)(2,1)S(1)}, bf16[256,768]{1,0:T(8,128)(2,1)S(1)}, u32[]{:S(2)}, u32[]{:S(2)}) %collective-permute-start.27) | collective-permute-done | bytes 393248 | tf_op jit(solution)/shard_map/ppermute | solution.py:97
  175.8 7.7 %collective-permute-done.30 = bf16[256,768]{1,0:T(8,128)(2,1)S(1)} collective-permute-done((bf16[256,768]{1,0:T(8,128)(2,1)S(1)}, bf16[256,768]{1,0:T(8,128)(2,1)S(1)}, u32[]{:S(2)}, u32[]{:S(2)}) %collective-permute-start.30) | collective-permute-done | bytes 393248 | tf_op jit(solution)/shard_map/ppermute | solution.py:97
  183.7 1.3 add_convert_fusion.3
  185.0 0.5 copy-done.3
  (65 shorter events, 1.8 us)
Async XLA Ops:
  0.6 50.1 %copy-start = (bf16[1280,768]{1,0:T(8,128)(2,1)S(1)}, bf16[1280,768]{1,0:T(8,128)(2,1)}, u32[]{:S(2)}) copy-start(bf16[1280,768]{1,0:T(8,128)(2,1)} %param.7) | copy-start | bytes 5898244
  1.9 10.7 %collective-permute-start.1 = (bf16[128,1280]{1,0:T(8,128)(2,1)S(1)}, bf16[128,1280]{1,0:T(8,128)(2,1)S(1)}, u32[]{:S(2)}, u32[]{:S(2)}) collective-permute-start(bf16[128,1280]{1,0:T(8,128)(2,1)S(1)} %get-tuple-element.26), channel_id=1, source_target_pairs={{0,2},{1,3},{2,0},{3,1},{4,6},{5,7},{6,4},{7,5},{8,10},{9,11},{10,... | collective-permute-start | bytes 983048 | tf_op jit(solution)/shard_map/ppermute | solution.py:31
  4.9 19.9 %collective-permute-start.5 = (bf16[128,1280]{1,0:T(8,128)(2,1)S(1)}, bf16[128,1280]{1,0:T(8,128)(2,1)S(1)}, u32[]{:S(2)}, u32[]{:S(2)}) collective-permute-start(bf16[128,1280]{1,0:T(8,128)(2,1)S(1)} %get-tuple-element.27), channel_id=1, source_target_pairs={{2,10},{3,14},{6,11},{7,15},{8,0},{9,4},{12,1},{13,5},{18,26},{19,... | collective-permute-start | bytes 983048 | tf_op jit(solution)/shard_map/ppermute | solution.py:41
  12.6 12.2 %copy-start.14 = (bf16[128,1280]{1,0:T(8,128)(2,1)}, bf16[128,1280]{1,0:T(8,128)(2,1)S(1)}, u32[]{:S(2)}) copy-start(bf16[128,1280]{1,0:T(8,128)(2,1)S(1)} %collective-permute-done.1) | copy-start | bytes 983044
  12.6 12.5 %collective-permute-start.6 = (bf16[128,1280]{1,0:T(8,128)(2,1)S(1)}, bf16[128,1280]{1,0:T(8,128)(2,1)S(1)}, u32[]{:S(2)}, u32[]{:S(2)}) collective-permute-start(bf16[128,1280]{1,0:T(8,128)(2,1)S(1)} %collective-permute-done.1), channel_id=1, source_target_pairs={{0,8},{1,12},{4,9},{5,13},{10,2},{11,6},{14,3},{15,7},{16,24},{17,... | collective-permute-start | bytes 983048 | tf_op jit(solution)/shard_map/ppermute | solution.py:41
  25.2 13.7 %collective-permute-start.7 = (bf16[128,1280]{1,0:T(8,128)(2,1)S(1)}, bf16[128,1280]{1,0:T(8,128)(2,1)S(1)}, u32[]{:S(2)}, u32[]{:S(2)}) collective-permute-start(bf16[128,1280]{1,0:T(8,128)(2,1)S(1)} %broadcast_select_fusion.2), channel_id=1, source_target_pairs={{0,2},{1,3},{2,0},{3,1},{4,6},{5,7},{6,4},{7,5},{8,10},{9,11},{10,... | collective-permute-start | bytes 983048 | tf_op jit(solution)/shard_map/ppermute | solution.py:45
  33.9 6.1 %collective-permute-start = (bf16[128,1280]{1,0:T(8,128)(2,1)S(1)}, bf16[128,1280]{1,0:T(8,128)(2,1)S(1)}, u32[]{:S(2)}, u32[]{:S(2)}) collective-permute-start(bf16[128,1280]{1,0:T(8,128)(2,1)S(1)} %get-tuple-element.27), channel_id=1, source_target_pairs={{0,0},{1,4},{4,1},{5,5},{10,10},{11,14},{14,11},{15,15},{16,16},{1... | collective-permute-start | bytes 983048 | tf_op jit(solution)/shard_map/ppermute | solution.py:41
  35.2 1.8 copy-start.15
  36.9 2.9 %copy-start.5 = (bf16[1280,768]{1,0:T(8,128)(2,1)S(1)}, bf16[1280,768]{1,0:T(8,128)(2,1)}, u32[]{:S(2)}) copy-start(bf16[1280,768]{1,0:T(8,128)(2,1)} %param.9) | copy-start | bytes 5898244
  37.0 3.0 %collective-permute-start.2 = (bf16[128,1280]{1,0:T(8,128)(2,1)S(1)}, bf16[128,1280]{1,0:T(8,128)(2,1)S(1)}, u32[]{:S(2)}, u32[]{:S(2)}) collective-permute-start(bf16[128,1280]{1,0:T(8,128)(2,1)S(1)} %copy-done.15), channel_id=1, source_target_pairs={{2,2},{3,6},{6,3},{7,7},{8,8},{9,12},{12,9},{13,13},{18,18},{19,22... | collective-permute-start | bytes 983048 | tf_op jit(solution)/shard_map/ppermute | solution.py:41
  39.0 2.5 %collective-permute-start.8 = (bf16[256,1280]{1,0:T(8,128)(2,1)S(1)}, bf16[256,1280]{1,0:T(8,128)(2,1)S(1)}, u32[]{:S(2)}, u32[]{:S(2)}) collective-permute-start(bf16[256,1280]{1,0:T(8,128)(2,1)S(1)} %pad_maximum_fusion.3), channel_id=1, source_target_pairs={{0,1},{1,0},{2,3},{3,2},{4,5},{5,4},{6,7},{7,6},{8,9},{9,8},{10,11... | collective-permute-start | bytes 1966088 | tf_op jit(solution)/shard_map/ppermute | solution.py:49
  40.1 10.4 %collective-permute-start.3 = (bf16[128,1280]{1,0:T(8,128)(2,1)S(1)}, bf16[128,1280]{1,0:T(8,128)(2,1)S(1)}, u32[]{:S(2)}, u32[]{:S(2)}) collective-permute-start(bf16[128,1280]{1,0:T(8,128)(2,1)S(1)} %broadcast_select_fusion.5), channel_id=1, source_target_pairs={{0,2},{1,3},{2,0},{3,1},{4,6},{5,7},{6,4},{7,5},{8,10},{9,11},{10,... | collective-permute-start | bytes 983048 | tf_op jit(solution)/shard_map/ppermute | solution.py:45
  43.9 24.5 %collective-permute-start.14 = (f16[256,1536]{1,0:T(8,128)(2,1)S(1)}, f16[256,1536]{1,0:T(8,128)(2,1)S(1)}, u32[]{:S(2)}, u32[]{:S(2)}) collective-permute-start(f16[256,1536]{1,0:T(8,128)(2,1)S(1)} %dynamic-slice_bitcast_fusion), channel_id=1, source_target_pairs={{0,4},{12,8},{1,5},{13,9},{2,6},{14,10},{3,7},{15,11},{16,20},{28,... | collective-permute-start | bytes 2359304 | tf_op jit(solution)/shard_map/ppermute | solution.py:72
  50.6 23.4 %collective-permute-start.4 = (bf16[256,1280]{1,0:T(8,128)(2,1)S(1)}, bf16[256,1280]{1,0:T(8,128)(2,1)S(1)}, u32[]{:S(2)}, u32[]{:S(2)}) collective-permute-start(bf16[256,1280]{1,0:T(8,128)(2,1)S(1)} %pad_maximum_fusion.2), channel_id=1, source_target_pairs={{0,1},{1,0},{2,3},{3,2},{4,5},{5,4},{6,7},{7,6},{8,9},{9,8},{10,11... | collective-permute-start | bytes 1966088 | tf_op jit(solution)/shard_map/ppermute | solution.py:49
  52.0 24.8 %collective-permute-start.9 = (f16[256,768]{1,0:T(8,128)(2,1)S(1)}, f16[256,768]{1,0:T(8,128)(2,1)S(1)}, u32[]{:S(2)}, u32[]{:S(2)}) collective-permute-start(f16[256,768]{1,0:T(8,128)(2,1)S(1)} %dynamic-slice_bitcast_fusion.4), channel_id=1, source_target_pairs={{0,4},{12,8},{1,5},{13,9},{2,6},{14,10},{3,7},{15,11},{16,20},{28,... | collective-permute-start | bytes 1179656 | tf_op jit(solution)/shard_map/ppermute | solution.py:72
  68.8 24.8 %collective-permute-start.15 = (f16[256,1536]{1,0:T(8,128)(2,1)S(1)}, f16[256,1536]{1,0:T(8,128)(2,1)S(1)}, u32[]{:S(2)}, u32[]{:S(2)}) collective-permute-start(f16[256,1536]{1,0:T(8,128)(2,1)S(1)} %fusion.6), channel_id=1, source_target_pairs={{0,4},{4,8},{1,5},{5,9},{2,6},{6,10},{3,7},{7,11},{16,20},{20,24},... | collective-permute-start | bytes 2359304 | tf_op jit(solution)/shard_map/ppermute | solution.py:74
  73.3 20.4 %collective-permute-start.17 = (f16[256,1536]{1,0:T(8,128)(2,1)S(1)}, f16[256,1536]{1,0:T(8,128)(2,1)S(1)}, u32[]{:S(2)}, u32[]{:S(2)}) collective-permute-start(f16[256,1536]{1,0:T(8,128)(2,1)S(1)} %fusion.6), channel_id=1, source_target_pairs={{12,8},{8,4},{13,9},{9,5},{14,10},{10,6},{15,11},{11,7},{28,24},{2... | collective-permute-start | bytes 2359304 | tf_op jit(solution)/shard_map/ppermute | solution.py:75
  77.0 25.1 %collective-permute-start.10 = (f16[256,768]{1,0:T(8,128)(2,1)S(1)}, f16[256,768]{1,0:T(8,128)(2,1)S(1)}, u32[]{:S(2)}, u32[]{:S(2)}) collective-permute-start(f16[256,768]{1,0:T(8,128)(2,1)S(1)} %fusion.10), channel_id=1, source_target_pairs={{0,4},{4,8},{1,5},{5,9},{2,6},{6,10},{3,7},{7,11},{16,20},{20,24},... | collective-permute-start | bytes 1179656 | tf_op jit(solution)/shard_map/ppermute | solution.py:74
  81.4 20.7 %collective-permute-start.12 = (f16[256,768]{1,0:T(8,128)(2,1)S(1)}, f16[256,768]{1,0:T(8,128)(2,1)S(1)}, u32[]{:S(2)}, u32[]{:S(2)}) collective-permute-start(f16[256,768]{1,0:T(8,128)(2,1)S(1)} %fusion.10), channel_id=1, source_target_pairs={{12,8},{8,4},{13,9},{9,5},{14,10},{10,6},{15,11},{11,7},{28,24},{2... | collective-permute-start | bytes 1179656 | tf_op jit(solution)/shard_map/ppermute | solution.py:75
  94.2 20.1 %collective-permute-start.18 = (f16[256,1536]{1,0:T(8,128)(2,1)S(1)}, f16[256,1536]{1,0:T(8,128)(2,1)S(1)}, u32[]{:S(2)}, u32[]{:S(2)}) collective-permute-start(f16[256,1536]{1,0:T(8,128)(2,1)S(1)} %get-tuple-element.19), channel_id=1, source_target_pairs={{12,8},{8,4},{4,0},{13,9},{9,5},{5,1},{14,10},{10,6},{6,2},{15,11}... | collective-permute-start | bytes 2359304 | tf_op jit(solution)/shard_map/ppermute | solution.py:80
  95.5 23.4 %collective-permute-start.16 = (f16[256,1536]{1,0:T(8,128)(2,1)S(1)}, f16[256,1536]{1,0:T(8,128)(2,1)S(1)}, u32[]{:S(2)}, u32[]{:S(2)}) collective-permute-start(f16[256,1536]{1,0:T(8,128)(2,1)S(1)} %get-tuple-element.18), channel_id=1, source_target_pairs={{0,4},{4,8},{8,12},{1,5},{5,9},{9,13},{2,6},{6,10},{10,14},{3,7},{... | collective-permute-start | bytes 2359304 | tf_op jit(solution)/shard_map/ppermute | solution.py:79
  102.4 25.1 %collective-permute-start.13 = (f16[256,768]{1,0:T(8,128)(2,1)S(1)}, f16[256,768]{1,0:T(8,128)(2,1)S(1)}, u32[]{:S(2)}, u32[]{:S(2)}) collective-permute-start(f16[256,768]{1,0:T(8,128)(2,1)S(1)} %get-tuple-element.21), channel_id=1, source_target_pairs={{12,8},{8,4},{4,0},{13,9},{9,5},{5,1},{14,10},{10,6},{6,2},{15,11}... | collective-permute-start | bytes 1179656 | tf_op jit(solution)/shard_map/ppermute | solution.py:80
  103.7 24.7 %collective-permute-start.11 = (f16[256,768]{1,0:T(8,128)(2,1)S(1)}, f16[256,768]{1,0:T(8,128)(2,1)S(1)}, u32[]{:S(2)}, u32[]{:S(2)}) collective-permute-start(f16[256,768]{1,0:T(8,128)(2,1)S(1)} %get-tuple-element.20), channel_id=1, source_target_pairs={{0,4},{4,8},{8,12},{1,5},{5,9},{9,13},{2,6},{6,10},{10,14},{3,7},{... | collective-permute-start | bytes 1179656 | tf_op jit(solution)/shard_map/ppermute | solution.py:79
  121.5 7.9 %copy-start.1 = (bf16[256,768]{1,0:T(8,128)(2,1)}, bf16[256,768]{1,0:T(8,128)(2,1)S(1)}, u32[]{:S(2)}) copy-start(bf16[256,768]{1,0:T(8,128)(2,1)S(1)} %get-tuple-element.10.value_ref) | copy-start | bytes 1179652
  121.5 20.2 %collective-permute-start.19 = (bf16[256,768]{1,0:T(8,128)(2,1)}, bf16[256,768]{1,0:T(8,128)(2,1)S(1)}, u32[]{:S(2)}, u32[]{:S(2)}) collective-permute-start(bf16[256,768]{1,0:T(8,128)(2,1)} %get-tuple-element.9.key_ref), channel_id=1, source_target_pairs={{0,4},{4,0},{8,12},{12,8},{1,5},{5,1},{9,13},{13,9},{2,6},{6,2},{1... | collective-permute-start | bytes 1179656 | tf_op jit(solution)/shard_map/ppermute | solution.py:87
  123.9 17.7 %collective-permute-start.20 = (bf16[256,768]{1,0:T(8,128)(2,1)}, bf16[256,768]{1,0:T(8,128)(2,1)S(1)}, u32[]{:S(2)}, u32[]{:S(2)}) collective-permute-start(bf16[256,768]{1,0:T(8,128)(2,1)} %get-tuple-element.9.key_ref), channel_id=1, source_target_pairs={{4,8},{8,4},{5,9},{9,5},{6,10},{10,6},{7,11},{11,7},{20,24},{24,20... | collective-permute-start | bytes 1179656 | tf_op jit(solution)/shard_map/ppermute | solution.py:88
  124.6 17.1 %collective-permute-start.21 = (bf16[256,768]{1,0:T(8,128)(2,1)S(1)}, bf16[256,768]{1,0:T(8,128)(2,1)S(1)}, u32[]{:S(2)}, u32[]{:S(2)}) collective-permute-start(bf16[256,768]{1,0:T(8,128)(2,1)S(1)} %get-tuple-element.10.value_ref), channel_id=1, source_target_pairs={{0,4},{4,0},{8,12},{12,8},{1,5},{5,1},{9,13},{13,9},{2,6},{6,2},{1... | collective-permute-start | bytes 1179656 | tf_op jit(solution)/shard_map/ppermute | solution.py:87
  127.5 14.2 %collective-permute-start.22 = (bf16[256,768]{1,0:T(8,128)(2,1)S(1)}, bf16[256,768]{1,0:T(8,128)(2,1)S(1)}, u32[]{:S(2)}, u32[]{:S(2)}) collective-permute-start(bf16[256,768]{1,0:T(8,128)(2,1)S(1)} %get-tuple-element.10.value_ref), channel_id=1, source_target_pairs={{4,8},{8,4},{5,9},{9,5},{6,10},{10,6},{7,11},{11,7},{20,24},{24,20... | collective-permute-start | bytes 1179656 | tf_op jit(solution)/shard_map/ppermute | solution.py:88
  141.6 0.7 copy-start.12
  141.7 0.9 copy-start.10
  141.7 1.0 copy-start.6
  142.7 0.8 copy-start.8
  143.4 5.5 %collective-permute-start.23 = (bf16[256,2560]{1,0:T(8,128)(2,1)}, bf16[256,2560]{1,0:T(8,128)(2,1)S(1)}, u32[]{:S(2)}, u32[]{:S(2)}) collective-permute-start(bf16[256,2560]{1,0:T(8,128)(2,1)} %get-tuple-element.13), channel_id=1, source_target_pairs={{0,1},{1,0},{2,3},{3,2},{4,5},{5,4},{6,7},{7,6},{8,9},{9,8},{10,11... | collective-permute-start | bytes 3932168 | tf_op jit(solution)/shard_map/ppermute | solution.py:218
  143.4 1.4 copy-start.11
  143.4 3.4 %copy-start.9 = (bf16[256,768]{1,0:T(8,128)(2,1)S(1)}, bf16[256,768]{1,0:T(8,128)(2,1)}, u32[]{:S(2)}) copy-start(bf16[256,768]{1,0:T(8,128)(2,1)} %copy-done.8) | copy-start | bytes 1179652
  143.4 4.7 %copy-start.7 = (bf16[256,768]{1,0:T(8,128)(2,1)S(1)}, bf16[256,768]{1,0:T(8,128)(2,1)}, u32[]{:S(2)}) copy-start(bf16[256,768]{1,0:T(8,128)(2,1)} %copy-done.6) | copy-start | bytes 1179652
  143.4 5.5 %copy-start.4 = (f32[256,2560]{1,0:T(8,128)S(1)}, f32[256,2560]{1,0:T(8,128)}, u32[]{:S(2)}) copy-start(f32[256,2560]{1,0:T(8,128)} %get-tuple-element.11) | copy-start | bytes 7864324
  143.7 6.9 %copy-start.13 = (bf16[256,768]{1,0:T(8,128)(2,1)S(1)}, bf16[256,768]{1,0:T(8,128)(2,1)}, u32[]{:S(2)}) copy-start(bf16[256,768]{1,0:T(8,128)(2,1)} %copy-done.12) | copy-start | bytes 1179652
  144.9 13.8 %collective-permute-start.25 = (bf16[256,768]{1,0:T(8,128)(2,1)S(1)}, bf16[256,768]{1,0:T(8,128)(2,1)S(1)}, u32[]{:S(2)}, u32[]{:S(2)}) collective-permute-start(bf16[256,768]{1,0:T(8,128)(2,1)S(1)} %copy-done.11), channel_id=1, source_target_pairs={{4,0},{8,12},{5,1},{9,13},{6,2},{10,14},{7,3},{11,15},{20,16},{24,... | collective-permute-start | bytes 1179656 | tf_op jit(solution)/shard_map/ppermute | solution.py:96
  146.2 2.9 %collective-permute-start.26 = (bf16[256,768]{1,0:T(8,128)(2,1)}, bf16[256,768]{1,0:T(8,128)(2,1)S(1)}, u32[]{:S(2)}, u32[]{:S(2)}) collective-permute-start(bf16[256,768]{1,0:T(8,128)(2,1)} %copy-done.12), channel_id=1, source_target_pairs={{4,8},{8,4},{5,9},{9,5},{6,10},{10,6},{7,11},{11,7},{20,24},{24,20... | collective-permute-start | bytes 1179656 | tf_op jit(solution)/shard_map/ppermute | solution.py:95
  146.9 28.8 %collective-permute-start.28 = (bf16[256,768]{1,0:T(8,128)(2,1)S(1)}, bf16[256,768]{1,0:T(8,128)(2,1)S(1)}, u32[]{:S(2)}, u32[]{:S(2)}) collective-permute-start(bf16[256,768]{1,0:T(8,128)(2,1)S(1)} %copy-done.9), channel_id=1, source_target_pairs={{4,0},{8,12},{5,1},{9,13},{6,2},{10,14},{7,3},{11,15},{20,16},{24,... | collective-permute-start | bytes 1179656 | tf_op jit(solution)/shard_map/ppermute | solution.py:96
  148.2 11.2 %collective-permute-start.29 = (bf16[256,768]{1,0:T(8,128)(2,1)S(1)}, bf16[256,768]{1,0:T(8,128)(2,1)S(1)}, u32[]{:S(2)}, u32[]{:S(2)}) collective-permute-start(bf16[256,768]{1,0:T(8,128)(2,1)S(1)} %copy-done.7), channel_id=1, source_target_pairs={{4,8},{8,4},{5,9},{9,5},{6,10},{10,6},{7,11},{11,7},{20,24},{24,20... | collective-permute-start | bytes 1179656 | tf_op jit(solution)/shard_map/ppermute | solution.py:95
  149.1 26.5 %copy-start.2 = (bf16[256,768]{1,0:T(8,128)(2,1)S(1)}, bf16[256,768]{1,0:T(8,128)(2,1)}, u32[]{:S(2)}) copy-start(bf16[256,768]{1,0:T(8,128)(2,1)} %copy-done.1) | copy-start | bytes 1179652
  149.1 26.4 %collective-permute-start.27 = (bf16[256,768]{1,0:T(8,128)(2,1)S(1)}, bf16[256,768]{1,0:T(8,128)(2,1)S(1)}, u32[]{:S(2)}, u32[]{:S(2)}) collective-permute-start(bf16[256,768]{1,0:T(8,128)(2,1)S(1)} %collective-permute-done.26), channel_id=1, source_target_pairs={{4,0},{8,12},{5,1},{9,13},{6,2},{10,14},{7,3},{11,15},{20,16},{24,... | collective-permute-start | bytes 1179656 | tf_op jit(solution)/shard_map/ppermute | solution.py:97
  158.8 24.9 %collective-permute-start.24 = (bf16[256,1280]{1,0:T(8,128)(2,1)S(1)}, bf16[256,1280]{1,0:T(8,128)(2,1)S(1)}, u32[]{:S(2)}, u32[]{:S(2)}) collective-permute-start(bf16[256,1280]{1,0:T(8,128)(2,1)S(1)} %add_convert_fusion.4), channel_id=1, source_target_pairs={{0,2},{1,3},{2,0},{3,1},{4,6},{5,7},{6,4},{7,5},{8,10},{9,11},{10,... | collective-permute-start | bytes 1966088 | tf_op jit(solution)/shard_map/ppermute | solution.py:229
  159.4 24.1 %collective-permute-start.30 = (bf16[256,768]{1,0:T(8,128)(2,1)S(1)}, bf16[256,768]{1,0:T(8,128)(2,1)S(1)}, u32[]{:S(2)}, u32[]{:S(2)}) collective-permute-start(bf16[256,768]{1,0:T(8,128)(2,1)S(1)} %collective-permute-done.29), channel_id=1, source_target_pairs={{4,0},{8,12},{5,1},{9,13},{6,2},{10,14},{7,3},{11,15},{20,16},{24,... | collective-permute-start | bytes 1179656 | tf_op jit(solution)/shard_map/ppermute | solution.py:97
  183.7 1.9 %copy-start.3 = (bf16[2,1024,768]{2,1,0:T(8,128)(2,1)}, bf16[2,1024,768]{2,1,0:T(8,128)(2,1)S(1)}, u32[]{:S(2)}) copy-start(bf16[2,1024,768]{2,1,0:T(8,128)(2,1)S(1)} %bitcast_dynamic-update-slice_fusion) | copy-start | bytes 9437188
